TPU v7x, 32 devices: a whole 2x2x4 slice. The times are simulated.
32 devices in a mesh: grp: 2 (over x), slab: 16 (over z, y, core).
Axes of the slice: x: 2, y: 2, z: 4, core: 2. Of those that a mesh axis runs over, the one named last changes fastest.
Arguments:
- directions: float32 [8, 64, 256, 128], P('grp', 'slab'), parts along dimension 0, may hold values from -36 to 36
- eigen_basis: float32 [32, 64, 256, 128], P('grp', 'slab'), parts along dimension 0, may hold values from -11 to 11
- flow_first: float32 [64, 256, 128], P('slab'), may hold values from -0.15 to 0.15
- flow_second: float32 [64, 256, 128], P('slab'), may hold values from -0.15 to 0.15
- flow_depth: float32 [64, 256, 128], P('slab'), may hold values from -0.15 to 0.15
- face_codes: int32 [4], replicated, may hold values from 0 to 1
- sensor_cells: int32 [131072], P(('grp', 'slab')), parts along dimension 0, may hold values from 0 to 131071
- sensor_weight: float32 [131072], P(('grp', 'slab')), parts along dimension 0, may hold values from 0.5 to 4
Outputs:
- new_directions: float32 [8, 64, 256, 128], P('grp', 'slab'), parts along dimension 0
- coeffs: float32 [32, 4], P('grp'), parts along dimension 0
There are 2 independent parts, one for each index of `grp`. A program takes and returns all parts, laid end to end along the dimension named above; an argument that names none is the same for every part. Nothing has to cross between parts.
Inputs may be any that keep to these rules, and one draw needn't show every extreme that they name: `face_codes`: 0 marks a face with zero boundary values, 1 a closed face. `sensor_cells`: block b of 4096 entries lies in planes b * 4 to (b + 1) * 4 - 1 and holds offsets counted from that block's first cell.
All inputs are finite; a program needn't handle non-finite values.
Results may differ from a plain program's by a relative error of at most 0.00015.
Values sent between devices are 32-bit elements; how exact they have to be, the bound alone decides.
No kernel may reach another device: no remote copies, remote signals or barrier semaphores. Data moves between devices by JAX's collectives and lax.ppermute only.
A program may use at most 128 MiB of HBM per device.

v0:
```python
import functools

import jax
import jax.numpy as jnp
from jax import lax
from jax.experimental import pallas as pl
from jax.experimental.pallas import tpu as pltpu
from jax.sharding import PartitionSpec as P

STEPS = 2
SWEEPS = 3


DIFFUSION = 0.2
GAMMA = 0.5


def from_behind(value, axis, steps):
    count = lax.axis_size(axis)
    first, last = (max(0, -steps), min(count, count - steps))
    return lax.ppermute(value, axis, [(source, source + steps) for source in range(first, last)])


def extended(cells, sides, width):
    for axis, dim in sides:
        count = lax.axis_size(axis)
        ends = count - 1
        head = lax.slice_in_dim(cells, 0, width, axis=dim)
        tail = lax.slice_in_dim(cells, cells.shape[dim] - width, cells.shape[dim], axis=dim)
        cells = jnp.concatenate(
            [
                lax.ppermute(tail, axis, [(i, (i + 1) % count) for i in range(ends)]),
                cells,
                lax.ppermute(head, axis, [((i + 1) % count, i) for i in range(ends)]),
            ],
            axis=dim,
        )
    return cells


def lower_along(values, dimension):
    length = values.shape[dimension]
    leading = jnp.zeros_like(lax.slice_in_dim(values, 0, 1, axis=dimension))
    return jnp.concatenate(
        [leading, lax.slice_in_dim(values, 0, length - 1, axis=dimension)], dimension
    )


def end_factors(code_start, code_end, length):
    position = jnp.arange(length)
    open_start = jnp.where(code_start == 0, 1.0, 0.0).astype(jnp.float32)
    open_end = jnp.where(code_end == 0, 1.0, 0.0).astype(jnp.float32)
    at_start = jnp.where(position == 0, open_start, 1.0)
    at_end = jnp.where(position == length - 1, open_end, 1.0)
    return (at_start, at_end)


def diagonal_of(flows, face_codes):
    flow_first, first_below, flow_second, second_below, flow_depth, depth_below = flows
    start_one, end_one = end_factors(face_codes[0], face_codes[1], flow_first.shape[1])
    start_two, end_two = end_factors(face_codes[2], face_codes[3], flow_first.shape[2])
    start_one = start_one[None, :, None]
    end_one = end_one[None, :, None]
    start_two = start_two[None, None, :]
    end_two = end_two[None, None, :]
    diagonal = 1.0 + end_one * (DIFFUSION + jax.nn.relu(flow_first))
    diagonal = diagonal + start_one * (DIFFUSION + jax.nn.relu(-first_below))
    diagonal = diagonal + end_two * (DIFFUSION + jax.nn.relu(flow_second))
    diagonal = diagonal + start_two * (DIFFUSION + jax.nn.relu(-second_below))
    diagonal = diagonal + (DIFFUSION + jax.nn.relu(flow_depth))
    diagonal = diagonal + (DIFFUSION + jax.nn.relu(-depth_below))
    return diagonal


def neighbor_sum(padded, flows, adjoint):
    flow_first, first_below, flow_second, second_below, flow_depth, depth_below = flows
    orient = 1.0 if adjoint else -1.0
    middle = padded[:, 1:-1]
    along_first = jnp.pad(middle, ((0, 0), (0, 0), (1, 1), (0, 0)))
    along_second = jnp.pad(middle, ((0, 0), (0, 0), (0, 0), (1, 1)))
    summed = (DIFFUSION + jax.nn.relu(orient * flow_first)) * along_first[:, :, 2:]
    summed = summed + (DIFFUSION + jax.nn.relu(-orient * first_below)) * along_first[:, :, :-2]
    summed = summed + (DIFFUSION + jax.nn.relu(orient * flow_second)) * along_second[:, :, :, 2:]
    summed = summed + (DIFFUSION + jax.nn.relu(-orient * second_below)) * along_second[:, :, :, :-2]
    summed = summed + (DIFFUSION + jax.nn.relu(orient * flow_depth)) * padded[:, 2:]
    summed = summed + (DIFFUSION + jax.nn.relu(-orient * depth_below)) * padded[:, :-2]
    return summed


LANES = 128
EXACT = lax.Precision.HIGHEST


def lane_sums(stack):
    ones = jnp.ones((8, LANES), jnp.float32)
    return lax.dot_general(
        ones, stack, (((1,), (1,)), ((), ())), precision=EXACT, preferred_element_type=jnp.float32
    )


def gram_kernel(basis_ref, out_ref, acc_ref):
    rank = basis_ref.shape[0]
    rows = basis_ref.shape[1]
    step = pl.program_id(0)
    tile = 4

    @pl.when(step == 0)
    def _():
        acc_ref[...] = jnp.zeros_like(acc_ref)

    for i0 in range(0, rank, tile):
        for j0 in range(i0, rank, tile):
            pairs = [(i, j) for i in range(i0, i0 + tile) for j in range(j0, j0 + tile) if i <= j]

            def add(k, sums, i0=i0, j0=j0, pairs=pairs):
                at = pl.ds(pl.multiple_of(k * 8, 8), 8)
                left = {i: basis_ref[i, at, :] for i in range(i0, i0 + tile)}
                right = left if i0 == j0 else {j: basis_ref[j, at, :] for j in range(j0, j0 + tile)}
                return [s + left[i] * right[j] for s, (i, j) in zip(sums, pairs)]

            sums = [jnp.zeros((8, LANES), jnp.float32) for _ in pairs]
            sums = lax.fori_loop(0, rows // 8, add, sums, unroll=4)
            for (i, j), s in zip(pairs, sums):
                acc_ref[i, j] += s

    @pl.when(step == pl.num_programs(0) - 1)
    def _():
        row = lax.broadcasted_iota(jnp.int32, (rank, rank), 0)
        col = lax.broadcasted_iota(jnp.int32, (rank, rank), 1)
        gram = jnp.zeros((rank, rank), jnp.float32)
        for i in range(rank):
            sums = lane_sums(jnp.sum(acc_ref[i], axis=1))
            gram = jnp.where(row == i, jnp.broadcast_to(sums[0:1, :], (rank, rank)), gram)
        upper = jnp.where(col >= row, gram, 0.0)
        strict = jnp.where(col > row, gram, 0.0)
        whole = upper + strict.T
        for r in range(out_ref.shape[0] // rank):
            out_ref[r * rank : (r + 1) * rank, 0:rank] = whole


def gram_parts(basis, count):
    rank, rows, _ = basis.shape
    chunk = 128
    return pl.pallas_call(
        gram_kernel,
        grid=(rows // chunk,),
        in_specs=[pl.BlockSpec((rank, chunk, LANES), lambda k: (0, k, 0))],
        out_specs=pl.BlockSpec((count * rank, LANES), lambda k: (0, 0)),
        out_shape=jax.ShapeDtypeStruct((count * rank, LANES), jnp.float32),
        scratch_shapes=[pltpu.VMEM((rank, rank, 8, LANES), jnp.float32)],
        compiler_params=pltpu.CompilerParams(vmem_limit_bytes=32 << 20),
        cost_estimate=pl.CostEstimate(
            flops=rank * rank * rows * LANES, bytes_accessed=rank * rows * LANES * 4, transcendentals=0
        ),
        name="gram",
    )(basis)


def spread(tile, count):
    return lax.all_to_all(tile, "slab", 0, 0, tiled=True) if count > 1 else tile


def projection_kernel(basis_ref, image_ref, out_ref, acc_ref):
    rank = basis_ref.shape[0]
    dirs, rows, _ = image_ref.shape
    step = pl.program_id(0)
    tile = 8

    @pl.when(step == 0)
    def _():
        acc_ref[...] = jnp.zeros_like(acc_ref)

    for i0 in range(0, rank, tile):

        def add(k, sums, i0=i0):
            at = pl.ds(pl.multiple_of(k * 8, 8), 8)
            image = [image_ref[d, at, :] for d in range(dirs)]
            out = []
            for i in range(tile):
                q = basis_ref[i0 + i, at, :]
                out += [sums[i * dirs + d] + q * image[d] for d in range(dirs)]
            return out

        sums = [jnp.zeros((8, LANES), jnp.float32) for _ in range(tile * dirs)]
        sums = lax.fori_loop(0, rows // 8, add, sums, unroll=4)
        for i in range(tile):
            for d in range(dirs):
                acc_ref[d, i0 + i] += sums[i * dirs + d]

    @pl.when(step == pl.num_programs(0) - 1)
    def _():
        row = lax.broadcasted_iota(jnp.int32, (8, rank), 0)
        table = jnp.zeros((8, rank), jnp.float32)
        for d in range(dirs):
            table = jnp.where(row == d, lane_sums(jnp.sum(acc_ref[d], axis=1)), table)
        for r in range(out_ref.shape[0] // 8):
            out_ref[r * 8 : (r + 1) * 8, 0:rank] = table


def projection_parts(basis, image, count):
    rank, rows, _ = basis.shape
    dirs = image.shape[0]
    chunk = 128
    return pl.pallas_call(
        projection_kernel,
        grid=(rows // chunk,),
        in_specs=[
            pl.BlockSpec((rank, chunk, LANES), lambda k: (0, k, 0)),
            pl.BlockSpec((dirs, chunk, LANES), lambda k: (0, k, 0)),
        ],
        out_specs=pl.BlockSpec((count * 8, LANES), lambda k: (0, 0)),
        out_shape=jax.ShapeDtypeStruct((count * 8, LANES), jnp.float32),
        scratch_shapes=[pltpu.VMEM((dirs, rank, 8, LANES), jnp.float32)],
        compiler_params=pltpu.CompilerParams(vmem_limit_bytes=32 << 20),
        cost_estimate=pl.CostEstimate(
            flops=2 * rank * dirs * rows * LANES,
            bytes_accessed=(rank + dirs) * rows * LANES * 4,
            transcendentals=0,
        ),
        name="projections",
    )(basis, image)


def summed_tile(parts_ref):
    total = parts_ref[0:8, :]
    for r in range(1, parts_ref.shape[0] // 8):
        total = total + parts_ref[r * 8 : (r + 1) * 8, :]
    return total


def remainder_kernel(
    parts_ref, inverse_ref, basis_ref, image_ref, rem_ref, coeffs_ref, out_ref, splat_ref, energy_ref
):
    rank = basis_ref.shape[0]
    dirs, rows, _ = image_ref.shape
    step = pl.program_id(0)
    tile = 4

    @pl.when(step == 0)
    def _():
        table = summed_tile(parts_ref)[:, 0:rank]
        inverse = inverse_ref[...]
        half = lax.dot_general(
            table, inverse, (((1,), (1,)), ((), ())), precision=EXACT,
            preferred_element_type=jnp.float32,
        )
        flat = lax.dot_general(
            half, inverse, (((1,), (0,)), ((), ())), precision=EXACT,
            preferred_element_type=jnp.float32,
        )
        coeffs_ref[...] = flat.T[:, 0:dirs]
        for d in range(dirs):
            for j in range(rank):
                splat_ref[d * rank + j] = jnp.broadcast_to(flat[d : d + 1, j : j + 1], (8, LANES))
        energy_ref[...] = jnp.zeros_like(energy_ref)

    for j0 in range(0, rank, tile):
        last = j0 + tile == rank
        weights = [[splat_ref[d * rank + j] for j in range(j0, j0 + tile)] for d in range(dirs)]

        def take(k, energy, j0=j0, last=last, weights=weights):
            at = pl.ds(pl.multiple_of(k * 8, 8), 8)
            basis = [basis_ref[j, at, :] for j in range(j0, j0 + tile)]
            out = []
            for d in range(dirs):
                left = image_ref[d, at, :] if j0 == 0 else rem_ref[d, at, :]
                parts = [w * q for w, q in zip(weights[d], basis)]
                left = left - ((parts[0] + parts[1]) + (parts[2] + parts[3]))
                rem_ref[d, at, :] = left
                out.append(energy[d] + left * left if last else energy[d])
            return out

        energy = [jnp.zeros((8, LANES), jnp.float32) for _ in range(dirs)]
        energy = lax.fori_loop(0, rows // 8, take, energy, unroll=4)
        if last:
            for d in range(dirs):
                energy_ref[d] += energy[d]

    @pl.when(step == pl.num_programs(0) - 1)
    def _():
        row = lax.broadcasted_iota(jnp.int32, (8, LANES), 0)
        tile_out = jnp.zeros((8, LANES), jnp.float32)
        for d in range(dirs):
            total = jnp.sum(jnp.sum(energy_ref[d], axis=0, keepdims=True), axis=1, keepdims=True)
            tile_out = jnp.where(row == d, jnp.broadcast_to(total, (8, LANES)), tile_out)
        for r in range(out_ref.shape[0] // 8):
            out_ref[r * 8 : (r + 1) * 8, :] = tile_out


def remainders(parts, inverse, basis, image, count):
    rank, rows, _ = basis.shape
    dirs = image.shape[0]
    chunk = 128
    whole = lambda *shape: pl.BlockSpec(shape, lambda k: (0,) * len(shape))
    return pl.pallas_call(
        remainder_kernel,
        grid=(rows // chunk,),
        in_specs=[
            whole(count * 8, LANES),
            whole(rank, rank),
            pl.BlockSpec((rank, chunk, LANES), lambda k: (0, k, 0)),
            pl.BlockSpec((dirs, chunk, LANES), lambda k: (0, k, 0)),
        ],
        out_specs=[
            pl.BlockSpec((dirs, chunk, LANES), lambda k: (0, k, 0)),
            whole(rank, dirs),
            whole(count * 8, LANES),
        ],
        out_shape=[
            jax.ShapeDtypeStruct((dirs, rows, LANES), jnp.float32),
            jax.ShapeDtypeStruct((rank, dirs), jnp.float32),
            jax.ShapeDtypeStruct((count * 8, LANES), jnp.float32),
        ],
        scratch_shapes=[
            pltpu.VMEM((dirs * rank, 8, LANES), jnp.float32),
            pltpu.VMEM((dirs, 8, LANES), jnp.float32),
        ],
        compiler_params=pltpu.CompilerParams(vmem_limit_bytes=32 << 20),
        cost_estimate=pl.CostEstimate(
            flops=2 * rank * dirs * rows * LANES,
            bytes_accessed=(rank + 2 * dirs) * rows * LANES * 4,
            transcendentals=0,
        ),
        name="remainder",
    )(parts, inverse, basis, image)


def scale_kernel(cells, parts_ref, rem_ref, new_ref):
    energy = summed_tile(parts_ref)
    value = energy / cells + 1e-06
    root = lax.rsqrt(value)
    root = root * (1.5 - (0.5 * value * root) * root)
    for d in range(rem_ref.shape[0]):
        new_ref[d] = rem_ref[d] * root[d : d + 1, :]


def scaled(parts, rem, cells, count):
    dirs, rows, _ = rem.shape
    chunk = 256
    return pl.pallas_call(
        functools.partial(scale_kernel, cells),
        grid=(rows // chunk,),
        in_specs=[
            pl.BlockSpec((count * 8, LANES), lambda k: (0, 0)),
            pl.BlockSpec((dirs, chunk, LANES), lambda k: (0, k, 0)),
        ],
        out_specs=pl.BlockSpec((dirs, chunk, LANES), lambda k: (0, k, 0)),
        out_shape=jax.ShapeDtypeStruct((dirs, rows, LANES), jnp.float32),
        compiler_params=pltpu.CompilerParams(vmem_limit_bytes=32 << 20),
        name="scale",
    )(parts, rem)


def sensor_kernel(first_row, planes, width, cells_ref, weight_ref, out_ref):
    height = out_ref.shape[0] // planes
    first = first_row if isinstance(first_row, int) else first_row()
    sensors = cells_ref.shape[1]
    chunk = 512
    targets = out_ref.shape[0]
    rows = lax.broadcasted_iota(jnp.int32, (targets, chunk), 0)
    lanes = lax.broadcasted_iota(jnp.int32, (LANES, chunk), 0)
    total = jnp.zeros((targets, 3 * LANES), jnp.float32)
    for k in range(sensors // chunk):
        cell = cells_ref[0:1, k * chunk : (k + 1) * chunk]
        weight = weight_ref[0:1, k * chunk : (k + 1) * chunk]
        line = cell // LANES
        lane = cell - line * LANES
        plane = line // width
        row = line - plane * width - first
        inside = (row >= 0) & (row < height)
        target = jnp.where(inside, plane * height + row, -1)
        high = weight.astype(jnp.bfloat16).astype(jnp.float32)
        rest = weight - high
        middle = rest.astype(jnp.bfloat16).astype(jnp.float32)
        low = rest - middle
        hot = jnp.where(rows == target, 1.0, 0.0).astype(jnp.bfloat16)
        here = lanes == lane
        parts = [jnp.where(here, part, 0.0).astype(jnp.bfloat16) for part in (high, middle, low)]
        total += lax.dot_general(
            hot, jnp.concatenate(parts, 0), (((1,), (1,)), ((), ())),
            preferred_element_type=jnp.float32,
        )
    out_ref[...] = total[:, 0:LANES] + total[:, LANES : 2 * LANES] + total[:, 2 * LANES :]


def sensor_weights(cells, weights, planes, width):
    targets = planes * width
    return pl.pallas_call(
        functools.partial(sensor_kernel, 0, planes, width),
        out_shape=jax.ShapeDtypeStruct((targets, LANES), jnp.float32),
        compiler_params=pltpu.CompilerParams(vmem_limit_bytes=32 << 20),
        name="sensors",
    )(cells[None], weights[None])


def body(
    directions,
    eigen_basis,
    flow_first,
    flow_second,
    flow_depth,
    face_codes,
    sensor_cells,
    sensor_weight,
):
    planes = directions.shape[1]
    slab_count = lax.axis_size("slab")
    top_faces = from_behind(flow_depth[-1:], "slab", 1)
    depth_below = jnp.concatenate([top_faces, flow_depth[:-1]], 0)
    first_below = lower_along(flow_first, 1)
    second_below = lower_along(flow_second, 2)
    flows = (flow_first, first_below, flow_second, second_below, flow_depth, depth_below)
    diagonal = diagonal_of(flows, face_codes)

    def solve(rhs, adjoint):
        iterate = rhs
        for repeat in range(SWEEPS):
            padded = extended(iterate, (("slab", 1),), 1)
            iterate = (rhs + neighbor_sum(padded, flows, adjoint)) / diagonal
        return iterate

    rank = eigen_basis.shape[0]
    dirs, _, width, _ = directions.shape
    basis = eigen_basis.reshape(rank, planes * width, LANES)
    gram = spread(gram_parts(basis, slab_count), slab_count)
    gram = jnp.sum(gram.reshape(slab_count, rank, LANES), 0)[:, :rank]
    factor_lower = jnp.linalg.cholesky(gram)
    inverse = lax.linalg.triangular_solve(
        factor_lower, jnp.eye(rank, dtype=jnp.float32), left_side=True, lower=True
    )
    cell_weight = sensor_weights(sensor_cells, sensor_weight, planes, width)
    state = jnp.zeros_like(directions)
    for moment in range(STEPS):
        state = solve(state + directions, False)
    forcing = state * cell_weight.reshape(state.shape[1:])[None]
    adjoint_state = forcing
    summed = jnp.zeros_like(directions)
    for moment in range(STEPS):
        adjoint_state = solve(adjoint_state, True)
        summed = summed + adjoint_state
    image = (summed + GAMMA * directions).reshape(dirs, planes * width, LANES)
    parts = spread(projection_parts(basis, image, slab_count), slab_count)
    rem, coeffs, parts = remainders(parts, inverse, basis, image, slab_count)
    total_cells = planes * slab_count * width * LANES
    new_directions = scaled(spread(parts, slab_count), rem, total_cells, slab_count)
    return (new_directions.reshape(directions.shape), coeffs)


def solution(mesh):
    return jax.shard_map(
        body,
        mesh=mesh,
        in_specs=(
            P("grp", "slab", None, None),
            P("grp", "slab", None, None),
            P("slab", None, None),
            P("slab", None, None),
            P("slab", None, None),
            P(),
            P(("grp", "slab")),
            P(("grp", "slab")),
        ),
        out_specs=(P("grp", "slab", None, None), P("grp", None)),
        check_vma=False,
    )
```

profile of v0, /device:TPU:0, one launch (start us, length us, event | category | flops | bytes accessed | tf_op | source)
XLA Modules:
  0.0 287.2 jit_solution(7770503370214212593)
XLA Ops:
  6.7 5.2 %collective-permute-start.2 = (f32[4,1,256,128]{3,2,1,0:T(8,128)S(1)}, f32[4,1,256,128]{3,2,1,0:T(8,128)S(1)}, u32[]{:S(2)}, u32[]{:S(2)}) collective-permute-start(f32[4,1,256,128]{3,2,1,0:T(8,128)S(1)} %get-tuple-element.35), channel_id=1, source_target_pairs={{0,1},{1,2},{2,3},{3,4},{4,5},{5,6},{6,7},{7,8},{8,9},{9,10},{10,1... | collective-permute-start | bytes 1572872 | tf_op jit(solution)/shard_map/ppermute | solution.py:32
  20.2 10.1 %collective-permute-start.4 = (f32[4,1,256,128]{3,2,1,0:T(8,128)S(1)}, f32[4,1,256,128]{3,2,1,0:T(8,128)S(1)}, u32[]{:S(2)}, u32[]{:S(2)}) collective-permute-start(f32[4,1,256,128]{3,2,1,0:T(8,128)S(1)} %get-tuple-element.33), channel_id=1, source_target_pairs={{0,1},{1,2},{2,3},{3,4},{4,5},{5,6},{6,7},{7,8},{8,9},{9,10},{10,1... | collective-permute-start | bytes 1572872 | tf_op jit(solution)/shard_map/ppermute | solution.py:32
  35.2 10.6 %collective-permute-start.6 = (f32[4,1,256,128]{3,2,1,0:T(8,128)S(1)}, f32[4,1,256,128]{3,2,1,0:T(8,128)S(1)}, u32[]{:S(2)}, u32[]{:S(2)}) collective-permute-start(f32[4,1,256,128]{3,2,1,0:T(8,128)S(1)} %get-tuple-element.31), channel_id=1, source_target_pairs={{0,1},{1,2},{2,3},{3,4},{4,5},{5,6},{6,7},{7,8},{8,9},{9,10},{10,1... | collective-permute-start | bytes 1572872 | tf_op jit(solution)/shard_map/ppermute | solution.py:32
  50.8 12.3 %collective-permute-start.8 = (f32[4,1,256,128]{3,2,1,0:T(8,128)S(1)}, f32[4,1,256,128]{3,2,1,0:T(8,128)S(1)}, u32[]{:S(2)}, u32[]{:S(2)}) collective-permute-start(f32[4,1,256,128]{3,2,1,0:T(8,128)S(1)} %get-tuple-element.29), channel_id=1, source_target_pairs={{0,1},{1,2},{2,3},{3,4},{4,5},{5,6},{6,7},{7,8},{8,9},{9,10},{10,1... | collective-permute-start | bytes 1572872 | tf_op jit(solution)/shard_map/ppermute | solution.py:32
  66.6 10.0 %collective-permute-start.10 = (f32[4,1,256,128]{3,2,1,0:T(8,128)S(1)}, f32[4,1,256,128]{3,2,1,0:T(8,128)S(1)}, u32[]{:S(2)}, u32[]{:S(2)}) collective-permute-start(f32[4,1,256,128]{3,2,1,0:T(8,128)S(1)} %get-tuple-element.27), channel_id=1, source_target_pairs={{0,1},{1,2},{2,3},{3,4},{4,5},{5,6},{6,7},{7,8},{8,9},{9,10},{10,1... | collective-permute-start | bytes 1572872 | tf_op jit(solution)/shard_map/ppermute | solution.py:32
  78.1 4.3 %collective-permute-done.9 = f32[4,1,256,128]{3,2,1,0:T(8,128)S(1)} collective-permute-done((f32[4,1,256,128]{3,2,1,0:T(8,128)S(1)}, f32[4,1,256,128]{3,2,1,0:T(8,128)S(1)}, u32[]{:S(2)}, u32[]{:S(2)}) %collective-permute-start.9) | collective-permute-done | bytes 524320 | tf_op jit(solution)/shard_map/ppermute | solution.py:34
  85.8 9.9 %collective-permute-start.12 = (f32[4,1,256,128]{3,2,1,0:T(8,128)S(1)}, f32[4,1,256,128]{3,2,1,0:T(8,128)S(1)}, u32[]{:S(2)}, u32[]{:S(2)}) collective-permute-start(f32[4,1,256,128]{3,2,1,0:T(8,128)S(1)} %get-tuple-element.25), channel_id=1, source_target_pairs={{0,1},{1,2},{2,3},{3,4},{4,5},{5,6},{6,7},{7,8},{8,9},{9,10},{10,1... | collective-permute-start | bytes 1572872 | tf_op jit(solution)/shard_map/ppermute | solution.py:32
  95.8 4.6 %sensors.1 = f32[1024,128]{1,0:T(8,128)S(1)} custom-call(s32[1,4096]{1,0:T(1,128)S(1)} %bitcast.38, f32[1,4096]{1,0:T(1,128)S(1)} %bitcast.39), custom_call_target="tpu_custom_call" | custom-call | tf_op jit(solution)/shard_map/sensors/pallas_call | solution.py:388
  103.9 11.2 %collective-permute-start.14 = (f32[4,1,256,128]{3,2,1,0:T(8,128)S(1)}, f32[4,1,256,128]{3,2,1,0:T(8,128)S(1)}, u32[]{:S(2)}, u32[]{:S(2)}) collective-permute-start(f32[4,1,256,128]{3,2,1,0:T(8,128)S(1)} %get-tuple-element.23), channel_id=1, source_target_pairs={{0,1},{1,2},{2,3},{3,4},{4,5},{5,6},{6,7},{7,8},{8,9},{9,10},{10,1... | collective-permute-start | bytes 1572872 | tf_op jit(solution)/shard_map/ppermute | solution.py:32
  119.9 12.2 %collective-permute-start.16 = (f32[4,1,256,128]{3,2,1,0:T(8,128)S(1)}, f32[4,1,256,128]{3,2,1,0:T(8,128)S(1)}, u32[]{:S(2)}, u32[]{:S(2)}) collective-permute-start(f32[4,1,256,128]{3,2,1,0:T(8,128)S(1)} %get-tuple-element.21), channel_id=1, source_target_pairs={{0,1},{1,2},{2,3},{3,4},{4,5},{5,6},{6,7},{7,8},{8,9},{9,10},{10,1... | collective-permute-start | bytes 1572872 | tf_op jit(solution)/shard_map/ppermute | solution.py:32
  137.0 10.7 %collective-permute-start.18 = (f32[4,1,256,128]{3,2,1,0:T(8,128)S(1)}, f32[4,1,256,128]{3,2,1,0:T(8,128)S(1)}, u32[]{:S(2)}, u32[]{:S(2)}) collective-permute-start(f32[4,1,256,128]{3,2,1,0:T(8,128)S(1)} %get-tuple-element.19), channel_id=1, source_target_pairs={{0,1},{1,2},{2,3},{3,4},{4,5},{5,6},{6,7},{7,8},{8,9},{9,10},{10,1... | collective-permute-start | bytes 1572872 | tf_op jit(solution)/shard_map/ppermute | solution.py:32
  152.9 12.3 %collective-permute-start.20 = (f32[4,1,256,128]{3,2,1,0:T(8,128)S(1)}, f32[4,1,256,128]{3,2,1,0:T(8,128)S(1)}, u32[]{:S(2)}, u32[]{:S(2)}) collective-permute-start(f32[4,1,256,128]{3,2,1,0:T(8,128)S(1)} %get-tuple-element.17), channel_id=1, source_target_pairs={{0,1},{1,2},{2,3},{3,4},{4,5},{5,6},{6,7},{7,8},{8,9},{9,10},{10,1... | collective-permute-start | bytes 1572872 | tf_op jit(solution)/shard_map/ppermute | solution.py:32
  171.2 11.5 %collective-permute-start.22 = (f32[4,1,256,128]{3,2,1,0:T(8,128)}, f32[4,1,256,128]{3,2,1,0:T(8,128)}, u32[]{:S(2)}, u32[]{:S(2)}) collective-permute-start(f32[4,1,256,128]{3,2,1,0:T(8,128)} %get-tuple-element.15), channel_id=1, source_target_pairs={{0,1},{1,2},{2,3},{3,4},{4,5},{5,6},{6,7},{7,8},{8,9},{9,10},{10,1... | collective-permute-start | bytes 1572872 | tf_op jit(solution)/shard_map/ppermute | solution.py:32
  182.8 7.8 %gram.1 = f32[256,128]{1,0:T(8,128)S(1)} custom-call(f32[16,1024,128]{2,1,0:T(8,128)S(1)} %bitcast.29), custom_call_target="tpu_custom_call" | custom-call | flops 33554432 | bytes 8388608 | tf_op jit(solution)/shard_map/gram/pallas_call | solution.py:144
  190.6 21.4 %all_to_all.31 = f32[16,16,128]{2,1,0:T(8,128)S(1)} all-to-all(f32[16,16,128]{2,1,0:T(8,128)S(1)} %bitcast.35), channel_id=1, replica_groups=mesh['grp'=2,'slab'=16] {'slab'}, dimensions={0} | all-to-all | bytes 262144 | tf_op jit(solution)/shard_map/all_to_all | solution.py:160
  212.2 7.2 %fusion.87 = f32[4,4,256,128]{3,2,1,0:T(8,128)S(1)} fusion(f32[4,4,256,128]{3,2,1,0:T(8,128)S(1)} %fusion.71, f32[4,4,256,128]{3,2,1,0:T(8,128)} %copy-done.14, f32[4,1,256,128]{3,2,1,0:T(8,128)} %collective-permute-done.22, f32[4,1,256,128]{3,2,1,0:T(8,128)} %collective-permute-done.21, f32[4,256,128]{2,1,0:T(8,128)} %copy-done.12, ...), kind=kLoop, calls=%fused_computation.111 | loop fusion | flops 7864320 | bytes 11010048 | tf_op jit(solution)/shard_map/div | solution.py:419
  222.1 3.9 %collective-permute-start.24 = (f32[4,1,256,128]{3,2,1,0:T(8,128)S(1)}, f32[4,1,256,128]{3,2,1,0:T(8,128)}, u32[]{:S(2)}, u32[]{:S(2)}) collective-permute-start(f32[4,1,256,128]{3,2,1,0:T(8,128)S(1)} %get-tuple-element.13), channel_id=1, source_target_pairs={{0,1},{1,2},{2,3},{3,4},{4,5},{5,6},{6,7},{7,8},{8,9},{9,10},{10,1... | collective-permute-start | bytes 1572872 | tf_op jit(solution)/shard_map/ppermute | solution.py:32
  230.8 8.4 %fusion.97 = f32[4,4,256,128]{3,2,1,0:T(8,128)S(1)} fusion(f32[4,4,256,128]{3,2,1,0:T(8,128)} %copy-done.7, f32[4,4,256,128]{3,2,1,0:T(8,128)} %copy-done.13, f32[4,1,256,128]{3,2,1,0:T(8,128)} %collective-permute-done.24, f32[4,1,256,128]{3,2,1,0:T(8,128)} %copy-done.18, f32[4,4,256,128]{3,2,1,0:T(8,128)} %param.8, f32[4,256,128]{2,1,0:T(8,128)} %copy-done.12, ...), kind=kLoop, calls=%fused_computation.121 | loop fusion | flops 9437184 | bytes 13107200 | tf_op jit(solution)/shard_map/add | solution.py:441
  242.6 4.7 %projections.1 = f32[128,128]{1,0:T(8,128)} custom-call(f32[16,1024,128]{2,1,0:T(8,128)S(1)} %bitcast.30, f32[4,1024,128]{2,1,0:T(8,128)S(1)} %bitcast.32), custom_call_target="tpu_custom_call" | custom-call | flops 16777216 | bytes 10485760 | tf_op jit(solution)/shard_map/projections/pallas_call | solution.py:204
  247.3 9.1 %all-to-all-start = ((f32[16,8,128]{2,1,0:T(8,128)}), f32[16,8,128]{2,1,0:T(8,128)S(1)}, u32[]{:S(2)}, u32[]{:S(2)}) async-start(f32[16,8,128]{2,1,0:T(8,128)} %bitcast.9), calls=%async_computation | async-start | bytes 131072 | tf_op jit(solution)/shard_map/all_to_all | solution.py:160
  256.6 6.7 %all-to-all-done = f32[16,8,128]{2,1,0:T(8,128)S(1)} async-done(((f32[16,8,128]{2,1,0:T(8,128)}), f32[16,8,128]{2,1,0:T(8,128)S(1)}, u32[]{:S(2)}, u32[]{:S(2)}) %all-to-all-start) | async-done | bytes 65568 | tf_op jit(solution)/shard_map/all_to_all | solution.py:160
  266.7 5.2 %remainder.1 = (f32[4,1024,128]{2,1,0:T(8,128)S(1)}, f32[16,4]{1,0:T(8,128)S(1)}, f32[128,128]{1,0:T(8,128)}) custom-call(f32[128,128]{1,0:T(8,128)S(1)} %bitcast.36, f32[16,16]{1,0:T(8,128)S(1)} %fusion.125.inverse_ref, f32[16,1024,128]{2,1,0:T(8,128)S(1)} %bitcast.31, f32[4,1024,128]{2,1,0:T(8,128)S(1)} %bitcast.33), custom_call_target="tpu_custom_call" | custom-call | flops 16777216 | bytes 12582912 | tf_op jit(solution)/shard_map/remainder/pallas_call | solution.py:295
  273.3 3.5 %all-to-all-start.2 = ((f32[16,8,128]{2,1,0:T(8,128)}), f32[16,8,128]{2,1,0:T(8,128)S(1)}, u32[]{:S(2)}, u32[]{:S(2)}) async-start(f32[16,8,128]{2,1,0:T(8,128)} %bitcast.15), calls=%async_computation.2 | async-start | bytes 131072 | tf_op jit(solution)/shard_map/all_to_all | solution.py:160
  277.4 6.2 %all-to-all-done.2 = f32[16,8,128]{2,1,0:T(8,128)S(1)} async-done(((f32[16,8,128]{2,1,0:T(8,128)}), f32[16,8,128]{2,1,0:T(8,128)S(1)}, u32[]{:S(2)}, u32[]{:S(2)}) %all-to-all-start.2) | async-done | bytes 65568 | tf_op jit(solution)/shard_map/all_to_all | solution.py:160
  (122 shorter events, 74.1 us)
Async XLA Ops:
  1.7 13.4 %collective-permute-start.1 = (f32[1,256,128]{2,1,0:T(8,128)S(1)}, f32[1,256,128]{2,1,0:T(8,128)S(1)}, u32[]{:S(2)}, u32[]{:S(2)}) collective-permute-start(f32[1,256,128]{2,1,0:T(8,128)S(1)} %slice.357), channel_id=1, source_target_pairs={{0,1},{1,2},{2,3},{3,4},{4,5},{5,6},{6,7},{7,8},{8,9},{9,10},{10,1... | collective-permute-start | bytes 393224 | tf_op jit(solution)/shard_map/ppermute | solution.py:21
  5.4 10.9 %collective-permute-start = (f32[4,1,256,128]{3,2,1,0:T(8,128)S(1)}, f32[4,1,256,128]{3,2,1,0:T(8,128)S(1)}, u32[]{:S(2)}, u32[]{:S(2)}) collective-permute-start(f32[4,1,256,128]{3,2,1,0:T(8,128)S(1)} %get-tuple-element.34), channel_id=1, source_target_pairs={{1,0},{2,1},{3,2},{4,3},{5,4},{6,5},{7,6},{8,7},{9,8},{10,9},{11,1... | collective-permute-start | bytes 1572872 | tf_op jit(solution)/shard_map/ppermute | solution.py:34
  6.7 9.6 %collective-permute-start.2 = (f32[4,1,256,128]{3,2,1,0:T(8,128)S(1)}, f32[4,1,256,128]{3,2,1,0:T(8,128)S(1)}, u32[]{:S(2)}, u32[]{:S(2)}) collective-permute-start(f32[4,1,256,128]{3,2,1,0:T(8,128)S(1)} %get-tuple-element.35), channel_id=1, source_target_pairs={{0,1},{1,2},{2,3},{3,4},{4,5},{5,6},{6,7},{7,8},{8,9},{9,10},{10,1... | collective-permute-start | bytes 1572872 | tf_op jit(solution)/shard_map/ppermute | solution.py:32
  18.9 11.4 %collective-permute-start.3 = (f32[4,1,256,128]{3,2,1,0:T(8,128)S(1)}, f32[4,1,256,128]{3,2,1,0:T(8,128)S(1)}, u32[]{:S(2)}, u32[]{:S(2)}) collective-permute-start(f32[4,1,256,128]{3,2,1,0:T(8,128)S(1)} %get-tuple-element.32), channel_id=1, source_target_pairs={{1,0},{2,1},{3,2},{4,3},{5,4},{6,5},{7,6},{8,7},{9,8},{10,9},{11,1... | collective-permute-start | bytes 1572872 | tf_op jit(solution)/shard_map/ppermute | solution.py:34
  20.2 11.6 %collective-permute-start.4 = (f32[4,1,256,128]{3,2,1,0:T(8,128)S(1)}, f32[4,1,256,128]{3,2,1,0:T(8,128)S(1)}, u32[]{:S(2)}, u32[]{:S(2)}) collective-permute-start(f32[4,1,256,128]{3,2,1,0:T(8,128)S(1)} %get-tuple-element.33), channel_id=1, source_target_pairs={{0,1},{1,2},{2,3},{3,4},{4,5},{5,6},{6,7},{7,8},{8,9},{9,10},{10,1... | collective-permute-start | bytes 1572872 | tf_op jit(solution)/shard_map/ppermute | solution.py:32
  33.9 12.0 %collective-permute-start.5 = (f32[4,1,256,128]{3,2,1,0:T(8,128)S(1)}, f32[4,1,256,128]{3,2,1,0:T(8,128)S(1)}, u32[]{:S(2)}, u32[]{:S(2)}) collective-permute-start(f32[4,1,256,128]{3,2,1,0:T(8,128)S(1)} %get-tuple-element.30), channel_id=1, source_target_pairs={{1,0},{2,1},{3,2},{4,3},{5,4},{6,5},{7,6},{8,7},{9,8},{10,9},{11,1... | collective-permute-start | bytes 1572872 | tf_op jit(solution)/shard_map/ppermute | solution.py:34
  35.2 12.1 %collective-permute-start.6 = (f32[4,1,256,128]{3,2,1,0:T(8,128)S(1)}, f32[4,1,256,128]{3,2,1,0:T(8,128)S(1)}, u32[]{:S(2)}, u32[]{:S(2)}) collective-permute-start(f32[4,1,256,128]{3,2,1,0:T(8,128)S(1)} %get-tuple-element.31), channel_id=1, source_target_pairs={{0,1},{1,2},{2,3},{3,4},{4,5},{5,6},{6,7},{7,8},{8,9},{9,10},{10,1... | collective-permute-start | bytes 1572872 | tf_op jit(solution)/shard_map/ppermute | solution.py:32
  49.5 13.6 %collective-permute-start.7 = (f32[4,1,256,128]{3,2,1,0:T(8,128)S(1)}, f32[4,1,256,128]{3,2,1,0:T(8,128)S(1)}, u32[]{:S(2)}, u32[]{:S(2)}) collective-permute-start(f32[4,1,256,128]{3,2,1,0:T(8,128)S(1)} %get-tuple-element.28), channel_id=1, source_target_pairs={{1,0},{2,1},{3,2},{4,3},{5,4},{6,5},{7,6},{8,7},{9,8},{10,9},{11,1... | collective-permute-start | bytes 1572872 | tf_op jit(solution)/shard_map/ppermute | solution.py:34
  50.8 13.8 %collective-permute-start.8 = (f32[4,1,256,128]{3,2,1,0:T(8,128)S(1)}, f32[4,1,256,128]{3,2,1,0:T(8,128)S(1)}, u32[]{:S(2)}, u32[]{:S(2)}) collective-permute-start(f32[4,1,256,128]{3,2,1,0:T(8,128)S(1)} %get-tuple-element.29), channel_id=1, source_target_pairs={{0,1},{1,2},{2,3},{3,4},{4,5},{5,6},{6,7},{7,8},{8,9},{9,10},{10,1... | collective-permute-start | bytes 1572872 | tf_op jit(solution)/shard_map/ppermute | solution.py:32
  66.6 11.5 %collective-permute-start.10 = (f32[4,1,256,128]{3,2,1,0:T(8,128)S(1)}, f32[4,1,256,128]{3,2,1,0:T(8,128)S(1)}, u32[]{:S(2)}, u32[]{:S(2)}) collective-permute-start(f32[4,1,256,128]{3,2,1,0:T(8,128)S(1)} %get-tuple-element.27), channel_id=1, source_target_pairs={{0,1},{1,2},{2,3},{3,4},{4,5},{5,6},{6,7},{7,8},{8,9},{9,10},{10,1... | collective-permute-start | bytes 1572872 | tf_op jit(solution)/shard_map/ppermute | solution.py:32
  84.5 15.8 %collective-permute-start.11 = (f32[4,1,256,128]{3,2,1,0:T(8,128)S(1)}, f32[4,1,256,128]{3,2,1,0:T(8,128)S(1)}, u32[]{:S(2)}, u32[]{:S(2)}) collective-permute-start(f32[4,1,256,128]{3,2,1,0:T(8,128)S(1)} %get-tuple-element.24), channel_id=1, source_target_pairs={{1,0},{2,1},{3,2},{4,3},{5,4},{6,5},{7,6},{8,7},{9,8},{10,9},{11,1... | collective-permute-start | bytes 1572872 | tf_op jit(solution)/shard_map/ppermute | solution.py:34
  85.8 14.6 %collective-permute-start.12 = (f32[4,1,256,128]{3,2,1,0:T(8,128)S(1)}, f32[4,1,256,128]{3,2,1,0:T(8,128)S(1)}, u32[]{:S(2)}, u32[]{:S(2)}) collective-permute-start(f32[4,1,256,128]{3,2,1,0:T(8,128)S(1)} %get-tuple-element.25), channel_id=1, source_target_pairs={{0,1},{1,2},{2,3},{3,4},{4,5},{5,6},{6,7},{7,8},{8,9},{9,10},{10,1... | collective-permute-start | bytes 1572872 | tf_op jit(solution)/shard_map/ppermute | solution.py:32
  102.6 12.5 %collective-permute-start.13 = (f32[4,1,256,128]{3,2,1,0:T(8,128)S(1)}, f32[4,1,256,128]{3,2,1,0:T(8,128)S(1)}, u32[]{:S(2)}, u32[]{:S(2)}) collective-permute-start(f32[4,1,256,128]{3,2,1,0:T(8,128)S(1)} %get-tuple-element.22), channel_id=1, source_target_pairs={{1,0},{2,1},{3,2},{4,3},{5,4},{6,5},{7,6},{8,7},{9,8},{10,9},{11,1... | collective-permute-start | bytes 1572872 | tf_op jit(solution)/shard_map/ppermute | solution.py:34
  103.9 12.7 %collective-permute-start.14 = (f32[4,1,256,128]{3,2,1,0:T(8,128)S(1)}, f32[4,1,256,128]{3,2,1,0:T(8,128)S(1)}, u32[]{:S(2)}, u32[]{:S(2)}) collective-permute-start(f32[4,1,256,128]{3,2,1,0:T(8,128)S(1)} %get-tuple-element.23), channel_id=1, source_target_pairs={{0,1},{1,2},{2,3},{3,4},{4,5},{5,6},{6,7},{7,8},{8,9},{9,10},{10,1... | collective-permute-start | bytes 1572872 | tf_op jit(solution)/shard_map/ppermute | solution.py:32
  118.6 13.5 %collective-permute-start.15 = (f32[4,1,256,128]{3,2,1,0:T(8,128)S(1)}, f32[4,1,256,128]{3,2,1,0:T(8,128)S(1)}, u32[]{:S(2)}, u32[]{:S(2)}) collective-permute-start(f32[4,1,256,128]{3,2,1,0:T(8,128)S(1)} %get-tuple-element.20), channel_id=1, source_target_pairs={{1,0},{2,1},{3,2},{4,3},{5,4},{6,5},{7,6},{8,7},{9,8},{10,9},{11,1... | collective-permute-start | bytes 1572872 | tf_op jit(solution)/shard_map/ppermute | solution.py:34
  119.9 13.7 %collective-permute-start.16 = (f32[4,1,256,128]{3,2,1,0:T(8,128)S(1)}, f32[4,1,256,128]{3,2,1,0:T(8,128)S(1)}, u32[]{:S(2)}, u32[]{:S(2)}) collective-permute-start(f32[4,1,256,128]{3,2,1,0:T(8,128)S(1)} %get-tuple-element.21), channel_id=1, source_target_pairs={{0,1},{1,2},{2,3},{3,4},{4,5},{5,6},{6,7},{7,8},{8,9},{9,10},{10,1... | collective-permute-start | bytes 1572872 | tf_op jit(solution)/shard_map/ppermute | solution.py:32
  135.7 12.1 %collective-permute-start.17 = (f32[4,1,256,128]{3,2,1,0:T(8,128)S(1)}, f32[4,1,256,128]{3,2,1,0:T(8,128)S(1)}, u32[]{:S(2)}, u32[]{:S(2)}) collective-permute-start(f32[4,1,256,128]{3,2,1,0:T(8,128)S(1)} %get-tuple-element.18), channel_id=1, source_target_pairs={{1,0},{2,1},{3,2},{4,3},{5,4},{6,5},{7,6},{8,7},{9,8},{10,9},{11,1... | collective-permute-start | bytes 1572872 | tf_op jit(solution)/shard_map/ppermute | solution.py:34
  137.0 12.2 %collective-permute-start.18 = (f32[4,1,256,128]{3,2,1,0:T(8,128)S(1)}, f32[4,1,256,128]{3,2,1,0:T(8,128)S(1)}, u32[]{:S(2)}, u32[]{:S(2)}) collective-permute-start(f32[4,1,256,128]{3,2,1,0:T(8,128)S(1)} %get-tuple-element.19), channel_id=1, source_target_pairs={{0,1},{1,2},{2,3},{3,4},{4,5},{5,6},{6,7},{7,8},{8,9},{9,10},{10,1... | collective-permute-start | bytes 1572872 | tf_op jit(solution)/shard_map/ppermute | solution.py:32
  151.4 13.9 %collective-permute-start.19 = (f32[4,1,256,128]{3,2,1,0:T(8,128)S(1)}, f32[4,1,256,128]{3,2,1,0:T(8,128)S(1)}, u32[]{:S(2)}, u32[]{:S(2)}) collective-permute-start(f32[4,1,256,128]{3,2,1,0:T(8,128)S(1)} %get-tuple-element.16), channel_id=1, source_target_pairs={{1,0},{2,1},{3,2},{4,3},{5,4},{6,5},{7,6},{8,7},{9,8},{10,9},{11,1... | collective-permute-start | bytes 1572872 | tf_op jit(solution)/shard_map/ppermute | solution.py:34
  152.9 13.8 %collective-permute-start.20 = (f32[4,1,256,128]{3,2,1,0:T(8,128)S(1)}, f32[4,1,256,128]{3,2,1,0:T(8,128)S(1)}, u32[]{:S(2)}, u32[]{:S(2)}) collective-permute-start(f32[4,1,256,128]{3,2,1,0:T(8,128)S(1)} %get-tuple-element.17), channel_id=1, source_target_pairs={{0,1},{1,2},{2,3},{3,4},{4,5},{5,6},{6,7},{7,8},{8,9},{9,10},{10,1... | collective-permute-start | bytes 1572872 | tf_op jit(solution)/shard_map/ppermute | solution.py:32
  170.0 42.2 %collective-permute-start.21 = (f32[4,1,256,128]{3,2,1,0:T(8,128)}, f32[4,1,256,128]{3,2,1,0:T(8,128)}, u32[]{:S(2)}, u32[]{:S(2)}) collective-permute-start(f32[4,1,256,128]{3,2,1,0:T(8,128)} %get-tuple-element.14), channel_id=1, source_target_pairs={{1,0},{2,1},{3,2},{4,3},{5,4},{6,5},{7,6},{8,7},{9,8},{10,9},{11,1... | collective-permute-start | bytes 1572872 | tf_op jit(solution)/shard_map/ppermute | solution.py:34
  171.2 40.9 %collective-permute-start.22 = (f32[4,1,256,128]{3,2,1,0:T(8,128)}, f32[4,1,256,128]{3,2,1,0:T(8,128)}, u32[]{:S(2)}, u32[]{:S(2)}) collective-permute-start(f32[4,1,256,128]{3,2,1,0:T(8,128)} %get-tuple-element.15), channel_id=1, source_target_pairs={{0,1},{1,2},{2,3},{3,4},{4,5},{5,6},{6,7},{7,8},{8,9},{9,10},{10,1... | collective-permute-start | bytes 1572872 | tf_op jit(solution)/shard_map/ppermute | solution.py:32
  247.3 16.0 %all-to-all-start = ((f32[16,8,128]{2,1,0:T(8,128)}), f32[16,8,128]{2,1,0:T(8,128)S(1)}, u32[]{:S(2)}, u32[]{:S(2)}) async-start(f32[16,8,128]{2,1,0:T(8,128)} %bitcast.9), calls=%async_computation | async-start | bytes 131072 | tf_op jit(solution)/shard_map/all_to_all | solution.py:160
  273.3 10.4 %all-to-all-start.2 = ((f32[16,8,128]{2,1,0:T(8,128)}), f32[16,8,128]{2,1,0:T(8,128)S(1)}, u32[]{:S(2)}, u32[]{:S(2)}) async-start(f32[16,8,128]{2,1,0:T(8,128)} %bitcast.15), calls=%async_computation.2 | async-start | bytes 131072 | tf_op jit(solution)/shard_map/all_to_all | solution.py:160
  (26 other events, 1029.2 us)
where the time goes:
time: 288 us; the launch traced here: 287 us
  starting transfers between devices  151 us (52%)
  other arithmetic  40.9 us (14%)
  waiting for transfers between devices  27.7 us (10%)
  Pallas kernels  24.4 us (8%)
  blocking collectives  21.4 us (7%)
  local copies, waits for them, and re-layouts  18 us (6%)
  between operations  3.96 us (1%)
    ppermute x12, starting transfers between devices, extended(): lax.ppermute(tail, axis, [(i, (i + 1) % count) for i in range(ends)])  120 us
    div x9, other arithmetic, solve(): iterate = (rhs + neighbor_sum(padded, flows, adjoint)) / diagonal  23.2 us
    all_to_all x1, blocking collectives, spread(): return lax.all_to_all(tile, 'slab', 0, 0, tiled=True) if count > 1 else tile  21.4 us
    ppermute x12, starting transfers between devices, extended(): lax.ppermute(head, axis, [((i + 1) % count, i) for i in range(ends)])  15.8 us
    unnamed x46, local copies, waits for them, and re-layouts  13.1 us
    all_to_all x2, waiting for transfers between devices, spread(): return lax.all_to_all(tile, 'slab', 0, 0, tiled=True) if count > 1 else tile  12.9 us
    all_to_all x2, starting transfers between devices, spread(): return lax.all_to_all(tile, 'slab', 0, 0, tiled=True) if count > 1 else tile  12.6 us
    ppermute x12, waiting for transfers between devices, extended(): lax.ppermute(tail, axis, [(i, (i + 1) % count) for i in range(ends)])  10.5 us
  transfers between devices with their start and end apart: 27, of which 11 were waited for; matrix products, arithmetic and copies ran while one was open for 3% of the time, Pallas kernels for 4%

commit v1 on v0

v1 whole, which is shorter than its diff:
```python
import functools
import math

import jax
import jax.numpy as jnp
from jax import lax
from jax.experimental import pallas as pl
from jax.experimental.pallas import tpu as pltpu
from jax.sharding import PartitionSpec as P

STEPS = 2
SWEEPS = 3
GROUPS = 2


DIFFUSION = 0.2
GAMMA = 0.5

LANES = 128
EXACT = lax.Precision.HIGHEST


def lane_sums(stack):
    ones = jnp.ones((8, LANES), jnp.float32)
    return lax.dot_general(
        ones, stack, (((1,), (1,)), ((), ())), precision=EXACT, preferred_element_type=jnp.float32
    )


def gram_kernel(basis_ref, out_ref, acc_ref):
    rank = basis_ref.shape[0]
    rows = basis_ref.shape[1]
    step = pl.program_id(0)
    tile = 4

    @pl.when(step == 0)
    def _():
        acc_ref[...] = jnp.zeros_like(acc_ref)

    for i0 in range(0, rank, tile):
        for j0 in range(i0, rank, tile):
            pairs = [(i, j) for i in range(i0, i0 + tile) for j in range(j0, j0 + tile) if i <= j]

            def add(k, sums, i0=i0, j0=j0, pairs=pairs):
                at = pl.ds(pl.multiple_of(k * 8, 8), 8)
                left = {i: basis_ref[i, at, :] for i in range(i0, i0 + tile)}
                right = left if i0 == j0 else {j: basis_ref[j, at, :] for j in range(j0, j0 + tile)}
                return [s + left[i] * right[j] for s, (i, j) in zip(sums, pairs)]

            sums = [jnp.zeros((8, LANES), jnp.float32) for _ in pairs]
            sums = lax.fori_loop(0, rows // 8, add, sums, unroll=4)
            for (i, j), s in zip(pairs, sums):
                acc_ref[i, j] += s

    @pl.when(step == pl.num_programs(0) - 1)
    def _():
        row = lax.broadcasted_iota(jnp.int32, (rank, rank), 0)
        col = lax.broadcasted_iota(jnp.int32, (rank, rank), 1)
        gram = jnp.zeros((rank, rank), jnp.float32)
        for i in range(rank):
            sums = lane_sums(jnp.sum(acc_ref[i], axis=1))
            gram = jnp.where(row == i, jnp.broadcast_to(sums[0:1, :], (rank, rank)), gram)
        upper = jnp.where(col >= row, gram, 0.0)
        strict = jnp.where(col > row, gram, 0.0)
        whole = upper + strict.T
        for r in range(out_ref.shape[0] // 8):
            for k in range(0, rank, 8):
                out_ref[r * 8 : (r + 1) * 8, k * rank // 8 : (k + 8) * rank // 8] = whole[k : k + 8]


def gram_parts(basis, count):
    rank, rows, _ = basis.shape
    chunk = 128
    return pl.pallas_call(
        gram_kernel,
        grid=(rows // chunk,),
        in_specs=[pl.BlockSpec((rank, chunk, LANES), lambda k: (0, k, 0))],
        out_specs=pl.BlockSpec((count * 8, LANES), lambda k: (0, 0)),
        out_shape=jax.ShapeDtypeStruct((count * 8, LANES), jnp.float32),
        scratch_shapes=[pltpu.VMEM((rank, rank, 8, LANES), jnp.float32)],
        compiler_params=pltpu.CompilerParams(vmem_limit_bytes=16 << 20),
        cost_estimate=pl.CostEstimate(
            flops=rank * rank * rows * LANES, bytes_accessed=rank * rows * LANES * 4, transcendentals=0
        ),
        name="gram",
    )(basis)


def spread(tile, count):
    return lax.all_to_all(tile, "slab", 0, 0, tiled=True) if count > 1 else tile


def projection_kernel(groups, where_ref, basis_ref, dirs_ref, *refs):
    halves, (out_ref, image_ref, acc_ref) = refs[: 2 * groups], refs[2 * groups :]
    rank = basis_ref.shape[0]
    dirs, rows, _ = image_ref.shape
    step = pl.program_id(0)
    tile = 8
    each = dirs // groups

    @pl.when(step == 0)
    def _():
        acc_ref[...] = jnp.zeros_like(acc_ref)

    for side in range(2):

        @pl.when((step < pl.num_programs(0) // 2) == (side == 0))
        def _(side=side):
            for d in range(dirs):
                image_ref[d] = halves[2 * (d // each) + side][d % each, 0] + GAMMA * dirs_ref[d]

    for i0 in range(0, rank, tile):

        def add(k, sums, i0=i0):
            at = pl.ds(pl.multiple_of(k * 8, 8), 8)
            image = [image_ref[d, at, :] for d in range(dirs)]
            out = []
            for i in range(tile):
                q = basis_ref[i0 + i, at, :]
                out += [sums[i * dirs + d] + q * image[d] for d in range(dirs)]
            return out

        sums = [jnp.zeros((8, LANES), jnp.float32) for _ in range(tile * dirs)]
        sums = lax.fori_loop(0, rows // 8, add, sums, unroll=4)
        for i in range(tile):
            for d in range(dirs):
                acc_ref[d, i0 + i] += sums[i * dirs + d]

    @pl.when(step == pl.num_programs(0) - 1)
    def _():
        row = lax.broadcasted_iota(jnp.int32, (8, rank), 0)
        table = jnp.zeros((8, rank), jnp.float32)
        for d in range(dirs):
            table = jnp.where(row == d, lane_sums(jnp.sum(acc_ref[d], axis=1)), table)
        for r in range(out_ref.shape[0] // 8):
            out_ref[r * 8 : (r + 1) * 8, 0:rank] = table


def projection_parts(where, basis, directions, returned, count):
    rank, rows, _ = basis.shape
    dirs, planes, width, _ = directions.shape
    half = width // 2
    groups = len(returned)

    def line(k, where_ref):
        part = jnp.where(k < planes, where_ref[1], 1 - where_ref[1])
        return (0, 2 * lax.rem(k, planes) + part, 0)

    def side(which):
        def index(k, where_ref):
            at = jnp.minimum(k, planes - 1) if which == 0 else jnp.maximum(k - planes, 0)
            return (0, at, 0, 0)

        return pl.BlockSpec((dirs // groups, 1, half, LANES), index)

    return pl.pallas_call(
        functools.partial(projection_kernel, groups),
        grid_spec=pltpu.PrefetchScalarGridSpec(
            num_scalar_prefetch=1,
            grid=(2 * planes,),
            in_specs=[
                pl.BlockSpec((rank, half, LANES), line),
                pl.BlockSpec((dirs, half, LANES), line),
            ]
            + [side(which) for _ in returned for which in range(2)],
            out_specs=[
                pl.BlockSpec((count * 8, LANES), lambda k, where_ref: (0, 0)),
                pl.BlockSpec((dirs, half, LANES), line),
            ],
            scratch_shapes=[pltpu.VMEM((dirs, rank, 8, LANES), jnp.float32)],
        ),
        out_shape=[
            jax.ShapeDtypeStruct((count * 8, LANES), jnp.float32),
            jax.ShapeDtypeStruct((dirs, rows, LANES), jnp.float32),
        ],
        compiler_params=pltpu.CompilerParams(vmem_limit_bytes=16 << 20),
        cost_estimate=pl.CostEstimate(
            flops=2 * rank * dirs * rows * LANES,
            bytes_accessed=(rank + 3 * dirs) * rows * LANES * 4,
            transcendentals=0,
        ),
        name="projections",
    )(where, basis, directions.reshape(dirs, rows, LANES), *[h for pair in returned for h in pair])


def summed_tile(parts_ref):
    total = parts_ref[0:8, :]
    for r in range(1, parts_ref.shape[0] // 8):
        total = total + parts_ref[r * 8 : (r + 1) * 8, :]
    return total


def remainder_kernel(
    parts_ref, inverse_ref, basis_ref, image_ref, rem_ref, coeffs_ref, out_ref, splat_ref, energy_ref
):
    rank = basis_ref.shape[0]
    dirs, rows, _ = image_ref.shape
    step = pl.program_id(0)
    tile = 4

    @pl.when(step == 0)
    def _():
        table = summed_tile(parts_ref)[:, 0:rank]
        inverse = inverse_ref[...]
        half = lax.dot_general(
            table, inverse, (((1,), (1,)), ((), ())), precision=EXACT,
            preferred_element_type=jnp.float32,
        )
        flat = lax.dot_general(
            half, inverse, (((1,), (0,)), ((), ())), precision=EXACT,
            preferred_element_type=jnp.float32,
        )
        coeffs_ref[...] = flat.T[:, 0:dirs]
        for d in range(dirs):
            for j in range(rank):
                splat_ref[d * rank + j] = jnp.broadcast_to(flat[d : d + 1, j : j + 1], (8, LANES))
        energy_ref[...] = jnp.zeros_like(energy_ref)

    for j0 in range(0, rank, tile):
        last = j0 + tile == rank
        weights = [[splat_ref[d * rank + j] for j in range(j0, j0 + tile)] for d in range(dirs)]

        def take(k, energy, j0=j0, last=last, weights=weights):
            at = pl.ds(pl.multiple_of(k * 8, 8), 8)
            basis = [basis_ref[j, at, :] for j in range(j0, j0 + tile)]
            out = []
            for d in range(dirs):
                left = image_ref[d, at, :] if j0 == 0 else rem_ref[d, at, :]
                parts = [w * q for w, q in zip(weights[d], basis)]
                left = left - ((parts[0] + parts[1]) + (parts[2] + parts[3]))
                rem_ref[d, at, :] = left
                out.append(energy[d] + left * left if last else energy[d])
            return out

        energy = [jnp.zeros((8, LANES), jnp.float32) for _ in range(dirs)]
        energy = lax.fori_loop(0, rows // 8, take, energy, unroll=4)
        if last:
            for d in range(dirs):
                energy_ref[d] += energy[d]

    @pl.when(step == pl.num_programs(0) - 1)
    def _():
        row = lax.broadcasted_iota(jnp.int32, (8, LANES), 0)
        tile_out = jnp.zeros((8, LANES), jnp.float32)
        for d in range(dirs):
            total = jnp.sum(jnp.sum(energy_ref[d], axis=0, keepdims=True), axis=1, keepdims=True)
            tile_out = jnp.where(row == d, jnp.broadcast_to(total, (8, LANES)), tile_out)
        for r in range(out_ref.shape[0] // 8):
            out_ref[r * 8 : (r + 1) * 8, :] = tile_out


def remainders(parts, inverse, basis, image, count):
    rank, rows, _ = basis.shape
    dirs = image.shape[0]
    chunk = 128
    whole = lambda *shape: pl.BlockSpec(shape, lambda k: (0,) * len(shape))
    return pl.pallas_call(
        remainder_kernel,
        grid=(rows // chunk,),
        in_specs=[
            whole(count * 8, LANES),
            whole(rank, rank),
            pl.BlockSpec((rank, chunk, LANES), lambda k: (0, k, 0)),
            pl.BlockSpec((dirs, chunk, LANES), lambda k: (0, k, 0)),
        ],
        out_specs=[
            pl.BlockSpec((dirs, chunk, LANES), lambda k: (0, k, 0)),
            whole(rank, dirs),
            whole(count * 8, LANES),
        ],
        out_shape=[
            jax.ShapeDtypeStruct((dirs, rows, LANES), jnp.float32),
            jax.ShapeDtypeStruct((rank, dirs), jnp.float32),
            jax.ShapeDtypeStruct((count * 8, LANES), jnp.float32),
        ],
        scratch_shapes=[
            pltpu.VMEM((dirs * rank, 8, LANES), jnp.float32),
            pltpu.VMEM((dirs, 8, LANES), jnp.float32),
        ],
        compiler_params=pltpu.CompilerParams(vmem_limit_bytes=16 << 20),
        cost_estimate=pl.CostEstimate(
            flops=2 * rank * dirs * rows * LANES,
            bytes_accessed=(rank + 2 * dirs) * rows * LANES * 4,
            transcendentals=0,
        ),
        name="remainder",
    )(parts, inverse, basis, image)


def scale_kernel(cells, parts_ref, rem_ref, new_ref):
    energy = summed_tile(parts_ref)
    value = energy / cells + 1e-06
    root = lax.rsqrt(value)
    root = root * (1.5 - (0.5 * value * root) * root)
    for d in range(rem_ref.shape[0]):
        new_ref[d] = rem_ref[d] * root[d : d + 1, :]


def scaled(parts, rem, cells, count):
    dirs, rows, _ = rem.shape
    chunk = 256
    return pl.pallas_call(
        functools.partial(scale_kernel, cells),
        grid=(rows // chunk,),
        in_specs=[
            pl.BlockSpec((count * 8, LANES), lambda k: (0, 0)),
            pl.BlockSpec((dirs, chunk, LANES), lambda k: (0, k, 0)),
        ],
        out_specs=pl.BlockSpec((dirs, chunk, LANES), lambda k: (0, k, 0)),
        out_shape=jax.ShapeDtypeStruct((dirs, rows, LANES), jnp.float32),
        compiler_params=pltpu.CompilerParams(vmem_limit_bytes=16 << 20),
        name="scale",
    )(parts, rem)


SPARE = 16
REACH = STEPS * SWEEPS
PAD = 8


def quad(count):
    own, other, above = [], [], []
    for s in range(count):
        q, a, b = s // 4, s // 2 % 2, s % 2
        own.append((s, 4 * q + 2 * b + a))
        other.append((s, 4 * q + 2 * (1 - b) + a))
        up = s + 1 if b == 0 else s + 3
        if up < count:
            above.append((s, up))
    return own, other, above


def back(pairs):
    return [(target, source) for source, target in pairs]


def cut_kernel(where_ref, *refs):
    sources, own_ref, other_ref = refs[:-2], refs[-2], refs[-1]
    height = own_ref.shape[2]
    width = sources[0].shape[-2]
    b = where_ref[1]
    for ref, part in ((own_ref, b), (other_ref, 1 - b)):
        start = pl.multiple_of(part * (width - height), 16)
        k = 0
        for source in sources:
            if len(source.shape) == 3:
                ref[k] = source[:, pl.ds(start, height), :]
                k += 1
            else:
                for d in range(source.shape[0]):
                    ref[k] = source[d, :, pl.ds(start, height), :]
                    k += 1


SMEM = pl.BlockSpec(memory_space=pltpu.SMEM)
VMEM = pl.BlockSpec(memory_space=pltpu.VMEM)


def call(kernel, name, ins, outs, scratch=(), limit=20, flops=0):
    moved = sum(x.size * 4 for x in ins[1:]) + sum(4 * math.prod(s) for s in outs)
    return pl.pallas_call(
        kernel,
        in_specs=[SMEM] + [VMEM] * (len(ins) - 1),
        out_specs=[VMEM] * len(outs),
        out_shape=[jax.ShapeDtypeStruct(s, jnp.float32) for s in outs],
        scratch_shapes=list(scratch),
        compiler_params=pltpu.CompilerParams(vmem_limit_bytes=limit << 20),
        cost_estimate=pl.CostEstimate(flops=flops, bytes_accessed=moved, transcendentals=0),
        name=name,
    )(*ins)


def pack_kernel(where_ref, own_ref, other_ref, up_ref, down_ref):
    planes = own_ref.shape[1]
    reach = up_ref.shape[1]
    skip = 2 * planes - reach

    def join(first, second):
        up_ref[:, 0 : planes - skip] = first[:, skip:]
        up_ref[:, planes - skip :] = second[...]
        down_ref[:, 0:planes] = first[...]
        down_ref[:, planes:] = second[:, 0 : reach - planes]

    @pl.when(where_ref[0] == 0)
    def _():
        join(own_ref, other_ref)

    @pl.when(where_ref[0] == 1)
    def _():
        join(other_ref, own_ref)


def sensor_kernel(width, where_ref, own_ref, other_ref, out_ref):
    a = where_ref[0]
    _, planes, height, _ = out_ref.shape
    first = a * (width - height)
    sensors = own_ref.shape[1]
    chunk = 512
    targets = planes * height
    rows = lax.broadcasted_iota(jnp.int32, (targets, chunk), 0)
    lanes = lax.broadcasted_iota(jnp.int32, (LANES, chunk), 0)
    for ref, at in ((own_ref, a), (other_ref, 1 - a)):
        total = jnp.zeros((targets, 3 * LANES), jnp.float32)
        for k in range(sensors // chunk):
            cell = ref[0:1, k * chunk : (k + 1) * chunk].astype(jnp.int32)
            weight = ref[1:2, k * chunk : (k + 1) * chunk]
            line = cell // LANES
            lane = cell - line * LANES
            plane = line // width
            row = line - plane * width - first
            inside = (row >= 0) & (row < height)
            target = jnp.where(inside, plane * height + row, -1)
            high = weight.astype(jnp.bfloat16).astype(jnp.float32)
            rest = weight - high
            middle = rest.astype(jnp.bfloat16).astype(jnp.float32)
            low = rest - middle
            hot = jnp.where(rows == target, 1.0, 0.0).astype(jnp.bfloat16)
            here = lanes == lane
            parts = [jnp.where(here, part, 0.0).astype(jnp.bfloat16) for part in (high, middle, low)]
            total += lax.dot_general(
                hot,
                jnp.concatenate(parts, 0),
                (((1,), (1,)), ((), ())),
                preferred_element_type=jnp.float32,
            )
        total = total[:, 0:LANES] + total[:, LANES : 2 * LANES] + total[:, 2 * LANES :]
        out_ref[at] = total.reshape(planes, height, LANES)


def relu(x):
    return jnp.maximum(x, 0.0)


def solve_kernel(adjoint, width, where_ref, f_up, f_down, f_lo, f_hi, v_up, v_down, v_lo, v_hi, *refs):
    if adjoint:
        first_out, second_out, flow, coef, rhs, start, ping, pong = refs
        weight_ref = None
    else:
        weight_ref, up_out, down_out, flow, coef, rhs, start, ping, pong = refs
    dirs, reach, height, _ = v_up.shape
    depth = rhs.shape[1]
    own = depth - 2 * reach
    chunks = height // 8
    a, at_bottom, at_top = where_ref[0], where_ref[2], where_ref[3]
    code = [where_ref[4 + k] for k in range(4)]

    def gather(into, up, down, lo, hi, rows):
        into[:, 0:reach, rows, :] = lo[...]
        into[:, reach : 2 * reach, rows, :] = down[...]
        into[:, 2 * reach : reach + own, rows, :] = up[:, 2 * reach - own :]
        into[:, reach + own :, rows, :] = hi[...]

    gather(flow, f_up, f_down, f_lo, f_hi, pl.ds(0, height))
    gather(start, v_up, v_down, v_lo, v_hi, pl.ds(PAD, height))
    for ref in (start, ping, pong):
        for d in range(dirs):
            for p in range(depth):
                ref[d, p, 0:PAD, :] = jnp.zeros((PAD, LANES), jnp.float32)
                ref[d, p, PAD + height :, :] = jnp.zeros((PAD, LANES), jnp.float32)

    shape = (height, LANES)
    row = lax.broadcasted_iota(jnp.int32, shape, 0) + a * (width - height)
    lane = lax.broadcasted_iota(jnp.int32, shape, 1)
    opened = [jnp.where(c == 0, 1.0, 0.0).astype(jnp.float32) for c in code]
    low_one = jnp.where(row == 0, opened[0], 1.0)
    high_one = jnp.where(row == width - 1, opened[1], 1.0)
    low_two = jnp.where(lane == 0, opened[2], 1.0)
    high_two = jnp.where(lane == LANES - 1, opened[3], 1.0)

    def coefficients(p, carry):
        one, two, three = flow[0, p], flow[1, p], flow[2, p]
        one_below = jnp.where(row == 0, 0.0, pltpu.roll(one, 1, 0))
        two_below = jnp.where(lane == 0, 0.0, pltpu.roll(two, 1, 1))
        three_below = flow[2, p - 1]
        up = [DIFFUSION + relu(x) for x in (one, two, three)]
        down = [DIFFUSION + relu(-x) for x in (one_below, two_below, three_below)]
        diagonal = 1.0 + high_one * up[0] + low_one * down[0] + high_two * up[1]
        diagonal = diagonal + low_two * down[1] + up[2] + down[2]
        outside = ((p < reach) & (at_bottom == 1)) | ((p >= reach + own) & (at_top == 1))
        inverse = jnp.where(outside, 0.0, 1.0) / diagonal
        if not adjoint:
            up = [DIFFUSION + relu(-x) for x in (one, two, three)]
            down = [DIFFUSION + relu(x) for x in (one_below, two_below, three_below)]
        coef[0, p] = up[0] * inverse
        coef[1, p] = down[0] * inverse
        coef[2, p] = jnp.where(lane == LANES - 1, 0.0, up[1] * inverse)
        coef[3, p] = jnp.where(lane == 0, 0.0, down[1] * inverse)
        coef[4, p] = up[2] * inverse
        coef[5, p] = down[2] * inverse
        coef[6, p] = inverse
        return carry

    lax.fori_loop(1, depth - 1, coefficients, 0)

    def sweep(source, lead, planes, offset, count, store):
        def at_plane(p, carry):
            for r in range(count):
                here = pl.ds(offset + r * 8, 8)
                c = [coef[k, p, here, :] for k in range(7 if lead else 6)]
                base = offset + PAD + r * 8
                for d in range(dirs):
                    value = source[d, p, pl.ds(base, 8), :]
                    if lead:
                        total = value * c[6]
                        rhs[d, p, here, :] = total
                    else:
                        total = rhs[d, p, here, :]
                    total = total + c[0] * source[d, p, pl.ds(base + 1, 8), :]
                    total = total + c[1] * source[d, p, pl.ds(base - 1, 8), :]
                    total = total + c[2] * pltpu.roll(value, LANES - 1, 1)
                    total = total + c[3] * pltpu.roll(value, 1, 1)
                    total = total + c[4] * source[d, p + 1, pl.ds(base, 8), :]
                    total = total + c[5] * source[d, p - 1, pl.ds(base, 8), :]
                    store(d, p, base, r, total)
            return carry

        for low, high in planes:
            lax.fori_loop(low, high, at_plane, 0)

    def into(ref):
        def store(d, p, base, r, total):
            ref[d, p, pl.ds(base, 8), :] = total

        return store

    def again(d, p, base, r, total):
        if not adjoint:
            total = total + start[d, p, pl.ds(base, 8), :]
        start[d, p, pl.ds(base, 8), :] = total

    def full(source, lead, step, store):
        sweep(source, lead, [(1 + step, depth - 1 - step)], 0, chunks, store)

    full(start, True, 0, into(ping))
    full(ping, False, 1, into(pong))
    full(pong, False, 2, again)
    full(start, True, 3, into(ping))
    full(ping, False, 4, into(pong))

    if adjoint:
        kept = 2 * (height - SPARE) // 2 // 8
        half = own // 2
        shift = pl.multiple_of(a * SPARE, 8)
        for out, side in ((first_out, a), (second_out, 1 - a)):
            low = reach + side * half

            def finish(d, p, base, r, total, out=out, low=low):
                out[d, p - low, r * 8 : r * 8 + 8, :] = total + start[d, p, pl.ds(base, 8), :]

            sweep(pong, False, [(low, low + half)], shift, kept, finish)
    else:

        def emit(kinds):
            def finish(d, p, base, r, total):
                i = p - reach
                total = total * weight_ref[i // (own // 2), i % (own // 2), r * 8 : r * 8 + 8, :]
                if "d" in kinds:
                    down_out[d, i, r * 8 : r * 8 + 8, :] = total
                if "u" in kinds:
                    up_out[d, i - (own - reach), r * 8 : r * 8 + 8, :] = total

            return finish

        for low, high, kinds in ((0, own - reach, "d"), (own - reach, reach, "du"), (reach, own, "u")):
            sweep(pong, False, [(reach + low, reach + high)], 0, chunks, emit(kinds))


def solves(adjoint, width, where, flows, values, weight=None):
    dirs, reach, height, _ = values[0].shape
    blocks = 2 * (where[1])
    depth = blocks + 2 * reach
    ins = [where[0], *flows, *values]
    if adjoint:
        outs = [(dirs, blocks // 2, height - SPARE, LANES)] * 2
    else:
        ins.append(weight)
        outs = [values[0].shape] * 2
    padded = (dirs, depth, height + 2 * PAD, LANES)
    scratch = [
        pltpu.VMEM((3, depth, height, LANES), jnp.float32),
        pltpu.VMEM((7, depth, height, LANES), jnp.float32),
        pltpu.VMEM((dirs, depth, height, LANES), jnp.float32),
    ] + [pltpu.VMEM(padded, jnp.float32)] * 3
    name = "adjoint" if adjoint else "forward"
    return call(
        functools.partial(solve_kernel, adjoint, width), name, ins, outs, scratch, 48,
        flops=6 * 14 * dirs * depth * height * LANES,
    )


def body(
    directions,
    eigen_basis,
    flow_first,
    flow_second,
    flow_depth,
    face_codes,
    sensor_cells,
    sensor_weight,
):
    dirs, planes, width, _ = directions.shape
    rank = eigen_basis.shape[0]
    count = lax.axis_size("slab")
    height = width // 2 + SPARE
    own, other, above = quad(count)
    me = lax.axis_index("slab")
    a, b = me // 2 % 2, me % 2
    place = [a, b, (me - 2 * a == 0), (me + 2 * (1 - a) == count - 1)]
    where = jnp.concatenate([jnp.stack([x.astype(jnp.int32) for x in place]), face_codes])
    both = (where, planes)

    def regroup(first, second):
        return lax.ppermute(first, "slab", own), lax.ppermute(second, "slab", other)

    def cut(arrays, parts):
        return call(cut_kernel, "cut", [where, *arrays], [(parts, planes, height, LANES)] * 2)

    def beyond(up, down):
        return up, down, lax.ppermute(up, "slab", above), lax.ppermute(down, "slab", back(above))

    def pack(pair):
        shape = (pair[0].shape[0], REACH, height, LANES)
        return call(pack_kernel, "pack", [where, *pair], [shape] * 2)

    flows = regroup(*cut([flow_first, flow_second, flow_depth], 3))
    groups = [directions[k : k + dirs // GROUPS] for k in range(0, dirs, dirs // GROUPS)]
    moved = [regroup(*cut([g], dirs // GROUPS)) for g in groups]
    sensors = jnp.stack([sensor_cells.astype(jnp.float32), sensor_weight])
    sensors = regroup(sensors, sensors)

    basis = eigen_basis.reshape(rank, planes * width, LANES)
    gram = spread(gram_parts(basis, count), count)
    gram = jnp.sum(gram.reshape(count, 8, LANES), 0)
    gram = jnp.concatenate([gram[:, k : k + rank] for k in range(0, rank * rank // 8, rank)], 0)
    factor_lower = jnp.linalg.cholesky(gram)
    inverse = lax.linalg.triangular_solve(
        factor_lower, jnp.eye(rank, dtype=jnp.float32), left_side=True, lower=True
    )
    (weight,) = call(
        functools.partial(sensor_kernel, width), "sensors", [where, *sensors],
        [(2, planes, height, LANES)], limit=32,
    )
    flows = beyond(*pack(flows))
    values = [beyond(*pack(m)) for m in moved]
    forcing = [beyond(*solves(False, width, both, flows, v, weight)) for v in values]
    summed = [solves(True, width, both, flows, f) for f in forcing]
    returned = [
        (lax.ppermute(s[0], "slab", back(own)), lax.ppermute(s[1], "slab", back(other)))
        for s in summed
    ]
    parts, image = projection_parts(where, basis, directions, returned, count)
    parts = spread(parts, count)
    rem, coeffs, parts = remainders(parts, inverse, basis, image, count)
    new_directions = scaled(spread(parts, count), rem, planes * count * width * LANES, count)
    return (new_directions.reshape(directions.shape), coeffs)


def solution(mesh):
    return jax.shard_map(
        body,
        mesh=mesh,
        in_specs=(
            P("grp", "slab", None, None),
            P("grp", "slab", None, None),
            P("slab", None, None),
            P("slab", None, None),
            P("slab", None, None),
            P(),
            P(("grp", "slab")),
            P(("grp", "slab")),
        ),
        out_specs=(P("grp", "slab", None, None), P("grp", None)),
        check_vma=False,
    )
```

time: 288 us -> 259 us (0.90)
  Pallas kernels: 24.4 us -> 111 us
  starting transfers between devices: 151 us -> 74.8 us
  other arithmetic: 40.9 us -> 4.22 us
  waiting for transfers between devices: 27.7 us -> 35.8 us
  blocking collectives: 21.4 us -> 14.3 us
    pallas_call x2 -> x12, Pallas kernels: 9.32 us -> 95.4 us  [the longest x11 89.1 us: call(): pl.pallas_call(kernel, in_specs=[SMEM] + [VMEM] * (len(ins) - 1), out_spe...]
    ppermute x25 -> x22, starting transfers between devices: 138 us -> 67.8 us  [the longest x5 28.5 us: beyond(): lax.ppermute(up, 'slab', above)]
    div x9 -> x0, other arithmetic: 23.2 us -> none  [solve(): iterate = (rhs + neighbor_sum(padded, flows, adjoint)) / diagonal]
    add x3 -> x0, other arithmetic: 11.5 us -> none  [the longest x1 8.45 us: body(): image = (summed + GAMMA * directions).reshape(dirs, planes * width, LANES)]
    ppermute x25 -> x22, waiting for transfers between devices: 14.8 us -> 22.9 us  [the longest x4 14.1 us: regroup(): lax.ppermute(second, 'slab', other)]
    all_to_all x1, blocking collectives: 21.4 us -> 14.3 us  [spread(): return lax.all_to_all(tile, 'slab', 0, 0, tiled=True) if count > 1 else tile]
    all_to_all x2, starting transfers between devices: 12.6 us -> 7 us  [spread(): return lax.all_to_all(tile, 'slab', 0, 0, tiled=True) if count > 1 else tile]
    slice x16 -> x2, local copies, waits for them, and re-layouts: 4.88 us -> 1.85 us  [the longest x1 1.78 us: body(): directions[k:k + dirs // GROUPS]]
  transfers between devices with their start and end apart: 27 -> 24, of which waited for: 11 -> 4; matrix products, arithmetic and copies ran while one was open for 3% -> 2% of each run, Pallas kernels for 4% -> 37%
where the time goes in v1:
time: 259 us; the launch traced here: 258 us
  Pallas kernels  111 us (43%)
  starting transfers between devices  74.8 us (29%)
  waiting for transfers between devices  35.8 us (14%)
  local copies, waits for them, and re-layouts  17.4 us (7%)
  blocking collectives  14.3 us (6%)
  other arithmetic  4.22 us (2%)
    pallas_call x11, Pallas kernels, call(): pl.pallas_call(kernel, in_specs=[SMEM] + [VMEM] * (len(ins) - 1), out_spe...  89.1 us
    ppermute x5, starting transfers between devices, beyond(): lax.ppermute(up, 'slab', above)  28.5 us
    ppermute x4, starting transfers between devices, regroup(): lax.ppermute(second, 'slab', other)  24 us
    unnamed x41, local copies, waits for them, and re-layouts  15.3 us
    all_to_all x1, blocking collectives, spread(): return lax.all_to_all(tile, 'slab', 0, 0, tiled=True) if count > 1 else tile  14.3 us
    ppermute x4, waiting for transfers between devices, regroup(): lax.ppermute(second, 'slab', other)  14.1 us
    all_to_all x2, waiting for transfers between devices, spread(): return lax.all_to_all(tile, 'slab', 0, 0, tiled=True) if count > 1 else tile  12.9 us
    ppermute x2, waiting for transfers between devices, body(): lax.ppermute(s[1], 'slab', back(other))  8.82 us
  transfers between devices with their start and end apart: 24, of which 4 were waited for; matrix products, arithmetic and copies ran while one was open for 2% of the time, Pallas kernels for 37%

profile of v1, /device:TPU:0, one launch (start us, length us, event | category | flops | bytes accessed | tf_op | source)
XLA Modules:
  0.0 258.5 jit_solution(10180671743695277642)
XLA Ops:
  3.9 4.2 %collective-permute-start.15 = (f32[2,4,144,128]{3,2,1,0:T(8,128)S(1)}, f32[2,4,144,128]{3,2,1,0:T(8,128)S(1)}, u32[]{:S(2)}, u32[]{:S(2)}) collective-permute-start(f32[2,4,144,128]{3,2,1,0:T(8,128)S(1)} %get-tuple-element.40), channel_id=1, source_target_pairs={{0,2},{1,0},{2,3},{3,1},{4,6},{5,4},{6,7},{7,5},{8,10},{9,8},{10,1... | collective-permute-start | bytes 1769480 | tf_op jit(solution)/shard_map/ppermute | solution.py:613
  14.9 8.2 %collective-permute-start.5 = (f32[2,4,144,128]{3,2,1,0:T(8,128)S(1)}, f32[2,4,144,128]{3,2,1,0:T(8,128)S(1)}, u32[]{:S(2)}, u32[]{:S(2)}) collective-permute-start(f32[2,4,144,128]{3,2,1,0:T(8,128)S(1)} %get-tuple-element.32), channel_id=1, source_target_pairs={{0,2},{1,0},{2,3},{3,1},{4,6},{5,4},{6,7},{7,5},{8,10},{9,8},{10,1... | collective-permute-start | bytes 1769480 | tf_op jit(solution)/shard_map/ppermute | solution.py:613
  26.7 14.1 %collective-permute-done.1.other_ref = f32[3,4,144,128]{3,2,1,0:T(8,128)S(1)} collective-permute-done((f32[3,4,144,128]{3,2,1,0:T(8,128)S(1)}, f32[3,4,144,128]{3,2,1,0:T(8,128)S(1)}, u32[]{:S(2)}, u32[]{:S(2)}) %collective-permute-start.1) | collective-permute-done | bytes 884768 | tf_op jit(solution)/shard_map/ppermute | solution.py:613
  41.5 5.4 %collective-permute-start.2 = (f32[3,6,144,128]{3,2,1,0:T(8,128)S(1)}, f32[3,6,144,128]{3,2,1,0:T(8,128)S(1)}, u32[]{:S(2)}, u32[]{:S(2)}) collective-permute-start(f32[3,6,144,128]{3,2,1,0:T(8,128)S(1)} %get-tuple-element.29.f_up), channel_id=1, source_target_pairs={{0,1},{1,4},{2,3},{3,6},{4,5},{5,8},{6,7},{7,10},{8,9},{9,12},{10,... | collective-permute-start | bytes 3981320 | tf_op jit(solution)/shard_map/ppermute | solution.py:619
  48.2 8.6 %collective-permute-start.9 = (f32[2,4096]{1,0:T(2,128)S(1)}, f32[2,4096]{1,0:T(2,128)S(1)}, u32[]{:S(2)}, u32[]{:S(2)}) collective-permute-start(f32[2,4096]{1,0:T(2,128)S(1)} %pad_maximum_fusion), channel_id=1, source_target_pairs={{0,2},{1,0},{2,3},{3,1},{4,6},{5,4},{6,7},{7,5},{8,10},{9,8},{10,1... | collective-permute-start | bytes 98312 | tf_op jit(solution)/shard_map/ppermute | solution.py:613
  59.7 4.0 %collective-permute-start.6 = (f32[2,6,144,128]{3,2,1,0:T(8,128)S(1)}, f32[2,6,144,128]{3,2,1,0:T(8,128)}, u32[]{:S(2)}, u32[]{:S(2)}) collective-permute-start(f32[2,6,144,128]{3,2,1,0:T(8,128)S(1)} %get-tuple-element.33.v_up), channel_id=1, source_target_pairs={{0,1},{1,4},{2,3},{3,6},{4,5},{5,8},{6,7},{7,10},{8,9},{9,12},{10,... | collective-permute-start | bytes 2654216 | tf_op jit(solution)/shard_map/ppermute | solution.py:619
  64.9 5.7 %sensors.1.refs_0_ = f32[2,4,144,128]{3,2,1,0:T(8,128)S(1)} custom-call(s32[8]{0:T(128)S(1)} %concatenate.6.where_ref, f32[2,4096]{1,0:T(2,128)S(1)} %collective-permute-done.8.own_ref, f32[2,4096]{1,0:T(2,128)S(1)} %collective-permute-done.9.other_ref), custom_call_target="tpu_custom_call" | custom-call | bytes 655360 | tf_op jit(solution)/shard_map/sensors/pallas_call | solution.py:361
  71.7 19.6 %forward.3 = (f32[2,6,144,128]{3,2,1,0:T(8,128)}, f32[2,6,144,128]{3,2,1,0:T(8,128)}) custom-call(s32[8]{0:T(128)S(1)} %concatenate.6.where_ref, f32[3,6,144,128]{3,2,1,0:T(8,128)} %copy-done.2, f32[3,6,144,128]{3,2,1,0:T(8,128)} %copy-done.4, f32[3,6,144,128]{3,2,1,0:T(8,128)} %copy-done.13, f32[3,6,144,128]{3,2,1,0:T(8,128)} %collective-permute-done.3.f_hi, ...), custom_call_target="tpu_custom_call" | custom-call | flops 61931520 | bytes 11206656 | tf_op jit(solution)/shard_map/forward/pallas_call | solution.py:361
  91.3 13.9 %collective-permute-start.18 = (f32[2,6,144,128]{3,2,1,0:T(8,128)}, f32[2,6,144,128]{3,2,1,0:T(8,128)}, u32[]{:S(2)}, u32[]{:S(2)}) collective-permute-start(f32[2,6,144,128]{3,2,1,0:T(8,128)} %get-tuple-element.43.v_up), channel_id=1, source_target_pairs={{0,1},{1,4},{2,3},{3,6},{4,5},{5,8},{6,7},{7,10},{8,9},{9,12},{10,... | collective-permute-start | bytes 2654216 | tf_op jit(solution)/shard_map/ppermute | solution.py:619
  108.2 20.2 %forward.2 = (f32[2,6,144,128]{3,2,1,0:T(8,128)}, f32[2,6,144,128]{3,2,1,0:T(8,128)}) custom-call(s32[8]{0:T(128)S(1)} %concatenate.6.where_ref, f32[3,6,144,128]{3,2,1,0:T(8,128)} %copy-done.2, f32[3,6,144,128]{3,2,1,0:T(8,128)} %copy-done.4, f32[3,6,144,128]{3,2,1,0:T(8,128)} %copy-done.13, f32[3,6,144,128]{3,2,1,0:T(8,128)} %collective-permute-done.3.f_hi, ...), custom_call_target="tpu_custom_call" | custom-call | flops 61931520 | bytes 11206656 | tf_op jit(solution)/shard_map/forward/pallas_call | solution.py:361
  128.3 3.1 %collective-permute-start.10 = (f32[2,6,144,128]{3,2,1,0:T(8,128)}, f32[2,6,144,128]{3,2,1,0:T(8,128)S(1)}, u32[]{:S(2)}, u32[]{:S(2)}) collective-permute-start(f32[2,6,144,128]{3,2,1,0:T(8,128)} %get-tuple-element.35.v_up), channel_id=1, source_target_pairs={{0,1},{1,4},{2,3},{3,6},{4,5},{5,8},{6,7},{7,10},{8,9},{9,12},{10,... | collective-permute-start | bytes 2654216 | tf_op jit(solution)/shard_map/ppermute | solution.py:619
  132.8 7.9 %gram.1 = f32[128,128]{1,0:T(8,128)S(1)} custom-call(f32[16,1024,128]{2,1,0:T(8,128)S(1)} %bitcast.25), custom_call_target="tpu_custom_call" | custom-call | flops 33554432 | bytes 8388608 | tf_op jit(solution)/shard_map/gram/pallas_call | solution.py:74
  140.7 14.3 %all_to_all.31 = f32[16,8,128]{2,1,0:T(8,128)S(1)} all-to-all(f32[16,8,128]{2,1,0:T(8,128)S(1)} %bitcast.31), channel_id=1, replica_groups=mesh['grp'=2,'slab'=16] {'slab'}, dimensions={0} | all-to-all | bytes 131072 | tf_op jit(solution)/shard_map/all_to_all | solution.py:90
  155.4 19.5 %adjoint.3 = (f32[2,4,128,128]{3,2,1,0:T(8,128)}, f32[2,4,128,128]{3,2,1,0:T(8,128)}) custom-call(s32[8]{0:T(128)S(1)} %concatenate.6.where_ref, f32[3,6,144,128]{3,2,1,0:T(8,128)S(1)} %copy-done.3, f32[3,6,144,128]{3,2,1,0:T(8,128)} %copy-done.4, f32[3,6,144,128]{3,2,1,0:T(8,128)} %copy-done.13, f32[3,6,144,128]{3,2,1,0:T(8,128)} %collective-permute-done.3.f_hi, ...), custom_call_target="tpu_custom_call" | custom-call | flops 61931520 | bytes 9895936 | tf_op jit(solution)/shard_map/adjoint/pallas_call | solution.py:361
  177.1 19.2 %adjoint.2 = (f32[2,4,128,128]{3,2,1,0:T(8,128)}, f32[2,4,128,128]{3,2,1,0:T(8,128)}) custom-call(s32[8]{0:T(128)S(1)} %concatenate.6.where_ref, f32[3,6,144,128]{3,2,1,0:T(8,128)S(1)} %copy-done.3, f32[3,6,144,128]{3,2,1,0:T(8,128)} %copy-done.4, f32[3,6,144,128]{3,2,1,0:T(8,128)} %copy-done.13, f32[3,6,144,128]{3,2,1,0:T(8,128)} %collective-permute-done.3.f_hi, ...), custom_call_target="tpu_custom_call" | custom-call | flops 61931520 | bytes 9895936 | tf_op jit(solution)/shard_map/adjoint/pallas_call | solution.py:361
  204.1 8.8 %collective-permute-done.13.refs_1_ = f32[2,4,128,128]{3,2,1,0:T(8,128)S(1)} collective-permute-done((f32[2,4,128,128]{3,2,1,0:T(8,128)}, f32[2,4,128,128]{3,2,1,0:T(8,128)S(1)}, u32[]{:S(2)}, u32[]{:S(2)}) %collective-permute-start.13) | collective-permute-done | bytes 524320 | tf_op jit(solution)/shard_map/ppermute | solution.py:648
  212.9 3.4 %copy-done = f32[16,4,256,128]{3,2,1,0:T(8,128)S(1)} copy-done((f32[16,4,256,128]{3,2,1,0:T(8,128)S(1)}, f32[16,4,256,128]{3,2,1,0:T(8,128)}, u32[]{:S(2)}) %copy-start) | copy-done | bytes 8388632
  217.8 6.3 %projections.1 = (f32[128,128]{1,0:T(8,128)}, f32[4,1024,128]{2,1,0:T(8,128)S(1)}) custom-call(s32[8]{0:T(128)S(1)} %concatenate.6.where_ref, f32[16,1024,128]{2,1,0:T(8,128)S(1)} %bitcast.26, f32[4,1024,128]{2,1,0:T(8,128)S(1)} %bitcast.28, f32[2,4,128,128]{3,2,1,0:T(8,128)S(1)} %collective-permute-done.12.refs_0_, ...), custom_call_target="tpu_custom_call" | custom-call | flops 16777216 | bytes 14680064 | tf_op jit(solution)/shard_map/projections/pallas_call | solution.py:156
  225.5 3.5 %all-to-all-start = ((f32[16,8,128]{2,1,0:T(8,128)}), f32[16,8,128]{2,1,0:T(8,128)S(1)}, u32[]{:S(2)}, u32[]{:S(2)}) async-start(f32[16,8,128]{2,1,0:T(8,128)} %bitcast.8), calls=%async_computation | async-start | bytes 131072 | tf_op jit(solution)/shard_map/all_to_all | solution.py:90
  229.2 6.7 %all-to-all-done = f32[16,8,128]{2,1,0:T(8,128)S(1)} async-done(((f32[16,8,128]{2,1,0:T(8,128)}), f32[16,8,128]{2,1,0:T(8,128)S(1)}, u32[]{:S(2)}, u32[]{:S(2)}) %all-to-all-start) | async-done | bytes 65568 | tf_op jit(solution)/shard_map/all_to_all | solution.py:90
  235.8 3.4 %copy-done.1 = f32[16,4,256,128]{3,2,1,0:T(8,128)S(1)} copy-done((f32[16,4,256,128]{3,2,1,0:T(8,128)S(1)}, f32[16,4,256,128]{3,2,1,0:T(8,128)}, u32[]{:S(2)}) %copy-start.1) | copy-done | bytes 8388632
  240.8 5.3 %remainder.1 = (f32[4,1024,128]{2,1,0:T(8,128)S(1)}, f32[16,4]{1,0:T(8,128)S(1)}, f32[128,128]{1,0:T(8,128)}) custom-call(f32[128,128]{1,0:T(8,128)S(1)} %bitcast.29, f32[16,16]{1,0:T(8,128)S(1)} %fusion.1.inverse_ref, f32[16,1024,128]{2,1,0:T(8,128)S(1)} %bitcast.27, f32[4,1024,128]{2,1,0:T(8,128)S(1)} %copy-done.7), custom_call_target="tpu_custom_call" | custom-call | flops 16777216 | bytes 12582912 | tf_op jit(solution)/shard_map/remainder/pallas_call | solution.py:257
  246.1 3.5 %all-to-all-start.2 = ((f32[16,8,128]{2,1,0:T(8,128)}), f32[16,8,128]{2,1,0:T(8,128)S(1)}, u32[]{:S(2)}, u32[]{:S(2)}) async-start(f32[16,8,128]{2,1,0:T(8,128)} %bitcast.14), calls=%async_computation.2 | async-start | bytes 131072 | tf_op jit(solution)/shard_map/all_to_all | solution.py:90
  250.2 6.2 %all-to-all-done.2 = f32[16,8,128]{2,1,0:T(8,128)S(1)} async-done(((f32[16,8,128]{2,1,0:T(8,128)}), f32[16,8,128]{2,1,0:T(8,128)S(1)}, u32[]{:S(2)}, u32[]{:S(2)}) %all-to-all-start.2) | async-done | bytes 65568 | tf_op jit(solution)/shard_map/all_to_all | solution.py:90
  (97 shorter events, 42.5 us)
Async XLA Ops:
  3.2 11.7 %collective-permute-start.14 = (f32[2,4,144,128]{3,2,1,0:T(8,128)S(1)}, f32[2,4,144,128]{3,2,1,0:T(8,128)S(1)}, u32[]{:S(2)}, u32[]{:S(2)}) collective-permute-start(f32[2,4,144,128]{3,2,1,0:T(8,128)S(1)} %get-tuple-element.39), channel_id=1, source_target_pairs={{0,0},{1,2},{2,1},{3,3},{4,4},{5,6},{6,5},{7,7},{8,8},{9,10},{10,9... | collective-permute-start | bytes 1769480 | tf_op jit(solution)/shard_map/ppermute | solution.py:613
  3.9 19.2 %collective-permute-start.15 = (f32[2,4,144,128]{3,2,1,0:T(8,128)S(1)}, f32[2,4,144,128]{3,2,1,0:T(8,128)S(1)}, u32[]{:S(2)}, u32[]{:S(2)}) collective-permute-start(f32[2,4,144,128]{3,2,1,0:T(8,128)S(1)} %get-tuple-element.40), channel_id=1, source_target_pairs={{0,2},{1,0},{2,3},{3,1},{4,6},{5,4},{6,7},{7,5},{8,10},{9,8},{10,1... | collective-permute-start | bytes 1769480 | tf_op jit(solution)/shard_map/ppermute | solution.py:613
  9.9 16.2 %collective-permute-start = (f32[3,4,144,128]{3,2,1,0:T(8,128)S(1)}, f32[3,4,144,128]{3,2,1,0:T(8,128)S(1)}, u32[]{:S(2)}, u32[]{:S(2)}) collective-permute-start(f32[3,4,144,128]{3,2,1,0:T(8,128)S(1)} %get-tuple-element.27), channel_id=1, source_target_pairs={{0,0},{1,2},{2,1},{3,3},{4,4},{5,6},{6,5},{7,7},{8,8},{9,10},{10,9... | collective-permute-start | bytes 2654216 | tf_op jit(solution)/shard_map/ppermute | solution.py:613
  10.6 30.2 %collective-permute-start.1 = (f32[3,4,144,128]{3,2,1,0:T(8,128)S(1)}, f32[3,4,144,128]{3,2,1,0:T(8,128)S(1)}, u32[]{:S(2)}, u32[]{:S(2)}) collective-permute-start(f32[3,4,144,128]{3,2,1,0:T(8,128)S(1)} %get-tuple-element.28), channel_id=1, source_target_pairs={{0,2},{1,0},{2,3},{3,1},{4,6},{5,4},{6,7},{7,5},{8,10},{9,8},{10,1... | collective-permute-start | bytes 2654216 | tf_op jit(solution)/shard_map/ppermute | solution.py:613
  14.2 34.0 %collective-permute-start.4 = (f32[2,4,144,128]{3,2,1,0:T(8,128)S(1)}, f32[2,4,144,128]{3,2,1,0:T(8,128)S(1)}, u32[]{:S(2)}, u32[]{:S(2)}) collective-permute-start(f32[2,4,144,128]{3,2,1,0:T(8,128)S(1)} %get-tuple-element.31), channel_id=1, source_target_pairs={{0,0},{1,2},{2,1},{3,3},{4,4},{5,6},{6,5},{7,7},{8,8},{9,10},{10,9... | collective-permute-start | bytes 1769480 | tf_op jit(solution)/shard_map/ppermute | solution.py:613
  14.9 41.8 %collective-permute-start.5 = (f32[2,4,144,128]{3,2,1,0:T(8,128)S(1)}, f32[2,4,144,128]{3,2,1,0:T(8,128)S(1)}, u32[]{:S(2)}, u32[]{:S(2)}) collective-permute-start(f32[2,4,144,128]{3,2,1,0:T(8,128)S(1)} %get-tuple-element.32), channel_id=1, source_target_pairs={{0,2},{1,0},{2,3},{3,1},{4,6},{5,4},{6,7},{7,5},{8,10},{9,8},{10,1... | collective-permute-start | bytes 1769480 | tf_op jit(solution)/shard_map/ppermute | solution.py:613
  23.8 39.8 %collective-permute-start.16 = (f32[2,6,144,128]{3,2,1,0:T(8,128)S(1)}, f32[2,6,144,128]{3,2,1,0:T(8,128)S(1)}, u32[]{:S(2)}, u32[]{:S(2)}) collective-permute-start(f32[2,6,144,128]{3,2,1,0:T(8,128)S(1)} %get-tuple-element.41.v_up), channel_id=1, source_target_pairs={{0,1},{1,4},{2,3},{3,6},{4,5},{5,8},{6,7},{7,10},{8,9},{9,12},{10,... | collective-permute-start | bytes 2654216 | tf_op jit(solution)/shard_map/ppermute | solution.py:619
  26.0 20.9 %collective-permute-start.8 = (f32[2,4096]{1,0:T(2,128)S(1)}, f32[2,4096]{1,0:T(2,128)S(1)}, u32[]{:S(2)}, u32[]{:S(2)}) collective-permute-start(f32[2,4096]{1,0:T(2,128)S(1)} %pad_maximum_fusion), channel_id=1, source_target_pairs={{0,0},{1,2},{2,1},{3,3},{4,4},{5,6},{6,5},{7,7},{8,8},{9,10},{10,9... | collective-permute-start | bytes 98312 | tf_op jit(solution)/shard_map/ppermute | solution.py:613
  41.5 29.1 %collective-permute-start.2 = (f32[3,6,144,128]{3,2,1,0:T(8,128)S(1)}, f32[3,6,144,128]{3,2,1,0:T(8,128)S(1)}, u32[]{:S(2)}, u32[]{:S(2)}) collective-permute-start(f32[3,6,144,128]{3,2,1,0:T(8,128)S(1)} %get-tuple-element.29.f_up), channel_id=1, source_target_pairs={{0,1},{1,4},{2,3},{3,6},{4,5},{5,8},{6,7},{7,10},{8,9},{9,12},{10,... | collective-permute-start | bytes 3981320 | tf_op jit(solution)/shard_map/ppermute | solution.py:619
  46.9 23.7 %collective-permute-start.3 = (f32[3,6,144,128]{3,2,1,0:T(8,128)S(1)}, f32[3,6,144,128]{3,2,1,0:T(8,128)}, u32[]{:S(2)}, u32[]{:S(2)}) collective-permute-start(f32[3,6,144,128]{3,2,1,0:T(8,128)S(1)} %get-tuple-element.30.f_down), channel_id=1, source_target_pairs={{1,0},{4,1},{3,2},{6,3},{5,4},{8,5},{7,6},{10,7},{9,8},{12,9},{11,... | collective-permute-start | bytes 3981320 | tf_op jit(solution)/shard_map/ppermute | solution.py:619
  48.2 11.5 %collective-permute-start.9 = (f32[2,4096]{1,0:T(2,128)S(1)}, f32[2,4096]{1,0:T(2,128)S(1)}, u32[]{:S(2)}, u32[]{:S(2)}) collective-permute-start(f32[2,4096]{1,0:T(2,128)S(1)} %pad_maximum_fusion), channel_id=1, source_target_pairs={{0,2},{1,0},{2,3},{3,1},{4,6},{5,4},{6,7},{7,5},{8,10},{9,8},{10,1... | collective-permute-start | bytes 98312 | tf_op jit(solution)/shard_map/ppermute | solution.py:613
  56.8 13.8 %collective-permute-start.17 = (f32[2,6,144,128]{3,2,1,0:T(8,128)S(1)}, f32[2,6,144,128]{3,2,1,0:T(8,128)S(1)}, u32[]{:S(2)}, u32[]{:S(2)}) collective-permute-start(f32[2,6,144,128]{3,2,1,0:T(8,128)S(1)} %get-tuple-element.42.v_down), channel_id=1, source_target_pairs={{1,0},{4,1},{3,2},{6,3},{5,4},{8,5},{7,6},{10,7},{9,8},{12,9},{11,... | collective-permute-start | bytes 2654216 | tf_op jit(solution)/shard_map/ppermute | solution.py:619
  59.7 47.3 %collective-permute-start.6 = (f32[2,6,144,128]{3,2,1,0:T(8,128)S(1)}, f32[2,6,144,128]{3,2,1,0:T(8,128)}, u32[]{:S(2)}, u32[]{:S(2)}) collective-permute-start(f32[2,6,144,128]{3,2,1,0:T(8,128)S(1)} %get-tuple-element.33.v_up), channel_id=1, source_target_pairs={{0,1},{1,4},{2,3},{3,6},{4,5},{5,8},{6,7},{7,10},{8,9},{9,12},{10,... | collective-permute-start | bytes 2654216 | tf_op jit(solution)/shard_map/ppermute | solution.py:619
  63.6 43.4 %collective-permute-start.7 = (f32[2,6,144,128]{3,2,1,0:T(8,128)}, f32[2,6,144,128]{3,2,1,0:T(8,128)}, u32[]{:S(2)}, u32[]{:S(2)}) collective-permute-start(f32[2,6,144,128]{3,2,1,0:T(8,128)} %get-tuple-element.34.v_down), channel_id=1, source_target_pairs={{1,0},{4,1},{3,2},{6,3},{5,4},{8,5},{7,6},{10,7},{9,8},{12,9},{11,... | collective-permute-start | bytes 2654216 | tf_op jit(solution)/shard_map/ppermute | solution.py:619
  91.3 64.1 %collective-permute-start.18 = (f32[2,6,144,128]{3,2,1,0:T(8,128)}, f32[2,6,144,128]{3,2,1,0:T(8,128)}, u32[]{:S(2)}, u32[]{:S(2)}) collective-permute-start(f32[2,6,144,128]{3,2,1,0:T(8,128)} %get-tuple-element.43.v_up), channel_id=1, source_target_pairs={{0,1},{1,4},{2,3},{3,6},{4,5},{5,8},{6,7},{7,10},{8,9},{9,12},{10,... | collective-permute-start | bytes 2654216 | tf_op jit(solution)/shard_map/ppermute | solution.py:619
  105.3 50.1 %collective-permute-start.19 = (f32[2,6,144,128]{3,2,1,0:T(8,128)}, f32[2,6,144,128]{3,2,1,0:T(8,128)}, u32[]{:S(2)}, u32[]{:S(2)}) collective-permute-start(f32[2,6,144,128]{3,2,1,0:T(8,128)} %get-tuple-element.44.v_down), channel_id=1, source_target_pairs={{1,0},{4,1},{3,2},{6,3},{5,4},{8,5},{7,6},{10,7},{9,8},{12,9},{11,... | collective-permute-start | bytes 2654216 | tf_op jit(solution)/shard_map/ppermute | solution.py:619
  128.3 48.7 %collective-permute-start.10 = (f32[2,6,144,128]{3,2,1,0:T(8,128)}, f32[2,6,144,128]{3,2,1,0:T(8,128)S(1)}, u32[]{:S(2)}, u32[]{:S(2)}) collective-permute-start(f32[2,6,144,128]{3,2,1,0:T(8,128)} %get-tuple-element.35.v_up), channel_id=1, source_target_pairs={{0,1},{1,4},{2,3},{3,6},{4,5},{5,8},{6,7},{7,10},{8,9},{9,12},{10,... | collective-permute-start | bytes 2654216 | tf_op jit(solution)/shard_map/ppermute | solution.py:619
  131.4 45.7 %collective-permute-start.11 = (f32[2,6,144,128]{3,2,1,0:T(8,128)}, f32[2,6,144,128]{3,2,1,0:T(8,128)}, u32[]{:S(2)}, u32[]{:S(2)}) collective-permute-start(f32[2,6,144,128]{3,2,1,0:T(8,128)} %get-tuple-element.36.v_down), channel_id=1, source_target_pairs={{1,0},{4,1},{3,2},{6,3},{5,4},{8,5},{7,6},{10,7},{9,8},{12,9},{11,... | collective-permute-start | bytes 2654216 | tf_op jit(solution)/shard_map/ppermute | solution.py:619
  174.9 29.1 %collective-permute-start.20 = (f32[2,4,128,128]{3,2,1,0:T(8,128)}, f32[2,4,128,128]{3,2,1,0:T(8,128)S(1)}, u32[]{:S(2)}, u32[]{:S(2)}) collective-permute-start(f32[2,4,128,128]{3,2,1,0:T(8,128)} %get-tuple-element.45), channel_id=1, source_target_pairs={{0,0},{2,1},{1,2},{3,3},{4,4},{6,5},{5,6},{7,7},{8,8},{10,9},{9,10... | collective-permute-start | bytes 1572872 | tf_op jit(solution)/shard_map/ppermute | solution.py:648
  176.6 27.4 %collective-permute-start.21 = (f32[2,4,128,128]{3,2,1,0:T(8,128)}, f32[2,4,128,128]{3,2,1,0:T(8,128)S(1)}, u32[]{:S(2)}, u32[]{:S(2)}) collective-permute-start(f32[2,4,128,128]{3,2,1,0:T(8,128)} %get-tuple-element.46), channel_id=1, source_target_pairs={{2,0},{0,1},{3,2},{1,3},{6,4},{4,5},{7,6},{5,7},{10,8},{8,9},{11,1... | collective-permute-start | bytes 1572872 | tf_op jit(solution)/shard_map/ppermute | solution.py:648
  196.3 7.7 %collective-permute-start.12 = (f32[2,4,128,128]{3,2,1,0:T(8,128)}, f32[2,4,128,128]{3,2,1,0:T(8,128)S(1)}, u32[]{:S(2)}, u32[]{:S(2)}) collective-permute-start(f32[2,4,128,128]{3,2,1,0:T(8,128)} %get-tuple-element.37), channel_id=1, source_target_pairs={{0,0},{2,1},{1,2},{3,3},{4,4},{6,5},{5,6},{7,7},{8,8},{10,9},{9,10... | collective-permute-start | bytes 1572872 | tf_op jit(solution)/shard_map/ppermute | solution.py:648
  198.0 14.8 %collective-permute-start.13 = (f32[2,4,128,128]{3,2,1,0:T(8,128)}, f32[2,4,128,128]{3,2,1,0:T(8,128)S(1)}, u32[]{:S(2)}, u32[]{:S(2)}) collective-permute-start(f32[2,4,128,128]{3,2,1,0:T(8,128)} %get-tuple-element.38), channel_id=1, source_target_pairs={{2,0},{0,1},{3,2},{1,3},{6,4},{4,5},{7,6},{5,7},{10,8},{8,9},{11,1... | collective-permute-start | bytes 1572872 | tf_op jit(solution)/shard_map/ppermute | solution.py:648
  225.5 10.4 %all-to-all-start = ((f32[16,8,128]{2,1,0:T(8,128)}), f32[16,8,128]{2,1,0:T(8,128)S(1)}, u32[]{:S(2)}, u32[]{:S(2)}) async-start(f32[16,8,128]{2,1,0:T(8,128)} %bitcast.8), calls=%async_computation | async-start | bytes 131072 | tf_op jit(solution)/shard_map/all_to_all | solution.py:90
  246.1 10.4 %all-to-all-start.2 = ((f32[16,8,128]{2,1,0:T(8,128)}), f32[16,8,128]{2,1,0:T(8,128)S(1)}, u32[]{:S(2)}, u32[]{:S(2)}) async-start(f32[16,8,128]{2,1,0:T(8,128)} %bitcast.14), calls=%async_computation.2 | async-start | bytes 131072 | tf_op jit(solution)/shard_map/all_to_all | solution.py:90
  (19 other events, 268.2 us)

commit v2 on v1

v2 whole, which is shorter than its diff:
```python
import functools

import jax
import jax.numpy as jnp
from jax import lax
from jax.experimental import pallas as pl
from jax.experimental.pallas import tpu as pltpu
from jax.sharding import PartitionSpec as P

STEPS = 2
SWEEPS = 3
GROUPS = 2
SPARE = 16
REACH = STEPS * SWEEPS


DIFFUSION = 0.2
GAMMA = 0.5
LANES = 128
EXACT = lax.Precision.HIGHEST
SMEM = pl.BlockSpec(memory_space=pltpu.SMEM)
VMEM = pl.BlockSpec(memory_space=pltpu.VMEM)
ANY = pl.BlockSpec(memory_space=pl.ANY)
VECTOR = 150


def floats(*shape):
    return jax.ShapeDtypeStruct(shape, jnp.float32)


def cost(flops, moved):
    return pl.CostEstimate(flops=int(flops), bytes_accessed=int(moved), transcendentals=0)


def lane_sums(stack):
    ones = jnp.ones((8, LANES), jnp.float32)
    return lax.dot_general(
        ones, stack, (((1,), (1,)), ((), ())), precision=EXACT, preferred_element_type=jnp.float32
    )


def gram_kernel(where_ref, basis_ref, out_ref, where_out, acc_ref):
    rank = basis_ref.shape[0]
    rows = basis_ref.shape[1]
    step = pl.program_id(0)
    tile = 4

    @pl.when(step == 0)
    def _():
        acc_ref[...] = jnp.zeros_like(acc_ref)
        for k in range(where_ref.shape[0]):
            where_out[k] = where_ref[k]

    for i0 in range(0, rank, tile):
        for j0 in range(i0, rank, tile):
            pairs = [(i, j) for i in range(i0, i0 + tile) for j in range(j0, j0 + tile) if i <= j]

            def add(k, sums, i0=i0, j0=j0, pairs=pairs):
                at = pl.ds(pl.multiple_of(k * 8, 8), 8)
                left = {i: basis_ref[i, at, :] for i in range(i0, i0 + tile)}
                right = left if i0 == j0 else {j: basis_ref[j, at, :] for j in range(j0, j0 + tile)}
                return [s + left[i] * right[j] for s, (i, j) in zip(sums, pairs)]

            sums = [jnp.zeros((8, LANES), jnp.float32) for _ in pairs]
            sums = lax.fori_loop(0, rows // 8, add, sums, unroll=8)
            for (i, j), s in zip(pairs, sums):
                acc_ref[i, j] += s

    @pl.when(step == pl.num_programs(0) - 1)
    def _():
        row = lax.broadcasted_iota(jnp.int32, (rank, rank), 0)
        col = lax.broadcasted_iota(jnp.int32, (rank, rank), 1)
        gram = jnp.zeros((rank, rank), jnp.float32)
        for i in range(rank):
            sums = lane_sums(jnp.sum(acc_ref[i], axis=1))
            gram = jnp.where(row == i, jnp.broadcast_to(sums[0:1, :], (rank, rank)), gram)
        upper = jnp.where(col >= row, gram, 0.0)
        strict = jnp.where(col > row, gram, 0.0)
        whole = upper + strict.T
        out_ref[...] = jnp.zeros_like(out_ref)
        for k in range(0, rank, 8):
            at = rank + k * rank // 8
            out_ref[:, at : at + rank] = whole[k : k + 8]


def gram_tile(where, basis):
    rank, rows, _ = basis.shape
    chunk = 128
    return pl.pallas_call(
        gram_kernel,
        grid=(rows // chunk,),
        in_specs=[SMEM, pl.BlockSpec((rank, chunk, LANES), lambda k: (0, k, 0))],
        out_specs=[pl.BlockSpec((8, LANES), lambda k: (0, 0)), SMEM],
        out_shape=[floats(8, LANES), jax.ShapeDtypeStruct(where.shape, where.dtype)],
        scratch_shapes=[pltpu.VMEM((rank, rank, 8, LANES), jnp.float32)],
        compiler_params=pltpu.CompilerParams(vmem_limit_bytes=16 << 20),
        cost_estimate=cost(VECTOR * rank * rank * rows * LANES, rank * rows * LANES * 4),
        name="gram",
    )(where, basis)


def spread(tile, count):
    return lax.all_to_all(tile, "slab", 0, 0, tiled=True) if count > 1 else tile


def projection_kernel(dirs, first, last, where_ref, basis_ref, dirs_ref, own_ref, other_ref, tile_ref, out_ref, image_ref, acc_ref):
    rank = basis_ref.shape[0]
    rows = image_ref.shape[1]
    step = pl.program_id(0)
    tile = 8

    @pl.when(step == 0)
    def _():
        acc_ref[...] = jnp.zeros_like(acc_ref)

    for side, ref in enumerate((own_ref, other_ref)):

        @pl.when((step < pl.num_programs(0) // 2) == (side == 0))
        def _(ref=ref):
            for d in range(dirs):
                image_ref[d] = ref[d, 0] + GAMMA * dirs_ref[d]

    for i0 in range(0, rank, tile):

        def add(k, sums, i0=i0):
            at = pl.ds(pl.multiple_of(k * 8, 8), 8)
            image = [image_ref[d, at, :] for d in range(dirs)]
            out = []
            for i in range(tile):
                q = basis_ref[i0 + i, at, :]
                out += [sums[i * dirs + d] + q * image[d] for d in range(dirs)]
            return out

        sums = [jnp.zeros((8, LANES), jnp.float32) for _ in range(tile * dirs)]
        sums = lax.fori_loop(0, rows // 8, add, sums, unroll=8)
        for i in range(tile):
            for d in range(dirs):
                acc_ref[d, i0 + i] += sums[i * dirs + d]

    @pl.when(step == pl.num_programs(0) - 1)
    def _():
        row = lax.broadcasted_iota(jnp.int32, (8, LANES), 0)
        lane = lax.broadcasted_iota(jnp.int32, (8, LANES), 1)
        table = tile_ref[...]
        for d in range(dirs):
            sums = jnp.sum(acc_ref[d], axis=1)
            sums = jnp.concatenate([sums, jnp.zeros((LANES - rank, LANES), jnp.float32)], 0)
            table = jnp.where((row == first + d) & (lane < rank), lane_sums(sums), table)
        for r in range(out_ref.shape[0] // 8):
            out_ref[r * 8 : (r + 1) * 8, :] = table


def projections(where, basis, directions, first, halves, tile, count):
    rank, rows, _ = basis.shape
    _, planes, width, _ = directions.shape
    dirs = halves[0].shape[0]
    half = width // 2

    def line(k, where_ref):
        part = jnp.where(k < planes, where_ref[1], 1 - where_ref[1])
        return 2 * lax.rem(k, planes) + part

    def side(which):
        def index(k, where_ref):
            return (0, jnp.minimum(k, planes - 1) if which == 0 else jnp.maximum(k - planes, 0), 0, 0)

        return pl.BlockSpec((dirs, 1, half, LANES), index)

    return pl.pallas_call(
        functools.partial(projection_kernel, dirs, first, count > 1),
        grid_spec=pltpu.PrefetchScalarGridSpec(
            num_scalar_prefetch=1,
            grid=(2 * planes,),
            in_specs=[
                pl.BlockSpec((rank, half, LANES), lambda k, w: (0, line(k, w), 0)),
                pl.BlockSpec((dirs, half, LANES), lambda k, w: (first // dirs, line(k, w), 0)),
                side(0),
                side(1),
                pl.BlockSpec((8, LANES), lambda k, w: (0, 0)),
            ],
            out_specs=[
                pl.BlockSpec((count * 8, LANES), lambda k, w: (0, 0)),
                pl.BlockSpec((dirs, half, LANES), lambda k, w: (0, line(k, w), 0)),
            ],
            scratch_shapes=[pltpu.VMEM((dirs, rank, 8, LANES), jnp.float32)],
        ),
        out_shape=[floats(count * 8, LANES), floats(dirs, rows, LANES)],
        compiler_params=pltpu.CompilerParams(vmem_limit_bytes=52 << 20),
        cost_estimate=cost(
            VECTOR * 2 * rank * dirs * rows * LANES, (rank + 3 * dirs) * rows * LANES * 4
        ),
        name="projections",
    )(where, basis, directions.reshape(-1, rows, LANES), *halves, tile)


def summed_tile(parts_ref):
    tiles = [parts_ref[r : r + 8, :] for r in range(0, parts_ref.shape[0], 8)]
    while len(tiles) > 1:
        tiles = [sum(tiles[k : k + 2]) for k in range(0, len(tiles), 2)]
    return tiles[0]


def solved(tile, rank):
    gram = [tile[:, rank + k * rank // 8 :][:, :rank] for k in range(0, rank, 8)]
    table = jnp.concatenate(
        [
            jnp.concatenate(gram, 0),
            tile[:, 0:rank].T,
            jnp.zeros((rank, LANES - rank - 8), jnp.float32),
        ],
        1,
    )
    row = lax.broadcasted_iota(jnp.int32, (rank, LANES), 0)
    for k in range(rank):
        scaled_row = table[k : k + 1, :] / table[k : k + 1, k : k + 1]
        table = jnp.where(row == k, scaled_row, table - table[:, k : k + 1] * scaled_row)
    return table


def remainder_kernel(dirs, parts_ref, basis_ref, *refs):
    groups = len(refs) - 5
    images, (rem_ref, coeffs_ref, out_ref, splat_ref, energy_ref) = refs[:groups], refs[groups:]
    each = dirs // groups
    rank = basis_ref.shape[0]
    rows = rem_ref.shape[1]
    step = pl.program_id(0)
    tile = 4

    @pl.when(step == 0)
    def _():
        table = solved(summed_tile(parts_ref), rank)
        coeffs_ref[...] = table[:, rank : rank + dirs]
        for d in range(dirs):
            for j in range(rank):
                splat_ref[d * rank + j] = jnp.broadcast_to(
                    table[j : j + 1, rank + d : rank + d + 1], (8, LANES)
                )
        energy_ref[...] = jnp.zeros_like(energy_ref)

    for j0 in range(0, rank, tile):
        last = j0 + tile == rank
        weights = [[splat_ref[d * rank + j] for j in range(j0, j0 + tile)] for d in range(dirs)]

        def take(k, energy, j0=j0, last=last, weights=weights):
            at = pl.ds(pl.multiple_of(k * 8, 8), 8)
            basis = [basis_ref[j, at, :] for j in range(j0, j0 + tile)]
            out = []
            for d in range(dirs):
                left = images[d // each][d % each, at, :] if j0 == 0 else rem_ref[d, at, :]
                parts = [w * q for w, q in zip(weights[d], basis)]
                left = left - ((parts[0] + parts[1]) + (parts[2] + parts[3]))
                rem_ref[d, at, :] = left
                out.append(energy[d] + left * left if last else energy[d])
            return out

        energy = [jnp.zeros((8, LANES), jnp.float32) for _ in range(dirs)]
        energy = lax.fori_loop(0, rows // 8, take, energy, unroll=4)
        if last:
            for d in range(dirs):
                energy_ref[d] += energy[d]

    @pl.when(step == pl.num_programs(0) - 1)
    def _():
        row = lax.broadcasted_iota(jnp.int32, (8, LANES), 0)
        tile_out = jnp.zeros((8, LANES), jnp.float32)
        for d in range(dirs):
            total = jnp.sum(jnp.sum(energy_ref[d], axis=0, keepdims=True), axis=1, keepdims=True)
            tile_out = jnp.where(row == d, jnp.broadcast_to(total, (8, LANES)), tile_out)
        for r in range(out_ref.shape[0] // 8):
            out_ref[r * 8 : (r + 1) * 8, :] = tile_out


def remainders(parts, basis, images, count):
    rank, rows, _ = basis.shape
    dirs = sum(i.shape[0] for i in images)
    chunk = 128
    whole = lambda *shape: pl.BlockSpec(shape, lambda k: (0,) * len(shape))
    line = lambda n: pl.BlockSpec((n, chunk, LANES), lambda k: (0, k, 0))
    return pl.pallas_call(
        functools.partial(remainder_kernel, dirs),
        grid=(rows // chunk,),
        in_specs=[whole(count * 8, LANES), line(rank)] + [line(i.shape[0]) for i in images],
        out_specs=[line(dirs), whole(rank, dirs), whole(count * 8, LANES)],
        out_shape=[floats(dirs, rows, LANES), floats(rank, dirs), floats(count * 8, LANES)],
        scratch_shapes=[
            pltpu.VMEM((dirs * rank, 8, LANES), jnp.float32),
            pltpu.VMEM((dirs, 8, LANES), jnp.float32),
        ],
        compiler_params=pltpu.CompilerParams(vmem_limit_bytes=52 << 20),
        cost_estimate=cost(
            VECTOR * 2 * rank * dirs * rows * LANES, (rank + 2 * dirs) * rows * LANES * 4
        ),
        name="remainder",
    )(parts, basis, *images)


def scale_kernel(cells, parts_ref, rem_ref, new_ref):
    energy = summed_tile(parts_ref)
    value = energy / cells + 1e-06
    root = lax.rsqrt(value)
    root = root * (1.5 - (0.5 * value * root) * root)
    for d in range(rem_ref.shape[0]):
        new_ref[d] = rem_ref[d] * root[d : d + 1, :]


def scaled(parts, rem, cells, count):
    dirs, rows, _ = rem.shape
    chunk = 256
    return pl.pallas_call(
        functools.partial(scale_kernel, cells),
        grid=(rows // chunk,),
        in_specs=[
            pl.BlockSpec((count * 8, LANES), lambda k: (0, 0)),
            pl.BlockSpec((dirs, chunk, LANES), lambda k: (0, k, 0)),
        ],
        out_specs=pl.BlockSpec((dirs, chunk, LANES), lambda k: (0, k, 0)),
        out_shape=floats(dirs, rows, LANES),
        compiler_params=pltpu.CompilerParams(vmem_limit_bytes=16 << 20),
        name="scale",
    )(parts, rem)


def quad(count):
    own, other, above = [], [], []
    for s in range(count):
        q, a, b = s // 4, s // 2 % 2, s % 2
        own.append((s, 4 * q + 2 * b + a))
        other.append((s, 4 * q + 2 * (1 - b) + a))
        up = s + 1 if b == 0 else s + 3
        if up < count:
            above.append((s, up))
    return own, other, above


def back(pairs):
    return [(target, source) for source, target in pairs]


def call(kernel, name, ins, outs, scratch=(), limit=16, work=0, specs=None, grid=()):
    moved = sum(x.size * 4 for x in ins[1:]) + sum(o.size * 4 for o in outs)
    return pl.pallas_call(
        kernel,
        grid=grid,
        in_specs=[SMEM] + (specs or [VMEM] * (len(ins) - 1)),
        out_specs=[VMEM] * len(outs),
        out_shape=outs,
        scratch_shapes=list(scratch),
        compiler_params=pltpu.CompilerParams(vmem_limit_bytes=limit << 20),
        cost_estimate=cost(VECTOR * work, moved),
        name=name,
    )(*ins)


def cut_kernel(height, where_ref, *refs):
    sources, own_ref, other_ref = refs[:-2], refs[-2], refs[-1]
    b = where_ref[1]
    for ref, part in ((own_ref, b), (other_ref, 1 - b)):
        k = 0
        for source in sources:
            if len(source.shape) == 2:
                rows = source.shape[0]
                ref[k : k + rows, :] = source[...].astype(jnp.float32)
                k += rows
                continue
            start = pl.multiple_of(part * (source.shape[-2] - height), 16)
            for d in range(source.shape[0] if len(source.shape) == 4 else 1):
                block = source.at[d] if len(source.shape) == 4 else source
                for p in range(block.shape[0]):
                    ref[k : k + height, :] = block[p, pl.ds(start, height), :]
                    k += height


def pack_kernel(planes, where_ref, own_ref, other_ref, up_ref, down_ref):
    count, reach, height, _ = up_ref.shape
    skip = 2 * planes - reach

    def join(first, second):
        for d in range(count):
            for p in range(2 * planes):
                ref = first if p < planes else second
                at = (d * planes + p % planes) * height
                value = ref[at : at + height, :]
                if p >= skip:
                    up_ref[d, p - skip] = value
                if p < reach:
                    down_ref[d, p] = value

    @pl.when(where_ref[0] == 0)
    def _():
        join(own_ref, other_ref)

    @pl.when(where_ref[0] == 1)
    def _():
        join(other_ref, own_ref)


def sensor_kernel(width, skip, where_ref, own_ref, other_ref, out_ref):
    a = where_ref[0]
    _, planes, height, _ = out_ref.shape
    first = a * (width - height)
    count = (own_ref.shape[0] - skip) // 2
    group = 4
    chunk = group * LANES
    targets = planes * height
    rows = lax.broadcasted_iota(jnp.int32, (targets, chunk), 0)
    lanes = lax.broadcasted_iota(jnp.int32, (LANES, chunk), 0)
    for ref, at in ((own_ref, a), (other_ref, 1 - a)):
        total = jnp.zeros((targets, 3 * LANES), jnp.float32)
        for k in range(skip, skip + count, group):
            take = lambda at: jnp.concatenate([ref[at + g : at + g + 1, :] for g in range(group)], 1)
            cell = take(k).astype(jnp.int32)
            weight = take(count + k)
            line = cell // LANES
            lane = cell - line * LANES
            plane = line // width
            row = line - plane * width - first
            inside = (row >= 0) & (row < height)
            target = jnp.where(inside, plane * height + row, -1)
            high = weight.astype(jnp.bfloat16).astype(jnp.float32)
            rest = weight - high
            middle = rest.astype(jnp.bfloat16).astype(jnp.float32)
            low = rest - middle
            hot = jnp.where(rows == target, 1.0, 0.0).astype(jnp.bfloat16)
            here = lanes == lane
            parts = [jnp.where(here, part, 0.0).astype(jnp.bfloat16) for part in (high, middle, low)]
            total += lax.dot_general(
                hot,
                jnp.concatenate(parts, 0),
                (((1,), (1,)), ((), ())),
                preferred_element_type=jnp.float32,
            )
        total = total[:, 0:LANES] + total[:, LANES : 2 * LANES] + total[:, 2 * LANES :]
        out_ref[at] = total.reshape(planes, height, LANES)


def solve_kernel(adjoint, width, where_ref, *refs):
    flow_parts, value_parts = refs[0:4], refs[4:8]
    if adjoint:
        outs, (flow, coef, rhs, start, ping, pong, sems) = refs[8:10], refs[10:]
    else:
        weight_ref, outs, (flow, coef, rhs, start, ping, pong, sems) = refs[8], refs[9:11], refs[11:]
    dirs, depth, height, _ = rhs.shape
    reach = REACH
    own = depth - 2 * reach
    chunks = height // 8
    a, at_bottom, at_top = where_ref[0], where_ref[2], where_ref[3]
    code = [where_ref[4 + k] for k in range(4)]

    def arrivals(parts, into, first):
        up, down, lo, hi = parts
        moves = (
            (lo, into.at[:, 0:reach]),
            (down, into.at[:, reach : 2 * reach]),
            (up.at[:, 2 * reach - own : reach], into.at[:, 2 * reach : reach + own]),
            (hi, into.at[:, reach + own : depth]),
        )
        return [pltpu.make_async_copy(s, t, sems.at[first + k]) for k, (s, t) in enumerate(moves)]

    flow_moves = arrivals(flow_parts, flow, 0)
    value_moves = arrivals(value_parts, start, 4)
    for move in flow_moves + value_moves:
        move.start()

    shape = (8, LANES)
    sub = lax.broadcasted_iota(jnp.int32, shape, 0)
    lane = lax.broadcasted_iota(jnp.int32, shape, 1)
    top_sub, bottom_sub = sub == 7, sub == 0
    last_lane, first_lane = lane == LANES - 1, lane == 0
    zero = jnp.zeros(shape, jnp.float32)
    opened = [jnp.where(c == 0, 1.0, 0.0).astype(jnp.float32) for c in code]
    low_one = jnp.where(bottom_sub & (a == 0), opened[0], 1.0)
    high_one = jnp.where(top_sub & (a == 1), opened[1], 1.0)
    low_two = jnp.where(first_lane, opened[2], 1.0)
    high_two = jnp.where(last_lane, opened[3], 1.0)

    def both(x):
        positive = DIFFUSION + jnp.maximum(x, 0.0)
        return positive, positive - x

    def coefficients(p, carry):
        outside = ((p < reach) & (at_bottom == 1)) | ((p >= reach + own) & (at_top == 1))
        inside = jnp.where(outside, 0.0, 1.0)
        turned = zero
        for r in range(chunks):
            here = slice(r * 8, r * 8 + 8)
            one, two, three = flow[0, p, here, :], flow[1, p, here, :], flow[2, p, here, :]
            one_turned = pltpu.roll(one, 1, 0)
            one_below = jnp.where(bottom_sub, turned, one_turned)
            turned = one_turned
            two_below = jnp.where(first_lane, 0.0, pltpu.roll(two, 1, 1))
            up = [both(x) for x in (one, two, three)]
            down = [both(x) for x in (one_below, two_below, flow[2, p - 1, here, :])]
            first = up[0][0] if r < chunks - 1 else high_one * up[0][0]
            second = down[0][1] if r > 0 else low_one * down[0][1]
            diagonal = (1.0 + first) + (second + high_two * up[1][0])
            diagonal = diagonal + (low_two * down[1][1] + (up[2][0] + down[2][1]))
            inverse = inside / diagonal
            which = 0 if adjoint else 1
            coef[0, p, here, :] = up[0][which] * inverse
            coef[1, p, here, :] = down[0][1 - which] * inverse
            coef[2, p, here, :] = jnp.where(last_lane, 0.0, up[1][which] * inverse)
            coef[3, p, here, :] = jnp.where(first_lane, 0.0, down[1][1 - which] * inverse)
            coef[4, p, here, :] = up[2][which] * inverse
            coef[5, p, here, :] = down[2][1 - which] * inverse
            coef[6, p, here, :] = inverse
        return carry

    for move in flow_moves:
        move.wait()
    lax.fori_loop(1, depth - 1, coefficients, 0)
    for move in value_moves:
        move.wait()

    def sweep(source, lead, low, high, offset, count, store):
        def rows(r):
            return pl.ds(offset + r * 8, 8)

        def at_plane(p, carry):
            value = [source[d, p, rows(0), :] for d in range(dirs)]
            up = [pltpu.roll(v, 7, 0) for v in value]
            down = [pltpu.roll(v, 1, 0) for v in value]
            before = [zero] * dirs
            if count < chunks:
                for d in range(dirs):
                    outer = source[d, p, pl.ds(pl.multiple_of(jnp.maximum(offset - 8, 0), 8), 8), :]
                    before[d] = jnp.where(a == 0, 0.0, pltpu.roll(outer, 1, 0))
            for r in range(count):
                c = [coef[k, p, rows(r), :] for k in range(7 if lead else 6)]
                for d in range(dirs):
                    if r + 1 < count:
                        following = source[d, p, rows(r + 1), :]
                        next_up, next_down = pltpu.roll(following, 7, 0), pltpu.roll(following, 1, 0)
                    elif count < chunks:
                        at = pl.multiple_of(jnp.minimum(offset + count * 8, height - 8), 8)
                        following = source[d, p, pl.ds(at, 8), :]
                        next_up, next_down = jnp.where(a == 1, 0.0, pltpu.roll(following, 7, 0)), zero
                    else:
                        following, next_up, next_down = zero, zero, zero
                    if lead:
                        total = value[d] * c[6]
                        rhs[d, p, rows(r), :] = total
                    else:
                        total = rhs[d, p, rows(r), :]
                    total = total + c[4] * source[d, p + 1, rows(r), :]
                    total = total + c[5] * source[d, p - 1, rows(r), :]
                    total = total + c[0] * jnp.where(top_sub, next_up, up[d])
                    total = total + c[1] * jnp.where(bottom_sub, before[d], down[d])
                    total = total + c[2] * pltpu.roll(value[d], LANES - 1, 1)
                    total = total + c[3] * pltpu.roll(value[d], 1, 1)
                    store(d, p, rows(r), r, total)
                    value[d], up[d], before[d], down[d] = following, next_up, down[d], next_down
            return carry

        lax.fori_loop(low, high, at_plane, 0)

    def into(ref):
        def store(d, p, here, r, total):
            ref[d, p, here, :] = total

        return store

    def again(d, p, here, r, total):
        start[d, p, here, :] = total if adjoint else total + start[d, p, here, :]

    def full(source, lead, step, store):
        sweep(source, lead, 1 + step, depth - 1 - step, 0, chunks, store)

    full(start, True, 0, into(ping))
    full(ping, False, 1, into(pong))
    full(pong, False, 2, again)
    full(start, True, 3, into(ping))
    full(ping, False, 4, into(pong))

    half = own // 2
    if adjoint:
        for out, side in zip(outs, (a, 1 - a)):
            low = reach + side * half

            def finish(d, p, here, r, total, out=out, low=low):
                out[d, p - low, r * 8 : r * 8 + 8, :] = total + start[d, p, here, :]

            shift = pl.multiple_of(a * SPARE, 8)
            sweep(pong, False, low, low + half, shift, (height - SPARE) // 8, finish)
    else:
        up_out, down_out = outs

        def emit(kinds):
            def finish(d, p, here, r, total):
                i = p - reach
                total = total * weight_ref[i // half, i % half, here, :]
                if "d" in kinds:
                    down_out[d, i, here, :] = total
                if "u" in kinds:
                    up_out[d, i - (own - reach), here, :] = total

            return finish

        for low, high, kinds in ((0, own - reach, "d"), (own - reach, reach, "du"), (reach, own, "u")):
            sweep(pong, False, reach + low, reach + high, 0, chunks, emit(kinds))


def solves(adjoint, width, where, planes, flows, values, weight=None):
    dirs, reach, height, _ = values[0].shape
    depth = 2 * planes + 2 * reach
    ins = [where, *flows, *values]
    specs = [ANY] * 8
    if adjoint:
        outs = [floats(dirs, planes, height - SPARE, LANES)] * 2
    else:
        ins.append(weight)
        specs.append(VMEM)
        outs = [floats(*values[0].shape)] * 2
    scratch = [pltpu.VMEM((n, depth, height, LANES), jnp.float32) for n in (3, 7) + (dirs,) * 4]
    scratch.append(pltpu.SemaphoreType.DMA((8,)))
    return call(
        functools.partial(solve_kernel, adjoint, width),
        "adjoint" if adjoint else "forward",
        ins, outs, scratch, 36, 6 * 20 * dirs * depth * height * LANES, specs,
    )


def body(
    directions,
    eigen_basis,
    flow_first,
    flow_second,
    flow_depth,
    face_codes,
    sensor_cells,
    sensor_weight,
):
    dirs, planes, width, _ = directions.shape
    rank = eigen_basis.shape[0]
    count = lax.axis_size("slab")
    height = width // 2 + SPARE
    own, other, above = quad(count)
    me = lax.axis_index("slab")
    a, b = me // 2 % 2, me % 2
    place = [a, b, (me - 2 * a == 0), (me + 2 * (1 - a) == count - 1)]
    where = jnp.concatenate([jnp.stack([x.astype(jnp.int32) for x in place]), face_codes])
    each = dirs // GROUPS

    def regroup(first, second):
        return lax.ppermute(first, "slab", own), lax.ppermute(second, "slab", other)

    def cut(arrays, rows, group=None):
        specs, grid = [VMEM] * len(arrays), ()
        if group is not None:
            arrays, specs = [directions, *arrays], [group_of(group), *specs]
            grid = (1,)
        outs = [floats(rows, LANES)] * 2
        return call(functools.partial(cut_kernel, height), "cut", [where, *arrays], outs, specs=specs, grid=grid)

    def group_of(k):
        return pl.BlockSpec((each, planes, width, LANES), lambda _: (k, 0, 0, 0))

    def beyond(up, down):
        return up, down, lax.ppermute(up, "slab", above), lax.ppermute(down, "slab", back(above))

    def pack(scalars, pair, parts):
        outs = [floats(parts, REACH, height, LANES)] * 2
        return call(functools.partial(pack_kernel, planes), "pack", [scalars, *pair], outs)

    sensors = [x.reshape(-1, LANES) for x in (sensor_cells, sensor_weight)]
    listed = 2 * sensors[0].shape[0]
    block = planes * height
    flows = regroup(*cut([flow_first, flow_second, flow_depth], 3 * block))
    moved = [regroup(*cut(sensors, each * block + listed, 0))]
    moved += [regroup(*cut([], each * block, k)) for k in range(1, GROUPS)]

    basis = eigen_basis.reshape(rank, planes * width, LANES)
    tile, later = gram_tile(where, basis)
    flows = beyond(*pack(later, flows, 3))
    (weight,) = call(
        functools.partial(sensor_kernel, width, each * block), "sensors",
        [later, *moved[0]], [floats(2, planes, height, LANES)], work=planes * height * listed * 20,
    )
    values = [beyond(*pack(later, m, each)) for m in moved]
    forcing = [beyond(*solves(False, width, where, planes, flows, v, weight)) for v in values]
    summed = [solves(True, width, where, planes, flows, f) for f in forcing]
    returned = [
        (lax.ppermute(s[0], "slab", back(own)), lax.ppermute(s[1], "slab", back(other)))
        for s in summed
    ]
    images = []
    for k, halves in enumerate(returned):
        copies = count if k == GROUPS - 1 else 1
        tile, image = projections(where, basis, directions, k * each, halves, tile, copies)
        images.append(image)
    rem, coeffs, parts = remainders(spread(tile, count), basis, images, count)
    new_directions = scaled(spread(parts, count), rem, planes * count * width * LANES, count)
    return (new_directions.reshape(directions.shape), coeffs)


def solution(mesh):
    return jax.shard_map(
        body,
        mesh=mesh,
        in_specs=(
            P("grp", "slab", None, None),
            P("grp", "slab", None, None),
            P("slab", None, None),
            P("slab", None, None),
            P("slab", None, None),
            P(),
            P(("grp", "slab")),
            P(("grp", "slab")),
        ),
        out_specs=(P("grp", "slab", None, None), P("grp", None)),
        check_vma=False,
    )
```

time: 259 us -> 212 us (0.82)
  starting transfers between devices: 74.8 us -> 48.1 us
  waiting for transfers between devices: 35.8 us -> 26.4 us
  local copies, waits for them, and re-layouts: 17.4 us -> 12.5 us
  other arithmetic: 4.22 us -> 0 us
    ppermute x4 -> x3, starting transfers between devices: 24 us -> 9.92 us  [regroup(): lax.ppermute(second, 'slab', other)]
    ppermute x5, starting transfers between devices: 28.5 us -> 18 us  [beyond(): lax.ppermute(up, 'slab', above)]
    all_to_all x2 -> x1, waiting for transfers between devices: 12.9 us -> 6.21 us  [spread(): return lax.all_to_all(tile, 'slab', 0, 0, tiled=True) if count > 1 else tile]
    ppermute x2, starting transfers between devices: 2.38 us -> 6.55 us  [body(): lax.ppermute(s[1], 'slab', back(other))]
    another operation x6 -> x0, other arithmetic: 4.04 us -> none  [the longest x3 2.13 us: body(): factor_lower = jnp.linalg.cholesky(gram)]
    unnamed x41 -> x21, local copies, waits for them, and re-layouts: 15.3 us -> 11.8 us
    all_to_all x2 -> x1, starting transfers between devices: 7 us -> 3.5 us  [spread(): return lax.all_to_all(tile, 'slab', 0, 0, tiled=True) if count > 1 else tile]
    ppermute x2, waiting for transfers between devices: 8.82 us -> 5.4 us  [body(): lax.ppermute(s[1], 'slab', back(other))]
  transfers between devices with their start and end apart: 24 -> 21, of which waited for: 4 -> 5; matrix products, arithmetic and copies ran while one was open for 2% -> 0% of each run, Pallas kernels for 37% -> 42%
where the time goes in v2:
time: 212 us; the launch traced here: 211 us
  Pallas kernels  109 us (51%)
  starting transfers between devices  48.1 us (23%)
  waiting for transfers between devices  26.4 us (12%)
  blocking collectives  13.3 us (6%)
  local copies, waits for them, and re-layouts  12.5 us (6%)
    pallas_call x11, Pallas kernels, call(): pl.pallas_call(kernel, grid=grid, in_specs=[SMEM] + (specs or [VMEM] * (l...  72.6 us
    ppermute x5, starting transfers between devices, beyond(): lax.ppermute(up, 'slab', above)  18 us
    pallas_call x2, Pallas kernels, projections(): pl.pallas_call(functools.partial(projection_kernel, dirs, first, count >...  16.3 us
    ppermute x3, waiting for transfers between devices, regroup(): lax.ppermute(second, 'slab', other)  14.8 us
    all_to_all x1, blocking collectives, spread(): return lax.all_to_all(tile, 'slab', 0, 0, tiled=True) if count > 1 else tile  13.3 us
    unnamed x21, local copies, waits for them, and re-layouts  11.8 us
    pallas_call x1, Pallas kernels, remainders(): pl.pallas_call(functools.partial(remainder_kernel, dirs), grid=(rows // c...  10.1 us
    ppermute x3, starting transfers between devices, regroup(): lax.ppermute(second, 'slab', other)  9.92 us
  transfers between devices with their start and end apart: 21, of which 5 were waited for; matrix products, arithmetic and copies ran while one was open for 0% of the time, Pallas kernels for 42%

profile of v2, /device:TPU:0, one launch (start us, length us, event | category | flops | bytes accessed | tf_op | source)
XLA Modules:
  0.0 210.6 jit_solution(5495529240569095763)
XLA Ops:
  5.9 4.2 %collective-permute-start.1 = (f32[1728,128]{1,0:T(8,128)S(1)}, f32[1728,128]{1,0:T(8,128)S(1)}, u32[]{:S(2)}, u32[]{:S(2)}) collective-permute-start(f32[1728,128]{1,0:T(8,128)S(1)} %get-tuple-element.33), channel_id=1, source_target_pairs={{0,2},{1,0},{2,3},{3,1},{4,6},{5,4},{6,7},{7,5},{8,10},{9,8},{10,1... | collective-permute-start | bytes 2654216 | tf_op jit(solution)/shard_map/ppermute | solution.py:644
  14.5 3.0 %collective-permute-start.9 = (f32[1216,128]{1,0:T(8,128)S(1)}, f32[1216,128]{1,0:T(8,128)S(1)}, u32[]{:S(2)}, u32[]{:S(2)}) collective-permute-start(f32[1216,128]{1,0:T(8,128)S(1)} %get-tuple-element.41), channel_id=1, source_target_pairs={{0,2},{1,0},{2,3},{3,1},{4,6},{5,4},{6,7},{7,5},{8,10},{9,8},{10,1... | collective-permute-start | bytes 1867784 | tf_op jit(solution)/shard_map/ppermute | solution.py:644
  17.4 3.4 %copy-done = f32[16,4,256,128]{3,2,1,0:T(8,128)S(1)} copy-done((f32[16,4,256,128]{3,2,1,0:T(8,128)S(1)}, f32[16,4,256,128]{3,2,1,0:T(8,128)}, u32[]{:S(2)}) %copy-start) | copy-done | bytes 8388632
  20.8 8.3 %gram.1 = (f32[8,128]{1,0:T(8,128)S(1)}, s32[8]{0:T(128)S(1)}) custom-call(s32[8]{0:T(128)S(1)} %concatenate.3.where_ref, f32[16,1024,128]{2,1,0:T(8,128)S(1)} %bitcast.16), custom_call_target="tpu_custom_call" | custom-call | flops 5033164800 | bytes 8388608 | tf_op jit(solution)/shard_map/gram/pallas_call | solution.py:89
  30.8 3.5 %collective-permute-start.2 = (f32[3,6,144,128]{3,2,1,0:T(8,128)S(1)}, f32[3,6,144,128]{3,2,1,0:T(8,128)S(1)}, u32[]{:S(2)}, u32[]{:S(2)}) collective-permute-start(f32[3,6,144,128]{3,2,1,0:T(8,128)S(1)} %get-tuple-element.34.refs_0_), channel_id=1, source_target_pairs={{0,1},{1,4},{2,3},{3,6},{4,5},{5,8},{6,7},{7,10},{8,9},{9,12},{10,... | collective-permute-start | bytes 3981320 | tf_op jit(solution)/shard_map/ppermute | solution.py:658
  37.0 6.4 %collective-permute-done.9.other_ref = f32[1216,128]{1,0:T(8,128)S(1)} collective-permute-done((f32[1216,128]{1,0:T(8,128)S(1)}, f32[1216,128]{1,0:T(8,128)S(1)}, u32[]{:S(2)}, u32[]{:S(2)}) %collective-permute-start.9) | collective-permute-done | bytes 622624 | tf_op jit(solution)/shard_map/ppermute | solution.py:644
  44.1 3.5 %collective-permute-start.14 = (f32[2,6,144,128]{3,2,1,0:T(8,128)S(1)}, f32[2,6,144,128]{3,2,1,0:T(8,128)S(1)}, u32[]{:S(2)}, u32[]{:S(2)}) collective-permute-start(f32[2,6,144,128]{3,2,1,0:T(8,128)S(1)} %get-tuple-element.46.refs_4_), channel_id=1, source_target_pairs={{0,1},{1,4},{2,3},{3,6},{4,5},{5,8},{6,7},{7,10},{8,9},{9,12},{10,... | collective-permute-start | bytes 2654216 | tf_op jit(solution)/shard_map/ppermute | solution.py:658
  48.9 2.8 %collective-permute-start.5 = (f32[1152,128]{1,0:T(8,128)S(1)}, f32[1152,128]{1,0:T(8,128)S(1)}, u32[]{:S(2)}, u32[]{:S(2)}) collective-permute-start(f32[1152,128]{1,0:T(8,128)S(1)} %get-tuple-element.37), channel_id=1, source_target_pairs={{0,2},{1,0},{2,3},{3,1},{4,6},{5,4},{6,7},{7,5},{8,10},{9,8},{10,1... | collective-permute-start | bytes 1769480 | tf_op jit(solution)/shard_map/ppermute | solution.py:644
  51.7 7.4 %collective-permute-done.5.other_ref = f32[1152,128]{1,0:T(8,128)S(1)} collective-permute-done((f32[1152,128]{1,0:T(8,128)S(1)}, f32[1152,128]{1,0:T(8,128)S(1)}, u32[]{:S(2)}, u32[]{:S(2)}) %collective-permute-start.5) | collective-permute-done | bytes 589856 | tf_op jit(solution)/shard_map/ppermute | solution.py:644
  61.8 5.7 %sensors.1.refs_8_ = f32[2,4,144,128]{3,2,1,0:T(8,128)S(1)} custom-call(s32[8]{0:T(128)S(1)} %get-tuple-element.31.where_ref, f32[1216,128]{1,0:T(8,128)S(1)} %collective-permute-done.8.own_ref, f32[1216,128]{1,0:T(8,128)S(1)} %collective-permute-done.9.other_ref), custom_call_target="tpu_custom_call" | custom-call | flops 110592000 | bytes 1835008 | tf_op jit(solution)/shard_map/sensors/pallas_call | solution.py:341
  68.8 15.9 %forward.3 = (f32[2,6,144,128]{3,2,1,0:T(8,128)S(1)}, f32[2,6,144,128]{3,2,1,0:T(8,128)S(1)}) custom-call(s32[8]{0:T(128)S(1)} %concatenate.3.where_ref, f32[3,6,144,128]{3,2,1,0:T(8,128)S(1)} %get-tuple-element.34.refs_0_, f32[3,6,144,128]{3,2,1,0:T(8,128)S(1)} %get-tuple-element.35.refs_1_, f32[3,6,144,128]{3,2,1,0:T(8,128)S(1)} %collective-permute-done.2.refs_2_, ...), custom_call_target="tpu_custom_call" | custom-call | flops 13271040000 | bytes 11206656 | tf_op jit(solution)/shard_map/forward/pallas_call | solution.py:341
  84.7 4.7 %collective-permute-start.16 = (f32[2,6,144,128]{3,2,1,0:T(8,128)S(1)}, f32[2,6,144,128]{3,2,1,0:T(8,128)S(1)}, u32[]{:S(2)}, u32[]{:S(2)}) collective-permute-start(f32[2,6,144,128]{3,2,1,0:T(8,128)S(1)} %get-tuple-element.48.refs_4_), channel_id=1, source_target_pairs={{0,1},{1,4},{2,3},{3,6},{4,5},{5,8},{6,7},{7,10},{8,9},{9,12},{10,... | collective-permute-start | bytes 2654216 | tf_op jit(solution)/shard_map/ppermute | solution.py:658
  90.9 15.9 %forward.2 = (f32[2,6,144,128]{3,2,1,0:T(8,128)S(1)}, f32[2,6,144,128]{3,2,1,0:T(8,128)S(1)}) custom-call(s32[8]{0:T(128)S(1)} %concatenate.3.where_ref, f32[3,6,144,128]{3,2,1,0:T(8,128)S(1)} %get-tuple-element.34.refs_0_, f32[3,6,144,128]{3,2,1,0:T(8,128)S(1)} %get-tuple-element.35.refs_1_, f32[3,6,144,128]{3,2,1,0:T(8,128)S(1)} %collective-permute-done.2.refs_2_, ...), custom_call_target="tpu_custom_call" | custom-call | flops 13271040000 | bytes 11206656 | tf_op jit(solution)/shard_map/forward/pallas_call | solution.py:341
  106.7 4.3 %collective-permute-start.10 = (f32[2,6,144,128]{3,2,1,0:T(8,128)S(1)}, f32[2,6,144,128]{3,2,1,0:T(8,128)S(1)}, u32[]{:S(2)}, u32[]{:S(2)}) collective-permute-start(f32[2,6,144,128]{3,2,1,0:T(8,128)S(1)} %get-tuple-element.42.refs_4_), channel_id=1, source_target_pairs={{0,1},{1,4},{2,3},{3,6},{4,5},{5,8},{6,7},{7,10},{8,9},{9,12},{10,... | collective-permute-start | bytes 2654216 | tf_op jit(solution)/shard_map/ppermute | solution.py:658
  112.3 15.6 %adjoint.3 = (f32[2,4,128,128]{3,2,1,0:T(8,128)S(1)}, f32[2,4,128,128]{3,2,1,0:T(8,128)S(1)}) custom-call(s32[8]{0:T(128)S(1)} %concatenate.3.where_ref, f32[3,6,144,128]{3,2,1,0:T(8,128)S(1)} %get-tuple-element.34.refs_0_, f32[3,6,144,128]{3,2,1,0:T(8,128)S(1)} %get-tuple-element.35.refs_1_, f32[3,6,144,128]{3,2,1,0:T(8,128)S(1)} %collective-permute-done.2.refs_2_, ...), custom_call_target="tpu_custom_call" | custom-call | flops 13271040000 | bytes 9895936 | tf_op jit(solution)/shard_map/adjoint/pallas_call | solution.py:341
  128.7 3.8 %collective-permute-start.19 = (f32[2,4,128,128]{3,2,1,0:T(8,128)S(1)}, f32[2,4,128,128]{3,2,1,0:T(8,128)S(1)}, u32[]{:S(2)}, u32[]{:S(2)}) collective-permute-start(f32[2,4,128,128]{3,2,1,0:T(8,128)S(1)} %get-tuple-element.51), channel_id=1, source_target_pairs={{2,0},{0,1},{3,2},{1,3},{6,4},{4,5},{7,6},{5,7},{10,8},{8,9},{11,1... | collective-permute-start | bytes 1572872 | tf_op jit(solution)/shard_map/ppermute | solution.py:682
  132.5 15.6 %adjoint.2 = (f32[2,4,128,128]{3,2,1,0:T(8,128)S(1)}, f32[2,4,128,128]{3,2,1,0:T(8,128)S(1)}) custom-call(s32[8]{0:T(128)S(1)} %concatenate.3.where_ref, f32[3,6,144,128]{3,2,1,0:T(8,128)S(1)} %get-tuple-element.34.refs_0_, f32[3,6,144,128]{3,2,1,0:T(8,128)S(1)} %get-tuple-element.35.refs_1_, f32[3,6,144,128]{3,2,1,0:T(8,128)S(1)} %collective-permute-done.2.refs_2_, ...), custom_call_target="tpu_custom_call" | custom-call | flops 13271040000 | bytes 9895936 | tf_op jit(solution)/shard_map/adjoint/pallas_call | solution.py:341
  151.5 8.2 %projections.2 = (f32[8,128]{1,0:T(8,128)S(1)}, f32[2,1024,128]{2,1,0:T(8,128)}) custom-call(s32[8]{0:T(128)S(1)} %concatenate.3.where_ref, f32[16,1024,128]{2,1,0:T(8,128)} %bitcast.13, f32[4,1024,128]{2,1,0:T(8,128)} %bitcast.17, f32[2,4,128,128]{3,2,1,0:T(8,128)S(1)} %collective-permute-done.18.own_ref, ...), custom_call_target="tpu_custom_call" | custom-call | flops 1258291200 | bytes 11534336 | tf_op jit(solution)/shard_map/projections/pallas_call | solution.py:169
  159.7 5.4 %collective-permute-done.13.other_ref = f32[2,4,128,128]{3,2,1,0:T(8,128)S(1)} collective-permute-done((f32[2,4,128,128]{3,2,1,0:T(8,128)S(1)}, f32[2,4,128,128]{3,2,1,0:T(8,128)S(1)}, u32[]{:S(2)}, u32[]{:S(2)}) %collective-permute-start.13) | collective-permute-done | bytes 524320 | tf_op jit(solution)/shard_map/ppermute | solution.py:682
  165.1 8.1 %projections.3 = (f32[128,128]{1,0:T(8,128)S(1)}, f32[2,1024,128]{2,1,0:T(8,128)}) custom-call(s32[8]{0:T(128)S(1)} %concatenate.3.where_ref, f32[16,1024,128]{2,1,0:T(8,128)} %bitcast.14, f32[4,1024,128]{2,1,0:T(8,128)} %bitcast.18, f32[2,4,128,128]{3,2,1,0:T(8,128)S(1)} %collective-permute-done.12.own_ref, ...), custom_call_target="tpu_custom_call" | custom-call | flops 1258291200 | bytes 11534336 | tf_op jit(solution)/shard_map/projections/pallas_call | solution.py:169
  173.3 13.3 %all_to_all.22 = f32[16,8,128]{2,1,0:T(8,128)S(1)} all-to-all(f32[16,8,128]{2,1,0:T(8,128)S(1)} %bitcast.21), channel_id=1, replica_groups=mesh['grp'=2,'slab'=16] {'slab'}, dimensions={0} | all-to-all | bytes 131072 | tf_op jit(solution)/shard_map/all_to_all | solution.py:103
  186.6 10.1 %remainder.1 = (f32[4,1024,128]{2,1,0:T(8,128)}, f32[16,4]{1,0:T(8,128)S(1)}, f32[128,128]{1,0:T(8,128)}) custom-call(f32[128,128]{1,0:T(8,128)S(1)} %bitcast.20, f32[16,1024,128]{2,1,0:T(8,128)} %bitcast.15, f32[2,1024,128]{2,1,0:T(8,128)S(1)} %copy-done.4, f32[2,1024,128]{2,1,0:T(8,128)} %get-tuple-element.56.refs_1_), custom_call_target="tpu_custom_call" | custom-call | flops 2516582400 | bytes 12582912 | tf_op jit(solution)/shard_map/remainder/pallas_call | solution.py:279
  196.7 3.5 %all-to-all-start.1 = ((f32[16,8,128]{2,1,0:T(8,128)}), f32[16,8,128]{2,1,0:T(8,128)S(1)}, u32[]{:S(2)}, u32[]{:S(2)}) async-start(f32[16,8,128]{2,1,0:T(8,128)} %bitcast.10), calls=%async_computation.1 | async-start | bytes 131072 | tf_op jit(solution)/shard_map/all_to_all | solution.py:103
  200.8 6.2 %all-to-all-done.1 = f32[16,8,128]{2,1,0:T(8,128)S(1)} async-done(((f32[16,8,128]{2,1,0:T(8,128)}), f32[16,8,128]{2,1,0:T(8,128)S(1)}, u32[]{:S(2)}, u32[]{:S(2)}) %all-to-all-start.1) | async-done | bytes 65568 | tf_op jit(solution)/shard_map/all_to_all | solution.py:103
  (57 shorter events, 30.9 us)
Async XLA Ops:
  5.2 24.0 %collective-permute-start = (f32[1728,128]{1,0:T(8,128)S(1)}, f32[1728,128]{1,0:T(8,128)S(1)}, u32[]{:S(2)}, u32[]{:S(2)}) collective-permute-start(f32[1728,128]{1,0:T(8,128)S(1)} %get-tuple-element.32), channel_id=1, source_target_pairs={{0,0},{1,2},{2,1},{3,3},{4,4},{5,6},{6,5},{7,7},{8,8},{9,10},{10,9... | collective-permute-start | bytes 2654216 | tf_op jit(solution)/shard_map/ppermute | solution.py:644
  5.9 24.2 %collective-permute-start.1 = (f32[1728,128]{1,0:T(8,128)S(1)}, f32[1728,128]{1,0:T(8,128)S(1)}, u32[]{:S(2)}, u32[]{:S(2)}) collective-permute-start(f32[1728,128]{1,0:T(8,128)S(1)} %get-tuple-element.33), channel_id=1, source_target_pairs={{0,2},{1,0},{2,3},{3,1},{4,6},{5,4},{6,7},{7,5},{8,10},{9,8},{10,1... | collective-permute-start | bytes 2654216 | tf_op jit(solution)/shard_map/ppermute | solution.py:644
  13.8 23.2 %collective-permute-start.8 = (f32[1216,128]{1,0:T(8,128)S(1)}, f32[1216,128]{1,0:T(8,128)S(1)}, u32[]{:S(2)}, u32[]{:S(2)}) collective-permute-start(f32[1216,128]{1,0:T(8,128)S(1)} %get-tuple-element.40), channel_id=1, source_target_pairs={{0,0},{1,2},{2,1},{3,3},{4,4},{5,6},{6,5},{7,7},{8,8},{9,10},{10,9... | collective-permute-start | bytes 1867784 | tf_op jit(solution)/shard_map/ppermute | solution.py:644
  14.5 29.0 %collective-permute-start.9 = (f32[1216,128]{1,0:T(8,128)S(1)}, f32[1216,128]{1,0:T(8,128)S(1)}, u32[]{:S(2)}, u32[]{:S(2)}) collective-permute-start(f32[1216,128]{1,0:T(8,128)S(1)} %get-tuple-element.41), channel_id=1, source_target_pairs={{0,2},{1,0},{2,3},{3,1},{4,6},{5,4},{6,7},{7,5},{8,10},{9,8},{10,1... | collective-permute-start | bytes 1867784 | tf_op jit(solution)/shard_map/ppermute | solution.py:644
  17.4 3.4 %copy-start = (f32[16,4,256,128]{3,2,1,0:T(8,128)S(1)}, f32[16,4,256,128]{3,2,1,0:T(8,128)}, u32[]{:S(2)}) copy-start(f32[16,4,256,128]{3,2,1,0:T(8,128)} %param.9) | copy-start | bytes 25165828
  20.8 14.8 %copy-start.2 = (f32[4,4,256,128]{3,2,1,0:T(8,128)S(1)}, f32[4,4,256,128]{3,2,1,0:T(8,128)}, u32[]{:S(2)}) copy-start(f32[4,4,256,128]{3,2,1,0:T(8,128)} %refs_0_.5) | copy-start | bytes 6291460
  30.8 38.0 %collective-permute-start.2 = (f32[3,6,144,128]{3,2,1,0:T(8,128)S(1)}, f32[3,6,144,128]{3,2,1,0:T(8,128)S(1)}, u32[]{:S(2)}, u32[]{:S(2)}) collective-permute-start(f32[3,6,144,128]{3,2,1,0:T(8,128)S(1)} %get-tuple-element.34.refs_0_), channel_id=1, source_target_pairs={{0,1},{1,4},{2,3},{3,6},{4,5},{5,8},{6,7},{7,10},{8,9},{9,12},{10,... | collective-permute-start | bytes 3981320 | tf_op jit(solution)/shard_map/ppermute | solution.py:658
  34.3 34.5 %collective-permute-start.3 = (f32[3,6,144,128]{3,2,1,0:T(8,128)S(1)}, f32[3,6,144,128]{3,2,1,0:T(8,128)S(1)}, u32[]{:S(2)}, u32[]{:S(2)}) collective-permute-start(f32[3,6,144,128]{3,2,1,0:T(8,128)S(1)} %get-tuple-element.35.refs_1_), channel_id=1, source_target_pairs={{1,0},{4,1},{3,2},{6,3},{5,4},{8,5},{7,6},{10,7},{9,8},{12,9},{11,... | collective-permute-start | bytes 3981320 | tf_op jit(solution)/shard_map/ppermute | solution.py:658
  36.3 12.6 %collective-permute-start.4 = (f32[1152,128]{1,0:T(8,128)S(1)}, f32[1152,128]{1,0:T(8,128)S(1)}, u32[]{:S(2)}, u32[]{:S(2)}) collective-permute-start(f32[1152,128]{1,0:T(8,128)S(1)} %get-tuple-element.36), channel_id=1, source_target_pairs={{0,0},{1,2},{2,1},{3,3},{4,4},{5,6},{6,5},{7,7},{8,8},{9,10},{10,9... | collective-permute-start | bytes 1769480 | tf_op jit(solution)/shard_map/ppermute | solution.py:644
  44.1 23.4 %collective-permute-start.14 = (f32[2,6,144,128]{3,2,1,0:T(8,128)S(1)}, f32[2,6,144,128]{3,2,1,0:T(8,128)S(1)}, u32[]{:S(2)}, u32[]{:S(2)}) collective-permute-start(f32[2,6,144,128]{3,2,1,0:T(8,128)S(1)} %get-tuple-element.46.refs_4_), channel_id=1, source_target_pairs={{0,1},{1,4},{2,3},{3,6},{4,5},{5,8},{6,7},{7,10},{8,9},{9,12},{10,... | collective-permute-start | bytes 2654216 | tf_op jit(solution)/shard_map/ppermute | solution.py:658
  47.6 21.2 %collective-permute-start.15 = (f32[2,6,144,128]{3,2,1,0:T(8,128)S(1)}, f32[2,6,144,128]{3,2,1,0:T(8,128)S(1)}, u32[]{:S(2)}, u32[]{:S(2)}) collective-permute-start(f32[2,6,144,128]{3,2,1,0:T(8,128)S(1)} %get-tuple-element.47.refs_5_), channel_id=1, source_target_pairs={{1,0},{4,1},{3,2},{6,3},{5,4},{8,5},{7,6},{10,7},{9,8},{12,9},{11,... | collective-permute-start | bytes 2654216 | tf_op jit(solution)/shard_map/ppermute | solution.py:658
  48.9 10.2 %collective-permute-start.5 = (f32[1152,128]{1,0:T(8,128)S(1)}, f32[1152,128]{1,0:T(8,128)S(1)}, u32[]{:S(2)}, u32[]{:S(2)}) collective-permute-start(f32[1152,128]{1,0:T(8,128)S(1)} %get-tuple-element.37), channel_id=1, source_target_pairs={{0,2},{1,0},{2,3},{3,1},{4,6},{5,4},{6,7},{7,5},{8,10},{9,8},{10,1... | collective-permute-start | bytes 1769480 | tf_op jit(solution)/shard_map/ppermute | solution.py:644
  59.7 31.1 %collective-permute-start.6 = (f32[2,6,144,128]{3,2,1,0:T(8,128)S(1)}, f32[2,6,144,128]{3,2,1,0:T(8,128)S(1)}, u32[]{:S(2)}, u32[]{:S(2)}) collective-permute-start(f32[2,6,144,128]{3,2,1,0:T(8,128)S(1)} %get-tuple-element.38.refs_4_), channel_id=1, source_target_pairs={{0,1},{1,4},{2,3},{3,6},{4,5},{5,8},{6,7},{7,10},{8,9},{9,12},{10,... | collective-permute-start | bytes 2654216 | tf_op jit(solution)/shard_map/ppermute | solution.py:658
  67.5 23.4 %collective-permute-start.7 = (f32[2,6,144,128]{3,2,1,0:T(8,128)S(1)}, f32[2,6,144,128]{3,2,1,0:T(8,128)S(1)}, u32[]{:S(2)}, u32[]{:S(2)}) collective-permute-start(f32[2,6,144,128]{3,2,1,0:T(8,128)S(1)} %get-tuple-element.39.refs_5_), channel_id=1, source_target_pairs={{1,0},{4,1},{3,2},{6,3},{5,4},{8,5},{7,6},{10,7},{9,8},{12,9},{11,... | collective-permute-start | bytes 2654216 | tf_op jit(solution)/shard_map/ppermute | solution.py:658
  84.7 27.6 %collective-permute-start.16 = (f32[2,6,144,128]{3,2,1,0:T(8,128)S(1)}, f32[2,6,144,128]{3,2,1,0:T(8,128)S(1)}, u32[]{:S(2)}, u32[]{:S(2)}) collective-permute-start(f32[2,6,144,128]{3,2,1,0:T(8,128)S(1)} %get-tuple-element.48.refs_4_), channel_id=1, source_target_pairs={{0,1},{1,4},{2,3},{3,6},{4,5},{5,8},{6,7},{7,10},{8,9},{9,12},{10,... | collective-permute-start | bytes 2654216 | tf_op jit(solution)/shard_map/ppermute | solution.py:658
  89.4 23.0 %collective-permute-start.17 = (f32[2,6,144,128]{3,2,1,0:T(8,128)S(1)}, f32[2,6,144,128]{3,2,1,0:T(8,128)S(1)}, u32[]{:S(2)}, u32[]{:S(2)}) collective-permute-start(f32[2,6,144,128]{3,2,1,0:T(8,128)S(1)} %get-tuple-element.49.refs_5_), channel_id=1, source_target_pairs={{1,0},{4,1},{3,2},{6,3},{5,4},{8,5},{7,6},{10,7},{9,8},{12,9},{11,... | collective-permute-start | bytes 2654216 | tf_op jit(solution)/shard_map/ppermute | solution.py:658
  106.7 25.8 %collective-permute-start.10 = (f32[2,6,144,128]{3,2,1,0:T(8,128)S(1)}, f32[2,6,144,128]{3,2,1,0:T(8,128)S(1)}, u32[]{:S(2)}, u32[]{:S(2)}) collective-permute-start(f32[2,6,144,128]{3,2,1,0:T(8,128)S(1)} %get-tuple-element.42.refs_4_), channel_id=1, source_target_pairs={{0,1},{1,4},{2,3},{3,6},{4,5},{5,8},{6,7},{7,10},{8,9},{9,12},{10,... | collective-permute-start | bytes 2654216 | tf_op jit(solution)/shard_map/ppermute | solution.py:658
  111.0 21.5 %collective-permute-start.11 = (f32[2,6,144,128]{3,2,1,0:T(8,128)S(1)}, f32[2,6,144,128]{3,2,1,0:T(8,128)S(1)}, u32[]{:S(2)}, u32[]{:S(2)}) collective-permute-start(f32[2,6,144,128]{3,2,1,0:T(8,128)S(1)} %get-tuple-element.43.refs_5_), channel_id=1, source_target_pairs={{1,0},{4,1},{3,2},{6,3},{5,4},{8,5},{7,6},{10,7},{9,8},{12,9},{11,... | collective-permute-start | bytes 2654216 | tf_op jit(solution)/shard_map/ppermute | solution.py:658
  128.0 23.6 %collective-permute-start.18 = (f32[2,4,128,128]{3,2,1,0:T(8,128)S(1)}, f32[2,4,128,128]{3,2,1,0:T(8,128)S(1)}, u32[]{:S(2)}, u32[]{:S(2)}) collective-permute-start(f32[2,4,128,128]{3,2,1,0:T(8,128)S(1)} %get-tuple-element.50), channel_id=1, source_target_pairs={{0,0},{2,1},{1,2},{3,3},{4,4},{6,5},{5,6},{7,7},{8,8},{10,9},{9,10... | collective-permute-start | bytes 1572872 | tf_op jit(solution)/shard_map/ppermute | solution.py:682
  128.7 22.9 %collective-permute-start.19 = (f32[2,4,128,128]{3,2,1,0:T(8,128)S(1)}, f32[2,4,128,128]{3,2,1,0:T(8,128)S(1)}, u32[]{:S(2)}, u32[]{:S(2)}) collective-permute-start(f32[2,4,128,128]{3,2,1,0:T(8,128)S(1)} %get-tuple-element.51), channel_id=1, source_target_pairs={{2,0},{0,1},{3,2},{1,3},{6,4},{4,5},{7,6},{5,7},{10,8},{8,9},{11,1... | collective-permute-start | bytes 1572872 | tf_op jit(solution)/shard_map/ppermute | solution.py:682
  148.1 11.6 %collective-permute-start.12 = (f32[2,4,128,128]{3,2,1,0:T(8,128)S(1)}, f32[2,4,128,128]{3,2,1,0:T(8,128)S(1)}, u32[]{:S(2)}, u32[]{:S(2)}) collective-permute-start(f32[2,4,128,128]{3,2,1,0:T(8,128)S(1)} %get-tuple-element.44), channel_id=1, source_target_pairs={{0,0},{2,1},{1,2},{3,3},{4,4},{6,5},{5,6},{7,7},{8,8},{10,9},{9,10... | collective-permute-start | bytes 1572872 | tf_op jit(solution)/shard_map/ppermute | solution.py:682
  148.8 16.3 %collective-permute-start.13 = (f32[2,4,128,128]{3,2,1,0:T(8,128)S(1)}, f32[2,4,128,128]{3,2,1,0:T(8,128)S(1)}, u32[]{:S(2)}, u32[]{:S(2)}) collective-permute-start(f32[2,4,128,128]{3,2,1,0:T(8,128)S(1)} %get-tuple-element.45), channel_id=1, source_target_pairs={{2,0},{0,1},{3,2},{1,3},{6,4},{4,5},{7,6},{5,7},{10,8},{8,9},{11,1... | collective-permute-start | bytes 1572872 | tf_op jit(solution)/shard_map/ppermute | solution.py:682
  165.1 21.5 %copy-start.4 = (f32[2,1024,128]{2,1,0:T(8,128)S(1)}, f32[2,1024,128]{2,1,0:T(8,128)}, u32[]{:S(2)}) copy-start(f32[2,1024,128]{2,1,0:T(8,128)} %get-tuple-element.55.refs_0_) | copy-start | bytes 3145732
  196.7 10.4 %all-to-all-start.1 = ((f32[16,8,128]{2,1,0:T(8,128)}), f32[16,8,128]{2,1,0:T(8,128)S(1)}, u32[]{:S(2)}, u32[]{:S(2)}) async-start(f32[16,8,128]{2,1,0:T(8,128)} %bitcast.10), calls=%async_computation.1 | async-start | bytes 131072 | tf_op jit(solution)/shard_map/all_to_all | solution.py:103
  (7 other events, 7.7 us)

commit v3 on v2

v3 whole, which is shorter than its diff:
```python
import functools

import jax
import jax.numpy as jnp
from jax import lax
from jax.experimental import pallas as pl
from jax.experimental.pallas import tpu as pltpu
from jax.sharding import PartitionSpec as P

STEPS = 2
SWEEPS = 3
GROUPS = 2
SPARE = 16
REACH = STEPS * SWEEPS


DIFFUSION = 0.2
GAMMA = 0.5
LANES = 128
PIECES = 8
EXACT = lax.Precision.HIGHEST
SMEM = pl.BlockSpec(memory_space=pltpu.SMEM)
VMEM = pl.BlockSpec(memory_space=pltpu.VMEM)
ANY = pl.BlockSpec(memory_space=pl.ANY)
VECTOR = 150


def floats(*shape):
    return jax.ShapeDtypeStruct(shape, jnp.float32)


def cost(flops, moved):
    return pl.CostEstimate(flops=int(flops), bytes_accessed=int(moved), transcendentals=0)


def lane_sums(stack):
    ones = jnp.ones((8, LANES), jnp.float32)
    return lax.dot_general(
        ones, stack, (((1,), (1,)), ((), ())), precision=EXACT, preferred_element_type=jnp.float32
    )


def chunks_of(source, into, sems, pieces):
    rows = source.shape[1] // pieces
    return [
        pltpu.make_async_copy(
            source.at[:, pl.ds(k * rows, rows)], into.at[:, pl.ds(k * rows, rows)], sems.at[k]
        )
        for k in range(pieces)
    ]


def gram_kernel(where_ref, basis_hbm, out_ref, where_out, basis_ref, acc_ref, sems):
    rank, rows, _ = basis_ref.shape
    tile = 4
    moves = chunks_of(basis_hbm, basis_ref, sems, PIECES)
    for move in moves:
        move.start()
    for k in range(where_ref.shape[0]):
        where_out[k] = where_ref[k]
    acc_ref[...] = jnp.zeros_like(acc_ref)
    part = rows // PIECES
    for piece, move in enumerate(moves):
        move.wait()
        for i0 in range(0, rank, tile):
            for j0 in range(i0, rank, tile):
                pairs = [(i, j) for i in range(i0, i0 + tile) for j in range(j0, j0 + tile) if i <= j]

                def add(k, sums, i0=i0, j0=j0, pairs=pairs, piece=piece):
                    at = pl.ds(pl.multiple_of(piece * part + k * 8, 8), 8)
                    left = {i: basis_ref[i, at, :] for i in range(i0, i0 + tile)}
                    right = left if i0 == j0 else {j: basis_ref[j, at, :] for j in range(j0, j0 + tile)}
                    return [s + left[i] * right[j] for s, (i, j) in zip(sums, pairs)]

                sums = [jnp.zeros((8, LANES), jnp.float32) for _ in pairs]
                sums = lax.fori_loop(0, part // 8, add, sums, unroll=8)
                for (i, j), s in zip(pairs, sums):
                    acc_ref[i, j] += s

    row = lax.broadcasted_iota(jnp.int32, (rank, rank), 0)
    col = lax.broadcasted_iota(jnp.int32, (rank, rank), 1)
    gram = jnp.zeros((rank, rank), jnp.float32)
    for i in range(rank):
        sums = lane_sums(jnp.sum(acc_ref[i], axis=1))
        gram = jnp.where(row == i, jnp.broadcast_to(sums[0:1, :], (rank, rank)), gram)
    upper = jnp.where(col >= row, gram, 0.0)
    strict = jnp.where(col > row, gram, 0.0)
    whole = upper + strict.T
    out_ref[...] = jnp.zeros_like(out_ref)
    for k in range(0, rank, 8):
        at = rank + k * rank // 8
        out_ref[:, at : at + rank] = whole[k : k + 8]


def gram_tile(where, basis):
    rank, rows, _ = basis.shape
    return call(
        gram_kernel, "gram", [where, basis],
        [floats(8, LANES), jax.ShapeDtypeStruct(where.shape, where.dtype)],
        [
            pltpu.VMEM(basis.shape, jnp.float32),
            pltpu.VMEM((rank, rank, 8, LANES), jnp.float32),
            pltpu.SemaphoreType.DMA((PIECES,)),
        ],
        54, rank * rank * rows * LANES, [ANY], [VMEM, SMEM],
    )


def spread(tile, count):
    return lax.all_to_all(tile, "slab", 0, 0, tiled=True) if count > 1 else tile


def projection_kernel(
    first, where_ref, basis_hbm, dirs_hbm, own_hbm, other_hbm, tile_ref,
    out_ref, image_ref, basis_ref, dirs_ref, halves_ref, sems, side_sems,
):
    rank = basis_ref.shape[0]
    dirs, rows, _ = image_ref.shape
    planes, half = halves_ref.shape[2:4]
    b = where_ref[1]
    sides = [
        pltpu.make_async_copy(own_hbm, halves_ref.at[0], side_sems.at[0]),
        pltpu.make_async_copy(other_hbm, halves_ref.at[1], side_sems.at[1]),
        pltpu.make_async_copy(dirs_hbm.at[pl.ds(first, dirs)], dirs_ref, side_sems.at[2]),
    ]
    moves = chunks_of(basis_hbm, basis_ref, sems, PIECES)
    for move in sides + moves:
        move.start()
    for move in sides:
        move.wait()
    sums = [jnp.zeros((8, LANES), jnp.float32) for _ in range(rank * dirs)]
    for k in range(2 * planes):
        plane, part = k // 2, k % 2
        which = jnp.where(b == part, 0, 1)
        low = k * half
        piece = rows // PIECES
        for m in range(low // piece, -(-(low + half) // piece)):
            if m * piece >= low:
                moves[m].wait()

        def add(r, sums, plane=plane, which=which, low=low):
            at = pl.ds(pl.multiple_of(low + r * 8, 8), 8)
            here = pl.ds(pl.multiple_of(r * 8, 8), 8)
            image = []
            for d in range(dirs):
                value = halves_ref[which, d, plane, here, :] + GAMMA * dirs_ref[d, at, :]
                image_ref[d, at, :] = value
                image.append(value)
            out = []
            for i in range(rank):
                q = basis_ref[i, at, :]
                out += [sums[i * dirs + d] + q * image[d] for d in range(dirs)]
            return out

        sums = lax.fori_loop(0, half // 8, add, sums, unroll=4)

    row = lax.broadcasted_iota(jnp.int32, (8, LANES), 0)
    lane = lax.broadcasted_iota(jnp.int32, (8, LANES), 1)
    table = tile_ref[...]
    for d in range(dirs):
        lines = [jnp.sum(sums[i * dirs + d], axis=0, keepdims=True) for i in range(rank)]
        lines = jnp.concatenate(lines + [jnp.zeros((LANES - rank, LANES), jnp.float32)], 0)
        table = jnp.where((row == first + d) & (lane < rank), lane_sums(lines), table)
    for r in range(out_ref.shape[0] // 8):
        out_ref[r * 8 : (r + 1) * 8, :] = table


def projections(where, basis, directions, first, halves, tile, count):
    rank, rows, _ = basis.shape
    dirs = halves[0].shape[0]
    return call(
        functools.partial(projection_kernel, first), "projections",
        [where, basis, directions.reshape(-1, rows, LANES), *halves, tile],
        [floats(count * 8, LANES), floats(dirs, rows, LANES)],
        [
            pltpu.VMEM(basis.shape, jnp.float32),
            pltpu.VMEM((dirs, rows, LANES), jnp.float32),
            pltpu.VMEM((2, *halves[0].shape), jnp.float32),
            pltpu.SemaphoreType.DMA((PIECES,)),
            pltpu.SemaphoreType.DMA((3,)),
        ],
        52, 2 * rank * dirs * rows * LANES, [ANY] * 4 + [VMEM],
    )


def summed_tile(parts_ref):
    tiles = [parts_ref[r : r + 8, :] for r in range(0, parts_ref.shape[0], 8)]
    while len(tiles) > 1:
        tiles = [sum(tiles[k : k + 2]) for k in range(0, len(tiles), 2)]
    return tiles[0]


def solved(tile, rank):
    gram = [tile[:, rank + k * rank // 8 :][:, :rank] for k in range(0, rank, 8)]
    table = jnp.concatenate(
        [
            jnp.concatenate(gram, 0),
            tile[:, 0:rank].T,
            jnp.zeros((rank, LANES - rank - 8), jnp.float32),
        ],
        1,
    )
    row = lax.broadcasted_iota(jnp.int32, (rank, LANES), 0)
    for k in range(rank):
        scaled_row = table[k : k + 1, :] / table[k : k + 1, k : k + 1]
        table = jnp.where(row == k, scaled_row, table - table[:, k : k + 1] * scaled_row)
    return table


def remainder_kernel(dirs, parts_ref, basis_hbm, *refs):
    groups = len(refs) - 8
    images, (rem_ref, coeffs_ref, out_ref, basis_ref, image_ref, splat_ref, sems, side_sems) = (
        refs[:groups], refs[groups:]
    )
    each = dirs // groups
    rank, rows, _ = basis_ref.shape
    tile = 4
    sides = [
        pltpu.make_async_copy(image, image_ref.at[pl.ds(k * each, each)], side_sems.at[k])
        for k, image in enumerate(images)
    ]
    moves = chunks_of(basis_hbm, basis_ref, sems, PIECES)
    for move in sides + moves:
        move.start()
    table = solved(summed_tile(parts_ref), rank)
    coeffs_ref[...] = table[:, rank : rank + dirs]
    for d in range(dirs):
        for j in range(rank):
            splat_ref[d * rank + j] = jnp.broadcast_to(
                table[j : j + 1, rank + d : rank + d + 1], (8, LANES)
            )
    for move in sides:
        move.wait()
    energy = [jnp.zeros((8, LANES), jnp.float32) for _ in range(dirs)]
    part = rows // PIECES
    for piece, move in enumerate(moves):
        move.wait()
        for j0 in range(0, rank, tile):
            last = j0 + tile == rank
            weights = [[splat_ref[d * rank + j] for j in range(j0, j0 + tile)] for d in range(dirs)]

            def take(k, energy, j0=j0, last=last, weights=weights, piece=piece):
                at = pl.ds(pl.multiple_of(piece * part + k * 8, 8), 8)
                basis = [basis_ref[j, at, :] for j in range(j0, j0 + tile)]
                out = []
                for d in range(dirs):
                    left = image_ref[d, at, :] if j0 == 0 else rem_ref[d, at, :]
                    parts = [w * q for w, q in zip(weights[d], basis)]
                    left = left - ((parts[0] + parts[1]) + (parts[2] + parts[3]))
                    rem_ref[d, at, :] = left
                    out.append(energy[d] + left * left if last else energy[d])
                return out

            energy = lax.fori_loop(0, part // 8, take, energy, unroll=4)

    row = lax.broadcasted_iota(jnp.int32, (8, LANES), 0)
    tile_out = jnp.zeros((8, LANES), jnp.float32)
    for d in range(dirs):
        total = jnp.sum(jnp.sum(energy[d], axis=0, keepdims=True), axis=1, keepdims=True)
        tile_out = jnp.where(row == d, jnp.broadcast_to(total, (8, LANES)), tile_out)
    for r in range(out_ref.shape[0] // 8):
        out_ref[r * 8 : (r + 1) * 8, :] = tile_out


def remainders(parts, basis, images, count):
    rank, rows, _ = basis.shape
    dirs = sum(i.shape[0] for i in images)
    return call(
        functools.partial(remainder_kernel, dirs), "remainder", [parts, basis, *images],
        [floats(dirs, rows, LANES), floats(rank, dirs), floats(count * 8, LANES)],
        [
            pltpu.VMEM(basis.shape, jnp.float32),
            pltpu.VMEM((dirs, rows, LANES), jnp.float32),
            pltpu.VMEM((dirs * rank, 8, LANES), jnp.float32),
            pltpu.SemaphoreType.DMA((PIECES,)),
            pltpu.SemaphoreType.DMA((len(images),)),
        ],
        52, 2 * rank * dirs * rows * LANES, [ANY] * (1 + len(images)), first=VMEM,
    )


def scale_kernel(cells, parts_ref, rem_ref, new_ref):
    energy = summed_tile(parts_ref)
    value = energy / cells + 1e-06
    root = lax.rsqrt(value)
    root = root * (1.5 - (0.5 * value * root) * root)
    for d in range(rem_ref.shape[0]):
        new_ref[d] = rem_ref[d] * root[d : d + 1, :]


def scaled(parts, rem, cells, count):
    dirs, rows, _ = rem.shape
    chunk = 256
    return pl.pallas_call(
        functools.partial(scale_kernel, cells),
        grid=(rows // chunk,),
        in_specs=[
            pl.BlockSpec((count * 8, LANES), lambda k: (0, 0)),
            pl.BlockSpec((dirs, chunk, LANES), lambda k: (0, k, 0)),
        ],
        out_specs=pl.BlockSpec((dirs, chunk, LANES), lambda k: (0, k, 0)),
        out_shape=floats(dirs, rows, LANES),
        compiler_params=pltpu.CompilerParams(vmem_limit_bytes=16 << 20),
        name="scale",
    )(parts, rem)


def quad(count):
    own, other, above = [], [], []
    for s in range(count):
        q, a, b = s // 4, s // 2 % 2, s % 2
        own.append((s, 4 * q + 2 * b + a))
        other.append((s, 4 * q + 2 * (1 - b) + a))
        up = s + 1 if b == 0 else s + 3
        if up < count:
            above.append((s, up))
    return own, other, above


def back(pairs):
    return [(target, source) for source, target in pairs]


def call(kernel, name, ins, outs, scratch=(), limit=16, work=0, specs=None, out_specs=None, first=SMEM):
    moved = sum(x.size * 4 for x in ins[1:]) + sum(o.size * 4 for o in outs)
    return pl.pallas_call(
        kernel,
        in_specs=[first] + (specs or [VMEM] * (len(ins) - 1)),
        out_specs=out_specs or [VMEM] * len(outs),
        out_shape=outs,
        scratch_shapes=list(scratch),
        compiler_params=pltpu.CompilerParams(vmem_limit_bytes=limit << 20),
        cost_estimate=cost(VECTOR * work, moved),
        name=name,
    )(*ins)


def cut_kernel(height, group, listed, where_ref, *refs):
    lists, fields = refs[:listed], refs[listed:-4]
    own_ref, other_ref, list_ref, sems = refs[-4:]
    b = where_ref[1]
    moves = []

    def move(source, target):
        moves.append(pltpu.make_async_copy(source, target, sems.at[len(moves)]))
        moves[-1].start()

    k = 0
    for field in fields:
        start = pl.multiple_of(b * (field.shape[-2] - height), 16)
        rest = pl.multiple_of((1 - b) * (field.shape[-2] - height), 16)
        for d in group:
            for p in range(field.shape[-3]):
                at = (p,) if len(field.shape) == 3 else (d, p)
                for ref, low in ((own_ref, start), (other_ref, rest)):
                    move(field.at[(*at, pl.ds(low, height))], ref.at[pl.ds(k, height)])
                k += height
    low = 0
    for entries in lists:
        list_ref[low : low + entries.shape[0], :] = entries[...].astype(jnp.float32)
        low += entries.shape[0]
    if lists:
        for ref in (own_ref, other_ref):
            move(list_ref, ref.at[pl.ds(k, low)])
    for m in moves:
        m.wait()


def pack_kernel(planes, where_ref, own_ref, other_ref, up_ref, down_ref):
    count, reach, height, _ = up_ref.shape
    skip = 2 * planes - reach

    def join(first, second):
        for d in range(count):
            for p in range(2 * planes):
                ref = first if p < planes else second
                at = (d * planes + p % planes) * height
                value = ref[at : at + height, :]
                if p >= skip:
                    up_ref[d, p - skip] = value
                if p < reach:
                    down_ref[d, p] = value

    @pl.when(where_ref[0] == 0)
    def _():
        join(own_ref, other_ref)

    @pl.when(where_ref[0] == 1)
    def _():
        join(other_ref, own_ref)


def sensor_kernel(width, skip, where_ref, own_ref, other_ref, out_ref, where_out):
    for k in range(where_ref.shape[0]):
        where_out[k] = where_ref[k]
    a = where_ref[0]
    _, planes, height, _ = out_ref.shape
    first = a * (width - height)
    count = (own_ref.shape[0] - skip) // 2
    group = 4
    chunk = group * LANES
    targets = planes * height
    rows = lax.broadcasted_iota(jnp.int32, (targets, chunk), 0)
    lanes = lax.broadcasted_iota(jnp.int32, (LANES, chunk), 0)
    for ref, at in ((own_ref, a), (other_ref, 1 - a)):
        total = jnp.zeros((targets, 3 * LANES), jnp.float32)
        for k in range(skip, skip + count, group):
            take = lambda at: jnp.concatenate([ref[at + g : at + g + 1, :] for g in range(group)], 1)
            cell = take(k).astype(jnp.int32)
            weight = take(count + k)
            line = cell // LANES
            lane = cell - line * LANES
            plane = line // width
            row = line - plane * width - first
            inside = (row >= 0) & (row < height)
            target = jnp.where(inside, plane * height + row, -1)
            high = weight.astype(jnp.bfloat16).astype(jnp.float32)
            rest = weight - high
            middle = rest.astype(jnp.bfloat16).astype(jnp.float32)
            low = rest - middle
            hot = jnp.where(rows == target, 1.0, 0.0).astype(jnp.bfloat16)
            here = lanes == lane
            parts = [jnp.where(here, part, 0.0).astype(jnp.bfloat16) for part in (high, middle, low)]
            total += lax.dot_general(
                hot,
                jnp.concatenate(parts, 0),
                (((1,), (1,)), ((), ())),
                preferred_element_type=jnp.float32,
            )
        total = total[:, 0:LANES] + total[:, LANES : 2 * LANES] + total[:, 2 * LANES :]
        out_ref[at] = total.reshape(planes, height, LANES)


def solve_kernel(adjoint, width, where_ref, *refs):
    flow_parts, value_parts = refs[0:4], refs[4:8]
    if adjoint:
        outs, (flow, coef, rhs, start, ping, pong, sems) = refs[8:10], refs[10:]
    else:
        weight_ref, outs, (flow, coef, rhs, start, ping, pong, sems) = refs[8], refs[9:11], refs[11:]
    dirs, depth, height, _ = rhs.shape
    reach = REACH
    own = depth - 2 * reach
    chunks = height // 8
    a, at_bottom, at_top = where_ref[0], where_ref[2], where_ref[3]
    code = [where_ref[4 + k] for k in range(4)]

    def arrivals(parts, into, first):
        up, down, lo, hi = parts
        moves = (
            (lo, into.at[:, 0:reach]),
            (down, into.at[:, reach : 2 * reach]),
            (up.at[:, 2 * reach - own : reach], into.at[:, 2 * reach : reach + own]),
            (hi, into.at[:, reach + own : depth]),
        )
        return [pltpu.make_async_copy(s, t, sems.at[first + k]) for k, (s, t) in enumerate(moves)]

    flow_moves = arrivals(flow_parts, flow, 0)
    value_moves = arrivals(value_parts, start, 4)
    for move in flow_moves + value_moves:
        move.start()

    shape = (8, LANES)
    sub = lax.broadcasted_iota(jnp.int32, shape, 0)
    lane = lax.broadcasted_iota(jnp.int32, shape, 1)
    top_sub, bottom_sub = sub == 7, sub == 0
    last_lane, first_lane = lane == LANES - 1, lane == 0
    zero = jnp.zeros(shape, jnp.float32)
    opened = [jnp.where(c == 0, 1.0, 0.0).astype(jnp.float32) for c in code]
    low_one = jnp.where(bottom_sub & (a == 0), opened[0], 1.0)
    high_one = jnp.where(top_sub & (a == 1), opened[1], 1.0)
    low_two = jnp.where(first_lane, opened[2], 1.0)
    high_two = jnp.where(last_lane, opened[3], 1.0)

    def both(x):
        positive = DIFFUSION + jnp.maximum(x, 0.0)
        return positive, positive - x

    def coefficients(p, carry):
        outside = ((p < reach) & (at_bottom == 1)) | ((p >= reach + own) & (at_top == 1))
        inside = jnp.where(outside, 0.0, 1.0)
        turned = zero
        for r in range(chunks):
            here = slice(r * 8, r * 8 + 8)
            one, two, three = flow[0, p, here, :], flow[1, p, here, :], flow[2, p, here, :]
            one_turned = pltpu.roll(one, 1, 0)
            one_below = jnp.where(bottom_sub, turned, one_turned)
            turned = one_turned
            two_below = jnp.where(first_lane, 0.0, pltpu.roll(two, 1, 1))
            up = [both(x) for x in (one, two, three)]
            down = [both(x) for x in (one_below, two_below, flow[2, p - 1, here, :])]
            first = up[0][0] if r < chunks - 1 else high_one * up[0][0]
            second = down[0][1] if r > 0 else low_one * down[0][1]
            diagonal = (1.0 + first) + (second + high_two * up[1][0])
            diagonal = diagonal + (low_two * down[1][1] + (up[2][0] + down[2][1]))
            inverse = inside / diagonal
            which = 0 if adjoint else 1
            coef[0, p, here, :] = up[0][which] * inverse
            coef[1, p, here, :] = down[0][1 - which] * inverse
            coef[2, p, here, :] = jnp.where(last_lane, 0.0, up[1][which] * inverse)
            coef[3, p, here, :] = jnp.where(first_lane, 0.0, down[1][1 - which] * inverse)
            coef[4, p, here, :] = up[2][which] * inverse
            coef[5, p, here, :] = down[2][1 - which] * inverse
            coef[6, p, here, :] = inverse
        return carry

    for move in flow_moves:
        move.wait()
    lax.fori_loop(1, depth - 1, coefficients, 0, unroll=2)
    for move in value_moves:
        move.wait()

    def sweep(source, lead, low, planes, offset, count, store):
        def rows(r):
            return pl.ds(offset + r * 8, 8)

        def at_planes(k, carry):
            p = low + 2 * k
            each = [(q, d) for q in range(2) for d in range(dirs)]
            value = {(q, d): source[d, p + q, rows(0), :] for q, d in each}
            up = {e: pltpu.roll(v, 7, 0) for e, v in value.items()}
            down = {e: pltpu.roll(v, 1, 0) for e, v in value.items()}
            before = dict.fromkeys(each, zero)
            if count < chunks:
                at = pl.multiple_of(jnp.maximum(offset - 8, 0), 8)
                for q, d in each:
                    outer = pltpu.roll(source[d, p + q, pl.ds(at, 8), :], 1, 0)
                    before[q, d] = jnp.where(a == 0, 0.0, outer)
            for r in range(count):
                c = [[coef[m, p + q, rows(r), :] for m in range(7 if lead else 6)] for q in range(2)]
                plane = {d: [source[d, p - 1, rows(r), :], value[0, d], value[1, d], source[d, p + 2, rows(r), :]] for d in range(dirs)}
                for q, d in each:
                    here = value[q, d]
                    if r + 1 < count:
                        following = source[d, p + q, rows(r + 1), :]
                        next_up, next_down = pltpu.roll(following, 7, 0), pltpu.roll(following, 1, 0)
                    elif count < chunks:
                        at = pl.multiple_of(jnp.minimum(offset + count * 8, height - 8), 8)
                        following = source[d, p + q, pl.ds(at, 8), :]
                        next_up, next_down = jnp.where(a == 1, 0.0, pltpu.roll(following, 7, 0)), zero
                    else:
                        following, next_up, next_down = zero, zero, zero
                    if lead:
                        total = here * c[q][6]
                        rhs[d, p + q, rows(r), :] = total
                    else:
                        total = rhs[d, p + q, rows(r), :]
                    depth_sum = c[q][4] * plane[d][q + 2] + c[q][5] * plane[d][q]
                    first_sum = c[q][0] * jnp.where(top_sub, next_up, up[q, d])
                    first_sum = first_sum + c[q][1] * jnp.where(bottom_sub, before[q, d], down[q, d])
                    second_sum = c[q][2] * pltpu.roll(here, LANES - 1, 1) + c[q][3] * pltpu.roll(here, 1, 1)
                    total = (total + depth_sum) + (first_sum + second_sum)
                    store(d, p + q, rows(r), r, total)
                    value[q, d], up[q, d], before[q, d], down[q, d] = (
                        following, next_up, down[q, d], next_down
                    )
            return carry

        lax.fori_loop(0, planes // 2, at_planes, 0)

    def into(ref):
        def store(d, p, here, r, total):
            ref[d, p, here, :] = total

        return store

    def again(d, p, here, r, total):
        start[d, p, here, :] = total if adjoint else total + start[d, p, here, :]

    def full(source, lead, step, store):
        sweep(source, lead, 1 + step, depth - 2 - 2 * step, 0, chunks, store)

    full(start, True, 0, into(ping))
    full(ping, False, 1, into(pong))
    full(pong, False, 2, again)
    full(start, True, 3, into(ping))
    full(ping, False, 4, into(pong))

    half = own // 2
    if adjoint:
        for out, side in zip(outs, (a, 1 - a)):
            low = reach + side * half

            def finish(d, p, here, r, total, out=out, low=low):
                out[d, p - low, r * 8 : r * 8 + 8, :] = total + start[d, p, here, :]

            shift = pl.multiple_of(a * SPARE, 8)
            sweep(pong, False, low, half, shift, (height - SPARE) // 8, finish)
    else:
        up_out, down_out = outs

        def emit(kinds):
            def finish(d, p, here, r, total):
                i = p - reach
                total = total * weight_ref[i // half, i % half, here, :]
                if "d" in kinds:
                    down_out[d, i, here, :] = total
                if "u" in kinds:
                    up_out[d, i - (own - reach), here, :] = total

            return finish

        for low, high, kinds in ((0, own - reach, "d"), (own - reach, reach, "du"), (reach, own, "u")):
            sweep(pong, False, reach + low, high - low, 0, chunks, emit(kinds))


def solves(adjoint, width, where, planes, flows, values, weight=None):
    dirs, reach, height, _ = values[0].shape
    depth = 2 * planes + 2 * reach
    ins = [where, *flows, *values]
    specs = [ANY] * 8
    if adjoint:
        outs = [floats(dirs, planes, height - SPARE, LANES)] * 2
    else:
        ins.append(weight)
        specs.append(VMEM)
        outs = [floats(*values[0].shape)] * 2
    scratch = [pltpu.VMEM((n, depth, height, LANES), jnp.float32) for n in (3, 7) + (dirs,) * 4]
    scratch.append(pltpu.SemaphoreType.DMA((8,)))
    return call(
        functools.partial(solve_kernel, adjoint, width),
        "adjoint" if adjoint else "forward",
        ins, outs, scratch, 36, 6 * 20 * dirs * depth * height * LANES, specs,
    )


def body(
    directions,
    eigen_basis,
    flow_first,
    flow_second,
    flow_depth,
    face_codes,
    sensor_cells,
    sensor_weight,
):
    dirs, planes, width, _ = directions.shape
    rank = eigen_basis.shape[0]
    count = lax.axis_size("slab")
    height = width // 2 + SPARE
    own, other, above = quad(count)
    me = lax.axis_index("slab")
    a, b = me // 2 % 2, me % 2
    place = [a, b, (me - 2 * a == 0), (me + 2 * (1 - a) == count - 1)]
    where = jnp.concatenate([jnp.stack([x.astype(jnp.int32) for x in place]), face_codes])
    each = dirs // GROUPS

    def regroup(first, second):
        return lax.ppermute(first, "slab", own), lax.ppermute(second, "slab", other)

    def cut(scalars, fields, group, lists=()):
        parts = len(fields) * len(group)
        extra = sum(x.shape[0] for x in lists)
        outs = [floats(parts * planes * height + extra, LANES)] * 2
        scratch = [
            pltpu.VMEM((max(extra, 8), LANES), jnp.float32),
            pltpu.SemaphoreType.DMA((2 * parts * planes + 2,)),
        ]
        kernel = functools.partial(cut_kernel, height, group, len(lists))
        specs = [VMEM] * len(lists) + [ANY] * len(fields)
        return call(kernel, "cut", [scalars, *lists, *fields], outs, scratch, 54, 0, specs, [ANY] * 2)

    def beyond(up, down):
        return up, down, lax.ppermute(up, "slab", above), lax.ppermute(down, "slab", back(above))

    def pack(scalars, pair, parts):
        outs = [floats(parts, REACH, height, LANES)] * 2
        return call(functools.partial(pack_kernel, planes), "pack", [scalars, *pair], outs)

    sensors = [x.reshape(-1, LANES) for x in (sensor_cells, sensor_weight)]
    listed = 2 * sensors[0].shape[0]
    block = planes * height
    basis = eigen_basis.reshape(rank, planes * width, LANES)
    flows = regroup(*cut(where, [flow_first, flow_second, flow_depth], [0]))
    tile, later = gram_tile(where, basis)
    moved = [regroup(*cut(later, [directions], range(each), sensors))]
    for k in range(each, dirs, each):
        moved.append(regroup(*cut(later, [directions], range(k, k + each))))
    flows = beyond(*pack(later, flows, 3))
    weight, last = call(
        functools.partial(sensor_kernel, width, each * block), "sensors", [later, *moved[0]],
        [floats(2, planes, height, LANES), jax.ShapeDtypeStruct(where.shape, where.dtype)],
        work=planes * height * listed * 20, out_specs=[VMEM, SMEM],
    )
    scalars = [later] + [last] * (GROUPS - 1)
    values = [beyond(*pack(s, m, each)) for s, m in zip(scalars, moved)]
    forcing = [beyond(*solves(False, width, where, planes, flows, v, weight)) for v in values]
    summed = [solves(True, width, where, planes, flows, f) for f in forcing]
    returned = [
        (lax.ppermute(s[0], "slab", back(own)), lax.ppermute(s[1], "slab", back(other)))
        for s in summed
    ]
    images = []
    for k, halves in enumerate(returned):
        copies = count if k == GROUPS - 1 else 1
        tile, image = projections(where, basis, directions, k * each, halves, tile, copies)
        images.append(image)
    rem, coeffs, parts = remainders(spread(tile, count), basis, images, count)
    new_directions = scaled(spread(parts, count), rem, planes * count * width * LANES, count)
    return (new_directions.reshape(directions.shape), coeffs)


def solution(mesh):
    return jax.shard_map(
        body,
        mesh=mesh,
        in_specs=(
            P("grp", "slab", None, None),
            P("grp", "slab", None, None),
            P("slab", None, None),
            P("slab", None, None),
            P("slab", None, None),
            P(),
            P(("grp", "slab")),
            P(("grp", "slab")),
        ),
        out_specs=(P("grp", "slab", None, None), P("grp", None)),
        check_vma=False,
    )
```

time: 212 us -> 303 us (1.43)
  Pallas kernels: 109 us -> 219 us
  waiting for transfers between devices: 26.4 us -> 15 us
  local copies, waits for them, and re-layouts: 12.5 us -> 3.49 us
    pallas_call x15, Pallas kernels: 107 us -> 217 us  [call(): pl.pallas_call(kernel, in_specs=[first] + (specs or [VMEM] * (len(ins) -...]
    ppermute x3, waiting for transfers between devices: 14.8 us -> 1.89 us  [regroup(): lax.ppermute(second, 'slab', other)]
    unnamed x21 -> x13, local copies, waits for them, and re-layouts: 11.8 us -> 2.27 us
    ppermute x3, starting transfers between devices: 2.12 us -> 5.29 us  [regroup(): lax.ppermute(first, 'slab', own)]
  transfers between devices with their start and end apart: 21 -> 21, of which waited for: 5 -> 3; matrix products, arithmetic and copies ran while one was open for 0% -> 0% of each run, Pallas kernels for 42% -> 49%
where the time goes in v3:
time: 303 us; the launch traced here: 302 us
  Pallas kernels  219 us (72%)
  starting transfers between devices  50.9 us (17%)
  waiting for transfers between devices  15 us (5%)
  blocking collectives  13.4 us (4%)
  local copies, waits for them, and re-layouts  3.49 us (1%)
    pallas_call x15, Pallas kernels, call(): pl.pallas_call(kernel, in_specs=[first] + (specs or [VMEM] * (len(ins) -...  217 us
    ppermute x5, starting transfers between devices, beyond(): lax.ppermute(up, 'slab', above)  17 us
    all_to_all x1, blocking collectives, spread(): return lax.all_to_all(tile, 'slab', 0, 0, tiled=True) if count > 1 else tile  13.4 us
    ppermute x3, starting transfers between devices, regroup(): lax.ppermute(second, 'slab', other)  10.4 us
    ppermute x2, waiting for transfers between devices, body(): lax.ppermute(s[1], 'slab', back(other))  6.89 us
    ppermute x5, starting transfers between devices, beyond(): lax.ppermute(down, 'slab', back(above))  6.64 us
    ppermute x2, starting transfers between devices, body(): lax.ppermute(s[1], 'slab', back(other))  6.58 us
    all_to_all x1, waiting for transfers between devices, spread(): return lax.all_to_all(tile, 'slab', 0, 0, tiled=True) if count > 1 else tile  6.21 us
  transfers between devices with their start and end apart: 21, of which 3 were waited for; matrix products, arithmetic and copies ran while one was open for 0% of the time, Pallas kernels for 49%

profile of v3, /device:TPU:0, one launch (start us, length us, event | category | flops | bytes accessed | tf_op | source)
XLA Modules:
  0.0 302.5 jit_solution(8098454669098272373)
XLA Ops:
  1.9 55.6 %cut.3 = (f32[1728,128]{1,0:T(8,128)}, f32[1728,128]{1,0:T(8,128)}) custom-call(s32[8]{0:T(128)} %concatenate.3.where_ref, f32[4,256,128]{2,1,0:T(8,128)} %refs_0_.2, f32[4,256,128]{2,1,0:T(8,128)} %refs_1_.1, f32[4,256,128]{2,1,0:T(8,128)} %refs_2_.2), custom_call_target="tpu_custom_call" | custom-call | bytes 3342336 | tf_op jit(solution)/shard_map/cut/pallas_call | solution.py:326
  59.3 3.1 %collective-permute-start.1 = (f32[1728,128]{1,0:T(8,128)}, f32[1728,128]{1,0:T(8,128)S(1)}, u32[]{:S(2)}, u32[]{:S(2)}) collective-permute-start(f32[1728,128]{1,0:T(8,128)} %get-tuple-element.35), channel_id=1, source_target_pairs={{0,2},{1,0},{2,3},{3,1},{4,6},{5,4},{6,7},{7,5},{8,10},{9,8},{10,1... | collective-permute-start | bytes 2654216 | tf_op jit(solution)/shard_map/ppermute | solution.py:648
  62.4 8.9 %gram.1 = (f32[8,128]{1,0:T(8,128)}, s32[8]{0:T(128)}) custom-call(s32[8]{0:T(128)} %concatenate.3.where_ref, f32[16,1024,128]{2,1,0:T(8,128)} %bitcast.16), custom_call_target="tpu_custom_call" | custom-call | flops 5033164800 | bytes 8392736 | tf_op jit(solution)/shard_map/gram/pallas_call | solution.py:326
  71.3 37.8 %cut.4 = (f32[1216,128]{1,0:T(8,128)}, f32[1216,128]{1,0:T(8,128)}) custom-call(s32[8]{0:T(128)} %get-tuple-element.33.where_ref, s32[32,128]{1,0:T(8,128)} %bitcast.23, f32[32,128]{1,0:T(8,128)} %bitcast.24, f32[4,4,256,128]{3,2,1,0:T(8,128)} %refs_0_.3), custom_call_target="tpu_custom_call" | custom-call | bytes 3375104 | tf_op jit(solution)/shard_map/cut/pallas_call | solution.py:326
  116.3 37.7 %cut.5 = (f32[1152,128]{1,0:T(8,128)}, f32[1152,128]{1,0:T(8,128)}) custom-call(s32[8]{0:T(128)} %get-tuple-element.33.where_ref, f32[4,4,256,128]{3,2,1,0:T(8,128)} %refs_0_.3), custom_call_target="tpu_custom_call" | custom-call | bytes 3276800 | tf_op jit(solution)/shard_map/cut/pallas_call | solution.py:326
  156.4 5.0 %collective-permute-start.14 = (f32[2,6,144,128]{3,2,1,0:T(8,128)S(1)}, f32[2,6,144,128]{3,2,1,0:T(8,128)S(1)}, u32[]{:S(2)}, u32[]{:S(2)}) collective-permute-start(f32[2,6,144,128]{3,2,1,0:T(8,128)S(1)} %get-tuple-element.50.refs_4_), channel_id=1, source_target_pairs={{0,1},{1,4},{2,3},{3,6},{4,5},{5,8},{6,7},{7,10},{8,9},{9,12},{10,... | collective-permute-start | bytes 2654216 | tf_op jit(solution)/shard_map/ppermute | solution.py:663
  162.7 5.4 %collective-permute-start.7 = (f32[1152,128]{1,0:T(8,128)}, f32[1152,128]{1,0:T(8,128)S(1)}, u32[]{:S(2)}, u32[]{:S(2)}) collective-permute-start(f32[1152,128]{1,0:T(8,128)} %get-tuple-element.42), channel_id=1, source_target_pairs={{0,2},{1,0},{2,3},{3,1},{4,6},{5,4},{6,7},{7,5},{8,10},{9,8},{10,1... | collective-permute-start | bytes 1769480 | tf_op jit(solution)/shard_map/ppermute | solution.py:648
  168.1 5.8 %sensors.1 = (f32[2,4,144,128]{3,2,1,0:T(8,128)S(1)}, s32[8]{0:T(128)S(1)}) custom-call(s32[8]{0:T(128)S(1)} %copy-done.3, f32[1216,128]{1,0:T(8,128)S(1)} %collective-permute-done.4.own_ref, f32[1216,128]{1,0:T(8,128)S(1)} %collective-permute-done.5.other_ref), custom_call_target="tpu_custom_call" | custom-call | flops 110592000 | bytes 1835040 | tf_op jit(solution)/shard_map/sensors/pallas_call | solution.py:326
  176.5 3.3 %collective-permute-start.8 = (f32[2,6,144,128]{3,2,1,0:T(8,128)S(1)}, f32[2,6,144,128]{3,2,1,0:T(8,128)S(1)}, u32[]{:S(2)}, u32[]{:S(2)}) collective-permute-start(f32[2,6,144,128]{3,2,1,0:T(8,128)S(1)} %get-tuple-element.43.refs_4_), channel_id=1, source_target_pairs={{0,1},{1,4},{2,3},{3,6},{4,5},{5,8},{6,7},{7,10},{8,9},{9,12},{10,... | collective-permute-start | bytes 2654216 | tf_op jit(solution)/shard_map/ppermute | solution.py:663
  181.3 12.4 %forward.3 = (f32[2,6,144,128]{3,2,1,0:T(8,128)S(1)}, f32[2,6,144,128]{3,2,1,0:T(8,128)S(1)}) custom-call(s32[8]{0:T(128)S(1)} %copy-done.4, f32[3,6,144,128]{3,2,1,0:T(8,128)S(1)} %get-tuple-element.36.refs_0_, f32[3,6,144,128]{3,2,1,0:T(8,128)S(1)} %get-tuple-element.37.refs_1_, f32[3,6,144,128]{3,2,1,0:T(8,128)S(1)} %collective-permute-done.2.refs_2_, ...), custom_call_target="tpu_custom_call" | custom-call | flops 13271040000 | bytes 11206656 | tf_op jit(solution)/shard_map/forward/pallas_call | solution.py:326
  193.7 3.1 %collective-permute-start.16 = (f32[2,6,144,128]{3,2,1,0:T(8,128)S(1)}, f32[2,6,144,128]{3,2,1,0:T(8,128)S(1)}, u32[]{:S(2)}, u32[]{:S(2)}) collective-permute-start(f32[2,6,144,128]{3,2,1,0:T(8,128)S(1)} %get-tuple-element.52.refs_4_), channel_id=1, source_target_pairs={{0,1},{1,4},{2,3},{3,6},{4,5},{5,8},{6,7},{7,10},{8,9},{9,12},{10,... | collective-permute-start | bytes 2654216 | tf_op jit(solution)/shard_map/ppermute | solution.py:663
  198.1 12.4 %forward.2 = (f32[2,6,144,128]{3,2,1,0:T(8,128)S(1)}, f32[2,6,144,128]{3,2,1,0:T(8,128)S(1)}) custom-call(s32[8]{0:T(128)S(1)} %copy-done.4, f32[3,6,144,128]{3,2,1,0:T(8,128)S(1)} %get-tuple-element.36.refs_0_, f32[3,6,144,128]{3,2,1,0:T(8,128)S(1)} %get-tuple-element.37.refs_1_, f32[3,6,144,128]{3,2,1,0:T(8,128)S(1)} %collective-permute-done.2.refs_2_, ...), custom_call_target="tpu_custom_call" | custom-call | flops 13271040000 | bytes 11206656 | tf_op jit(solution)/shard_map/forward/pallas_call | solution.py:326
  210.5 4.3 %collective-permute-start.10 = (f32[2,6,144,128]{3,2,1,0:T(8,128)S(1)}, f32[2,6,144,128]{3,2,1,0:T(8,128)S(1)}, u32[]{:S(2)}, u32[]{:S(2)}) collective-permute-start(f32[2,6,144,128]{3,2,1,0:T(8,128)S(1)} %get-tuple-element.46.refs_4_), channel_id=1, source_target_pairs={{0,1},{1,4},{2,3},{3,6},{4,5},{5,8},{6,7},{7,10},{8,9},{9,12},{10,... | collective-permute-start | bytes 2654216 | tf_op jit(solution)/shard_map/ppermute | solution.py:663
  216.1 12.2 %adjoint.3 = (f32[2,4,128,128]{3,2,1,0:T(8,128)S(1)}, f32[2,4,128,128]{3,2,1,0:T(8,128)S(1)}) custom-call(s32[8]{0:T(128)S(1)} %copy-done.4, f32[3,6,144,128]{3,2,1,0:T(8,128)S(1)} %get-tuple-element.36.refs_0_, f32[3,6,144,128]{3,2,1,0:T(8,128)S(1)} %get-tuple-element.37.refs_1_, f32[3,6,144,128]{3,2,1,0:T(8,128)S(1)} %collective-permute-done.2.refs_2_, ...), custom_call_target="tpu_custom_call" | custom-call | flops 13271040000 | bytes 9895936 | tf_op jit(solution)/shard_map/adjoint/pallas_call | solution.py:326
  229.0 3.7 %collective-permute-start.19 = (f32[2,4,128,128]{3,2,1,0:T(8,128)S(1)}, f32[2,4,128,128]{3,2,1,0:T(8,128)S(1)}, u32[]{:S(2)}, u32[]{:S(2)}) collective-permute-start(f32[2,4,128,128]{3,2,1,0:T(8,128)S(1)} %get-tuple-element.55), channel_id=1, source_target_pairs={{2,0},{0,1},{3,2},{1,3},{6,4},{4,5},{7,6},{5,7},{10,8},{8,9},{11,1... | collective-permute-start | bytes 1572872 | tf_op jit(solution)/shard_map/ppermute | solution.py:689
  232.7 12.2 %adjoint.2 = (f32[2,4,128,128]{3,2,1,0:T(8,128)S(1)}, f32[2,4,128,128]{3,2,1,0:T(8,128)S(1)}) custom-call(s32[8]{0:T(128)S(1)} %copy-done.4, f32[3,6,144,128]{3,2,1,0:T(8,128)S(1)} %get-tuple-element.36.refs_0_, f32[3,6,144,128]{3,2,1,0:T(8,128)S(1)} %get-tuple-element.37.refs_1_, f32[3,6,144,128]{3,2,1,0:T(8,128)S(1)} %collective-permute-done.2.refs_2_, ...), custom_call_target="tpu_custom_call" | custom-call | flops 13271040000 | bytes 9895936 | tf_op jit(solution)/shard_map/adjoint/pallas_call | solution.py:326
  245.6 2.8 collective-permute-start.13
  248.4 6.5 %projections.2 = (f32[8,128]{1,0:T(8,128)S(1)}, f32[2,1024,128]{2,1,0:T(8,128)}) custom-call(s32[8]{0:T(128)S(1)} %copy-done.4, f32[16,1024,128]{2,1,0:T(8,128)} %bitcast.17, f32[4,1024,128]{2,1,0:T(8,128)} %bitcast.20, f32[2,4,128,128]{3,2,1,0:T(8,128)S(1)} %collective-permute-done.18.own_hbm, f32[2,4,128,128]{3,2,1,0:T(8,128)S(1)} %collective-permute-done.19.other_hbm, ...), custom_call_target="tpu_custom_call" | custom-call | flops 1258291200 | bytes 12591104 | tf_op jit(solution)/shard_map/projections/pallas_call | solution.py:326
  255.0 6.9 %collective-permute-done.13.other_hbm = f32[2,4,128,128]{3,2,1,0:T(8,128)S(1)} collective-permute-done((f32[2,4,128,128]{3,2,1,0:T(8,128)S(1)}, f32[2,4,128,128]{3,2,1,0:T(8,128)S(1)}, u32[]{:S(2)}, u32[]{:S(2)}) %collective-permute-start.13) | collective-permute-done | bytes 524320 | tf_op jit(solution)/shard_map/ppermute | solution.py:689
  261.9 6.6 %projections.3 = (f32[128,128]{1,0:T(8,128)S(1)}, f32[2,1024,128]{2,1,0:T(8,128)}) custom-call(s32[8]{0:T(128)S(1)} %copy-done.4, f32[16,1024,128]{2,1,0:T(8,128)} %bitcast.18, f32[4,1024,128]{2,1,0:T(8,128)} %bitcast.21, f32[2,4,128,128]{3,2,1,0:T(8,128)S(1)} %collective-permute-done.12.own_hbm, f32[2,4,128,128]{3,2,1,0:T(8,128)S(1)} %collective-permute-done.13.other_hbm, ...), custom_call_target="tpu_custom_call" | custom-call | flops 1258291200 | bytes 12652544 | tf_op jit(solution)/shard_map/projections/pallas_call | solution.py:326
  268.5 13.4 %all_to_all.22 = f32[16,8,128]{2,1,0:T(8,128)S(1)} all-to-all(f32[16,8,128]{2,1,0:T(8,128)S(1)} %bitcast.15), channel_id=1, replica_groups=mesh['grp'=2,'slab'=16] {'slab'}, dimensions={0} | all-to-all | bytes 131072 | tf_op jit(solution)/shard_map/all_to_all | solution.py:110
  281.8 6.7 %remainder.1 = (f32[4,1024,128]{2,1,0:T(8,128)}, f32[16,4]{1,0:T(8,128)S(1)}, f32[128,128]{1,0:T(8,128)}) custom-call(f32[128,128]{1,0:T(8,128)S(1)} %bitcast.14, f32[16,1024,128]{2,1,0:T(8,128)} %bitcast.19, f32[2,1024,128]{2,1,0:T(8,128)S(1)} %copy-done.1, f32[2,1024,128]{2,1,0:T(8,128)} %get-tuple-element.60.refs_1_), custom_call_target="tpu_custom_call" | custom-call | flops 2516582400 | bytes 12648704 | tf_op jit(solution)/shard_map/remainder/pallas_call | solution.py:326
  288.5 3.5 %all-to-all-start.1 = ((f32[16,8,128]{2,1,0:T(8,128)}), f32[16,8,128]{2,1,0:T(8,128)S(1)}, u32[]{:S(2)}, u32[]{:S(2)}) async-start(f32[16,8,128]{2,1,0:T(8,128)} %bitcast.10), calls=%async_computation.1 | async-start | bytes 131072 | tf_op jit(solution)/shard_map/all_to_all | solution.py:110
  292.7 6.2 %all-to-all-done.1 = f32[16,8,128]{2,1,0:T(8,128)S(1)} async-done(((f32[16,8,128]{2,1,0:T(8,128)}), f32[16,8,128]{2,1,0:T(8,128)S(1)}, u32[]{:S(2)}, u32[]{:S(2)}) %all-to-all-start.1) | async-done | bytes 65568 | tf_op jit(solution)/shard_map/all_to_all | solution.py:110
  (49 shorter events, 26.1 us)
Async XLA Ops:
  57.5 55.3 %collective-permute-start = (f32[1728,128]{1,0:T(8,128)}, f32[1728,128]{1,0:T(8,128)S(1)}, u32[]{:S(2)}, u32[]{:S(2)}) collective-permute-start(f32[1728,128]{1,0:T(8,128)} %get-tuple-element.34), channel_id=1, source_target_pairs={{0,0},{1,2},{2,1},{3,3},{4,4},{5,6},{6,5},{7,7},{8,8},{9,10},{10,9... | collective-permute-start | bytes 2654216 | tf_op jit(solution)/shard_map/ppermute | solution.py:648
  59.3 53.5 %collective-permute-start.1 = (f32[1728,128]{1,0:T(8,128)}, f32[1728,128]{1,0:T(8,128)S(1)}, u32[]{:S(2)}, u32[]{:S(2)}) collective-permute-start(f32[1728,128]{1,0:T(8,128)} %get-tuple-element.35), channel_id=1, source_target_pairs={{0,2},{1,0},{2,3},{3,1},{4,6},{5,4},{6,7},{7,5},{8,10},{9,8},{10,1... | collective-permute-start | bytes 2654216 | tf_op jit(solution)/shard_map/ppermute | solution.py:648
  71.3 41.5 %copy-start.2 = (s32[8]{0:T(128)S(1)}, s32[8]{0:T(128)}, u32[]{:S(2)}) copy-start(s32[8]{0:T(128)} %get-tuple-element.33.where_ref) | copy-start | bytes 100
  109.1 46.5 %copy-start.3 = (s32[8]{0:T(128)S(1)}, s32[8]{0:T(128)}, u32[]{:S(2)}) copy-start(s32[8]{0:T(128)} %get-tuple-element.33.where_ref) | copy-start | bytes 100
  109.2 46.5 %collective-permute-start.4 = (f32[1216,128]{1,0:T(8,128)}, f32[1216,128]{1,0:T(8,128)S(1)}, u32[]{:S(2)}, u32[]{:S(2)}) collective-permute-start(f32[1216,128]{1,0:T(8,128)} %get-tuple-element.38), channel_id=1, source_target_pairs={{0,0},{1,2},{2,1},{3,3},{4,4},{5,6},{6,5},{7,7},{8,8},{9,10},{10,9... | collective-permute-start | bytes 1867784 | tf_op jit(solution)/shard_map/ppermute | solution.py:648
  110.9 44.8 %collective-permute-start.5 = (f32[1216,128]{1,0:T(8,128)}, f32[1216,128]{1,0:T(8,128)S(1)}, u32[]{:S(2)}, u32[]{:S(2)}) collective-permute-start(f32[1216,128]{1,0:T(8,128)} %get-tuple-element.39), channel_id=1, source_target_pairs={{0,2},{1,0},{2,3},{3,1},{4,6},{5,4},{6,7},{7,5},{8,10},{9,8},{10,1... | collective-permute-start | bytes 1867784 | tf_op jit(solution)/shard_map/ppermute | solution.py:648
  113.6 67.7 %collective-permute-start.2 = (f32[3,6,144,128]{3,2,1,0:T(8,128)S(1)}, f32[3,6,144,128]{3,2,1,0:T(8,128)S(1)}, u32[]{:S(2)}, u32[]{:S(2)}) collective-permute-start(f32[3,6,144,128]{3,2,1,0:T(8,128)S(1)} %get-tuple-element.36.refs_0_), channel_id=1, source_target_pairs={{0,1},{1,4},{2,3},{3,6},{4,5},{5,8},{6,7},{7,10},{8,9},{9,12},{10,... | collective-permute-start | bytes 3981320 | tf_op jit(solution)/shard_map/ppermute | solution.py:663
  115.0 66.4 %collective-permute-start.3 = (f32[3,6,144,128]{3,2,1,0:T(8,128)S(1)}, f32[3,6,144,128]{3,2,1,0:T(8,128)S(1)}, u32[]{:S(2)}, u32[]{:S(2)}) collective-permute-start(f32[3,6,144,128]{3,2,1,0:T(8,128)S(1)} %get-tuple-element.37.refs_1_), channel_id=1, source_target_pairs={{1,0},{4,1},{3,2},{6,3},{5,4},{8,5},{7,6},{10,7},{9,8},{12,9},{11,... | collective-permute-start | bytes 3981320 | tf_op jit(solution)/shard_map/ppermute | solution.py:663
  153.9 27.4 %copy-start.4 = (s32[8]{0:T(128)S(1)}, s32[8]{0:T(128)}, u32[]{:S(2)}) copy-start(s32[8]{0:T(128)} %concatenate.3.where_ref) | copy-start | bytes 100
  153.9 8.8 %collective-permute-start.6 = (f32[1152,128]{1,0:T(8,128)}, f32[1152,128]{1,0:T(8,128)S(1)}, u32[]{:S(2)}, u32[]{:S(2)}) collective-permute-start(f32[1152,128]{1,0:T(8,128)} %get-tuple-element.41), channel_id=1, source_target_pairs={{0,0},{1,2},{2,1},{3,3},{4,4},{5,6},{6,5},{7,7},{8,8},{9,10},{10,9... | collective-permute-start | bytes 1769480 | tf_op jit(solution)/shard_map/ppermute | solution.py:648
  156.4 23.4 %collective-permute-start.14 = (f32[2,6,144,128]{3,2,1,0:T(8,128)S(1)}, f32[2,6,144,128]{3,2,1,0:T(8,128)S(1)}, u32[]{:S(2)}, u32[]{:S(2)}) collective-permute-start(f32[2,6,144,128]{3,2,1,0:T(8,128)S(1)} %get-tuple-element.50.refs_4_), channel_id=1, source_target_pairs={{0,1},{1,4},{2,3},{3,6},{4,5},{5,8},{6,7},{7,10},{8,9},{9,12},{10,... | collective-permute-start | bytes 2654216 | tf_op jit(solution)/shard_map/ppermute | solution.py:663
  161.4 19.9 %collective-permute-start.15 = (f32[2,6,144,128]{3,2,1,0:T(8,128)S(1)}, f32[2,6,144,128]{3,2,1,0:T(8,128)S(1)}, u32[]{:S(2)}, u32[]{:S(2)}) collective-permute-start(f32[2,6,144,128]{3,2,1,0:T(8,128)S(1)} %get-tuple-element.51.refs_5_), channel_id=1, source_target_pairs={{1,0},{4,1},{3,2},{6,3},{5,4},{8,5},{7,6},{10,7},{9,8},{12,9},{11,... | collective-permute-start | bytes 2654216 | tf_op jit(solution)/shard_map/ppermute | solution.py:663
  162.7 13.1 %collective-permute-start.7 = (f32[1152,128]{1,0:T(8,128)}, f32[1152,128]{1,0:T(8,128)S(1)}, u32[]{:S(2)}, u32[]{:S(2)}) collective-permute-start(f32[1152,128]{1,0:T(8,128)} %get-tuple-element.42), channel_id=1, source_target_pairs={{0,2},{1,0},{2,3},{3,1},{4,6},{5,4},{6,7},{7,5},{8,10},{9,8},{10,1... | collective-permute-start | bytes 1769480 | tf_op jit(solution)/shard_map/ppermute | solution.py:648
  176.5 21.6 %collective-permute-start.8 = (f32[2,6,144,128]{3,2,1,0:T(8,128)S(1)}, f32[2,6,144,128]{3,2,1,0:T(8,128)S(1)}, u32[]{:S(2)}, u32[]{:S(2)}) collective-permute-start(f32[2,6,144,128]{3,2,1,0:T(8,128)S(1)} %get-tuple-element.43.refs_4_), channel_id=1, source_target_pairs={{0,1},{1,4},{2,3},{3,6},{4,5},{5,8},{6,7},{7,10},{8,9},{9,12},{10,... | collective-permute-start | bytes 2654216 | tf_op jit(solution)/shard_map/ppermute | solution.py:663
  179.8 18.3 %collective-permute-start.9 = (f32[2,6,144,128]{3,2,1,0:T(8,128)S(1)}, f32[2,6,144,128]{3,2,1,0:T(8,128)S(1)}, u32[]{:S(2)}, u32[]{:S(2)}) collective-permute-start(f32[2,6,144,128]{3,2,1,0:T(8,128)S(1)} %get-tuple-element.44.refs_5_), channel_id=1, source_target_pairs={{1,0},{4,1},{3,2},{6,3},{5,4},{8,5},{7,6},{10,7},{9,8},{12,9},{11,... | collective-permute-start | bytes 2654216 | tf_op jit(solution)/shard_map/ppermute | solution.py:663
  193.7 22.4 %collective-permute-start.16 = (f32[2,6,144,128]{3,2,1,0:T(8,128)S(1)}, f32[2,6,144,128]{3,2,1,0:T(8,128)S(1)}, u32[]{:S(2)}, u32[]{:S(2)}) collective-permute-start(f32[2,6,144,128]{3,2,1,0:T(8,128)S(1)} %get-tuple-element.52.refs_4_), channel_id=1, source_target_pairs={{0,1},{1,4},{2,3},{3,6},{4,5},{5,8},{6,7},{7,10},{8,9},{9,12},{10,... | collective-permute-start | bytes 2654216 | tf_op jit(solution)/shard_map/ppermute | solution.py:663
  196.8 19.3 %collective-permute-start.17 = (f32[2,6,144,128]{3,2,1,0:T(8,128)S(1)}, f32[2,6,144,128]{3,2,1,0:T(8,128)S(1)}, u32[]{:S(2)}, u32[]{:S(2)}) collective-permute-start(f32[2,6,144,128]{3,2,1,0:T(8,128)S(1)} %get-tuple-element.53.refs_5_), channel_id=1, source_target_pairs={{1,0},{4,1},{3,2},{6,3},{5,4},{8,5},{7,6},{10,7},{9,8},{12,9},{11,... | collective-permute-start | bytes 2654216 | tf_op jit(solution)/shard_map/ppermute | solution.py:663
  210.5 22.2 %collective-permute-start.10 = (f32[2,6,144,128]{3,2,1,0:T(8,128)S(1)}, f32[2,6,144,128]{3,2,1,0:T(8,128)S(1)}, u32[]{:S(2)}, u32[]{:S(2)}) collective-permute-start(f32[2,6,144,128]{3,2,1,0:T(8,128)S(1)} %get-tuple-element.46.refs_4_), channel_id=1, source_target_pairs={{0,1},{1,4},{2,3},{3,6},{4,5},{5,8},{6,7},{7,10},{8,9},{9,12},{10,... | collective-permute-start | bytes 2654216 | tf_op jit(solution)/shard_map/ppermute | solution.py:663
  214.8 18.0 %collective-permute-start.11 = (f32[2,6,144,128]{3,2,1,0:T(8,128)S(1)}, f32[2,6,144,128]{3,2,1,0:T(8,128)S(1)}, u32[]{:S(2)}, u32[]{:S(2)}) collective-permute-start(f32[2,6,144,128]{3,2,1,0:T(8,128)S(1)} %get-tuple-element.47.refs_5_), channel_id=1, source_target_pairs={{1,0},{4,1},{3,2},{6,3},{5,4},{8,5},{7,6},{10,7},{9,8},{12,9},{11,... | collective-permute-start | bytes 2654216 | tf_op jit(solution)/shard_map/ppermute | solution.py:663
  228.3 20.2 %collective-permute-start.18 = (f32[2,4,128,128]{3,2,1,0:T(8,128)S(1)}, f32[2,4,128,128]{3,2,1,0:T(8,128)S(1)}, u32[]{:S(2)}, u32[]{:S(2)}) collective-permute-start(f32[2,4,128,128]{3,2,1,0:T(8,128)S(1)} %get-tuple-element.54), channel_id=1, source_target_pairs={{0,0},{2,1},{1,2},{3,3},{4,4},{6,5},{5,6},{7,7},{8,8},{10,9},{9,10... | collective-permute-start | bytes 1572872 | tf_op jit(solution)/shard_map/ppermute | solution.py:689
  229.0 19.5 %collective-permute-start.19 = (f32[2,4,128,128]{3,2,1,0:T(8,128)S(1)}, f32[2,4,128,128]{3,2,1,0:T(8,128)S(1)}, u32[]{:S(2)}, u32[]{:S(2)}) collective-permute-start(f32[2,4,128,128]{3,2,1,0:T(8,128)S(1)} %get-tuple-element.55), channel_id=1, source_target_pairs={{2,0},{0,1},{3,2},{1,3},{6,4},{4,5},{7,6},{5,7},{10,8},{8,9},{11,1... | collective-permute-start | bytes 1572872 | tf_op jit(solution)/shard_map/ppermute | solution.py:689
  244.9 10.1 %collective-permute-start.12 = (f32[2,4,128,128]{3,2,1,0:T(8,128)S(1)}, f32[2,4,128,128]{3,2,1,0:T(8,128)S(1)}, u32[]{:S(2)}, u32[]{:S(2)}) collective-permute-start(f32[2,4,128,128]{3,2,1,0:T(8,128)S(1)} %get-tuple-element.48), channel_id=1, source_target_pairs={{0,0},{2,1},{1,2},{3,3},{4,4},{6,5},{5,6},{7,7},{8,8},{10,9},{9,10... | collective-permute-start | bytes 1572872 | tf_op jit(solution)/shard_map/ppermute | solution.py:689
  245.6 16.3 %collective-permute-start.13 = (f32[2,4,128,128]{3,2,1,0:T(8,128)S(1)}, f32[2,4,128,128]{3,2,1,0:T(8,128)S(1)}, u32[]{:S(2)}, u32[]{:S(2)}) collective-permute-start(f32[2,4,128,128]{3,2,1,0:T(8,128)S(1)} %get-tuple-element.49), channel_id=1, source_target_pairs={{2,0},{0,1},{3,2},{1,3},{6,4},{4,5},{7,6},{5,7},{10,8},{8,9},{11,1... | collective-permute-start | bytes 1572872 | tf_op jit(solution)/shard_map/ppermute | solution.py:689
  288.5 10.4 %all-to-all-start.1 = ((f32[16,8,128]{2,1,0:T(8,128)}), f32[16,8,128]{2,1,0:T(8,128)S(1)}, u32[]{:S(2)}, u32[]{:S(2)}) async-start(f32[16,8,128]{2,1,0:T(8,128)} %bitcast.10), calls=%async_computation.1 | async-start | bytes 131072 | tf_op jit(solution)/shard_map/all_to_all | solution.py:110
  (3 other events, 41.0 us)

commit v4 on v3

--- a/solution.py
+++ b/solution.py
@@ -88,7 +88,7 @@
     whole = upper + strict.T
     out_ref[...] = jnp.zeros_like(out_ref)
     for k in range(0, rank, 8):
-        at = rank + k * rank // 8
+        at = 2 * rank + k * rank // 8
         out_ref[:, at : at + rank] = whole[k : k + 8]
 
 
@@ -110,10 +110,13 @@
     return lax.all_to_all(tile, "slab", 0, 0, tiled=True) if count > 1 else tile
 
 
-def projection_kernel(
-    first, where_ref, basis_hbm, dirs_hbm, own_hbm, other_hbm, tile_ref,
-    out_ref, image_ref, basis_ref, dirs_ref, halves_ref, sems, side_sems,
-):
+def projection_kernel(first, where_ref, basis_in, dirs_hbm, own_hbm, other_hbm, tile_ref, out_ref, image_ref, *refs):
+    moves = None
+    if first == 0:
+        basis_ref, dirs_ref, halves_ref, side_sems, sems = refs
+        moves = chunks_of(basis_in, basis_ref, sems, PIECES)
+    else:
+        basis_ref, (dirs_ref, halves_ref, side_sems) = basis_in, refs
     rank = basis_ref.shape[0]
     dirs, rows, _ = image_ref.shape
     planes, half = halves_ref.shape[2:4]
@@ -123,19 +126,18 @@
         pltpu.make_async_copy(other_hbm, halves_ref.at[1], side_sems.at[1]),
         pltpu.make_async_copy(dirs_hbm.at[pl.ds(first, dirs)], dirs_ref, side_sems.at[2]),
     ]
-    moves = chunks_of(basis_hbm, basis_ref, sems, PIECES)
-    for move in sides + moves:
+    for move in sides + (moves or []):
         move.start()
     for move in sides:
         move.wait()
-    sums = [jnp.zeros((8, LANES), jnp.float32) for _ in range(rank * dirs)]
+    sums = [jnp.zeros((8, LANES), jnp.float32) for _ in range((rank + 1) * dirs)]
+    piece = rows // PIECES
     for k in range(2 * planes):
         plane, part = k // 2, k % 2
         which = jnp.where(b == part, 0, 1)
         low = k * half
-        piece = rows // PIECES
-        for m in range(low // piece, -(-(low + half) // piece)):
-            if m * piece >= low:
+        if moves:
+            for m in range(-(-low // piece), -(-(low + half) // piece)):
                 moves[m].wait()
 
         def add(r, sums, plane=plane, which=which, low=low):
@@ -150,17 +152,22 @@
             for i in range(rank):
                 q = basis_ref[i, at, :]
                 out += [sums[i * dirs + d] + q * image[d] for d in range(dirs)]
-            return out
+            return out + [sums[rank * dirs + d] + image[d] * image[d] for d in range(dirs)]
 
         sums = lax.fori_loop(0, half // 8, add, sums, unroll=4)
 
     row = lax.broadcasted_iota(jnp.int32, (8, LANES), 0)
     lane = lax.broadcasted_iota(jnp.int32, (8, LANES), 1)
+    lines = [sums[i * dirs + d] for d in range(dirs) for i in range(rank)] + sums[rank * dirs :]
+    lines = [jnp.sum(line, axis=0, keepdims=True) for line in lines]
+    lines.append(jnp.zeros((LANES - len(lines), LANES), jnp.float32))
+    found = lane_sums(jnp.concatenate(lines, 0))
     table = tile_ref[...]
+    squares = pltpu.roll(found, (rank + first - rank * dirs) % LANES, 1)
     for d in range(dirs):
-        lines = [jnp.sum(sums[i * dirs + d], axis=0, keepdims=True) for i in range(rank)]
-        lines = jnp.concatenate(lines + [jnp.zeros((LANES - rank, LANES), jnp.float32)], 0)
-        table = jnp.where((row == first + d) & (lane < rank), lane_sums(lines), table)
+        products = pltpu.roll(found, (LANES - d * rank) % LANES, 1) if d else found
+        table = jnp.where((row == first + d) & (lane < rank), products, table)
+        table = jnp.where((row == first + d) & (lane == rank + first + d), squares, table)
     for r in range(out_ref.shape[0] // 8):
         out_ref[r * 8 : (r + 1) * 8, :] = table
 
@@ -168,19 +175,22 @@
 def projections(where, basis, directions, first, halves, tile, count):
     rank, rows, _ = basis.shape
     dirs = halves[0].shape[0]
-    return call(
+    outs = [floats(count * 8, LANES), floats(dirs, rows, LANES)]
+    scratch = [
+        pltpu.VMEM((dirs, rows, LANES), jnp.float32),
+        pltpu.VMEM((2, *halves[0].shape), jnp.float32),
+        pltpu.SemaphoreType.DMA((3,)),
+    ]
+    if first == 0:
+        outs.append(floats(*basis.shape))
+        scratch.append(pltpu.SemaphoreType.DMA((PIECES,)))
+    found = call(
         functools.partial(projection_kernel, first), "projections",
         [where, basis, directions.reshape(-1, rows, LANES), *halves, tile],
-        [floats(count * 8, LANES), floats(dirs, rows, LANES)],
-        [
-            pltpu.VMEM(basis.shape, jnp.float32),
-            pltpu.VMEM((dirs, rows, LANES), jnp.float32),
-            pltpu.VMEM((2, *halves[0].shape), jnp.float32),
-            pltpu.SemaphoreType.DMA((PIECES,)),
-            pltpu.SemaphoreType.DMA((3,)),
-        ],
-        52, 2 * rank * dirs * rows * LANES, [ANY] * 4 + [VMEM],
-    )
+        outs, scratch, 24, 2 * rank * dirs * rows * LANES,
+        [ANY if first == 0 else VMEM] + [ANY] * 3 + [VMEM],
+    )
+    return (*found, basis)[:3] if first else found
 
 
 def summed_tile(parts_ref):
@@ -190,8 +200,9 @@
     return tiles[0]
 
 
-def solved(tile, rank):
-    gram = [tile[:, rank + k * rank // 8 :][:, :rank] for k in range(0, rank, 8)]
+def eliminated(tile, rank):
+    gram = [tile[:, 2 * rank + k * rank // 8 :][:, :rank] for k in range(0, rank, 8)]
+    lane = lax.broadcasted_iota(jnp.int32, (8, LANES), 1)
     table = jnp.concatenate(
         [
             jnp.concatenate(gram, 0),
@@ -200,109 +211,141 @@
         ],
         1,
     )
-    row = lax.broadcasted_iota(jnp.int32, (rank, LANES), 0)
+    table = jnp.concatenate([table, jnp.where(lane < rank + 8, tile, 0.0)], 0)
+    row = lax.broadcasted_iota(jnp.int32, table.shape, 0)
     for k in range(rank):
-        scaled_row = table[k : k + 1, :] / table[k : k + 1, k : k + 1]
-        table = jnp.where(row == k, scaled_row, table - table[:, k : k + 1] * scaled_row)
+        pivot_row = table[k : k + 1, :] / table[k : k + 1, k : k + 1]
+        table = jnp.where(row == k, pivot_row, table - table[:, k : k + 1] * pivot_row)
     return table
 
 
-def remainder_kernel(dirs, parts_ref, basis_hbm, *refs):
+def inverse_root(value):
+    root = lax.rsqrt(value)
+    return root * (1.5 - (0.5 * value * root) * root)
+
+
+def remainder_kernel(dirs, cells, parts_ref, basis_ref, *refs):
     groups = len(refs) - 8
-    images, (rem_ref, coeffs_ref, out_ref, basis_ref, image_ref, splat_ref, sems, side_sems) = (
-        refs[:groups], refs[groups:]
-    )
+    images = refs[:groups]
+    new_hbm, coeffs_ref, scale_out, again_ref, rem_ref, splat_ref, scale_ref, sems = refs[groups:]
     each = dirs // groups
     rank, rows, _ = basis_ref.shape
     tile = 4
-    sides = [
-        pltpu.make_async_copy(image, image_ref.at[pl.ds(k * each, each)], side_sems.at[k])
-        for k, image in enumerate(images)
-    ]
-    moves = chunks_of(basis_hbm, basis_ref, sems, PIECES)
-    for move in sides + moves:
-        move.start()
-    table = solved(summed_tile(parts_ref), rank)
-    coeffs_ref[...] = table[:, rank : rank + dirs]
+    first = summed_tile(parts_ref)
+    table = eliminated(first, rank)
+    coeffs_ref[...] = table[0:rank, rank : rank + dirs]
     for d in range(dirs):
         for j in range(rank):
             splat_ref[d * rank + j] = jnp.broadcast_to(
                 table[j : j + 1, rank + d : rank + d + 1], (8, LANES)
             )
-    for move in sides:
-        move.wait()
-    energy = [jnp.zeros((8, LANES), jnp.float32) for _ in range(dirs)]
+    row = lax.broadcasted_iota(jnp.int32, (8, LANES), 0)
+    lane = lax.broadcasted_iota(jnp.int32, (8, LANES), 1)
+    energy, square = table[rank : rank + 8, :], first
+    unsure = (lane == rank + row) & (row < dirs) & jnp.logical_not(energy >= 0.01 * square)
+    again_ref[0] = jnp.max(jnp.where(unsure, 1.0, 0.0)).astype(jnp.int32)
+    scale = inverse_root(jnp.maximum(energy, 0.0) / cells + 1e-06)
+    scales = jnp.zeros((8, LANES), jnp.float32)
+    for d in range(dirs):
+        one = jnp.broadcast_to(scale[d : d + 1, rank + d : rank + d + 1], (8, LANES))
+        scale_ref[d] = one
+        scales = jnp.where(row == d, one, scales)
+    scale_out[...] = scales
     part = rows // PIECES
-    for piece, move in enumerate(moves):
-        move.wait()
+    moves = []
+    for piece in range(PIECES):
         for j0 in range(0, rank, tile):
             last = j0 + tile == rank
             weights = [[splat_ref[d * rank + j] for j in range(j0, j0 + tile)] for d in range(dirs)]
-
-            def take(k, energy, j0=j0, last=last, weights=weights, piece=piece):
+            scale = [scale_ref[d] for d in range(dirs)] if last else None
+
+            def take(k, carry, j0=j0, last=last, weights=weights, scale=scale, piece=piece):
                 at = pl.ds(pl.multiple_of(piece * part + k * 8, 8), 8)
                 basis = [basis_ref[j, at, :] for j in range(j0, j0 + tile)]
-                out = []
                 for d in range(dirs):
-                    left = image_ref[d, at, :] if j0 == 0 else rem_ref[d, at, :]
+                    left = images[d // each][d % each, at, :] if j0 == 0 else rem_ref[d, at, :]
                     parts = [w * q for w, q in zip(weights[d], basis)]
                     left = left - ((parts[0] + parts[1]) + (parts[2] + parts[3]))
-                    rem_ref[d, at, :] = left
-                    out.append(energy[d] + left * left if last else energy[d])
-                return out
-
-            energy = lax.fori_loop(0, part // 8, take, energy, unroll=4)
-
-    row = lax.broadcasted_iota(jnp.int32, (8, LANES), 0)
-    tile_out = jnp.zeros((8, LANES), jnp.float32)
-    for d in range(dirs):
-        total = jnp.sum(jnp.sum(energy[d], axis=0, keepdims=True), axis=1, keepdims=True)
-        tile_out = jnp.where(row == d, jnp.broadcast_to(total, (8, LANES)), tile_out)
-    for r in range(out_ref.shape[0] // 8):
-        out_ref[r * 8 : (r + 1) * 8, :] = tile_out
-
-
-def remainders(parts, basis, images, count):
+                    rem_ref[d, at, :] = left * scale[d] if last else left
+                return carry
+
+            lax.fori_loop(0, part // 8, take, 0, unroll=4)
+        at = pl.ds(piece * part, part)
+        moves.append(pltpu.make_async_copy(rem_ref.at[:, at], new_hbm.at[:, at], sems.at[piece]))
+        moves[-1].start()
+    for move in moves:
+        move.wait()
+
+
+def remainders(parts, basis, images, cells):
     rank, rows, _ = basis.shape
     dirs = sum(i.shape[0] for i in images)
     return call(
-        functools.partial(remainder_kernel, dirs), "remainder", [parts, basis, *images],
-        [floats(dirs, rows, LANES), floats(rank, dirs), floats(count * 8, LANES)],
+        functools.partial(remainder_kernel, dirs, cells), "remainder", [parts, basis, *images],
         [
-            pltpu.VMEM(basis.shape, jnp.float32),
+            floats(dirs, rows, LANES),
+            floats(rank, dirs),
+            floats(8, LANES),
+            jax.ShapeDtypeStruct((1,), jnp.int32),
+        ],
+        [
             pltpu.VMEM((dirs, rows, LANES), jnp.float32),
             pltpu.VMEM((dirs * rank, 8, LANES), jnp.float32),
+            pltpu.VMEM((dirs, 8, LANES), jnp.float32),
             pltpu.SemaphoreType.DMA((PIECES,)),
-            pltpu.SemaphoreType.DMA((len(images),)),
         ],
-        52, 2 * rank * dirs * rows * LANES, [ANY] * (1 + len(images)), first=VMEM,
-    )
-
-
-def scale_kernel(cells, parts_ref, rem_ref, new_ref):
-    energy = summed_tile(parts_ref)
-    value = energy / cells + 1e-06
-    root = lax.rsqrt(value)
-    root = root * (1.5 - (0.5 * value * root) * root)
-    for d in range(rem_ref.shape[0]):
-        new_ref[d] = rem_ref[d] * root[d : d + 1, :]
-
-
-def scaled(parts, rem, cells, count):
-    dirs, rows, _ = rem.shape
-    chunk = 256
+        24, 2 * rank * dirs * rows * LANES, first=VMEM, out_specs=[ANY, VMEM, VMEM, SMEM],
+    )
+
+
+def squares_kernel(new_ref, out_ref, sum_ref):
+    dirs = new_ref.shape[0]
+    row = lax.broadcasted_iota(jnp.int32, (8, LANES), 0)
+
+    @pl.when(pl.program_id(0) == 0)
+    def _():
+        sum_ref[...] = jnp.zeros_like(sum_ref)
+
+    for d in range(dirs):
+        lines = jnp.sum(new_ref[d] * new_ref[d], axis=0, keepdims=True)
+        total = jnp.broadcast_to(jnp.sum(lines, axis=1, keepdims=True), (8, LANES))
+        sum_ref[...] += jnp.where(row == d, total, 0.0)
+    for r in range(out_ref.shape[0] // 8):
+        out_ref[r * 8 : (r + 1) * 8, :] = sum_ref[...]
+
+
+def rescale_kernel(cells, parts_ref, scale_ref, new_ref, out_ref):
+    scale = scale_ref[...]
+    energy = summed_tile(parts_ref) / scale / scale
+    ratio = inverse_root(energy / cells + 1e-06) / scale
+    for d in range(new_ref.shape[0]):
+        out_ref[d] = new_ref[d] * ratio[d : d + 1, :]
+
+
+def rescaled(new, scales, cells, count):
+    dirs, rows, _ = new.shape
+    chunk = 128
+    lines = pl.BlockSpec((dirs, chunk, LANES), lambda k: (0, k, 0))
+    whole = lambda n: pl.BlockSpec((n, LANES), lambda k: (0, 0))
+    parts = pl.pallas_call(
+        squares_kernel,
+        grid=(rows // chunk,),
+        in_specs=[lines],
+        out_specs=whole(count * 8),
+        out_shape=floats(count * 8, LANES),
+        scratch_shapes=[pltpu.VMEM((8, LANES), jnp.float32)],
+        compiler_params=pltpu.CompilerParams(vmem_limit_bytes=16 << 20),
+        name="squares",
+    )(new)
     return pl.pallas_call(
-        functools.partial(scale_kernel, cells),
+        functools.partial(rescale_kernel, cells),
         grid=(rows // chunk,),
-        in_specs=[
-            pl.BlockSpec((count * 8, LANES), lambda k: (0, 0)),
-            pl.BlockSpec((dirs, chunk, LANES), lambda k: (0, k, 0)),
-        ],
-        out_specs=pl.BlockSpec((dirs, chunk, LANES), lambda k: (0, k, 0)),
+        in_specs=[whole(count * 8), whole(8), lines],
+        out_specs=lines,
         out_shape=floats(dirs, rows, LANES),
         compiler_params=pltpu.CompilerParams(vmem_limit_bytes=16 << 20),
-        name="scale",
-    )(parts, rem)
+        name="rescale",
+    )(spread(parts, count), scales, new)
 
 
 def quad(count):
@@ -336,8 +379,8 @@
 
 
 def cut_kernel(height, group, listed, where_ref, *refs):
-    lists, fields = refs[:listed], refs[listed:-4]
-    own_ref, other_ref, list_ref, sems = refs[-4:]
+    lists, fields = refs[:listed], refs[listed:-3]
+    own_ref, other_ref, sems = refs[-3:]
     b = where_ref[1]
     moves = []
 
@@ -355,13 +398,11 @@
                 for ref, low in ((own_ref, start), (other_ref, rest)):
                     move(field.at[(*at, pl.ds(low, height))], ref.at[pl.ds(k, height)])
                 k += height
-    low = 0
     for entries in lists:
-        list_ref[low : low + entries.shape[0], :] = entries[...].astype(jnp.float32)
-        low += entries.shape[0]
-    if lists:
+        rows = entries.shape[0]
         for ref in (own_ref, other_ref):
-            move(list_ref, ref.at[pl.ds(k, low)])
+            ref[k : k + rows, :] = entries[...].astype(jnp.float32)
+        k += rows
     for m in moves:
         m.wait()
 
@@ -651,13 +692,10 @@
         parts = len(fields) * len(group)
         extra = sum(x.shape[0] for x in lists)
         outs = [floats(parts * planes * height + extra, LANES)] * 2
-        scratch = [
-            pltpu.VMEM((max(extra, 8), LANES), jnp.float32),
-            pltpu.SemaphoreType.DMA((2 * parts * planes + 2,)),
-        ]
+        scratch = [pltpu.SemaphoreType.DMA((2 * parts * planes,))]
         kernel = functools.partial(cut_kernel, height, group, len(lists))
         specs = [VMEM] * len(lists) + [ANY] * len(fields)
-        return call(kernel, "cut", [scalars, *lists, *fields], outs, scratch, 54, 0, specs, [ANY] * 2)
+        return call(kernel, "cut", [scalars, *lists, *fields], outs, scratch, 54, 0, specs)
 
     def beyond(up, down):
         return up, down, lax.ppermute(up, "slab", above), lax.ppermute(down, "slab", back(above))
@@ -692,11 +730,16 @@
     images = []
     for k, halves in enumerate(returned):
         copies = count if k == GROUPS - 1 else 1
-        tile, image = projections(where, basis, directions, k * each, halves, tile, copies)
+        tile, image, basis = projections(where, basis, directions, k * each, halves, tile, copies)
         images.append(image)
-    rem, coeffs, parts = remainders(spread(tile, count), basis, images, count)
-    new_directions = scaled(spread(parts, count), rem, planes * count * width * LANES, count)
-    return (new_directions.reshape(directions.shape), coeffs)
+    cells = planes * count * width * LANES
+    new, coeffs, scales, again = remainders(spread(tile, count), basis, images, cells)
+    new, _ = lax.while_loop(
+        lambda state: state[1] > 0,
+        lambda state: (rescaled(state[0], scales, cells, count), jnp.int32(0)),
+        (new, again[0]),
+    )
+    return (new.reshape(directions.shape), coeffs)
 
 
 def solution(mesh):

time: 303 us -> 172 us (0.57)
  Pallas kernels: 219 us -> 87.5 us
  waiting for transfers between devices: 15 us -> 19.3 us
  starting transfers between devices: 50.9 us -> 46.9 us
    pallas_call x15, Pallas kernels: 217 us -> 87.5 us  [call(): pl.pallas_call(kernel, in_specs=[first] + (specs or [VMEM] * (len(ins) -...]
    ppermute x3, waiting for transfers between devices: 1.89 us -> 9.01 us  [regroup(): lax.ppermute(second, 'slab', other)]
    all_to_all x1 -> x0, waiting for transfers between devices: 6.21 us -> none  [spread(): return lax.all_to_all(tile, 'slab', 0, 0, tiled=True) if count > 1 else tile]
    all_to_all x1 -> x0, starting transfers between devices: 3.49 us -> none  [spread(): return lax.all_to_all(tile, 'slab', 0, 0, tiled=True) if count > 1 else tile]
    ppermute x2, waiting for transfers between devices: 6.89 us -> 10.3 us  [body(): lax.ppermute(s[1], 'slab', back(other))]
  transfers between devices with their start and end apart: 21 -> 20, of which waited for: 3 -> 4; matrix products, arithmetic and copies ran while one was open for 0% -> 0% of each run, Pallas kernels for 49% -> 44%
where the time goes in v4:
time: 172 us; the launch traced here: 171 us
  Pallas kernels  87.5 us (51%)
  starting transfers between devices  46.9 us (27%)
  waiting for transfers between devices  19.3 us (11%)
  blocking collectives  13.4 us (8%)
  local copies, waits for them, and re-layouts  2 us (1%)
    pallas_call x15, Pallas kernels, call(): pl.pallas_call(kernel, in_specs=[first] + (specs or [VMEM] * (len(ins) -...  87.5 us
    ppermute x5, starting transfers between devices, beyond(): lax.ppermute(up, 'slab', above)  18 us
    all_to_all x1, blocking collectives, spread(): return lax.all_to_all(tile, 'slab', 0, 0, tiled=True) if count > 1 else tile  13.4 us
    ppermute x2, waiting for transfers between devices, body(): lax.ppermute(s[1], 'slab', back(other))  10.3 us
    ppermute x3, starting transfers between devices, regroup(): lax.ppermute(second, 'slab', other)  9.01 us
    ppermute x3, waiting for transfers between devices, regroup(): lax.ppermute(second, 'slab', other)  9.01 us
    ppermute x5, starting transfers between devices, beyond(): lax.ppermute(down, 'slab', back(above))  6.64 us
    ppermute x2, starting transfers between devices, body(): lax.ppermute(s[1], 'slab', back(other))  6.58 us
  transfers between devices with their start and end apart: 20, of which 4 were waited for; matrix products, arithmetic and copies ran while one was open for 0% of the time, Pallas kernels for 44%

profile of v4, /device:TPU:0, one launch (start us, length us, event | category | flops | bytes accessed | tf_op | source)
XLA Modules:
  0.0 170.9 jit_solution(15781889017535023807)
XLA Ops:
  2.0 3.6 %cut.3 = (f32[1728,128]{1,0:T(8,128)}, f32[1728,128]{1,0:T(8,128)}) custom-call(s32[8]{0:T(128)} %concatenate.3.where_ref, f32[4,256,128]{2,1,0:T(8,128)} %refs_0_.2, f32[4,256,128]{2,1,0:T(8,128)} %refs_1_.1, f32[4,256,128]{2,1,0:T(8,128)} %refs_2_.2), custom_call_target="tpu_custom_call" | custom-call | bytes 3342336 | tf_op jit(solution)/shard_map/cut/pallas_call | solution.py:369
  7.4 3.1 %collective-permute-start.1 = (f32[1728,128]{1,0:T(8,128)}, f32[1728,128]{1,0:T(8,128)S(1)}, u32[]{:S(2)}, u32[]{:S(2)}) collective-permute-start(f32[1728,128]{1,0:T(8,128)} %get-tuple-element.53), channel_id=1, source_target_pairs={{0,2},{1,0},{2,3},{3,1},{4,6},{5,4},{6,7},{7,5},{8,10},{9,8},{10,1... | collective-permute-start | bytes 2654216 | tf_op jit(solution)/shard_map/ppermute | solution.py:689
  10.5 8.9 %gram.1 = (f32[8,128]{1,0:T(8,128)}, s32[8]{0:T(128)}) custom-call(s32[8]{0:T(128)} %concatenate.3.where_ref, f32[16,1024,128]{2,1,0:T(8,128)} %bitcast.16), custom_call_target="tpu_custom_call" | custom-call | flops 5033164800 | bytes 8392736 | tf_op jit(solution)/shard_map/gram/pallas_call | solution.py:369
  19.4 3.3 %cut.4 = (f32[1216,128]{1,0:T(8,128)}, f32[1216,128]{1,0:T(8,128)}) custom-call(s32[8]{0:T(128)} %get-tuple-element.51.where_ref, s32[32,128]{1,0:T(8,128)} %bitcast.24, f32[32,128]{1,0:T(8,128)} %bitcast.25, f32[4,4,256,128]{3,2,1,0:T(8,128)} %refs_0_.3), custom_call_target="tpu_custom_call" | custom-call | bytes 3375104 | tf_op jit(solution)/shard_map/cut/pallas_call | solution.py:369
  26.5 4.3 %collective-permute-done.1.other_ref = f32[1728,128]{1,0:T(8,128)S(1)} collective-permute-done((f32[1728,128]{1,0:T(8,128)}, f32[1728,128]{1,0:T(8,128)S(1)}, u32[]{:S(2)}, u32[]{:S(2)}) %collective-permute-start.1) | collective-permute-done | bytes 884768 | tf_op jit(solution)/shard_map/ppermute | solution.py:689
  31.5 3.4 %collective-permute-start.2 = (f32[3,6,144,128]{3,2,1,0:T(8,128)S(1)}, f32[3,6,144,128]{3,2,1,0:T(8,128)S(1)}, u32[]{:S(2)}, u32[]{:S(2)}) collective-permute-start(f32[3,6,144,128]{3,2,1,0:T(8,128)S(1)} %get-tuple-element.54.refs_0_), channel_id=1, source_target_pairs={{0,1},{1,4},{2,3},{3,6},{4,5},{5,8},{6,7},{7,10},{8,9},{9,12},{10,... | collective-permute-start | bytes 3981320 | tf_op jit(solution)/shard_map/ppermute | solution.py:701
  36.2 3.2 %cut.5 = (f32[1152,128]{1,0:T(8,128)}, f32[1152,128]{1,0:T(8,128)}) custom-call(s32[8]{0:T(128)} %get-tuple-element.51.where_ref, f32[4,4,256,128]{3,2,1,0:T(8,128)} %refs_0_.3), custom_call_target="tpu_custom_call" | custom-call | bytes 3276800 | tf_op jit(solution)/shard_map/cut/pallas_call | solution.py:369
  41.1 2.8 %collective-permute-done.5.other_ref = f32[1216,128]{1,0:T(8,128)S(1)} collective-permute-done((f32[1216,128]{1,0:T(8,128)}, f32[1216,128]{1,0:T(8,128)S(1)}, u32[]{:S(2)}, u32[]{:S(2)}) %collective-permute-start.5) | collective-permute-done | bytes 622624 | tf_op jit(solution)/shard_map/ppermute | solution.py:689
  48.3 4.0 %collective-permute-start.13 = (f32[1152,128]{1,0:T(8,128)}, f32[1152,128]{1,0:T(8,128)S(1)}, u32[]{:S(2)}, u32[]{:S(2)}) collective-permute-start(f32[1152,128]{1,0:T(8,128)} %get-tuple-element.69), channel_id=1, source_target_pairs={{0,2},{1,0},{2,3},{3,1},{4,6},{5,4},{6,7},{7,5},{8,10},{9,8},{10,1... | collective-permute-start | bytes 1769480 | tf_op jit(solution)/shard_map/ppermute | solution.py:689
  52.3 5.8 %sensors.1 = (f32[2,4,144,128]{3,2,1,0:T(8,128)S(1)}, s32[8]{0:T(128)S(1)}) custom-call(s32[8]{0:T(128)S(1)} %copy-done.2, f32[1216,128]{1,0:T(8,128)S(1)} %collective-permute-done.4.own_ref, f32[1216,128]{1,0:T(8,128)S(1)} %collective-permute-done.5.other_ref), custom_call_target="tpu_custom_call" | custom-call | flops 110592000 | bytes 1835040 | tf_op jit(solution)/shard_map/sensors/pallas_call | solution.py:369
  60.7 2.9 %collective-permute-start.14 = (f32[2,6,144,128]{3,2,1,0:T(8,128)S(1)}, f32[2,6,144,128]{3,2,1,0:T(8,128)S(1)}, u32[]{:S(2)}, u32[]{:S(2)}) collective-permute-start(f32[2,6,144,128]{3,2,1,0:T(8,128)S(1)} %get-tuple-element.70.refs_4_), channel_id=1, source_target_pairs={{0,1},{1,4},{2,3},{3,6},{4,5},{5,8},{6,7},{7,10},{8,9},{9,12},{10,... | collective-permute-start | bytes 2654216 | tf_op jit(solution)/shard_map/ppermute | solution.py:701
  65.1 12.4 %forward.2 = (f32[2,6,144,128]{3,2,1,0:T(8,128)S(1)}, f32[2,6,144,128]{3,2,1,0:T(8,128)S(1)}) custom-call(s32[8]{0:T(128)S(1)} %copy-done.3, f32[3,6,144,128]{3,2,1,0:T(8,128)S(1)} %get-tuple-element.54.refs_0_, f32[3,6,144,128]{3,2,1,0:T(8,128)S(1)} %get-tuple-element.55.refs_1_, f32[3,6,144,128]{3,2,1,0:T(8,128)S(1)} %collective-permute-done.2.refs_2_, ...), custom_call_target="tpu_custom_call" | custom-call | flops 13271040000 | bytes 11206656 | tf_op jit(solution)/shard_map/forward/pallas_call | solution.py:369
  77.5 5.1 %collective-permute-start.8 = (f32[2,6,144,128]{3,2,1,0:T(8,128)S(1)}, f32[2,6,144,128]{3,2,1,0:T(8,128)S(1)}, u32[]{:S(2)}, u32[]{:S(2)}) collective-permute-start(f32[2,6,144,128]{3,2,1,0:T(8,128)S(1)} %get-tuple-element.61.refs_4_), channel_id=1, source_target_pairs={{0,1},{1,4},{2,3},{3,6},{4,5},{5,8},{6,7},{7,10},{8,9},{9,12},{10,... | collective-permute-start | bytes 2654216 | tf_op jit(solution)/shard_map/ppermute | solution.py:701
  83.9 12.4 %forward.3 = (f32[2,6,144,128]{3,2,1,0:T(8,128)S(1)}, f32[2,6,144,128]{3,2,1,0:T(8,128)S(1)}) custom-call(s32[8]{0:T(128)S(1)} %copy-done.3, f32[3,6,144,128]{3,2,1,0:T(8,128)S(1)} %get-tuple-element.54.refs_0_, f32[3,6,144,128]{3,2,1,0:T(8,128)S(1)} %get-tuple-element.55.refs_1_, f32[3,6,144,128]{3,2,1,0:T(8,128)S(1)} %collective-permute-done.2.refs_2_, ...), custom_call_target="tpu_custom_call" | custom-call | flops 13271040000 | bytes 11206656 | tf_op jit(solution)/shard_map/forward/pallas_call | solution.py:369
  96.3 4.3 %collective-permute-start.16 = (f32[2,6,144,128]{3,2,1,0:T(8,128)S(1)}, f32[2,6,144,128]{3,2,1,0:T(8,128)S(1)}, u32[]{:S(2)}, u32[]{:S(2)}) collective-permute-start(f32[2,6,144,128]{3,2,1,0:T(8,128)S(1)} %get-tuple-element.72.refs_4_), channel_id=1, source_target_pairs={{0,1},{1,4},{2,3},{3,6},{4,5},{5,8},{6,7},{7,10},{8,9},{9,12},{10,... | collective-permute-start | bytes 2654216 | tf_op jit(solution)/shard_map/ppermute | solution.py:701
  101.9 12.2 %adjoint.2 = (f32[2,4,128,128]{3,2,1,0:T(8,128)S(1)}, f32[2,4,128,128]{3,2,1,0:T(8,128)S(1)}) custom-call(s32[8]{0:T(128)S(1)} %copy-done.3, f32[3,6,144,128]{3,2,1,0:T(8,128)S(1)} %get-tuple-element.54.refs_0_, f32[3,6,144,128]{3,2,1,0:T(8,128)S(1)} %get-tuple-element.55.refs_1_, f32[3,6,144,128]{3,2,1,0:T(8,128)S(1)} %collective-permute-done.2.refs_2_, ...), custom_call_target="tpu_custom_call" | custom-call | flops 13271040000 | bytes 9895936 | tf_op jit(solution)/shard_map/adjoint/pallas_call | solution.py:369
  114.8 3.7 %collective-permute-start.11 = (f32[2,4,128,128]{3,2,1,0:T(8,128)S(1)}, f32[2,4,128,128]{3,2,1,0:T(8,128)S(1)}, u32[]{:S(2)}, u32[]{:S(2)}) collective-permute-start(f32[2,4,128,128]{3,2,1,0:T(8,128)S(1)} %get-tuple-element.64), channel_id=1, source_target_pairs={{2,0},{0,1},{3,2},{1,3},{6,4},{4,5},{7,6},{5,7},{10,8},{8,9},{11,1... | collective-permute-start | bytes 1572872 | tf_op jit(solution)/shard_map/ppermute | solution.py:727
  118.5 12.2 %adjoint.3 = (f32[2,4,128,128]{3,2,1,0:T(8,128)S(1)}, f32[2,4,128,128]{3,2,1,0:T(8,128)S(1)}) custom-call(s32[8]{0:T(128)S(1)} %copy-done.3, f32[3,6,144,128]{3,2,1,0:T(8,128)S(1)} %get-tuple-element.54.refs_0_, f32[3,6,144,128]{3,2,1,0:T(8,128)S(1)} %get-tuple-element.55.refs_1_, f32[3,6,144,128]{3,2,1,0:T(8,128)S(1)} %collective-permute-done.2.refs_2_, ...), custom_call_target="tpu_custom_call" | custom-call | flops 13271040000 | bytes 9895936 | tf_op jit(solution)/shard_map/adjoint/pallas_call | solution.py:369
  131.4 2.8 %collective-permute-start.19 = (f32[2,4,128,128]{3,2,1,0:T(8,128)S(1)}, f32[2,4,128,128]{3,2,1,0:T(8,128)S(1)}, u32[]{:S(2)}, u32[]{:S(2)}) collective-permute-start(f32[2,4,128,128]{3,2,1,0:T(8,128)S(1)} %get-tuple-element.75), channel_id=1, source_target_pairs={{2,0},{0,1},{3,2},{1,3},{6,4},{4,5},{7,6},{5,7},{10,8},{8,9},{11,1... | collective-permute-start | bytes 1572872 | tf_op jit(solution)/shard_map/ppermute | solution.py:727
  134.3 3.2 %projections.2 = (f32[8,128]{1,0:T(8,128)S(1)}, f32[2,1024,128]{2,1,0:T(8,128)S(1)}, f32[16,1024,128]{2,1,0:T(8,128)S(1)}) custom-call(s32[8]{0:T(128)S(1)} %copy-done.3, f32[16,1024,128]{2,1,0:T(8,128)S(1)} %bitcast.19, f32[4,1024,128]{2,1,0:T(8,128)S(1)} %bitcast.14, f32[2,4,128,128]{3,2,1,0:T(8,128)S(1)} %collective-permute-done.10.own_hbm, ...), custom_call_target="tpu_custom_call" | custom-call | flops 1258291200 | bytes 20979712 | tf_op jit(solution)/shard_map/projections/pallas_call | solution.py:369
  137.5 10.3 %collective-permute-done.19.other_hbm = f32[2,4,128,128]{3,2,1,0:T(8,128)S(1)} collective-permute-done((f32[2,4,128,128]{3,2,1,0:T(8,128)S(1)}, f32[2,4,128,128]{3,2,1,0:T(8,128)S(1)}, u32[]{:S(2)}, u32[]{:S(2)}) %collective-permute-start.19) | collective-permute-done | bytes 524320 | tf_op jit(solution)/shard_map/ppermute | solution.py:727
  147.7 2.5 %projections.3 = (f32[128,128]{1,0:T(8,128)S(1)}, f32[2,1024,128]{2,1,0:T(8,128)S(1)}) custom-call(s32[8]{0:T(128)S(1)} %copy-done.3, f32[16,1024,128]{2,1,0:T(8,128)S(1)} %get-tuple-element.66.basis_in.basis_ref, f32[4,1024,128]{2,1,0:T(8,128)S(1)} %bitcast.15, f32[2,4,128,128]{3,2,1,0:T(8,128)S(1)} %collective-permute-done.18.own_hbm, ...), custom_call_target="tpu_custom_call" | custom-call | flops 1258291200 | bytes 12652544 | tf_op jit(solution)/shard_map/projections/pallas_call | solution.py:369
  150.2 13.4 %all_to_all.19 = f32[16,8,128]{2,1,0:T(8,128)S(1)} all-to-all(f32[16,8,128]{2,1,0:T(8,128)S(1)} %bitcast.22), channel_id=1, replica_groups=mesh['grp'=2,'slab'=16] {'slab'}, dimensions={0} | all-to-all | bytes 131072 | tf_op jit(solution)/shard_map/all_to_all | solution.py:110
  163.6 5.9 %remainder.1 = (f32[4,1024,128]{2,1,0:T(8,128)}, f32[16,4]{1,0:T(8,128)S(1)}, f32[8,128]{1,0:T(8,128)S(1)}, s32[1]{0:T(128)}) custom-call(f32[128,128]{1,0:T(8,128)S(1)} %bitcast.21, f32[16,1024,128]{2,1,0:T(8,128)S(1)} %get-tuple-element.66.basis_in.basis_ref, f32[2,1024,128]{2,1,0:T(8,128)S(1)} %get-tuple-element.78.refs_0_, ...), custom_call_target="tpu_custom_call" | custom-call | flops 2516582400 | bytes 12587268 | tf_op jit(solution)/shard_map/remainder/pallas_call | solution.py:369
  (50 shorter events, 24.2 us)
Async XLA Ops:
  5.6 20.9 %collective-permute-start = (f32[1728,128]{1,0:T(8,128)}, f32[1728,128]{1,0:T(8,128)S(1)}, u32[]{:S(2)}, u32[]{:S(2)}) collective-permute-start(f32[1728,128]{1,0:T(8,128)} %get-tuple-element.52), channel_id=1, source_target_pairs={{0,0},{1,2},{2,1},{3,3},{4,4},{5,6},{6,5},{7,7},{8,8},{9,10},{10,9... | collective-permute-start | bytes 2654216 | tf_op jit(solution)/shard_map/ppermute | solution.py:689
  7.4 23.4 %collective-permute-start.1 = (f32[1728,128]{1,0:T(8,128)}, f32[1728,128]{1,0:T(8,128)S(1)}, u32[]{:S(2)}, u32[]{:S(2)}) collective-permute-start(f32[1728,128]{1,0:T(8,128)} %get-tuple-element.53), channel_id=1, source_target_pairs={{0,2},{1,0},{2,3},{3,1},{4,6},{5,4},{6,7},{7,5},{8,10},{9,8},{10,1... | collective-permute-start | bytes 2654216 | tf_op jit(solution)/shard_map/ppermute | solution.py:689
  22.8 21.2 %copy-start.2 = (s32[8]{0:T(128)S(1)}, s32[8]{0:T(128)}, u32[]{:S(2)}) copy-start(s32[8]{0:T(128)} %get-tuple-element.51.where_ref) | copy-start | bytes 100
  22.8 18.4 %collective-permute-start.4 = (f32[1216,128]{1,0:T(8,128)}, f32[1216,128]{1,0:T(8,128)S(1)}, u32[]{:S(2)}, u32[]{:S(2)}) collective-permute-start(f32[1216,128]{1,0:T(8,128)} %get-tuple-element.56), channel_id=1, source_target_pairs={{0,0},{1,2},{2,1},{3,3},{4,4},{5,6},{6,5},{7,7},{8,8},{9,10},{10,9... | collective-permute-start | bytes 1867784 | tf_op jit(solution)/shard_map/ppermute | solution.py:689
  24.5 19.4 %collective-permute-start.5 = (f32[1216,128]{1,0:T(8,128)}, f32[1216,128]{1,0:T(8,128)S(1)}, u32[]{:S(2)}, u32[]{:S(2)}) collective-permute-start(f32[1216,128]{1,0:T(8,128)} %get-tuple-element.57), channel_id=1, source_target_pairs={{0,2},{1,0},{2,3},{3,1},{4,6},{5,4},{6,7},{7,5},{8,10},{9,8},{10,1... | collective-permute-start | bytes 1867784 | tf_op jit(solution)/shard_map/ppermute | solution.py:689
  31.5 33.5 %collective-permute-start.2 = (f32[3,6,144,128]{3,2,1,0:T(8,128)S(1)}, f32[3,6,144,128]{3,2,1,0:T(8,128)S(1)}, u32[]{:S(2)}, u32[]{:S(2)}) collective-permute-start(f32[3,6,144,128]{3,2,1,0:T(8,128)S(1)} %get-tuple-element.54.refs_0_), channel_id=1, source_target_pairs={{0,1},{1,4},{2,3},{3,6},{4,5},{5,8},{6,7},{7,10},{8,9},{9,12},{10,... | collective-permute-start | bytes 3981320 | tf_op jit(solution)/shard_map/ppermute | solution.py:701
  34.9 30.1 %collective-permute-start.3 = (f32[3,6,144,128]{3,2,1,0:T(8,128)S(1)}, f32[3,6,144,128]{3,2,1,0:T(8,128)S(1)}, u32[]{:S(2)}, u32[]{:S(2)}) collective-permute-start(f32[3,6,144,128]{3,2,1,0:T(8,128)S(1)} %get-tuple-element.55.refs_1_), channel_id=1, source_target_pairs={{1,0},{4,1},{3,2},{6,3},{5,4},{8,5},{7,6},{10,7},{9,8},{12,9},{11,... | collective-permute-start | bytes 3981320 | tf_op jit(solution)/shard_map/ppermute | solution.py:701
  39.4 25.7 %copy-start.3 = (s32[8]{0:T(128)S(1)}, s32[8]{0:T(128)}, u32[]{:S(2)}) copy-start(s32[8]{0:T(128)} %concatenate.3.where_ref) | copy-start | bytes 100
  39.4 8.9 %collective-permute-start.12 = (f32[1152,128]{1,0:T(8,128)}, f32[1152,128]{1,0:T(8,128)S(1)}, u32[]{:S(2)}, u32[]{:S(2)}) collective-permute-start(f32[1152,128]{1,0:T(8,128)} %get-tuple-element.68), channel_id=1, source_target_pairs={{0,0},{1,2},{2,1},{3,3},{4,4},{5,6},{6,5},{7,7},{8,8},{9,10},{10,9... | collective-permute-start | bytes 1769480 | tf_op jit(solution)/shard_map/ppermute | solution.py:689
  44.6 18.9 %collective-permute-start.6 = (f32[2,6,144,128]{3,2,1,0:T(8,128)S(1)}, f32[2,6,144,128]{3,2,1,0:T(8,128)S(1)}, u32[]{:S(2)}, u32[]{:S(2)}) collective-permute-start(f32[2,6,144,128]{3,2,1,0:T(8,128)S(1)} %get-tuple-element.58.refs_4_), channel_id=1, source_target_pairs={{0,1},{1,4},{2,3},{3,6},{4,5},{5,8},{6,7},{7,10},{8,9},{9,12},{10,... | collective-permute-start | bytes 2654216 | tf_op jit(solution)/shard_map/ppermute | solution.py:701
  47.0 18.1 %collective-permute-start.7 = (f32[2,6,144,128]{3,2,1,0:T(8,128)S(1)}, f32[2,6,144,128]{3,2,1,0:T(8,128)S(1)}, u32[]{:S(2)}, u32[]{:S(2)}) collective-permute-start(f32[2,6,144,128]{3,2,1,0:T(8,128)S(1)} %get-tuple-element.59.refs_5_), channel_id=1, source_target_pairs={{1,0},{4,1},{3,2},{6,3},{5,4},{8,5},{7,6},{10,7},{9,8},{12,9},{11,... | collective-permute-start | bytes 2654216 | tf_op jit(solution)/shard_map/ppermute | solution.py:701
  48.3 11.7 %collective-permute-start.13 = (f32[1152,128]{1,0:T(8,128)}, f32[1152,128]{1,0:T(8,128)S(1)}, u32[]{:S(2)}, u32[]{:S(2)}) collective-permute-start(f32[1152,128]{1,0:T(8,128)} %get-tuple-element.69), channel_id=1, source_target_pairs={{0,2},{1,0},{2,3},{3,1},{4,6},{5,4},{6,7},{7,5},{8,10},{9,8},{10,1... | collective-permute-start | bytes 1769480 | tf_op jit(solution)/shard_map/ppermute | solution.py:689
  60.7 23.2 %collective-permute-start.14 = (f32[2,6,144,128]{3,2,1,0:T(8,128)S(1)}, f32[2,6,144,128]{3,2,1,0:T(8,128)S(1)}, u32[]{:S(2)}, u32[]{:S(2)}) collective-permute-start(f32[2,6,144,128]{3,2,1,0:T(8,128)S(1)} %get-tuple-element.70.refs_4_), channel_id=1, source_target_pairs={{0,1},{1,4},{2,3},{3,6},{4,5},{5,8},{6,7},{7,10},{8,9},{9,12},{10,... | collective-permute-start | bytes 2654216 | tf_op jit(solution)/shard_map/ppermute | solution.py:701
  63.6 20.3 %collective-permute-start.15 = (f32[2,6,144,128]{3,2,1,0:T(8,128)S(1)}, f32[2,6,144,128]{3,2,1,0:T(8,128)S(1)}, u32[]{:S(2)}, u32[]{:S(2)}) collective-permute-start(f32[2,6,144,128]{3,2,1,0:T(8,128)S(1)} %get-tuple-element.71.refs_5_), channel_id=1, source_target_pairs={{1,0},{4,1},{3,2},{6,3},{5,4},{8,5},{7,6},{10,7},{9,8},{12,9},{11,... | collective-permute-start | bytes 2654216 | tf_op jit(solution)/shard_map/ppermute | solution.py:701
  77.5 24.4 %collective-permute-start.8 = (f32[2,6,144,128]{3,2,1,0:T(8,128)S(1)}, f32[2,6,144,128]{3,2,1,0:T(8,128)S(1)}, u32[]{:S(2)}, u32[]{:S(2)}) collective-permute-start(f32[2,6,144,128]{3,2,1,0:T(8,128)S(1)} %get-tuple-element.61.refs_4_), channel_id=1, source_target_pairs={{0,1},{1,4},{2,3},{3,6},{4,5},{5,8},{6,7},{7,10},{8,9},{9,12},{10,... | collective-permute-start | bytes 2654216 | tf_op jit(solution)/shard_map/ppermute | solution.py:701
  82.6 19.3 %collective-permute-start.9 = (f32[2,6,144,128]{3,2,1,0:T(8,128)S(1)}, f32[2,6,144,128]{3,2,1,0:T(8,128)S(1)}, u32[]{:S(2)}, u32[]{:S(2)}) collective-permute-start(f32[2,6,144,128]{3,2,1,0:T(8,128)S(1)} %get-tuple-element.62.refs_5_), channel_id=1, source_target_pairs={{1,0},{4,1},{3,2},{6,3},{5,4},{8,5},{7,6},{10,7},{9,8},{12,9},{11,... | collective-permute-start | bytes 2654216 | tf_op jit(solution)/shard_map/ppermute | solution.py:701
  96.3 22.3 %collective-permute-start.16 = (f32[2,6,144,128]{3,2,1,0:T(8,128)S(1)}, f32[2,6,144,128]{3,2,1,0:T(8,128)S(1)}, u32[]{:S(2)}, u32[]{:S(2)}) collective-permute-start(f32[2,6,144,128]{3,2,1,0:T(8,128)S(1)} %get-tuple-element.72.refs_4_), channel_id=1, source_target_pairs={{0,1},{1,4},{2,3},{3,6},{4,5},{5,8},{6,7},{7,10},{8,9},{9,12},{10,... | collective-permute-start | bytes 2654216 | tf_op jit(solution)/shard_map/ppermute | solution.py:701
  100.6 18.0 %collective-permute-start.17 = (f32[2,6,144,128]{3,2,1,0:T(8,128)S(1)}, f32[2,6,144,128]{3,2,1,0:T(8,128)S(1)}, u32[]{:S(2)}, u32[]{:S(2)}) collective-permute-start(f32[2,6,144,128]{3,2,1,0:T(8,128)S(1)} %get-tuple-element.73.refs_5_), channel_id=1, source_target_pairs={{1,0},{4,1},{3,2},{6,3},{5,4},{8,5},{7,6},{10,7},{9,8},{12,9},{11,... | collective-permute-start | bytes 2654216 | tf_op jit(solution)/shard_map/ppermute | solution.py:701
  114.0 20.2 %collective-permute-start.10 = (f32[2,4,128,128]{3,2,1,0:T(8,128)S(1)}, f32[2,4,128,128]{3,2,1,0:T(8,128)S(1)}, u32[]{:S(2)}, u32[]{:S(2)}) collective-permute-start(f32[2,4,128,128]{3,2,1,0:T(8,128)S(1)} %get-tuple-element.63), channel_id=1, source_target_pairs={{0,0},{2,1},{1,2},{3,3},{4,4},{6,5},{5,6},{7,7},{8,8},{10,9},{9,10... | collective-permute-start | bytes 1572872 | tf_op jit(solution)/shard_map/ppermute | solution.py:727
  114.7 19.5 %slice-start = ((s8[8388608]{0:T(1024)(128)(4,1)}), s8[4194304]{0:T(1024)(128)(4,1)S(1)}, s32[]{:S(2)}) async-start(s8[8388608]{0:T(1024)(128)(4,1)} %bitcast.17), calls=%async_computation.2 | async-start | bytes 8388608
  114.8 19.5 %copy-start = (f32[4,4,256,128]{3,2,1,0:T(8,128)S(1)}, f32[4,4,256,128]{3,2,1,0:T(8,128)}, u32[]{:S(2)}) copy-start(f32[4,4,256,128]{3,2,1,0:T(8,128)} %refs_0_.3) | copy-start | bytes 6291460
  114.8 19.5 %collective-permute-start.11 = (f32[2,4,128,128]{3,2,1,0:T(8,128)S(1)}, f32[2,4,128,128]{3,2,1,0:T(8,128)S(1)}, u32[]{:S(2)}, u32[]{:S(2)}) collective-permute-start(f32[2,4,128,128]{3,2,1,0:T(8,128)S(1)} %get-tuple-element.64), channel_id=1, source_target_pairs={{2,0},{0,1},{3,2},{1,3},{6,4},{4,5},{7,6},{5,7},{10,8},{8,9},{11,1... | collective-permute-start | bytes 1572872 | tf_op jit(solution)/shard_map/ppermute | solution.py:727
  130.7 6.7 %collective-permute-start.18 = (f32[2,4,128,128]{3,2,1,0:T(8,128)S(1)}, f32[2,4,128,128]{3,2,1,0:T(8,128)S(1)}, u32[]{:S(2)}, u32[]{:S(2)}) collective-permute-start(f32[2,4,128,128]{3,2,1,0:T(8,128)S(1)} %get-tuple-element.74), channel_id=1, source_target_pairs={{0,0},{2,1},{1,2},{3,3},{4,4},{6,5},{5,6},{7,7},{8,8},{10,9},{9,10... | collective-permute-start | bytes 1572872 | tf_op jit(solution)/shard_map/ppermute | solution.py:727
  131.4 16.3 %collective-permute-start.19 = (f32[2,4,128,128]{3,2,1,0:T(8,128)S(1)}, f32[2,4,128,128]{3,2,1,0:T(8,128)S(1)}, u32[]{:S(2)}, u32[]{:S(2)}) collective-permute-start(f32[2,4,128,128]{3,2,1,0:T(8,128)S(1)} %get-tuple-element.75), channel_id=1, source_target_pairs={{2,0},{0,1},{3,2},{1,3},{6,4},{4,5},{7,6},{5,7},{10,8},{8,9},{11,1... | collective-permute-start | bytes 1572872 | tf_op jit(solution)/shard_map/ppermute | solution.py:727
  (3 other events, 50.4 us)

commit v5 on v4

--- a/solution.py
+++ b/solution.py
@@ -25,6 +25,12 @@
 VECTOR = 150
 
 
+def place():
+    me, count = lax.axis_index("slab"), lax.axis_size("slab")
+    a, b = lax.rem(me // 2, 2), lax.rem(me, 2)
+    return a, b, me - 2 * a == 0, me + 2 * (1 - a) == count - 1
+
+
 def floats(*shape):
     return jax.ShapeDtypeStruct(shape, jnp.float32)
 
@@ -50,14 +56,13 @@
     ]
 
 
-def gram_kernel(where_ref, basis_hbm, out_ref, where_out, basis_ref, acc_ref, sems):
+def gram_kernel(basis_hbm, out_ref, after_ref, basis_ref, acc_ref, sems):
     rank, rows, _ = basis_ref.shape
     tile = 4
     moves = chunks_of(basis_hbm, basis_ref, sems, PIECES)
     for move in moves:
         move.start()
-    for k in range(where_ref.shape[0]):
-        where_out[k] = where_ref[k]
+    after_ref[0] = 0
     acc_ref[...] = jnp.zeros_like(acc_ref)
     part = rows // PIECES
     for piece, move in enumerate(moves):
@@ -92,11 +97,13 @@
         out_ref[:, at : at + rank] = whole[k : k + 8]
 
 
-def gram_tile(where, basis):
+TOKEN = jax.ShapeDtypeStruct((1,), jnp.int32)
+
+
+def gram_tile(basis):
     rank, rows, _ = basis.shape
     return call(
-        gram_kernel, "gram", [where, basis],
-        [floats(8, LANES), jax.ShapeDtypeStruct(where.shape, where.dtype)],
+        gram_kernel, "gram", [basis], [floats(8, LANES), TOKEN],
         [
             pltpu.VMEM(basis.shape, jnp.float32),
             pltpu.VMEM((rank, rank, 8, LANES), jnp.float32),
@@ -110,7 +117,7 @@
     return lax.all_to_all(tile, "slab", 0, 0, tiled=True) if count > 1 else tile
 
 
-def projection_kernel(first, where_ref, basis_in, dirs_hbm, own_hbm, other_hbm, tile_ref, out_ref, image_ref, *refs):
+def projection_kernel(first, basis_in, dirs_hbm, own_hbm, other_hbm, tile_ref, out_ref, image_ref, *refs):
     moves = None
     if first == 0:
         basis_ref, dirs_ref, halves_ref, side_sems, sems = refs
@@ -120,7 +127,7 @@
     rank = basis_ref.shape[0]
     dirs, rows, _ = image_ref.shape
     planes, half = halves_ref.shape[2:4]
-    b = where_ref[1]
+    b = place()[1]
     sides = [
         pltpu.make_async_copy(own_hbm, halves_ref.at[0], side_sems.at[0]),
         pltpu.make_async_copy(other_hbm, halves_ref.at[1], side_sems.at[1]),
@@ -172,7 +179,7 @@
         out_ref[r * 8 : (r + 1) * 8, :] = table
 
 
-def projections(where, basis, directions, first, halves, tile, count):
+def projections(basis, directions, first, halves, tile, count):
     rank, rows, _ = basis.shape
     dirs = halves[0].shape[0]
     outs = [floats(count * 8, LANES), floats(dirs, rows, LANES)]
@@ -186,7 +193,7 @@
         scratch.append(pltpu.SemaphoreType.DMA((PIECES,)))
     found = call(
         functools.partial(projection_kernel, first), "projections",
-        [where, basis, directions.reshape(-1, rows, LANES), *halves, tile],
+        [basis, directions.reshape(-1, rows, LANES), *halves, tile],
         outs, scratch, 24, 2 * rank * dirs * rows * LANES,
         [ANY if first == 0 else VMEM] + [ANY] * 3 + [VMEM],
     )
@@ -233,7 +240,7 @@
     tile = 4
     first = summed_tile(parts_ref)
     table = eliminated(first, rank)
-    coeffs_ref[...] = table[0:rank, rank : rank + dirs]
+    coeffs_ref[...] = table[0:rank, rank : rank + 8].T[0:dirs]
     for d in range(dirs):
         for j in range(rank):
             splat_ref[d * rank + j] = jnp.broadcast_to(
@@ -284,9 +291,9 @@
         functools.partial(remainder_kernel, dirs, cells), "remainder", [parts, basis, *images],
         [
             floats(dirs, rows, LANES),
-            floats(rank, dirs),
+            floats(dirs, rank),
             floats(8, LANES),
-            jax.ShapeDtypeStruct((1,), jnp.int32),
+            TOKEN,
         ],
         [
             pltpu.VMEM((dirs, rows, LANES), jnp.float32),
@@ -294,7 +301,7 @@
             pltpu.VMEM((dirs, 8, LANES), jnp.float32),
             pltpu.SemaphoreType.DMA((PIECES,)),
         ],
-        24, 2 * rank * dirs * rows * LANES, first=VMEM, out_specs=[ANY, VMEM, VMEM, SMEM],
+        24, 2 * rank * dirs * rows * LANES, out_specs=[ANY, VMEM, VMEM, SMEM],
     )
 
 
@@ -364,50 +371,65 @@
     return [(target, source) for source, target in pairs]
 
 
-def call(kernel, name, ins, outs, scratch=(), limit=16, work=0, specs=None, out_specs=None, first=SMEM):
-    moved = sum(x.size * 4 for x in ins[1:]) + sum(o.size * 4 for o in outs)
+def call(kernel, name, ins, outs, scratch=(), limit=16, work=0, specs=None, out_specs=None, aliases=None):
+    moved = sum(x.size * 4 for x in ins) + sum(o.size * 4 for o in outs)
     return pl.pallas_call(
         kernel,
-        in_specs=[first] + (specs or [VMEM] * (len(ins) - 1)),
+        in_specs=specs or [VMEM] * len(ins),
         out_specs=out_specs or [VMEM] * len(outs),
         out_shape=outs,
         scratch_shapes=list(scratch),
+        input_output_aliases=aliases or {},
         compiler_params=pltpu.CompilerParams(vmem_limit_bytes=limit << 20),
         cost_estimate=cost(VECTOR * work, moved),
         name=name,
     )(*ins)
 
 
-def cut_kernel(height, group, listed, where_ref, *refs):
-    lists, fields = refs[:listed], refs[listed:-3]
-    own_ref, other_ref, sems = refs[-3:]
-    b = where_ref[1]
+def row_parts(width, height):
+    b = place()[1]
+    return [pl.multiple_of(part * (width - height), 16) for part in (b, 1 - b)]
+
+
+def cut_flows_kernel(*refs):
+    fields, outs, sems = refs[:-3], refs[-3:-1], refs[-1]
+    planes, width, _ = fields[0].shape
+    height = outs[0].shape[1]
     moves = []
-
-    def move(source, target):
-        moves.append(pltpu.make_async_copy(source, target, sems.at[len(moves)]))
-        moves[-1].start()
-
-    k = 0
-    for field in fields:
-        start = pl.multiple_of(b * (field.shape[-2] - height), 16)
-        rest = pl.multiple_of((1 - b) * (field.shape[-2] - height), 16)
-        for d in group:
-            for p in range(field.shape[-3]):
-                at = (p,) if len(field.shape) == 3 else (d, p)
-                for ref, low in ((own_ref, start), (other_ref, rest)):
-                    move(field.at[(*at, pl.ds(low, height))], ref.at[pl.ds(k, height)])
-                k += height
-    for entries in lists:
-        rows = entries.shape[0]
-        for ref in (own_ref, other_ref):
-            ref[k : k + rows, :] = entries[...].astype(jnp.float32)
-        k += rows
-    for m in moves:
-        m.wait()
-
-
-def pack_kernel(planes, where_ref, own_ref, other_ref, up_ref, down_ref):
+    for k, field in enumerate(fields):
+        for out, low in zip(outs, row_parts(width, height)):
+            source, target = field.at[:, pl.ds(low, height)], out.at[pl.ds(k * planes, planes)]
+            moves.append(pltpu.make_async_copy(source, target, sems.at[len(moves)]))
+            moves[-1].start()
+    for move in moves:
+        move.wait()
+
+
+def cut_groups_kernel(height, token_ref, cells_ref, weights_ref, dirs_hbm, *refs):
+    outs, after_ref, sems = refs[:-2], refs[-2], refs[-1]
+    after_ref[0] = 0
+    dirs, planes, width, _ = dirs_hbm.shape
+    each = 2 * dirs // len(outs)
+    lows = row_parts(width, height)
+    moves = []
+    for d in range(dirs):
+        for p in range(planes):
+            at = pl.ds((d % each * planes + p) * height, height)
+            for side, low in enumerate(lows):
+                source = dirs_hbm.at[d, p, pl.ds(low, height)]
+                target = outs[2 * (d // each) + side].at[at]
+                moves.append(pltpu.make_async_copy(source, target, sems.at[len(moves)]))
+                moves[-1].start()
+    low, lines = each * planes * height, cells_ref.shape[0]
+    for out in outs[:2]:
+        out[low : low + lines, :] = cells_ref[...].astype(jnp.float32)
+        out[low + lines : low + 2 * lines, :] = weights_ref[...]
+    for move in moves:
+        move.wait()
+
+
+def pack_kernel(planes, held, token_ref, own_ref, other_ref, *refs):
+    up_ref, down_ref = refs[held : held + 2]
     count, reach, height, _ = up_ref.shape
     skip = 2 * planes - reach
 
@@ -415,26 +437,27 @@
         for d in range(count):
             for p in range(2 * planes):
                 ref = first if p < planes else second
-                at = (d * planes + p % planes) * height
-                value = ref[at : at + height, :]
+                k = d * planes + p % planes
+                value = ref[k] if len(ref.shape) == 3 else ref[k * height : (k + 1) * height, :]
                 if p >= skip:
                     up_ref[d, p - skip] = value
                 if p < reach:
                     down_ref[d, p] = value
 
-    @pl.when(where_ref[0] == 0)
+    a = place()[0]
+
+    @pl.when(a == 0)
     def _():
         join(own_ref, other_ref)
 
-    @pl.when(where_ref[0] == 1)
+    @pl.when(a == 1)
     def _():
         join(other_ref, own_ref)
 
 
-def sensor_kernel(width, skip, where_ref, own_ref, other_ref, out_ref, where_out):
-    for k in range(where_ref.shape[0]):
-        where_out[k] = where_ref[k]
-    a = where_ref[0]
+def sensor_kernel(width, skip, own_ref, other_ref, out_ref, after_ref):
+    after_ref[0] = 0
+    a = place()[0]
     _, planes, height, _ = out_ref.shape
     first = a * (width - height)
     count = (own_ref.shape[0] - skip) // 2
@@ -472,32 +495,27 @@
         out_ref[at] = total.reshape(planes, height, LANES)
 
 
-def solve_kernel(adjoint, width, where_ref, *refs):
-    flow_parts, value_parts = refs[0:4], refs[4:8]
-    if adjoint:
-        outs, (flow, coef, rhs, start, ping, pong, sems) = refs[8:10], refs[10:]
-    else:
-        weight_ref, outs, (flow, coef, rhs, start, ping, pong, sems) = refs[8], refs[9:11], refs[11:]
-    dirs, depth, height, _ = rhs.shape
-    reach = REACH
+def arrivals(parts, into, sems):
+    up, down, lo, hi = parts
+    reach, depth = REACH, into.shape[1]
     own = depth - 2 * reach
+    moves = (
+        (lo, into.at[:, 0:reach]),
+        (down, into.at[:, reach : 2 * reach]),
+        (up.at[:, 2 * reach - own : reach], into.at[:, 2 * reach : reach + own]),
+        (hi, into.at[:, reach + own : depth]),
+    )
+    return [pltpu.make_async_copy(s, t, sems.at[k]) for k, (s, t) in enumerate(moves)]
+
+
+def coefficient_kernel(code_ref, *refs):
+    parts, (ahead, behind, inverse_out, flow, sems) = refs[:4], refs[4:]
+    _, depth, height, _ = flow.shape
     chunks = height // 8
-    a, at_bottom, at_top = where_ref[0], where_ref[2], where_ref[3]
-    code = [where_ref[4 + k] for k in range(4)]
-
-    def arrivals(parts, into, first):
-        up, down, lo, hi = parts
-        moves = (
-            (lo, into.at[:, 0:reach]),
-            (down, into.at[:, reach : 2 * reach]),
-            (up.at[:, 2 * reach - own : reach], into.at[:, 2 * reach : reach + own]),
-            (hi, into.at[:, reach + own : depth]),
-        )
-        return [pltpu.make_async_copy(s, t, sems.at[first + k]) for k, (s, t) in enumerate(moves)]
-
-    flow_moves = arrivals(flow_parts, flow, 0)
-    value_moves = arrivals(value_parts, start, 4)
-    for move in flow_moves + value_moves:
+    own = depth - 2 * REACH
+    a, _, at_bottom, at_top = place()
+    moves = arrivals(parts, flow, sems)
+    for move in moves:
         move.start()
 
     shape = (8, LANES)
@@ -505,8 +523,7 @@
     lane = lax.broadcasted_iota(jnp.int32, shape, 1)
     top_sub, bottom_sub = sub == 7, sub == 0
     last_lane, first_lane = lane == LANES - 1, lane == 0
-    zero = jnp.zeros(shape, jnp.float32)
-    opened = [jnp.where(c == 0, 1.0, 0.0).astype(jnp.float32) for c in code]
+    opened = [jnp.where(code_ref[k] == 0, 1.0, 0.0).astype(jnp.float32) for k in range(4)]
     low_one = jnp.where(bottom_sub & (a == 0), opened[0], 1.0)
     high_one = jnp.where(top_sub & (a == 1), opened[1], 1.0)
     low_two = jnp.where(first_lane, opened[2], 1.0)
@@ -516,10 +533,10 @@
         positive = DIFFUSION + jnp.maximum(x, 0.0)
         return positive, positive - x
 
-    def coefficients(p, carry):
-        outside = ((p < reach) & (at_bottom == 1)) | ((p >= reach + own) & (at_top == 1))
+    def at_plane(p, carry):
+        outside = ((p < REACH) & at_bottom) | ((p >= REACH + own) & at_top)
         inside = jnp.where(outside, 0.0, 1.0)
-        turned = zero
+        turned = jnp.zeros(shape, jnp.float32)
         for r in range(chunks):
             here = slice(r * 8, r * 8 + 8)
             one, two, three = flow[0, p, here, :], flow[1, p, here, :], flow[2, p, here, :]
@@ -534,21 +551,41 @@
             diagonal = (1.0 + first) + (second + high_two * up[1][0])
             diagonal = diagonal + (low_two * down[1][1] + (up[2][0] + down[2][1]))
             inverse = inside / diagonal
-            which = 0 if adjoint else 1
-            coef[0, p, here, :] = up[0][which] * inverse
-            coef[1, p, here, :] = down[0][1 - which] * inverse
-            coef[2, p, here, :] = jnp.where(last_lane, 0.0, up[1][which] * inverse)
-            coef[3, p, here, :] = jnp.where(first_lane, 0.0, down[1][1 - which] * inverse)
-            coef[4, p, here, :] = up[2][which] * inverse
-            coef[5, p, here, :] = down[2][1 - which] * inverse
-            coef[6, p, here, :] = inverse
+            right, left = jnp.where(last_lane, 0.0, inverse), jnp.where(first_lane, 0.0, inverse)
+            for out, w in ((ahead, 1), (behind, 0)):
+                out[0, p, here, :] = up[0][w] * inverse
+                out[1, p, here, :] = down[0][1 - w] * inverse
+                out[2, p, here, :] = up[1][w] * right
+                out[3, p, here, :] = down[1][1 - w] * left
+                out[4, p, here, :] = up[2][w] * inverse
+                out[5, p, here, :] = down[2][1 - w] * inverse
+            inverse_out[p, here, :] = inverse
         return carry
 
-    for move in flow_moves:
+    for move in moves:
         move.wait()
-    lax.fori_loop(1, depth - 1, coefficients, 0, unroll=2)
-    for move in value_moves:
-        move.wait()
+    lax.fori_loop(1, depth - 1, at_plane, 0, unroll=2)
+
+
+def solve_kernel(adjoint, coef, inverse_ref, *refs):
+    value_parts = refs[0:4]
+    if adjoint:
+        outs, (rhs, start, ping, pong, sems) = refs[4:6], refs[6:]
+    else:
+        weight_ref, outs, (rhs, start, ping, pong, sems) = refs[4], refs[5:7], refs[7:]
+    dirs, depth, height, _ = rhs.shape
+    reach = REACH
+    own = depth - 2 * reach
+    chunks = height // 8
+    a = place()[0]
+    moves = arrivals(value_parts, start, sems)
+    for move in moves:
+        move.start()
+
+    shape = (8, LANES)
+    sub = lax.broadcasted_iota(jnp.int32, shape, 0)
+    top_sub, bottom_sub = sub == 7, sub == 0
+    zero = jnp.zeros(shape, jnp.float32)
 
     def sweep(source, lead, low, planes, offset, count, store):
         def rows(r):
@@ -567,7 +604,8 @@
                     outer = pltpu.roll(source[d, p + q, pl.ds(at, 8), :], 1, 0)
                     before[q, d] = jnp.where(a == 0, 0.0, outer)
             for r in range(count):
-                c = [[coef[m, p + q, rows(r), :] for m in range(7 if lead else 6)] for q in range(2)]
+                c = [[coef[m, p + q, rows(r), :] for m in range(6)] for q in range(2)]
+                inverse = [inverse_ref[p + q, rows(r), :] for q in range(2)] if lead else None
                 plane = {d: [source[d, p - 1, rows(r), :], value[0, d], value[1, d], source[d, p + 2, rows(r), :]] for d in range(dirs)}
                 for q, d in each:
                     here = value[q, d]
@@ -581,7 +619,7 @@
                     else:
                         following, next_up, next_down = zero, zero, zero
                     if lead:
-                        total = here * c[q][6]
+                        total = here * inverse[q]
                         rhs[d, p + q, rows(r), :] = total
                     else:
                         total = rhs[d, p + q, rows(r), :]
@@ -610,7 +648,12 @@
     def full(source, lead, step, store):
         sweep(source, lead, 1 + step, depth - 2 - 2 * step, 0, chunks, store)
 
-    full(start, True, 0, into(ping))
+    low = 1
+    for move, present in zip(moves, (reach, 2 * reach, reach + own, depth)):
+        move.wait()
+        ready = (present - 1 - low) // 2 * 2
+        sweep(start, True, low, ready, 0, chunks, into(ping))
+        low += ready
     full(ping, False, 1, into(pong))
     full(pong, False, 2, again)
     full(start, True, 3, into(ping))
@@ -644,23 +687,24 @@
             sweep(pong, False, reach + low, high - low, 0, chunks, emit(kinds))
 
 
-def solves(adjoint, width, where, planes, flows, values, weight=None):
+def solves(adjoint, planes, coefficients, values, weight=None):
     dirs, reach, height, _ = values[0].shape
     depth = 2 * planes + 2 * reach
-    ins = [where, *flows, *values]
-    specs = [ANY] * 8
+    ahead, behind, inverse = coefficients
+    ins = [behind if adjoint else ahead, inverse, *values]
+    specs = [VMEM] * 2 + [ANY] * 4
     if adjoint:
         outs = [floats(dirs, planes, height - SPARE, LANES)] * 2
     else:
         ins.append(weight)
         specs.append(VMEM)
         outs = [floats(*values[0].shape)] * 2
-    scratch = [pltpu.VMEM((n, depth, height, LANES), jnp.float32) for n in (3, 7) + (dirs,) * 4]
-    scratch.append(pltpu.SemaphoreType.DMA((8,)))
+    scratch = [pltpu.VMEM((dirs, depth, height, LANES), jnp.float32)] * 4
     return call(
-        functools.partial(solve_kernel, adjoint, width),
+        functools.partial(solve_kernel, adjoint),
         "adjoint" if adjoint else "forward",
-        ins, outs, scratch, 36, 6 * 20 * dirs * depth * height * LANES, specs,
+        ins, outs, scratch + [pltpu.SemaphoreType.DMA((4,))],
+        28, 6 * 16 * dirs * depth * height * LANES, specs,
     )
 
 
@@ -678,51 +722,62 @@
     rank = eigen_basis.shape[0]
     count = lax.axis_size("slab")
     height = width // 2 + SPARE
+    depth = 2 * planes + 2 * REACH
     own, other, above = quad(count)
-    me = lax.axis_index("slab")
-    a, b = me // 2 % 2, me % 2
-    place = [a, b, (me - 2 * a == 0), (me + 2 * (1 - a) == count - 1)]
-    where = jnp.concatenate([jnp.stack([x.astype(jnp.int32) for x in place]), face_codes])
     each = dirs // GROUPS
+    block = planes * height
 
     def regroup(first, second):
         return lax.ppermute(first, "slab", own), lax.ppermute(second, "slab", other)
 
-    def cut(scalars, fields, group, lists=()):
-        parts = len(fields) * len(group)
-        extra = sum(x.shape[0] for x in lists)
-        outs = [floats(parts * planes * height + extra, LANES)] * 2
-        scratch = [pltpu.SemaphoreType.DMA((2 * parts * planes,))]
-        kernel = functools.partial(cut_kernel, height, group, len(lists))
-        specs = [VMEM] * len(lists) + [ANY] * len(fields)
-        return call(kernel, "cut", [scalars, *lists, *fields], outs, scratch, 54, 0, specs)
-
     def beyond(up, down):
         return up, down, lax.ppermute(up, "slab", above), lax.ppermute(down, "slab", back(above))
 
-    def pack(scalars, pair, parts):
-        outs = [floats(parts, REACH, height, LANES)] * 2
-        return call(functools.partial(pack_kernel, planes), "pack", [scalars, *pair], outs)
-
+    def pack(token, pair, parts, held=()):
+        outs = [floats(parts, REACH, height, LANES)] * 2 + [floats(*h.shape) for h in held]
+        n = len(held)
+        found = call(
+            functools.partial(pack_kernel, planes, n), "pack", [token, *pair, *held], outs,
+            specs=[SMEM, VMEM, VMEM] + [ANY] * n, out_specs=[VMEM] * 2 + [ANY] * n,
+            aliases={3 + k: 2 + k for k in range(n)},
+        )
+        return found[:2], found[2:]
+
+    fields = [flow_first, flow_second, flow_depth]
+    flows = regroup(*call(
+        cut_flows_kernel, "cut", fields, [floats(len(fields) * planes, height, LANES)] * 2,
+        [pltpu.SemaphoreType.DMA((2 * len(fields),))], 54, 0, [ANY] * len(fields),
+    ))
+    basis = eigen_basis.reshape(rank, planes * width, LANES)
+    tile, token = gram_tile(basis)
     sensors = [x.reshape(-1, LANES) for x in (sensor_cells, sensor_weight)]
     listed = 2 * sensors[0].shape[0]
-    block = planes * height
-    basis = eigen_basis.reshape(rank, planes * width, LANES)
-    flows = regroup(*cut(where, [flow_first, flow_second, flow_depth], [0]))
-    tile, later = gram_tile(where, basis)
-    moved = [regroup(*cut(later, [directions], range(each), sensors))]
-    for k in range(each, dirs, each):
-        moved.append(regroup(*cut(later, [directions], range(k, k + each))))
-    flows = beyond(*pack(later, flows, 3))
-    weight, last = call(
-        functools.partial(sensor_kernel, width, each * block), "sensors", [later, *moved[0]],
-        [floats(2, planes, height, LANES), jax.ShapeDtypeStruct(where.shape, where.dtype)],
-        work=planes * height * listed * 20, out_specs=[VMEM, SMEM],
-    )
-    scalars = [later] + [last] * (GROUPS - 1)
-    values = [beyond(*pack(s, m, each)) for s, m in zip(scalars, moved)]
-    forcing = [beyond(*solves(False, width, where, planes, flows, v, weight)) for v in values]
-    summed = [solves(True, width, where, planes, flows, f) for f in forcing]
+    lines = [each * block + (listed if k == 0 else 0) for k in range(GROUPS)]
+    *cuts, token = call(
+        functools.partial(cut_groups_kernel, height), "cut", [token, *sensors, directions],
+        [floats(n, LANES) for n in lines for _ in range(2)] + [TOKEN],
+        [pltpu.SemaphoreType.DMA((2 * dirs * planes,))], 54, 0, [SMEM, VMEM, VMEM, ANY],
+        [VMEM] * (2 * GROUPS) + [SMEM],
+    )
+    moved = [regroup(*cuts[:2])]
+    flows, cuts = pack(token, flows, len(fields), cuts[2:])
+    flows = beyond(*flows)
+    moved += [regroup(*cuts[k : k + 2]) for k in range(0, len(cuts), 2)]
+    weight, later = call(
+        functools.partial(sensor_kernel, width, each * block), "sensors", [*moved[0]],
+        [floats(2, planes, height, LANES), TOKEN],
+        work=block * listed * 20, out_specs=[VMEM, SMEM],
+    )
+    tokens = [token] + [later] * (GROUPS - 1)
+    values = [beyond(*pack(t, m, each)[0]) for t, m in zip(tokens, moved)]
+    coefficients = call(
+        coefficient_kernel, "coefficients", [face_codes, *flows],
+        [floats(6, depth, height, LANES)] * 2 + [floats(depth, height, LANES)],
+        [pltpu.VMEM((3, depth, height, LANES), jnp.float32), pltpu.SemaphoreType.DMA((4,))],
+        26, 80 * depth * height * LANES, [SMEM] + [ANY] * 4,
+    )
+    forcing = [beyond(*solves(False, planes, coefficients, v, weight)) for v in values]
+    summed = [solves(True, planes, coefficients, f) for f in forcing]
     returned = [
         (lax.ppermute(s[0], "slab", back(own)), lax.ppermute(s[1], "slab", back(other)))
         for s in summed
@@ -730,7 +785,7 @@
     images = []
     for k, halves in enumerate(returned):
         copies = count if k == GROUPS - 1 else 1
-        tile, image, basis = projections(where, basis, directions, k * each, halves, tile, copies)
+        tile, image, basis = projections(basis, directions, k * each, halves, tile, copies)
         images.append(image)
     cells = planes * count * width * LANES
     new, coeffs, scales, again = remainders(spread(tile, count), basis, images, cells)
@@ -739,7 +794,7 @@
         lambda state: (rescaled(state[0], scales, cells, count), jnp.int32(0)),
         (new, again[0]),
     )
-    return (new.reshape(directions.shape), coeffs)
+    return (new.reshape(directions.shape), coeffs.T)
 
 
 def solution(mesh):

time: 172 us -> 191 us (1.11)
  local copies, waits for them, and re-layouts: 2 us -> 17.5 us
  starting transfers between devices: 46.9 us -> 61.1 us
  Pallas kernels: 87.5 us -> 78.6 us
    unnamed x15 -> x24, local copies, waits for them, and re-layouts: 0.69 us -> 17.5 us
    ppermute x3, starting transfers between devices: 9.01 us -> 19.6 us  [regroup(): lax.ppermute(second, 'slab', other)]
    pallas_call x15, Pallas kernels: 87.5 us -> 78.6 us  [call(): pl.pallas_call(kernel, in_specs=specs or [VMEM] * len(ins), out_specs=out...]
    ppermute x5, starting transfers between devices: 18 us -> 22.4 us  [beyond(): lax.ppermute(up, 'slab', above)]
  transfers between devices with their start and end apart: 20 -> 20, of which waited for: 4 -> 4; matrix products, arithmetic and copies ran while one was open for 0% -> 0% of each run, Pallas kernels for 44% -> 35%
where the time goes in v5:
time: 191 us
  Pallas kernels  78.6 us (41%)
  starting transfers between devices  61.1 us (32%)
  waiting for transfers between devices  18.4 us (10%)
  local copies, waits for them, and re-layouts  17.5 us (9%)
  blocking collectives  13.1 us (7%)
    pallas_call x15, Pallas kernels, call(): pl.pallas_call(kernel, in_specs=specs or [VMEM] * len(ins), out_specs=out...  78.6 us
    ppermute x5, starting transfers between devices, beyond(): lax.ppermute(up, 'slab', above)  22.4 us
    ppermute x3, starting transfers between devices, regroup(): lax.ppermute(second, 'slab', other)  19.6 us
    unnamed x24, local copies, waits for them, and re-layouts  17.5 us
    all_to_all x1, blocking collectives, spread(): return lax.all_to_all(tile, 'slab', 0, 0, tiled=True) if count > 1 else tile  13.1 us
    ppermute x2, waiting for transfers between devices, body(): lax.ppermute(s[1], 'slab', back(other))  9.67 us
    ppermute x3, waiting for transfers between devices, regroup(): lax.ppermute(second, 'slab', other)  8.73 us
    ppermute x2, starting transfers between devices, body(): lax.ppermute(s[1], 'slab', back(other))  6.71 us
  transfers between devices with their start and end apart: 20, of which 4 were waited for; matrix products, arithmetic and copies ran while one was open for 0% of the time, Pallas kernels for 35%

profile of v5, /device:TPU:0, one launch (start us, length us, event | category | flops | bytes accessed | tf_op | source)
XLA Modules:
  0.0 190.6 jit_solution(1933653044937664527)
XLA Ops:
  8.2 8.2 %gram.1 = (f32[8,128]{1,0:T(8,128)}, s32[1]{0:T(128)}) custom-call(f32[16,1024,128]{2,1,0:T(8,128)} %bitcast.13), custom_call_target="tpu_custom_call" | custom-call | flops 5033164800 | bytes 8392708 | tf_op jit(solution)/shard_map/gram/pallas_call | solution.py:376
  16.5 4.8 %cut.2 = (f32[1216,128]{1,0:T(8,128)}, f32[1216,128]{1,0:T(8,128)}, f32[1152,128]{1,0:T(8,128)}, f32[1152,128]{1,0:T(8,128)}, s32[1]{0:T(128)}) custom-call(s32[1]{0:T(128)} %get-tuple-element.57.token_ref, s32[32,128]{1,0:T(8,128)} %bitcast.21, f32[32,128]{1,0:T(8,128)} %bitcast.22, f32[4,4,256,128]{3,2,1,0:T(8,128)} %dirs_hbm.1), custom_call_target="tpu_custom_call" | custom-call | bytes 4554760 | tf_op jit(solution)/shard_map/cut/pallas_call | solution.py:376
  21.3 6.7 %collective-permute-done.1.other_ref = f32[12,144,128]{2,1,0:T(8,128)S(1)} collective-permute-done((f32[12,144,128]{2,1,0:T(8,128)}, f32[12,144,128]{2,1,0:T(8,128)S(1)}, u32[]{:S(2)}, u32[]{:S(2)}) %collective-permute-start.1) | collective-permute-done | bytes 884768 | tf_op jit(solution)/shard_map/ppermute | solution.py:731
  33.6 4.3 %collective-permute-start.5 = (f32[1216,128]{1,0:T(8,128)S(1)}, f32[1216,128]{1,0:T(8,128)S(1)}, u32[]{:S(2)}, u32[]{:S(2)}) collective-permute-start(f32[1216,128]{1,0:T(8,128)S(1)} %copy-done.8), channel_id=1, source_target_pairs={{0,2},{1,0},{2,3},{3,1},{4,6},{5,4},{6,7},{7,5},{8,10},{9,8},{10,1... | collective-permute-start | bytes 1867784 | tf_op jit(solution)/shard_map/ppermute | solution.py:731
  39.7 12.1 %collective-permute-start.13 = (f32[1152,128]{1,0:T(8,128)}, f32[1152,128]{1,0:T(8,128)S(1)}, u32[]{:S(2)}, u32[]{:S(2)}) collective-permute-start(f32[1152,128]{1,0:T(8,128)} %get-tuple-element.81), channel_id=1, source_target_pairs={{0,2},{1,0},{2,3},{3,1},{4,6},{5,4},{6,7},{7,5},{8,10},{9,8},{10,1... | collective-permute-start | bytes 1769480 | tf_op jit(solution)/shard_map/ppermute | solution.py:731
  56.1 5.2 %sensors.1 = (f32[2,4,144,128]{3,2,1,0:T(8,128)S(1)}, s32[1]{0:T(128)}) custom-call(f32[1216,128]{1,0:T(8,128)S(1)} %collective-permute-done.4.own_ref, f32[1216,128]{1,0:T(8,128)S(1)} %collective-permute-done.5.other_ref), custom_call_target="tpu_custom_call" | custom-call | flops 110592000 | bytes 1835012 | tf_op jit(solution)/shard_map/sensors/pallas_call | solution.py:376
  63.5 8.4 %collective-permute-start.14 = (f32[2,6,144,128]{3,2,1,0:T(8,128)S(1)}, f32[2,6,144,128]{3,2,1,0:T(8,128)S(1)}, u32[]{:S(2)}, u32[]{:S(2)}) collective-permute-start(f32[2,6,144,128]{3,2,1,0:T(8,128)S(1)} %get-tuple-element.82.refs_0_), channel_id=1, source_target_pairs={{0,1},{1,4},{2,3},{3,6},{4,5},{5,8},{6,7},{7,10},{8,9},{9,12},{10,... | collective-permute-start | bytes 2654216 | tf_op jit(solution)/shard_map/ppermute | solution.py:734
  73.4 3.9 %coefficients.1 = (f32[6,20,144,128]{3,2,1,0:T(8,128)S(1)}, f32[6,20,144,128]{3,2,1,0:T(8,128)S(1)}, f32[20,144,128]{2,1,0:T(8,128)S(1)}) custom-call(s32[4]{0:T(128)S(1)} %copy-done.2, f32[3,6,144,128]{3,2,1,0:T(8,128)S(1)} %get-tuple-element.63.refs_0_, f32[3,6,144,128]{3,2,1,0:T(8,128)S(1)} %get-tuple-element.64.refs_1_, ...), custom_call_target="tpu_custom_call" | custom-call | flops 4423680000 | bytes 24477712 | tf_op jit(solution)/shard_map/coefficients/pallas_call | solution.py:376
  77.3 3.5 %copy-done.3 = f32[6,20,144,128]{3,2,1,0:T(8,128)} copy-done((f32[6,20,144,128]{3,2,1,0:T(8,128)}, f32[6,20,144,128]{3,2,1,0:T(8,128)S(1)}, u32[]{:S(2)}) %copy-start.3) | copy-done | bytes 8847384
  80.8 3.4 %copy-done.6 = f32[6,20,144,128]{3,2,1,0:T(8,128)} copy-done((f32[6,20,144,128]{3,2,1,0:T(8,128)}, f32[6,20,144,128]{3,2,1,0:T(8,128)S(1)}, u32[]{:S(2)}) %copy-start.6) | copy-done | bytes 8847384
  84.3 3.5 %copy-done.7 = f32[6,20,144,128]{3,2,1,0:T(8,128)S(1)} copy-done((f32[6,20,144,128]{3,2,1,0:T(8,128)S(1)}, f32[6,20,144,128]{3,2,1,0:T(8,128)}, u32[]{:S(2)}) %copy-start.7) | copy-done | bytes 8847384
  87.8 10.3 %forward.2 = (f32[2,6,144,128]{3,2,1,0:T(8,128)S(1)}, f32[2,6,144,128]{3,2,1,0:T(8,128)S(1)}) custom-call(f32[6,20,144,128]{3,2,1,0:T(8,128)S(1)} %copy-done.7, f32[20,144,128]{2,1,0:T(8,128)S(1)} %get-tuple-element.66.inverse_ref, f32[2,6,144,128]{3,2,1,0:T(8,128)S(1)} %get-tuple-element.70.refs_0_, f32[2,6,144,128]{3,2,1,0:T(8,128)S(1)} %get-tuple-element.71.refs_1_, ...), custom_call_target="tpu_custom_call" | custom-call | flops 10616832000 | bytes 16220160 | tf_op jit(solution)/shard_map/forward/pallas_call | solution.py:376
  98.1 4.3 %collective-permute-start.8 = (f32[2,6,144,128]{3,2,1,0:T(8,128)S(1)}, f32[2,6,144,128]{3,2,1,0:T(8,128)S(1)}, u32[]{:S(2)}, u32[]{:S(2)}) collective-permute-start(f32[2,6,144,128]{3,2,1,0:T(8,128)S(1)} %get-tuple-element.73.refs_0_), channel_id=1, source_target_pairs={{0,1},{1,4},{2,3},{3,6},{4,5},{5,8},{6,7},{7,10},{8,9},{9,12},{10,... | collective-permute-start | bytes 2654216 | tf_op jit(solution)/shard_map/ppermute | solution.py:734
  103.7 10.3 %forward.3 = (f32[2,6,144,128]{3,2,1,0:T(8,128)S(1)}, f32[2,6,144,128]{3,2,1,0:T(8,128)S(1)}) custom-call(f32[6,20,144,128]{3,2,1,0:T(8,128)S(1)} %copy-done.7, f32[20,144,128]{2,1,0:T(8,128)S(1)} %get-tuple-element.66.inverse_ref, f32[2,6,144,128]{3,2,1,0:T(8,128)S(1)} %get-tuple-element.82.refs_0_, f32[2,6,144,128]{3,2,1,0:T(8,128)S(1)} %get-tuple-element.83.refs_1_, ...), custom_call_target="tpu_custom_call" | custom-call | flops 10616832000 | bytes 16220160 | tf_op jit(solution)/shard_map/forward/pallas_call | solution.py:376
  114.0 5.3 %collective-permute-start.16 = (f32[2,6,144,128]{3,2,1,0:T(8,128)S(1)}, f32[2,6,144,128]{3,2,1,0:T(8,128)S(1)}, u32[]{:S(2)}, u32[]{:S(2)}) collective-permute-start(f32[2,6,144,128]{3,2,1,0:T(8,128)S(1)} %get-tuple-element.84.refs_0_), channel_id=1, source_target_pairs={{0,1},{1,4},{2,3},{3,6},{4,5},{5,8},{6,7},{7,10},{8,9},{9,12},{10,... | collective-permute-start | bytes 2654216 | tf_op jit(solution)/shard_map/ppermute | solution.py:734
  120.7 3.5 %copy-done.4 = f32[6,20,144,128]{3,2,1,0:T(8,128)S(1)} copy-done((f32[6,20,144,128]{3,2,1,0:T(8,128)S(1)}, f32[6,20,144,128]{3,2,1,0:T(8,128)}, u32[]{:S(2)}) %copy-start.4) | copy-done | bytes 8847384
  124.2 10.1 %adjoint.2 = (f32[2,4,128,128]{3,2,1,0:T(8,128)S(1)}, f32[2,4,128,128]{3,2,1,0:T(8,128)S(1)}) custom-call(f32[6,20,144,128]{3,2,1,0:T(8,128)S(1)} %copy-done.4, f32[20,144,128]{2,1,0:T(8,128)S(1)} %get-tuple-element.66.inverse_ref, f32[2,6,144,128]{3,2,1,0:T(8,128)S(1)} %get-tuple-element.73.refs_0_, f32[2,6,144,128]{3,2,1,0:T(8,128)S(1)} %get-tuple-element.74.refs_1_, ...), custom_call_target="tpu_custom_call" | custom-call | flops 10616832000 | bytes 14909440 | tf_op jit(solution)/shard_map/adjoint/pallas_call | solution.py:376
  135.0 3.6 %collective-permute-start.11 = (f32[2,4,128,128]{3,2,1,0:T(8,128)S(1)}, f32[2,4,128,128]{3,2,1,0:T(8,128)S(1)}, u32[]{:S(2)}, u32[]{:S(2)}) collective-permute-start(f32[2,4,128,128]{3,2,1,0:T(8,128)S(1)} %get-tuple-element.76), channel_id=1, source_target_pairs={{2,0},{0,1},{3,2},{1,3},{6,4},{4,5},{7,6},{5,7},{10,8},{8,9},{11,1... | collective-permute-start | bytes 1572872 | tf_op jit(solution)/shard_map/ppermute | solution.py:782
  138.6 3.5 %copy-done.5 = f32[6,20,144,128]{3,2,1,0:T(8,128)S(1)} copy-done((f32[6,20,144,128]{3,2,1,0:T(8,128)S(1)}, f32[6,20,144,128]{3,2,1,0:T(8,128)}, u32[]{:S(2)}) %copy-start.5) | copy-done | bytes 8847384
  142.1 10.1 %adjoint.3 = (f32[2,4,128,128]{3,2,1,0:T(8,128)S(1)}, f32[2,4,128,128]{3,2,1,0:T(8,128)S(1)}) custom-call(f32[6,20,144,128]{3,2,1,0:T(8,128)S(1)} %copy-done.5, f32[20,144,128]{2,1,0:T(8,128)S(1)} %get-tuple-element.66.inverse_ref, f32[2,6,144,128]{3,2,1,0:T(8,128)S(1)} %get-tuple-element.84.refs_0_, f32[2,6,144,128]{3,2,1,0:T(8,128)S(1)} %get-tuple-element.85.refs_1_, ...), custom_call_target="tpu_custom_call" | custom-call | flops 10616832000 | bytes 14909440 | tf_op jit(solution)/shard_map/adjoint/pallas_call | solution.py:376
  153.2 3.2 %collective-permute-start.19 = (f32[2,4,128,128]{3,2,1,0:T(8,128)S(1)}, f32[2,4,128,128]{3,2,1,0:T(8,128)S(1)}, u32[]{:S(2)}, u32[]{:S(2)}) collective-permute-start(f32[2,4,128,128]{3,2,1,0:T(8,128)S(1)} %get-tuple-element.87), channel_id=1, source_target_pairs={{2,0},{0,1},{3,2},{1,3},{6,4},{4,5},{7,6},{5,7},{10,8},{8,9},{11,1... | collective-permute-start | bytes 1572872 | tf_op jit(solution)/shard_map/ppermute | solution.py:782
  159.1 9.7 %collective-permute-done.19.other_hbm = f32[2,4,128,128]{3,2,1,0:T(8,128)S(1)} collective-permute-done((f32[2,4,128,128]{3,2,1,0:T(8,128)S(1)}, f32[2,4,128,128]{3,2,1,0:T(8,128)S(1)}, u32[]{:S(2)}, u32[]{:S(2)}) %collective-permute-start.19) | collective-permute-done | bytes 524320 | tf_op jit(solution)/shard_map/ppermute | solution.py:782
  170.7 13.1 %all_to_all.19 = f32[16,8,128]{2,1,0:T(8,128)S(1)} all-to-all(f32[16,8,128]{2,1,0:T(8,128)S(1)} %bitcast.19), channel_id=1, replica_groups=mesh['grp'=2,'slab'=16] {'slab'}, dimensions={0} | all-to-all | bytes 131072 | tf_op jit(solution)/shard_map/all_to_all | solution.py:117
  183.8 6.0 %remainder.1 = (f32[4,1024,128]{2,1,0:T(8,128)}, f32[4,16]{1,0:T(4,128)}, f32[8,128]{1,0:T(8,128)S(1)}, s32[1]{0:T(128)}) custom-call(f32[128,128]{1,0:T(8,128)S(1)} %bitcast.18, f32[16,1024,128]{2,1,0:T(8,128)S(1)} %get-tuple-element.78.basis_in.basis_ref, f32[2,1024,128]{2,1,0:T(8,128)S(1)} %get-tuple-element.90.refs_0_, ...), custom_call_target="tpu_custom_call" | custom-call | flops 2516582400 | bytes 12652804 | tf_op jit(solution)/shard_map/remainder/pallas_call | solution.py:376
  (58 shorter events, 32.4 us)
Async XLA Ops:
  3.3 17.9 %collective-permute-start = (f32[12,144,128]{2,1,0:T(8,128)}, f32[12,144,128]{2,1,0:T(8,128)S(1)}, u32[]{:S(2)}, u32[]{:S(2)}) collective-permute-start(f32[12,144,128]{2,1,0:T(8,128)} %get-tuple-element.59), channel_id=1, source_target_pairs={{0,0},{1,2},{2,1},{3,3},{4,4},{5,6},{6,5},{7,7},{8,8},{9,10},{10,9... | collective-permute-start | bytes 2654216 | tf_op jit(solution)/shard_map/ppermute | solution.py:731
  5.2 22.8 %collective-permute-start.1 = (f32[12,144,128]{2,1,0:T(8,128)}, f32[12,144,128]{2,1,0:T(8,128)S(1)}, u32[]{:S(2)}, u32[]{:S(2)}) collective-permute-start(f32[12,144,128]{2,1,0:T(8,128)} %get-tuple-element.60), channel_id=1, source_target_pairs={{0,2},{1,0},{2,3},{3,1},{4,6},{5,4},{6,7},{7,5},{8,10},{9,8},{10,1... | collective-permute-start | bytes 2654216 | tf_op jit(solution)/shard_map/ppermute | solution.py:731
  28.8 44.6 %copy-start.2 = (s32[4]{0:T(128)S(1)}, s32[4]{0:T(128)}, u32[]{:S(2)}) copy-start(s32[4]{0:T(128)} %code_ref.1) | copy-start | bytes 52
  28.8 43.1 %collective-permute-start.2 = (f32[3,6,144,128]{3,2,1,0:T(8,128)S(1)}, f32[3,6,144,128]{3,2,1,0:T(8,128)S(1)}, u32[]{:S(2)}, u32[]{:S(2)}) collective-permute-start(f32[3,6,144,128]{3,2,1,0:T(8,128)S(1)} %get-tuple-element.63.refs_0_), channel_id=1, source_target_pairs={{0,1},{1,4},{2,3},{3,6},{4,5},{5,8},{6,7},{7,10},{8,9},{9,12},{10,... | collective-permute-start | bytes 3981320 | tf_op jit(solution)/shard_map/ppermute | solution.py:734
  31.6 41.8 %collective-permute-start.3 = (f32[3,6,144,128]{3,2,1,0:T(8,128)S(1)}, f32[3,6,144,128]{3,2,1,0:T(8,128)S(1)}, u32[]{:S(2)}, u32[]{:S(2)}) collective-permute-start(f32[3,6,144,128]{3,2,1,0:T(8,128)S(1)} %get-tuple-element.64.refs_1_), channel_id=1, source_target_pairs={{1,0},{4,1},{3,2},{6,3},{5,4},{8,5},{7,6},{10,7},{9,8},{12,9},{11,... | collective-permute-start | bytes 3981320 | tf_op jit(solution)/shard_map/ppermute | solution.py:734
  32.9 6.8 %collective-permute-start.4 = (f32[1216,128]{1,0:T(8,128)S(1)}, f32[1216,128]{1,0:T(8,128)S(1)}, u32[]{:S(2)}, u32[]{:S(2)}) collective-permute-start(f32[1216,128]{1,0:T(8,128)S(1)} %copy-done.9), channel_id=1, source_target_pairs={{0,0},{1,2},{2,1},{3,3},{4,4},{5,6},{6,5},{7,7},{8,8},{9,10},{10,9... | collective-permute-start | bytes 1867784 | tf_op jit(solution)/shard_map/ppermute | solution.py:731
  33.6 18.8 %collective-permute-start.5 = (f32[1216,128]{1,0:T(8,128)S(1)}, f32[1216,128]{1,0:T(8,128)S(1)}, u32[]{:S(2)}, u32[]{:S(2)}) collective-permute-start(f32[1216,128]{1,0:T(8,128)S(1)} %copy-done.8), channel_id=1, source_target_pairs={{0,2},{1,0},{2,3},{3,1},{4,6},{5,4},{6,7},{7,5},{8,10},{9,8},{10,1... | collective-permute-start | bytes 1867784 | tf_op jit(solution)/shard_map/ppermute | solution.py:731
  37.9 16.9 %collective-permute-start.12 = (f32[1152,128]{1,0:T(8,128)}, f32[1152,128]{1,0:T(8,128)S(1)}, u32[]{:S(2)}, u32[]{:S(2)}) collective-permute-start(f32[1152,128]{1,0:T(8,128)} %get-tuple-element.80), channel_id=1, source_target_pairs={{0,0},{1,2},{2,1},{3,3},{4,4},{5,6},{6,5},{7,7},{8,8},{9,10},{10,9... | collective-permute-start | bytes 1769480 | tf_op jit(solution)/shard_map/ppermute | solution.py:731
  39.7 23.1 %collective-permute-start.13 = (f32[1152,128]{1,0:T(8,128)}, f32[1152,128]{1,0:T(8,128)S(1)}, u32[]{:S(2)}, u32[]{:S(2)}) collective-permute-start(f32[1152,128]{1,0:T(8,128)} %get-tuple-element.81), channel_id=1, source_target_pairs={{0,2},{1,0},{2,3},{3,1},{4,6},{5,4},{6,7},{7,5},{8,10},{9,8},{10,1... | collective-permute-start | bytes 1769480 | tf_op jit(solution)/shard_map/ppermute | solution.py:731
  53.2 31.1 %collective-permute-start.6 = (f32[2,6,144,128]{3,2,1,0:T(8,128)S(1)}, f32[2,6,144,128]{3,2,1,0:T(8,128)S(1)}, u32[]{:S(2)}, u32[]{:S(2)}) collective-permute-start(f32[2,6,144,128]{3,2,1,0:T(8,128)S(1)} %get-tuple-element.70.refs_0_), channel_id=1, source_target_pairs={{0,1},{1,4},{2,3},{3,6},{4,5},{5,8},{6,7},{7,10},{8,9},{9,12},{10,... | collective-permute-start | bytes 2654216 | tf_op jit(solution)/shard_map/ppermute | solution.py:734
  54.8 29.4 %collective-permute-start.7 = (f32[2,6,144,128]{3,2,1,0:T(8,128)S(1)}, f32[2,6,144,128]{3,2,1,0:T(8,128)S(1)}, u32[]{:S(2)}, u32[]{:S(2)}) collective-permute-start(f32[2,6,144,128]{3,2,1,0:T(8,128)S(1)} %get-tuple-element.71.refs_1_), channel_id=1, source_target_pairs={{1,0},{4,1},{3,2},{6,3},{5,4},{8,5},{7,6},{10,7},{9,8},{12,9},{11,... | collective-permute-start | bytes 2654216 | tf_op jit(solution)/shard_map/ppermute | solution.py:734
  63.5 40.1 %collective-permute-start.14 = (f32[2,6,144,128]{3,2,1,0:T(8,128)S(1)}, f32[2,6,144,128]{3,2,1,0:T(8,128)S(1)}, u32[]{:S(2)}, u32[]{:S(2)}) collective-permute-start(f32[2,6,144,128]{3,2,1,0:T(8,128)S(1)} %get-tuple-element.82.refs_0_), channel_id=1, source_target_pairs={{0,1},{1,4},{2,3},{3,6},{4,5},{5,8},{6,7},{7,10},{8,9},{9,12},{10,... | collective-permute-start | bytes 2654216 | tf_op jit(solution)/shard_map/ppermute | solution.py:734
  71.9 31.7 %collective-permute-start.15 = (f32[2,6,144,128]{3,2,1,0:T(8,128)S(1)}, f32[2,6,144,128]{3,2,1,0:T(8,128)S(1)}, u32[]{:S(2)}, u32[]{:S(2)}) collective-permute-start(f32[2,6,144,128]{3,2,1,0:T(8,128)S(1)} %get-tuple-element.83.refs_1_), channel_id=1, source_target_pairs={{1,0},{4,1},{3,2},{6,3},{5,4},{8,5},{7,6},{10,7},{9,8},{12,9},{11,... | collective-permute-start | bytes 2654216 | tf_op jit(solution)/shard_map/ppermute | solution.py:734
  98.1 22.6 %collective-permute-start.8 = (f32[2,6,144,128]{3,2,1,0:T(8,128)S(1)}, f32[2,6,144,128]{3,2,1,0:T(8,128)S(1)}, u32[]{:S(2)}, u32[]{:S(2)}) collective-permute-start(f32[2,6,144,128]{3,2,1,0:T(8,128)S(1)} %get-tuple-element.73.refs_0_), channel_id=1, source_target_pairs={{0,1},{1,4},{2,3},{3,6},{4,5},{5,8},{6,7},{7,10},{8,9},{9,12},{10,... | collective-permute-start | bytes 2654216 | tf_op jit(solution)/shard_map/ppermute | solution.py:734
  102.4 18.3 %collective-permute-start.9 = (f32[2,6,144,128]{3,2,1,0:T(8,128)S(1)}, f32[2,6,144,128]{3,2,1,0:T(8,128)S(1)}, u32[]{:S(2)}, u32[]{:S(2)}) collective-permute-start(f32[2,6,144,128]{3,2,1,0:T(8,128)S(1)} %get-tuple-element.74.refs_1_), channel_id=1, source_target_pairs={{1,0},{4,1},{3,2},{6,3},{5,4},{8,5},{7,6},{10,7},{9,8},{12,9},{11,... | collective-permute-start | bytes 2654216 | tf_op jit(solution)/shard_map/ppermute | solution.py:734
  114.0 24.6 %collective-permute-start.16 = (f32[2,6,144,128]{3,2,1,0:T(8,128)S(1)}, f32[2,6,144,128]{3,2,1,0:T(8,128)S(1)}, u32[]{:S(2)}, u32[]{:S(2)}) collective-permute-start(f32[2,6,144,128]{3,2,1,0:T(8,128)S(1)} %get-tuple-element.84.refs_0_), channel_id=1, source_target_pairs={{0,1},{1,4},{2,3},{3,6},{4,5},{5,8},{6,7},{7,10},{8,9},{9,12},{10,... | collective-permute-start | bytes 2654216 | tf_op jit(solution)/shard_map/ppermute | solution.py:734
  119.3 19.3 %collective-permute-start.17 = (f32[2,6,144,128]{3,2,1,0:T(8,128)S(1)}, f32[2,6,144,128]{3,2,1,0:T(8,128)S(1)}, u32[]{:S(2)}, u32[]{:S(2)}) collective-permute-start(f32[2,6,144,128]{3,2,1,0:T(8,128)S(1)} %get-tuple-element.85.refs_1_), channel_id=1, source_target_pairs={{1,0},{4,1},{3,2},{6,3},{5,4},{8,5},{7,6},{10,7},{9,8},{12,9},{11,... | collective-permute-start | bytes 2654216 | tf_op jit(solution)/shard_map/ppermute | solution.py:734
  134.3 22.0 %collective-permute-start.10 = (f32[2,4,128,128]{3,2,1,0:T(8,128)S(1)}, f32[2,4,128,128]{3,2,1,0:T(8,128)S(1)}, u32[]{:S(2)}, u32[]{:S(2)}) collective-permute-start(f32[2,4,128,128]{3,2,1,0:T(8,128)S(1)} %get-tuple-element.75), channel_id=1, source_target_pairs={{0,0},{2,1},{1,2},{3,3},{4,4},{6,5},{5,6},{7,7},{8,8},{10,9},{9,10... | collective-permute-start | bytes 1572872 | tf_op jit(solution)/shard_map/ppermute | solution.py:782
  135.0 21.3 %slice-start = ((s8[8388608]{0:T(1024)(128)(4,1)}), s8[4194304]{0:T(1024)(128)(4,1)S(1)}, s32[]{:S(2)}) async-start(s8[8388608]{0:T(1024)(128)(4,1)} %bitcast.14), calls=%async_computation.2 | async-start | bytes 8388608
  135.0 21.3 %copy-start = (f32[4,4,256,128]{3,2,1,0:T(8,128)S(1)}, f32[4,4,256,128]{3,2,1,0:T(8,128)}, u32[]{:S(2)}) copy-start(f32[4,4,256,128]{3,2,1,0:T(8,128)} %dirs_hbm.1) | copy-start | bytes 6291460
  135.0 21.3 %slice-start.1 = ((s8[8388608]{0:T(1024)(128)(4,1)}), s8[4194304]{0:T(1024)(128)(4,1)S(1)}, s32[]{:S(2)}) async-start(s8[8388608]{0:T(1024)(128)(4,1)} %bitcast.14), calls=%async_computation.3 | async-start | bytes 8388608
  135.0 21.3 %collective-permute-start.11 = (f32[2,4,128,128]{3,2,1,0:T(8,128)S(1)}, f32[2,4,128,128]{3,2,1,0:T(8,128)S(1)}, u32[]{:S(2)}, u32[]{:S(2)}) collective-permute-start(f32[2,4,128,128]{3,2,1,0:T(8,128)S(1)} %get-tuple-element.76), channel_id=1, source_target_pairs={{2,0},{0,1},{3,2},{1,3},{6,4},{4,5},{7,6},{5,7},{10,8},{8,9},{11,1... | collective-permute-start | bytes 1572872 | tf_op jit(solution)/shard_map/ppermute | solution.py:782
  152.2 6.8 %collective-permute-start.18 = (f32[2,4,128,128]{3,2,1,0:T(8,128)S(1)}, f32[2,4,128,128]{3,2,1,0:T(8,128)S(1)}, u32[]{:S(2)}, u32[]{:S(2)}) collective-permute-start(f32[2,4,128,128]{3,2,1,0:T(8,128)S(1)} %get-tuple-element.86), channel_id=1, source_target_pairs={{0,0},{2,1},{1,2},{3,3},{4,4},{6,5},{5,6},{7,7},{8,8},{10,9},{9,10... | collective-permute-start | bytes 1572872 | tf_op jit(solution)/shard_map/ppermute | solution.py:782
  153.2 15.6 %collective-permute-start.19 = (f32[2,4,128,128]{3,2,1,0:T(8,128)S(1)}, f32[2,4,128,128]{3,2,1,0:T(8,128)S(1)}, u32[]{:S(2)}, u32[]{:S(2)}) collective-permute-start(f32[2,4,128,128]{3,2,1,0:T(8,128)S(1)} %get-tuple-element.87), channel_id=1, source_target_pairs={{2,0},{0,1},{3,2},{1,3},{6,4},{4,5},{7,6},{5,7},{10,8},{8,9},{11,1... | collective-permute-start | bytes 1572872 | tf_op jit(solution)/shard_map/ppermute | solution.py:782
  (8 other events, 62.8 us)

commit v6 on v5

--- a/solution.py
+++ b/solution.py
@@ -371,7 +371,7 @@
     return [(target, source) for source, target in pairs]
 
 
-def call(kernel, name, ins, outs, scratch=(), limit=16, work=0, specs=None, out_specs=None, aliases=None):
+def call(kernel, name, ins, outs, scratch=(), limit=16, work=0, specs=None, out_specs=None):
     moved = sum(x.size * 4 for x in ins) + sum(o.size * 4 for o in outs)
     return pl.pallas_call(
         kernel,
@@ -379,7 +379,6 @@
         out_specs=out_specs or [VMEM] * len(outs),
         out_shape=outs,
         scratch_shapes=list(scratch),
-        input_output_aliases=aliases or {},
         compiler_params=pltpu.CompilerParams(vmem_limit_bytes=limit << 20),
         cost_estimate=cost(VECTOR * work, moved),
         name=name,
@@ -405,31 +404,29 @@
         move.wait()
 
 
-def cut_groups_kernel(height, token_ref, cells_ref, weights_ref, dirs_hbm, *refs):
-    outs, after_ref, sems = refs[:-2], refs[-2], refs[-1]
+def cut_group_kernel(height, group, token_ref, *refs):
+    sensors, (dirs_hbm, *outs, after_ref, sems) = refs[:-5], refs[-5:]
     after_ref[0] = 0
-    dirs, planes, width, _ = dirs_hbm.shape
-    each = 2 * dirs // len(outs)
+    _, planes, width, _ = dirs_hbm.shape
+    moves, k = [], 0
     lows = row_parts(width, height)
-    moves = []
-    for d in range(dirs):
+    for d in group:
         for p in range(planes):
-            at = pl.ds((d % each * planes + p) * height, height)
-            for side, low in enumerate(lows):
-                source = dirs_hbm.at[d, p, pl.ds(low, height)]
-                target = outs[2 * (d // each) + side].at[at]
+            for out, low in zip(outs, lows):
+                source, target = dirs_hbm.at[d, p, pl.ds(low, height)], out.at[pl.ds(k, height)]
                 moves.append(pltpu.make_async_copy(source, target, sems.at[len(moves)]))
                 moves[-1].start()
-    low, lines = each * planes * height, cells_ref.shape[0]
-    for out in outs[:2]:
-        out[low : low + lines, :] = cells_ref[...].astype(jnp.float32)
-        out[low + lines : low + 2 * lines, :] = weights_ref[...]
+            k += height
+    for ref in sensors:
+        lines = ref.shape[0]
+        for out in outs:
+            out[k : k + lines, :] = ref[...].astype(jnp.float32)
+        k += lines
     for move in moves:
         move.wait()
 
 
-def pack_kernel(planes, held, token_ref, own_ref, other_ref, *refs):
-    up_ref, down_ref = refs[held : held + 2]
+def pack_kernel(planes, token_ref, own_ref, other_ref, up_ref, down_ref):
     count, reach, height, _ = up_ref.shape
     skip = 2 * planes - reach
 
@@ -508,16 +505,11 @@
     return [pltpu.make_async_copy(s, t, sems.at[k]) for k, (s, t) in enumerate(moves)]
 
 
-def coefficient_kernel(code_ref, *refs):
-    parts, (ahead, behind, inverse_out, flow, sems) = refs[:4], refs[4:]
+def coefficients(adjoint, code_ref, flow, coef):
     _, depth, height, _ = flow.shape
     chunks = height // 8
     own = depth - 2 * REACH
     a, _, at_bottom, at_top = place()
-    moves = arrivals(parts, flow, sems)
-    for move in moves:
-        move.start()
-
     shape = (8, LANES)
     sub = lax.broadcasted_iota(jnp.int32, shape, 0)
     lane = lax.broadcasted_iota(jnp.int32, shape, 1)
@@ -551,36 +543,36 @@
             diagonal = (1.0 + first) + (second + high_two * up[1][0])
             diagonal = diagonal + (low_two * down[1][1] + (up[2][0] + down[2][1]))
             inverse = inside / diagonal
-            right, left = jnp.where(last_lane, 0.0, inverse), jnp.where(first_lane, 0.0, inverse)
-            for out, w in ((ahead, 1), (behind, 0)):
-                out[0, p, here, :] = up[0][w] * inverse
-                out[1, p, here, :] = down[0][1 - w] * inverse
-                out[2, p, here, :] = up[1][w] * right
-                out[3, p, here, :] = down[1][1 - w] * left
-                out[4, p, here, :] = up[2][w] * inverse
-                out[5, p, here, :] = down[2][1 - w] * inverse
-            inverse_out[p, here, :] = inverse
+            which = 0 if adjoint else 1
+            coef[0, p, here, :] = up[0][which] * inverse
+            coef[1, p, here, :] = down[0][1 - which] * inverse
+            coef[2, p, here, :] = jnp.where(last_lane, 0.0, up[1][which] * inverse)
+            coef[3, p, here, :] = jnp.where(first_lane, 0.0, down[1][1 - which] * inverse)
+            coef[4, p, here, :] = up[2][which] * inverse
+            coef[5, p, here, :] = down[2][1 - which] * inverse
+            coef[6, p, here, :] = inverse
         return carry
 
-    for move in moves:
-        move.wait()
     lax.fori_loop(1, depth - 1, at_plane, 0, unroll=2)
 
 
-def solve_kernel(adjoint, coef, inverse_ref, *refs):
-    value_parts = refs[0:4]
-    if adjoint:
-        outs, (rhs, start, ping, pong, sems) = refs[4:6], refs[6:]
-    else:
-        weight_ref, outs, (rhs, start, ping, pong, sems) = refs[4], refs[5:7], refs[7:]
+def solve_kernel(adjoint, code_ref, *refs):
+    weight_ref = None if adjoint else refs[8]
+    refs = refs[:8] + refs[8 if adjoint else 9 :]
+    flow_parts, value_parts, outs = refs[0:4], refs[4:8], refs[8:10]
+    flow, coef, rhs, start, ping, pong, flow_sems, sems = refs[10:]
     dirs, depth, height, _ = rhs.shape
     reach = REACH
     own = depth - 2 * reach
     chunks = height // 8
     a = place()[0]
+    flow_moves = arrivals(flow_parts, flow, flow_sems)
     moves = arrivals(value_parts, start, sems)
-    for move in moves:
+    for move in flow_moves + moves:
         move.start()
+    for move in flow_moves:
+        move.wait()
+    coefficients(adjoint, code_ref, flow, coef)
 
     shape = (8, LANES)
     sub = lax.broadcasted_iota(jnp.int32, shape, 0)
@@ -605,7 +597,7 @@
                     before[q, d] = jnp.where(a == 0, 0.0, outer)
             for r in range(count):
                 c = [[coef[m, p + q, rows(r), :] for m in range(6)] for q in range(2)]
-                inverse = [inverse_ref[p + q, rows(r), :] for q in range(2)] if lead else None
+                inverse = [coef[6, p + q, rows(r), :] for q in range(2)] if lead else None
                 plane = {d: [source[d, p - 1, rows(r), :], value[0, d], value[1, d], source[d, p + 2, rows(r), :]] for d in range(dirs)}
                 for q, d in each:
                     here = value[q, d]
@@ -648,12 +640,9 @@
     def full(source, lead, step, store):
         sweep(source, lead, 1 + step, depth - 2 - 2 * step, 0, chunks, store)
 
-    low = 1
-    for move, present in zip(moves, (reach, 2 * reach, reach + own, depth)):
+    for move in moves:
         move.wait()
-        ready = (present - 1 - low) // 2 * 2
-        sweep(start, True, low, ready, 0, chunks, into(ping))
-        low += ready
+    full(start, True, 0, into(ping))
     full(ping, False, 1, into(pong))
     full(pong, False, 2, again)
     full(start, True, 3, into(ping))
@@ -687,24 +676,23 @@
             sweep(pong, False, reach + low, high - low, 0, chunks, emit(kinds))
 
 
-def solves(adjoint, planes, coefficients, values, weight=None):
+def solves(adjoint, planes, codes, flows, values, weight=None):
     dirs, reach, height, _ = values[0].shape
     depth = 2 * planes + 2 * reach
-    ahead, behind, inverse = coefficients
-    ins = [behind if adjoint else ahead, inverse, *values]
-    specs = [VMEM] * 2 + [ANY] * 4
+    ins = [codes, *flows, *values]
+    specs = [SMEM] + [ANY] * 8
     if adjoint:
         outs = [floats(dirs, planes, height - SPARE, LANES)] * 2
     else:
         ins.append(weight)
         specs.append(VMEM)
         outs = [floats(*values[0].shape)] * 2
-    scratch = [pltpu.VMEM((dirs, depth, height, LANES), jnp.float32)] * 4
+    scratch = [pltpu.VMEM((n, depth, height, LANES), jnp.float32) for n in (3, 7) + (dirs,) * 4]
     return call(
         functools.partial(solve_kernel, adjoint),
         "adjoint" if adjoint else "forward",
-        ins, outs, scratch + [pltpu.SemaphoreType.DMA((4,))],
-        28, 6 * 16 * dirs * depth * height * LANES, specs,
+        ins, outs, scratch + [pltpu.SemaphoreType.DMA((4,))] * 2,
+        36, 6 * 20 * dirs * depth * height * LANES, specs,
     )
 
 
@@ -722,7 +710,6 @@
     rank = eigen_basis.shape[0]
     count = lax.axis_size("slab")
     height = width // 2 + SPARE
-    depth = 2 * planes + 2 * REACH
     own, other, above = quad(count)
     each = dirs // GROUPS
     block = planes * height
@@ -733,15 +720,10 @@
     def beyond(up, down):
         return up, down, lax.ppermute(up, "slab", above), lax.ppermute(down, "slab", back(above))
 
-    def pack(token, pair, parts, held=()):
-        outs = [floats(parts, REACH, height, LANES)] * 2 + [floats(*h.shape) for h in held]
-        n = len(held)
-        found = call(
-            functools.partial(pack_kernel, planes, n), "pack", [token, *pair, *held], outs,
-            specs=[SMEM, VMEM, VMEM] + [ANY] * n, out_specs=[VMEM] * 2 + [ANY] * n,
-            aliases={3 + k: 2 + k for k in range(n)},
-        )
-        return found[:2], found[2:]
+    def pack(token, pair, parts):
+        outs = [floats(parts, REACH, height, LANES)] * 2
+        kernel = functools.partial(pack_kernel, planes)
+        return call(kernel, "pack", [token, *pair], outs, specs=[SMEM, VMEM, VMEM])
 
     fields = [flow_first, flow_second, flow_depth]
     flows = regroup(*call(
@@ -752,32 +734,31 @@
     tile, token = gram_tile(basis)
     sensors = [x.reshape(-1, LANES) for x in (sensor_cells, sensor_weight)]
     listed = 2 * sensors[0].shape[0]
-    lines = [each * block + (listed if k == 0 else 0) for k in range(GROUPS)]
-    *cuts, token = call(
-        functools.partial(cut_groups_kernel, height), "cut", [token, *sensors, directions],
-        [floats(n, LANES) for n in lines for _ in range(2)] + [TOKEN],
-        [pltpu.SemaphoreType.DMA((2 * dirs * planes,))], 54, 0, [SMEM, VMEM, VMEM, ANY],
-        [VMEM] * (2 * GROUPS) + [SMEM],
-    )
-    moved = [regroup(*cuts[:2])]
-    flows, cuts = pack(token, flows, len(fields), cuts[2:])
-    flows = beyond(*flows)
-    moved += [regroup(*cuts[k : k + 2]) for k in range(0, len(cuts), 2)]
+
+    def cut(token, group, sensors=()):
+        rows = each * block + sum(x.shape[0] for x in sensors)
+        n = len(sensors)
+        return call(
+            functools.partial(cut_group_kernel, height, group), "cut", [token, *sensors, directions],
+            [floats(rows, LANES)] * 2 + [TOKEN], [pltpu.SemaphoreType.DMA((2 * each * planes,))],
+            54, 0, [SMEM] + [VMEM] * n + [ANY], [VMEM, VMEM, SMEM],
+        )
+
+    *parts, _ = cut(token, range(each), sensors)
+    moved = [regroup(*parts)]
+    for k in range(each, dirs, each):
+        *parts, token = cut(token, range(k, k + each))
+        moved.append(regroup(*parts))
+    flows = beyond(*pack(token, flows, len(fields)))
     weight, later = call(
         functools.partial(sensor_kernel, width, each * block), "sensors", [*moved[0]],
         [floats(2, planes, height, LANES), TOKEN],
         work=block * listed * 20, out_specs=[VMEM, SMEM],
     )
     tokens = [token] + [later] * (GROUPS - 1)
-    values = [beyond(*pack(t, m, each)[0]) for t, m in zip(tokens, moved)]
-    coefficients = call(
-        coefficient_kernel, "coefficients", [face_codes, *flows],
-        [floats(6, depth, height, LANES)] * 2 + [floats(depth, height, LANES)],
-        [pltpu.VMEM((3, depth, height, LANES), jnp.float32), pltpu.SemaphoreType.DMA((4,))],
-        26, 80 * depth * height * LANES, [SMEM] + [ANY] * 4,
-    )
-    forcing = [beyond(*solves(False, planes, coefficients, v, weight)) for v in values]
-    summed = [solves(True, planes, coefficients, f) for f in forcing]
+    values = [beyond(*pack(t, m, each)) for t, m in zip(tokens, moved)]
+    forcing = [beyond(*solves(False, planes, face_codes, flows, v, weight)) for v in values]
+    summed = [solves(True, planes, face_codes, flows, f) for f in forcing]
     returned = [
         (lax.ppermute(s[0], "slab", back(own)), lax.ppermute(s[1], "slab", back(other)))
         for s in summed

time: 191 us -> 167 us (0.87)
  local copies, waits for them, and re-layouts: 17.5 us -> 0.03 us
  starting transfers between devices: 61.1 us -> 45.4 us
  Pallas kernels: 78.6 us -> 85.2 us
  waiting for transfers between devices: 18.4 us -> 20.5 us
    unnamed x24 -> x12, local copies, waits for them, and re-layouts: 17.5 us -> 0.03 us
    ppermute x3, starting transfers between devices: 19.6 us -> 7.68 us  [regroup(): lax.ppermute(second, 'slab', other)]
    pallas_call x15, Pallas kernels: 78.6 us -> 85.2 us  [call(): pl.pallas_call(kernel, in_specs=specs or [VMEM] * len(ins), out_specs=out...]
    ppermute x5, starting transfers between devices: 22.4 us -> 17.9 us  [beyond(): lax.ppermute(up, 'slab', above)]
  transfers between devices with their start and end apart: 20 -> 20, of which waited for: 4 -> 4; matrix products, arithmetic and copies ran while one was open for 0% -> 0% of each run, Pallas kernels for 35% -> 45%
where the time goes in v6:
time: 167 us; the launch traced here: 166 us
  Pallas kernels  85.2 us (51%)
  starting transfers between devices  45.4 us (27%)
  waiting for transfers between devices  20.5 us (12%)
  blocking collectives  13.4 us (8%)
    pallas_call x15, Pallas kernels, call(): pl.pallas_call(kernel, in_specs=specs or [VMEM] * len(ins), out_specs=out...  85.2 us
    ppermute x5, starting transfers between devices, beyond(): lax.ppermute(up, 'slab', above)  17.9 us
    all_to_all x1, blocking collectives, spread(): return lax.all_to_all(tile, 'slab', 0, 0, tiled=True) if count > 1 else tile  13.4 us
    ppermute x2, waiting for transfers between devices, body(): lax.ppermute(s[1], 'slab', back(other))  10.9 us
    ppermute x3, waiting for transfers between devices, regroup(): lax.ppermute(second, 'slab', other)  9.53 us
    ppermute x3, starting transfers between devices, regroup(): lax.ppermute(second, 'slab', other)  7.68 us
    ppermute x5, starting transfers between devices, beyond(): lax.ppermute(down, 'slab', back(above))  6.64 us
    ppermute x2, starting transfers between devices, body(): lax.ppermute(s[1], 'slab', back(other))  6.57 us
  transfers between devices with their start and end apart: 20, of which 4 were waited for; matrix products, arithmetic and copies ran while one was open for 0% of the time, Pallas kernels for 45%

profile of v6, /device:TPU:0, one launch (start us, length us, event | category | flops | bytes accessed | tf_op | source)
XLA Modules:
  0.0 166.2 jit_solution(12919310993089412391)
XLA Ops:
  0.6 2.7 %cut.4 = (f32[12,144,128]{2,1,0:T(8,128)}, f32[12,144,128]{2,1,0:T(8,128)}) custom-call(f32[4,256,128]{2,1,0:T(8,128)} %refs_0_.3, f32[4,256,128]{2,1,0:T(8,128)} %refs_1_.1, f32[4,256,128]{2,1,0:T(8,128)} %refs_2_.2), custom_call_target="tpu_custom_call" | custom-call | bytes 3342336 | tf_op jit(solution)/shard_map/cut/pallas_call | solution.py:376
  5.1 3.1 %collective-permute-start.1 = (f32[12,144,128]{2,1,0:T(8,128)}, f32[12,144,128]{2,1,0:T(8,128)S(1)}, u32[]{:S(2)}, u32[]{:S(2)}) collective-permute-start(f32[12,144,128]{2,1,0:T(8,128)} %get-tuple-element.55), channel_id=1, source_target_pairs={{0,2},{1,0},{2,3},{3,1},{4,6},{5,4},{6,7},{7,5},{8,10},{9,8},{10,1... | collective-permute-start | bytes 2654216 | tf_op jit(solution)/shard_map/ppermute | solution.py:718
  8.2 8.2 %gram.1 = (f32[8,128]{1,0:T(8,128)}, s32[1]{0:T(128)}) custom-call(f32[16,1024,128]{2,1,0:T(8,128)} %bitcast.13), custom_call_target="tpu_custom_call" | custom-call | flops 5033164800 | bytes 8392708 | tf_op jit(solution)/shard_map/gram/pallas_call | solution.py:376
  16.5 3.9 %cut.5 = (f32[1216,128]{1,0:T(8,128)}, f32[1216,128]{1,0:T(8,128)}, s32[1]{0:T(128)}) custom-call(s32[1]{0:T(128)} %get-tuple-element.52.token_ref, s32[32,128]{1,0:T(8,128)} %bitcast.21, f32[32,128]{1,0:T(8,128)} %bitcast.22, f32[4,4,256,128]{3,2,1,0:T(8,128)} %refs_2_.3), custom_call_target="tpu_custom_call" | custom-call | bytes 3375112 | tf_op jit(solution)/shard_map/cut/pallas_call | solution.py:376
  24.1 3.1 %cut.3 = (f32[1152,128]{1,0:T(8,128)}, f32[1152,128]{1,0:T(8,128)}, s32[1]{0:T(128)}) custom-call(s32[1]{0:T(128)} %get-tuple-element.52.token_ref, f32[4,4,256,128]{3,2,1,0:T(8,128)} %refs_2_.3), custom_call_target="tpu_custom_call" | custom-call | bytes 3276808 | tf_op jit(solution)/shard_map/cut/pallas_call | solution.py:376
  29.4 3.4 %collective-permute-start.2 = (f32[3,6,144,128]{3,2,1,0:T(8,128)S(1)}, f32[3,6,144,128]{3,2,1,0:T(8,128)S(1)}, u32[]{:S(2)}, u32[]{:S(2)}) collective-permute-start(f32[3,6,144,128]{3,2,1,0:T(8,128)S(1)} %get-tuple-element.56.refs_0_), channel_id=1, source_target_pairs={{0,1},{1,4},{2,3},{3,6},{4,5},{5,8},{6,7},{7,10},{8,9},{9,12},{10,... | collective-permute-start | bytes 3981320 | tf_op jit(solution)/shard_map/ppermute | solution.py:721
  35.8 6.1 %collective-permute-done.5.other_ref = f32[1216,128]{1,0:T(8,128)S(1)} collective-permute-done((f32[1216,128]{1,0:T(8,128)}, f32[1216,128]{1,0:T(8,128)S(1)}, u32[]{:S(2)}, u32[]{:S(2)}) %collective-permute-start.5) | collective-permute-done | bytes 622624 | tf_op jit(solution)/shard_map/ppermute | solution.py:718
  42.6 3.4 %collective-permute-start.6 = (f32[2,6,144,128]{3,2,1,0:T(8,128)S(1)}, f32[2,6,144,128]{3,2,1,0:T(8,128)S(1)}, u32[]{:S(2)}, u32[]{:S(2)}) collective-permute-start(f32[2,6,144,128]{3,2,1,0:T(8,128)S(1)} %get-tuple-element.60.refs_4_), channel_id=1, source_target_pairs={{0,1},{1,4},{2,3},{3,6},{4,5},{5,8},{6,7},{7,10},{8,9},{9,12},{10,... | collective-permute-start | bytes 2654216 | tf_op jit(solution)/shard_map/ppermute | solution.py:721
  47.3 2.7 %collective-permute-start.13 = (f32[1152,128]{1,0:T(8,128)S(1)}, f32[1152,128]{1,0:T(8,128)S(1)}, u32[]{:S(2)}, u32[]{:S(2)}) collective-permute-start(f32[1152,128]{1,0:T(8,128)S(1)} %copy-done.3), channel_id=1, source_target_pairs={{0,2},{1,0},{2,3},{3,1},{4,6},{5,4},{6,7},{7,5},{8,10},{9,8},{10,1... | collective-permute-start | bytes 1769480 | tf_op jit(solution)/shard_map/ppermute | solution.py:718
  50.0 5.2 %sensors.1 = (f32[2,4,144,128]{3,2,1,0:T(8,128)S(1)}, s32[1]{0:T(128)}) custom-call(f32[1216,128]{1,0:T(8,128)S(1)} %collective-permute-done.4.own_ref, f32[1216,128]{1,0:T(8,128)S(1)} %collective-permute-done.5.other_ref), custom_call_target="tpu_custom_call" | custom-call | flops 110592000 | bytes 1835012 | tf_op jit(solution)/shard_map/sensors/pallas_call | solution.py:376
  55.2 2.2 %collective-permute-done.13.other_ref = f32[1152,128]{1,0:T(8,128)S(1)} collective-permute-done((f32[1152,128]{1,0:T(8,128)S(1)}, f32[1152,128]{1,0:T(8,128)S(1)}, u32[]{:S(2)}, u32[]{:S(2)}) %collective-permute-start.13) | collective-permute-done | bytes 589856 | tf_op jit(solution)/shard_map/ppermute | solution.py:718
  58.2 2.1 %collective-permute-start.14 = (f32[2,6,144,128]{3,2,1,0:T(8,128)S(1)}, f32[2,6,144,128]{3,2,1,0:T(8,128)S(1)}, u32[]{:S(2)}, u32[]{:S(2)}) collective-permute-start(f32[2,6,144,128]{3,2,1,0:T(8,128)S(1)} %get-tuple-element.72.refs_4_), channel_id=1, source_target_pairs={{0,1},{1,4},{2,3},{3,6},{4,5},{5,8},{6,7},{7,10},{8,9},{9,12},{10,... | collective-permute-start | bytes 2654216 | tf_op jit(solution)/shard_map/ppermute | solution.py:721
  61.9 12.4 %forward.2 = (f32[2,6,144,128]{3,2,1,0:T(8,128)S(1)}, f32[2,6,144,128]{3,2,1,0:T(8,128)S(1)}) custom-call(s32[4]{0:T(128)S(1)} %copy-done.2, f32[3,6,144,128]{3,2,1,0:T(8,128)S(1)} %get-tuple-element.56.refs_0_, f32[3,6,144,128]{3,2,1,0:T(8,128)S(1)} %get-tuple-element.57.refs_1_, f32[3,6,144,128]{3,2,1,0:T(8,128)S(1)} %collective-permute-done.2.refs_2_, ...), custom_call_target="tpu_custom_call" | custom-call | flops 13271040000 | bytes 11206672 | tf_op jit(solution)/shard_map/forward/pallas_call | solution.py:376
  74.2 4.7 %collective-permute-start.8 = (f32[2,6,144,128]{3,2,1,0:T(8,128)S(1)}, f32[2,6,144,128]{3,2,1,0:T(8,128)S(1)}, u32[]{:S(2)}, u32[]{:S(2)}) collective-permute-start(f32[2,6,144,128]{3,2,1,0:T(8,128)S(1)} %get-tuple-element.63.refs_4_), channel_id=1, source_target_pairs={{0,1},{1,4},{2,3},{3,6},{4,5},{5,8},{6,7},{7,10},{8,9},{9,12},{10,... | collective-permute-start | bytes 2654216 | tf_op jit(solution)/shard_map/ppermute | solution.py:721
  80.2 12.4 %forward.3 = (f32[2,6,144,128]{3,2,1,0:T(8,128)S(1)}, f32[2,6,144,128]{3,2,1,0:T(8,128)S(1)}) custom-call(s32[4]{0:T(128)S(1)} %copy-done.2, f32[3,6,144,128]{3,2,1,0:T(8,128)S(1)} %get-tuple-element.56.refs_0_, f32[3,6,144,128]{3,2,1,0:T(8,128)S(1)} %get-tuple-element.57.refs_1_, f32[3,6,144,128]{3,2,1,0:T(8,128)S(1)} %collective-permute-done.2.refs_2_, ...), custom_call_target="tpu_custom_call" | custom-call | flops 13271040000 | bytes 11206672 | tf_op jit(solution)/shard_map/forward/pallas_call | solution.py:376
  92.6 4.3 %collective-permute-start.16 = (f32[2,6,144,128]{3,2,1,0:T(8,128)S(1)}, f32[2,6,144,128]{3,2,1,0:T(8,128)S(1)}, u32[]{:S(2)}, u32[]{:S(2)}) collective-permute-start(f32[2,6,144,128]{3,2,1,0:T(8,128)S(1)} %get-tuple-element.74.refs_4_), channel_id=1, source_target_pairs={{0,1},{1,4},{2,3},{3,6},{4,5},{5,8},{6,7},{7,10},{8,9},{9,12},{10,... | collective-permute-start | bytes 2654216 | tf_op jit(solution)/shard_map/ppermute | solution.py:721
  98.2 12.2 %adjoint.2 = (f32[2,4,128,128]{3,2,1,0:T(8,128)S(1)}, f32[2,4,128,128]{3,2,1,0:T(8,128)S(1)}) custom-call(s32[4]{0:T(128)S(1)} %copy-done.2, f32[3,6,144,128]{3,2,1,0:T(8,128)S(1)} %get-tuple-element.56.refs_0_, f32[3,6,144,128]{3,2,1,0:T(8,128)S(1)} %get-tuple-element.57.refs_1_, f32[3,6,144,128]{3,2,1,0:T(8,128)S(1)} %collective-permute-done.2.refs_2_, ...), custom_call_target="tpu_custom_call" | custom-call | flops 13271040000 | bytes 9895952 | tf_op jit(solution)/shard_map/adjoint/pallas_call | solution.py:376
  111.1 3.9 %collective-permute-start.11 = (f32[2,4,128,128]{3,2,1,0:T(8,128)S(1)}, f32[2,4,128,128]{3,2,1,0:T(8,128)S(1)}, u32[]{:S(2)}, u32[]{:S(2)}) collective-permute-start(f32[2,4,128,128]{3,2,1,0:T(8,128)S(1)} %get-tuple-element.66), channel_id=1, source_target_pairs={{2,0},{0,1},{3,2},{1,3},{6,4},{4,5},{7,6},{5,7},{10,8},{8,9},{11,1... | collective-permute-start | bytes 1572872 | tf_op jit(solution)/shard_map/ppermute | solution.py:763
  115.0 12.2 %adjoint.3 = (f32[2,4,128,128]{3,2,1,0:T(8,128)S(1)}, f32[2,4,128,128]{3,2,1,0:T(8,128)S(1)}) custom-call(s32[4]{0:T(128)S(1)} %copy-done.2, f32[3,6,144,128]{3,2,1,0:T(8,128)S(1)} %get-tuple-element.56.refs_0_, f32[3,6,144,128]{3,2,1,0:T(8,128)S(1)} %get-tuple-element.57.refs_1_, f32[3,6,144,128]{3,2,1,0:T(8,128)S(1)} %collective-permute-done.2.refs_2_, ...), custom_call_target="tpu_custom_call" | custom-call | flops 13271040000 | bytes 9895952 | tf_op jit(solution)/shard_map/adjoint/pallas_call | solution.py:376
  127.9 2.7 %collective-permute-start.19 = (f32[2,4,128,128]{3,2,1,0:T(8,128)S(1)}, f32[2,4,128,128]{3,2,1,0:T(8,128)S(1)}, u32[]{:S(2)}, u32[]{:S(2)}) collective-permute-start(f32[2,4,128,128]{3,2,1,0:T(8,128)S(1)} %get-tuple-element.77), channel_id=1, source_target_pairs={{2,0},{0,1},{3,2},{1,3},{6,4},{4,5},{7,6},{5,7},{10,8},{8,9},{11,1... | collective-permute-start | bytes 1572872 | tf_op jit(solution)/shard_map/ppermute | solution.py:763
  130.7 2.6 %projections.2 = (f32[8,128]{1,0:T(8,128)S(1)}, f32[2,1024,128]{2,1,0:T(8,128)S(1)}, f32[16,1024,128]{2,1,0:T(8,128)S(1)}) custom-call(f32[16,1024,128]{2,1,0:T(8,128)S(1)} %bitcast.16, f32[4,1024,128]{2,1,0:T(8,128)S(1)} %bitcast.11, f32[2,4,128,128]{3,2,1,0:T(8,128)S(1)} %collective-permute-done.10.own_hbm, ...), custom_call_target="tpu_custom_call" | custom-call | flops 1258291200 | bytes 20979712 | tf_op jit(solution)/shard_map/projections/pallas_call | solution.py:376
  133.3 10.9 %collective-permute-done.19.other_hbm = f32[2,4,128,128]{3,2,1,0:T(8,128)S(1)} collective-permute-done((f32[2,4,128,128]{3,2,1,0:T(8,128)S(1)}, f32[2,4,128,128]{3,2,1,0:T(8,128)S(1)}, u32[]{:S(2)}, u32[]{:S(2)}) %collective-permute-start.19) | collective-permute-done | bytes 524320 | tf_op jit(solution)/shard_map/ppermute | solution.py:763
  146.1 13.4 %all_to_all.19 = f32[16,8,128]{2,1,0:T(8,128)S(1)} all-to-all(f32[16,8,128]{2,1,0:T(8,128)S(1)} %bitcast.19), channel_id=1, replica_groups=mesh['grp'=2,'slab'=16] {'slab'}, dimensions={0} | all-to-all | bytes 131072 | tf_op jit(solution)/shard_map/all_to_all | solution.py:117
  159.5 6.0 %remainder.1 = (f32[4,1024,128]{2,1,0:T(8,128)}, f32[4,16]{1,0:T(4,128)}, f32[8,128]{1,0:T(8,128)S(1)}, s32[1]{0:T(128)}) custom-call(f32[128,128]{1,0:T(8,128)S(1)} %bitcast.18, f32[16,1024,128]{2,1,0:T(8,128)S(1)} %get-tuple-element.68.basis_in.basis_ref, f32[2,1024,128]{2,1,0:T(8,128)S(1)} %get-tuple-element.80.refs_0_, ...), custom_call_target="tpu_custom_call" | custom-call | flops 2516582400 | bytes 12652804 | tf_op jit(solution)/shard_map/remainder/pallas_call | solution.py:376
  (46 shorter events, 21.5 us)
Async XLA Ops:
  3.3 23.9 %collective-permute-start = (f32[12,144,128]{2,1,0:T(8,128)}, f32[12,144,128]{2,1,0:T(8,128)S(1)}, u32[]{:S(2)}, u32[]{:S(2)}) collective-permute-start(f32[12,144,128]{2,1,0:T(8,128)} %get-tuple-element.54), channel_id=1, source_target_pairs={{0,0},{1,2},{2,1},{3,3},{4,4},{5,6},{6,5},{7,7},{8,8},{9,10},{10,9... | collective-permute-start | bytes 2654216 | tf_op jit(solution)/shard_map/ppermute | solution.py:718
  5.1 23.4 %collective-permute-start.1 = (f32[12,144,128]{2,1,0:T(8,128)}, f32[12,144,128]{2,1,0:T(8,128)S(1)}, u32[]{:S(2)}, u32[]{:S(2)}) collective-permute-start(f32[12,144,128]{2,1,0:T(8,128)} %get-tuple-element.55), channel_id=1, source_target_pairs={{0,2},{1,0},{2,3},{3,1},{4,6},{5,4},{6,7},{7,5},{8,10},{9,8},{10,1... | collective-permute-start | bytes 2654216 | tf_op jit(solution)/shard_map/ppermute | solution.py:718
  20.4 15.4 %collective-permute-start.4 = (f32[1216,128]{1,0:T(8,128)}, f32[1216,128]{1,0:T(8,128)S(1)}, u32[]{:S(2)}, u32[]{:S(2)}) collective-permute-start(f32[1216,128]{1,0:T(8,128)} %get-tuple-element.58), channel_id=1, source_target_pairs={{0,0},{1,2},{2,1},{3,3},{4,4},{5,6},{6,5},{7,7},{8,8},{9,10},{10,9... | collective-permute-start | bytes 1867784 | tf_op jit(solution)/shard_map/ppermute | solution.py:718
  22.1 19.7 %collective-permute-start.5 = (f32[1216,128]{1,0:T(8,128)}, f32[1216,128]{1,0:T(8,128)S(1)}, u32[]{:S(2)}, u32[]{:S(2)}) collective-permute-start(f32[1216,128]{1,0:T(8,128)} %get-tuple-element.59), channel_id=1, source_target_pairs={{0,2},{1,0},{2,3},{3,1},{4,6},{5,4},{6,7},{7,5},{8,10},{9,8},{10,1... | collective-permute-start | bytes 1867784 | tf_op jit(solution)/shard_map/ppermute | solution.py:718
  27.2 20.1 %copy-start.3 = (f32[1152,128]{1,0:T(8,128)S(1)}, f32[1152,128]{1,0:T(8,128)}, u32[]{:S(2)}) copy-start(f32[1152,128]{1,0:T(8,128)} %get-tuple-element.71) | copy-start | bytes 1769476
  29.4 32.5 %copy-start.2 = (s32[4]{0:T(128)S(1)}, s32[4]{0:T(128)}, u32[]{:S(2)}) copy-start(s32[4]{0:T(128)} %code_ref.7) | copy-start | bytes 52
  29.4 32.5 %collective-permute-start.2 = (f32[3,6,144,128]{3,2,1,0:T(8,128)S(1)}, f32[3,6,144,128]{3,2,1,0:T(8,128)S(1)}, u32[]{:S(2)}, u32[]{:S(2)}) collective-permute-start(f32[3,6,144,128]{3,2,1,0:T(8,128)S(1)} %get-tuple-element.56.refs_0_), channel_id=1, source_target_pairs={{0,1},{1,4},{2,3},{3,6},{4,5},{5,8},{6,7},{7,10},{8,9},{9,12},{10,... | collective-permute-start | bytes 3981320 | tf_op jit(solution)/shard_map/ppermute | solution.py:721
  32.8 29.1 %collective-permute-start.3 = (f32[3,6,144,128]{3,2,1,0:T(8,128)S(1)}, f32[3,6,144,128]{3,2,1,0:T(8,128)S(1)}, u32[]{:S(2)}, u32[]{:S(2)}) collective-permute-start(f32[3,6,144,128]{3,2,1,0:T(8,128)S(1)} %get-tuple-element.57.refs_1_), channel_id=1, source_target_pairs={{1,0},{4,1},{3,2},{6,3},{5,4},{8,5},{7,6},{10,7},{9,8},{12,9},{11,... | collective-permute-start | bytes 3981320 | tf_op jit(solution)/shard_map/ppermute | solution.py:721
  34.1 13.2 %collective-permute-start.12 = (f32[1152,128]{1,0:T(8,128)}, f32[1152,128]{1,0:T(8,128)S(1)}, u32[]{:S(2)}, u32[]{:S(2)}) collective-permute-start(f32[1152,128]{1,0:T(8,128)} %get-tuple-element.70), channel_id=1, source_target_pairs={{0,0},{1,2},{2,1},{3,3},{4,4},{5,6},{6,5},{7,7},{8,8},{9,10},{10,9... | collective-permute-start | bytes 1769480 | tf_op jit(solution)/shard_map/ppermute | solution.py:718
  42.6 17.7 %collective-permute-start.6 = (f32[2,6,144,128]{3,2,1,0:T(8,128)S(1)}, f32[2,6,144,128]{3,2,1,0:T(8,128)S(1)}, u32[]{:S(2)}, u32[]{:S(2)}) collective-permute-start(f32[2,6,144,128]{3,2,1,0:T(8,128)S(1)} %get-tuple-element.60.refs_4_), channel_id=1, source_target_pairs={{0,1},{1,4},{2,3},{3,6},{4,5},{5,8},{6,7},{7,10},{8,9},{9,12},{10,... | collective-permute-start | bytes 2654216 | tf_op jit(solution)/shard_map/ppermute | solution.py:721
  46.0 15.8 %collective-permute-start.7 = (f32[2,6,144,128]{3,2,1,0:T(8,128)S(1)}, f32[2,6,144,128]{3,2,1,0:T(8,128)S(1)}, u32[]{:S(2)}, u32[]{:S(2)}) collective-permute-start(f32[2,6,144,128]{3,2,1,0:T(8,128)S(1)} %get-tuple-element.61.refs_5_), channel_id=1, source_target_pairs={{1,0},{4,1},{3,2},{6,3},{5,4},{8,5},{7,6},{10,7},{9,8},{12,9},{11,... | collective-permute-start | bytes 2654216 | tf_op jit(solution)/shard_map/ppermute | solution.py:721
  47.3 10.1 %collective-permute-start.13 = (f32[1152,128]{1,0:T(8,128)S(1)}, f32[1152,128]{1,0:T(8,128)S(1)}, u32[]{:S(2)}, u32[]{:S(2)}) collective-permute-start(f32[1152,128]{1,0:T(8,128)S(1)} %copy-done.3), channel_id=1, source_target_pairs={{0,2},{1,0},{2,3},{3,1},{4,6},{5,4},{6,7},{7,5},{8,10},{9,8},{10,1... | collective-permute-start | bytes 1769480 | tf_op jit(solution)/shard_map/ppermute | solution.py:718
  58.2 22.0 %collective-permute-start.14 = (f32[2,6,144,128]{3,2,1,0:T(8,128)S(1)}, f32[2,6,144,128]{3,2,1,0:T(8,128)S(1)}, u32[]{:S(2)}, u32[]{:S(2)}) collective-permute-start(f32[2,6,144,128]{3,2,1,0:T(8,128)S(1)} %get-tuple-element.72.refs_4_), channel_id=1, source_target_pairs={{0,1},{1,4},{2,3},{3,6},{4,5},{5,8},{6,7},{7,10},{8,9},{9,12},{10,... | collective-permute-start | bytes 2654216 | tf_op jit(solution)/shard_map/ppermute | solution.py:721
  60.4 19.9 %collective-permute-start.15 = (f32[2,6,144,128]{3,2,1,0:T(8,128)S(1)}, f32[2,6,144,128]{3,2,1,0:T(8,128)S(1)}, u32[]{:S(2)}, u32[]{:S(2)}) collective-permute-start(f32[2,6,144,128]{3,2,1,0:T(8,128)S(1)} %get-tuple-element.73.refs_5_), channel_id=1, source_target_pairs={{1,0},{4,1},{3,2},{6,3},{5,4},{8,5},{7,6},{10,7},{9,8},{12,9},{11,... | collective-permute-start | bytes 2654216 | tf_op jit(solution)/shard_map/ppermute | solution.py:721
  74.2 24.0 %collective-permute-start.8 = (f32[2,6,144,128]{3,2,1,0:T(8,128)S(1)}, f32[2,6,144,128]{3,2,1,0:T(8,128)S(1)}, u32[]{:S(2)}, u32[]{:S(2)}) collective-permute-start(f32[2,6,144,128]{3,2,1,0:T(8,128)S(1)} %get-tuple-element.63.refs_4_), channel_id=1, source_target_pairs={{0,1},{1,4},{2,3},{3,6},{4,5},{5,8},{6,7},{7,10},{8,9},{9,12},{10,... | collective-permute-start | bytes 2654216 | tf_op jit(solution)/shard_map/ppermute | solution.py:721
  78.9 19.3 %collective-permute-start.9 = (f32[2,6,144,128]{3,2,1,0:T(8,128)S(1)}, f32[2,6,144,128]{3,2,1,0:T(8,128)S(1)}, u32[]{:S(2)}, u32[]{:S(2)}) collective-permute-start(f32[2,6,144,128]{3,2,1,0:T(8,128)S(1)} %get-tuple-element.64.refs_5_), channel_id=1, source_target_pairs={{1,0},{4,1},{3,2},{6,3},{5,4},{8,5},{7,6},{10,7},{9,8},{12,9},{11,... | collective-permute-start | bytes 2654216 | tf_op jit(solution)/shard_map/ppermute | solution.py:721
  92.6 22.4 %collective-permute-start.16 = (f32[2,6,144,128]{3,2,1,0:T(8,128)S(1)}, f32[2,6,144,128]{3,2,1,0:T(8,128)S(1)}, u32[]{:S(2)}, u32[]{:S(2)}) collective-permute-start(f32[2,6,144,128]{3,2,1,0:T(8,128)S(1)} %get-tuple-element.74.refs_4_), channel_id=1, source_target_pairs={{0,1},{1,4},{2,3},{3,6},{4,5},{5,8},{6,7},{7,10},{8,9},{9,12},{10,... | collective-permute-start | bytes 2654216 | tf_op jit(solution)/shard_map/ppermute | solution.py:721
  96.9 18.1 %collective-permute-start.17 = (f32[2,6,144,128]{3,2,1,0:T(8,128)S(1)}, f32[2,6,144,128]{3,2,1,0:T(8,128)S(1)}, u32[]{:S(2)}, u32[]{:S(2)}) collective-permute-start(f32[2,6,144,128]{3,2,1,0:T(8,128)S(1)} %get-tuple-element.75.refs_5_), channel_id=1, source_target_pairs={{1,0},{4,1},{3,2},{6,3},{5,4},{8,5},{7,6},{10,7},{9,8},{12,9},{11,... | collective-permute-start | bytes 2654216 | tf_op jit(solution)/shard_map/ppermute | solution.py:721
  110.4 20.2 %collective-permute-start.10 = (f32[2,4,128,128]{3,2,1,0:T(8,128)S(1)}, f32[2,4,128,128]{3,2,1,0:T(8,128)S(1)}, u32[]{:S(2)}, u32[]{:S(2)}) collective-permute-start(f32[2,4,128,128]{3,2,1,0:T(8,128)S(1)} %get-tuple-element.65), channel_id=1, source_target_pairs={{0,0},{2,1},{1,2},{3,3},{4,4},{6,5},{5,6},{7,7},{8,8},{10,9},{9,10... | collective-permute-start | bytes 1572872 | tf_op jit(solution)/shard_map/ppermute | solution.py:763
  111.1 19.5 %slice-start = ((s8[8388608]{0:T(1024)(128)(4,1)}), s8[4194304]{0:T(1024)(128)(4,1)S(1)}, s32[]{:S(2)}) async-start(s8[8388608]{0:T(1024)(128)(4,1)} %bitcast.14), calls=%async_computation.2 | async-start | bytes 8388608
  111.1 19.5 %copy-start = (f32[4,4,256,128]{3,2,1,0:T(8,128)S(1)}, f32[4,4,256,128]{3,2,1,0:T(8,128)}, u32[]{:S(2)}) copy-start(f32[4,4,256,128]{3,2,1,0:T(8,128)} %refs_2_.3) | copy-start | bytes 6291460
  111.1 19.5 %collective-permute-start.11 = (f32[2,4,128,128]{3,2,1,0:T(8,128)S(1)}, f32[2,4,128,128]{3,2,1,0:T(8,128)S(1)}, u32[]{:S(2)}, u32[]{:S(2)}) collective-permute-start(f32[2,4,128,128]{3,2,1,0:T(8,128)S(1)} %get-tuple-element.66), channel_id=1, source_target_pairs={{2,0},{0,1},{3,2},{1,3},{6,4},{4,5},{7,6},{5,7},{10,8},{8,9},{11,1... | collective-permute-start | bytes 1572872 | tf_op jit(solution)/shard_map/ppermute | solution.py:763
  127.2 6.1 %collective-permute-start.18 = (f32[2,4,128,128]{3,2,1,0:T(8,128)S(1)}, f32[2,4,128,128]{3,2,1,0:T(8,128)S(1)}, u32[]{:S(2)}, u32[]{:S(2)}) collective-permute-start(f32[2,4,128,128]{3,2,1,0:T(8,128)S(1)} %get-tuple-element.76), channel_id=1, source_target_pairs={{0,0},{2,1},{1,2},{3,3},{4,4},{6,5},{5,6},{7,7},{8,8},{10,9},{9,10... | collective-permute-start | bytes 1572872 | tf_op jit(solution)/shard_map/ppermute | solution.py:763
  127.9 16.3 %collective-permute-start.19 = (f32[2,4,128,128]{3,2,1,0:T(8,128)S(1)}, f32[2,4,128,128]{3,2,1,0:T(8,128)S(1)}, u32[]{:S(2)}, u32[]{:S(2)}) collective-permute-start(f32[2,4,128,128]{3,2,1,0:T(8,128)S(1)} %get-tuple-element.77), channel_id=1, source_target_pairs={{2,0},{0,1},{3,2},{1,3},{6,4},{4,5},{7,6},{5,7},{10,8},{8,9},{11,1... | collective-permute-start | bytes 1572872 | tf_op jit(solution)/shard_map/ppermute | solution.py:763
  (2 other events, 39.0 us)

commit v7 on v6

--- a/solution.py
+++ b/solution.py
@@ -114,7 +114,7 @@
 
 
 def spread(tile, count):
-    return lax.all_to_all(tile, "slab", 0, 0, tiled=True) if count > 1 else tile
+    return lax.all_gather(tile, "slab", tiled=True) if count > 1 else tile
 
 
 def projection_kernel(first, basis_in, dirs_hbm, own_hbm, other_hbm, tile_ref, out_ref, image_ref, *refs):
@@ -352,7 +352,7 @@
         out_shape=floats(dirs, rows, LANES),
         compiler_params=pltpu.CompilerParams(vmem_limit_bytes=16 << 20),
         name="rescale",
-    )(spread(parts, count), scales, new)
+    )(lax.all_to_all(parts, "slab", 0, 0, tiled=True), scales, new)
 
 
 def quad(count):
@@ -505,7 +505,7 @@
     return [pltpu.make_async_copy(s, t, sems.at[k]) for k, (s, t) in enumerate(moves)]
 
 
-def coefficients(adjoint, code_ref, flow, coef):
+def coefficients(adjoint, code_ref, flow, coef, low, high):
     _, depth, height, _ = flow.shape
     chunks = height // 8
     own = depth - 2 * REACH
@@ -553,7 +553,7 @@
             coef[6, p, here, :] = inverse
         return carry
 
-    lax.fori_loop(1, depth - 1, at_plane, 0, unroll=2)
+    lax.fori_loop(low, high, at_plane, 0)
 
 
 def solve_kernel(adjoint, code_ref, *refs):
@@ -568,11 +568,17 @@
     a = place()[0]
     flow_moves = arrivals(flow_parts, flow, flow_sems)
     moves = arrivals(value_parts, start, sems)
-    for move in flow_moves + moves:
+    for move in flow_moves:
         move.start()
-    for move in flow_moves:
+    low = 1
+    for k, (move, present) in enumerate(zip(flow_moves, (reach, 2 * reach, reach + own, depth))):
         move.wait()
-    coefficients(adjoint, code_ref, flow, coef)
+        if k == len(moves) - 1:
+            for other in moves:
+                other.start()
+        high = min(present, depth - 1)
+        coefficients(adjoint, code_ref, flow, coef, low, high)
+        low = high
 
     shape = (8, LANES)
     sub = lax.broadcasted_iota(jnp.int32, shape, 0)
@@ -590,7 +596,7 @@
             up = {e: pltpu.roll(v, 7, 0) for e, v in value.items()}
             down = {e: pltpu.roll(v, 1, 0) for e, v in value.items()}
             before = dict.fromkeys(each, zero)
-            if count < chunks:
+            if count < chunks - 1:
                 at = pl.multiple_of(jnp.maximum(offset - 8, 0), 8)
                 for q, d in each:
                     outer = pltpu.roll(source[d, p + q, pl.ds(at, 8), :], 1, 0)
@@ -604,7 +610,7 @@
                     if r + 1 < count:
                         following = source[d, p + q, rows(r + 1), :]
                         next_up, next_down = pltpu.roll(following, 7, 0), pltpu.roll(following, 1, 0)
-                    elif count < chunks:
+                    elif count < chunks - 1:
                         at = pl.multiple_of(jnp.minimum(offset + count * 8, height - 8), 8)
                         following = source[d, p + q, pl.ds(at, 8), :]
                         next_up, next_down = jnp.where(a == 1, 0.0, pltpu.roll(following, 7, 0)), zero
@@ -638,7 +644,8 @@
         start[d, p, here, :] = total if adjoint else total + start[d, p, here, :]
 
     def full(source, lead, step, store):
-        sweep(source, lead, 1 + step, depth - 2 - 2 * step, 0, chunks, store)
+        offset = pl.multiple_of(a * 8, 8) if adjoint else 0
+        sweep(source, lead, 1 + step, depth - 2 - 2 * step, offset, chunks - adjoint, store)
 
     for move in moves:
         move.wait()
@@ -765,8 +772,7 @@
     ]
     images = []
     for k, halves in enumerate(returned):
-        copies = count if k == GROUPS - 1 else 1
-        tile, image, basis = projections(basis, directions, k * each, halves, tile, copies)
+        tile, image, basis = projections(basis, directions, k * each, halves, tile, 1)
         images.append(image)
     cells = planes * count * width * LANES
     new, coeffs, scales, again = remainders(spread(tile, count), basis, images, cells)

time: 167 us -> 177 us (1.060)
  blocking collectives: 13.4 us -> 21.5 us
    all_gather x0 -> x1, blocking collectives: none -> 21.5 us  [spread(): return lax.all_gather(tile, 'slab', tiled=True) if count > 1 else tile]
    all_to_all x1 -> x0, blocking collectives: 13.4 us -> none  [spread(): return lax.all_to_all(tile, 'slab', 0, 0, tiled=True) if count > 1 else tile]
  transfers between devices with their start and end apart: 20 -> 20, of which waited for: 4 -> 4; matrix products, arithmetic and copies ran while one was open for 0% -> 0% of each run, Pallas kernels for 45% -> 43%
where the time goes in v7:
time: 177 us; the launch traced here: 176 us
  Pallas kernels  86.4 us (49%)
  starting transfers between devices  45.6 us (26%)
  blocking collectives  21.5 us (12%)
  waiting for transfers between devices  20.5 us (12%)
    pallas_call x15, Pallas kernels, call(): pl.pallas_call(kernel, in_specs=specs or [VMEM] * len(ins), out_specs=out...  86.4 us
    all_gather x1, blocking collectives, spread(): return lax.all_gather(tile, 'slab', tiled=True) if count > 1 else tile  21.5 us
    ppermute x5, starting transfers between devices, beyond(): lax.ppermute(up, 'slab', above)  17.9 us
    ppermute x2, waiting for transfers between devices, body(): lax.ppermute(s[1], 'slab', back(other))  10.9 us
    ppermute x3, waiting for transfers between devices, regroup(): lax.ppermute(second, 'slab', other)  9.53 us
    ppermute x3, starting transfers between devices, regroup(): lax.ppermute(second, 'slab', other)  7.68 us
    ppermute x2, starting transfers between devices, body(): lax.ppermute(s[1], 'slab', back(other))  6.75 us
    ppermute x5, starting transfers between devices, beyond(): lax.ppermute(down, 'slab', back(above))  6.64 us
  transfers between devices with their start and end apart: 20, of which 4 were waited for; matrix products, arithmetic and copies ran while one was open for 0% of the time, Pallas kernels for 43%

profile of v7, /device:TPU:0, one launch (start us, length us, event | category | flops | bytes accessed | tf_op | source)
XLA Modules:
  0.0 175.8 jit_solution(4276338445007569799)
XLA Ops:
  0.6 2.7 %cut.4 = (f32[12,144,128]{2,1,0:T(8,128)}, f32[12,144,128]{2,1,0:T(8,128)}) custom-call(f32[4,256,128]{2,1,0:T(8,128)} %refs_0_.3, f32[4,256,128]{2,1,0:T(8,128)} %refs_1_.1, f32[4,256,128]{2,1,0:T(8,128)} %refs_2_.2), custom_call_target="tpu_custom_call" | custom-call | bytes 3342336 | tf_op jit(solution)/shard_map/cut/pallas_call | solution.py:376
  5.1 3.1 %collective-permute-start.1 = (f32[12,144,128]{2,1,0:T(8,128)}, f32[12,144,128]{2,1,0:T(8,128)S(1)}, u32[]{:S(2)}, u32[]{:S(2)}) collective-permute-start(f32[12,144,128]{2,1,0:T(8,128)} %get-tuple-element.55), channel_id=1, source_target_pairs={{0,2},{1,0},{2,3},{3,1},{4,6},{5,4},{6,7},{7,5},{8,10},{9,8},{10,1... | collective-permute-start | bytes 2654216 | tf_op jit(solution)/shard_map/ppermute | solution.py:725
  8.2 8.2 %gram.1 = (f32[8,128]{1,0:T(8,128)}, s32[1]{0:T(128)}) custom-call(f32[16,1024,128]{2,1,0:T(8,128)} %bitcast.11), custom_call_target="tpu_custom_call" | custom-call | flops 5033164800 | bytes 8392708 | tf_op jit(solution)/shard_map/gram/pallas_call | solution.py:376
  16.5 3.9 %cut.5 = (f32[1216,128]{1,0:T(8,128)}, f32[1216,128]{1,0:T(8,128)}, s32[1]{0:T(128)}) custom-call(s32[1]{0:T(128)} %get-tuple-element.52.token_ref, s32[32,128]{1,0:T(8,128)} %bitcast.17, f32[32,128]{1,0:T(8,128)} %bitcast.18, f32[4,4,256,128]{3,2,1,0:T(8,128)} %refs_2_.3), custom_call_target="tpu_custom_call" | custom-call | bytes 3375112 | tf_op jit(solution)/shard_map/cut/pallas_call | solution.py:376
  24.1 3.1 %cut.3 = (f32[1152,128]{1,0:T(8,128)}, f32[1152,128]{1,0:T(8,128)}, s32[1]{0:T(128)}) custom-call(s32[1]{0:T(128)} %get-tuple-element.52.token_ref, f32[4,4,256,128]{3,2,1,0:T(8,128)} %refs_2_.3), custom_call_target="tpu_custom_call" | custom-call | bytes 3276808 | tf_op jit(solution)/shard_map/cut/pallas_call | solution.py:376
  29.4 3.4 %collective-permute-start.2 = (f32[3,6,144,128]{3,2,1,0:T(8,128)S(1)}, f32[3,6,144,128]{3,2,1,0:T(8,128)S(1)}, u32[]{:S(2)}, u32[]{:S(2)}) collective-permute-start(f32[3,6,144,128]{3,2,1,0:T(8,128)S(1)} %get-tuple-element.56.refs_0_), channel_id=1, source_target_pairs={{0,1},{1,4},{2,3},{3,6},{4,5},{5,8},{6,7},{7,10},{8,9},{9,12},{10,... | collective-permute-start | bytes 3981320 | tf_op jit(solution)/shard_map/ppermute | solution.py:728
  35.8 6.1 %collective-permute-done.5.other_ref = f32[1216,128]{1,0:T(8,128)S(1)} collective-permute-done((f32[1216,128]{1,0:T(8,128)}, f32[1216,128]{1,0:T(8,128)S(1)}, u32[]{:S(2)}, u32[]{:S(2)}) %collective-permute-start.5) | collective-permute-done | bytes 622624 | tf_op jit(solution)/shard_map/ppermute | solution.py:725
  42.6 3.4 %collective-permute-start.6 = (f32[2,6,144,128]{3,2,1,0:T(8,128)S(1)}, f32[2,6,144,128]{3,2,1,0:T(8,128)S(1)}, u32[]{:S(2)}, u32[]{:S(2)}) collective-permute-start(f32[2,6,144,128]{3,2,1,0:T(8,128)S(1)} %get-tuple-element.60.refs_4_), channel_id=1, source_target_pairs={{0,1},{1,4},{2,3},{3,6},{4,5},{5,8},{6,7},{7,10},{8,9},{9,12},{10,... | collective-permute-start | bytes 2654216 | tf_op jit(solution)/shard_map/ppermute | solution.py:728
  47.3 2.7 %collective-permute-start.13 = (f32[1152,128]{1,0:T(8,128)S(1)}, f32[1152,128]{1,0:T(8,128)S(1)}, u32[]{:S(2)}, u32[]{:S(2)}) collective-permute-start(f32[1152,128]{1,0:T(8,128)S(1)} %copy-done.3), channel_id=1, source_target_pairs={{0,2},{1,0},{2,3},{3,1},{4,6},{5,4},{6,7},{7,5},{8,10},{9,8},{10,1... | collective-permute-start | bytes 1769480 | tf_op jit(solution)/shard_map/ppermute | solution.py:725
  50.0 5.2 %sensors.1 = (f32[2,4,144,128]{3,2,1,0:T(8,128)S(1)}, s32[1]{0:T(128)}) custom-call(f32[1216,128]{1,0:T(8,128)S(1)} %collective-permute-done.4.own_ref, f32[1216,128]{1,0:T(8,128)S(1)} %collective-permute-done.5.other_ref), custom_call_target="tpu_custom_call" | custom-call | flops 110592000 | bytes 1835012 | tf_op jit(solution)/shard_map/sensors/pallas_call | solution.py:376
  55.2 2.2 %collective-permute-done.13.other_ref = f32[1152,128]{1,0:T(8,128)S(1)} collective-permute-done((f32[1152,128]{1,0:T(8,128)S(1)}, f32[1152,128]{1,0:T(8,128)S(1)}, u32[]{:S(2)}, u32[]{:S(2)}) %collective-permute-start.13) | collective-permute-done | bytes 589856 | tf_op jit(solution)/shard_map/ppermute | solution.py:725
  58.2 2.1 %collective-permute-start.14 = (f32[2,6,144,128]{3,2,1,0:T(8,128)S(1)}, f32[2,6,144,128]{3,2,1,0:T(8,128)S(1)}, u32[]{:S(2)}, u32[]{:S(2)}) collective-permute-start(f32[2,6,144,128]{3,2,1,0:T(8,128)S(1)} %get-tuple-element.72.refs_4_), channel_id=1, source_target_pairs={{0,1},{1,4},{2,3},{3,6},{4,5},{5,8},{6,7},{7,10},{8,9},{9,12},{10,... | collective-permute-start | bytes 2654216 | tf_op jit(solution)/shard_map/ppermute | solution.py:728
  61.9 12.8 %forward.2 = (f32[2,6,144,128]{3,2,1,0:T(8,128)S(1)}, f32[2,6,144,128]{3,2,1,0:T(8,128)S(1)}) custom-call(s32[4]{0:T(128)S(1)} %copy-done.2, f32[3,6,144,128]{3,2,1,0:T(8,128)S(1)} %get-tuple-element.56.refs_0_, f32[3,6,144,128]{3,2,1,0:T(8,128)S(1)} %get-tuple-element.57.refs_1_, f32[3,6,144,128]{3,2,1,0:T(8,128)S(1)} %collective-permute-done.2.refs_2_, ...), custom_call_target="tpu_custom_call" | custom-call | flops 13271040000 | bytes 11206672 | tf_op jit(solution)/shard_map/forward/pallas_call | solution.py:376
  74.7 4.7 %collective-permute-start.8 = (f32[2,6,144,128]{3,2,1,0:T(8,128)S(1)}, f32[2,6,144,128]{3,2,1,0:T(8,128)S(1)}, u32[]{:S(2)}, u32[]{:S(2)}) collective-permute-start(f32[2,6,144,128]{3,2,1,0:T(8,128)S(1)} %get-tuple-element.63.refs_4_), channel_id=1, source_target_pairs={{0,1},{1,4},{2,3},{3,6},{4,5},{5,8},{6,7},{7,10},{8,9},{9,12},{10,... | collective-permute-start | bytes 2654216 | tf_op jit(solution)/shard_map/ppermute | solution.py:728
  80.7 12.8 %forward.3 = (f32[2,6,144,128]{3,2,1,0:T(8,128)S(1)}, f32[2,6,144,128]{3,2,1,0:T(8,128)S(1)}) custom-call(s32[4]{0:T(128)S(1)} %copy-done.2, f32[3,6,144,128]{3,2,1,0:T(8,128)S(1)} %get-tuple-element.56.refs_0_, f32[3,6,144,128]{3,2,1,0:T(8,128)S(1)} %get-tuple-element.57.refs_1_, f32[3,6,144,128]{3,2,1,0:T(8,128)S(1)} %collective-permute-done.2.refs_2_, ...), custom_call_target="tpu_custom_call" | custom-call | flops 13271040000 | bytes 11206672 | tf_op jit(solution)/shard_map/forward/pallas_call | solution.py:376
  93.5 4.3 %collective-permute-start.16 = (f32[2,6,144,128]{3,2,1,0:T(8,128)S(1)}, f32[2,6,144,128]{3,2,1,0:T(8,128)S(1)}, u32[]{:S(2)}, u32[]{:S(2)}) collective-permute-start(f32[2,6,144,128]{3,2,1,0:T(8,128)S(1)} %get-tuple-element.74.refs_4_), channel_id=1, source_target_pairs={{0,1},{1,4},{2,3},{3,6},{4,5},{5,8},{6,7},{7,10},{8,9},{9,12},{10,... | collective-permute-start | bytes 2654216 | tf_op jit(solution)/shard_map/ppermute | solution.py:728
  99.1 12.3 %adjoint.2 = (f32[2,4,128,128]{3,2,1,0:T(8,128)S(1)}, f32[2,4,128,128]{3,2,1,0:T(8,128)S(1)}) custom-call(s32[4]{0:T(128)S(1)} %copy-done.2, f32[3,6,144,128]{3,2,1,0:T(8,128)S(1)} %get-tuple-element.56.refs_0_, f32[3,6,144,128]{3,2,1,0:T(8,128)S(1)} %get-tuple-element.57.refs_1_, f32[3,6,144,128]{3,2,1,0:T(8,128)S(1)} %collective-permute-done.2.refs_2_, ...), custom_call_target="tpu_custom_call" | custom-call | flops 13271040000 | bytes 9895952 | tf_op jit(solution)/shard_map/adjoint/pallas_call | solution.py:376
  112.2 4.0 %collective-permute-start.11 = (f32[2,4,128,128]{3,2,1,0:T(8,128)S(1)}, f32[2,4,128,128]{3,2,1,0:T(8,128)S(1)}, u32[]{:S(2)}, u32[]{:S(2)}) collective-permute-start(f32[2,4,128,128]{3,2,1,0:T(8,128)S(1)} %get-tuple-element.66), channel_id=1, source_target_pairs={{2,0},{0,1},{3,2},{1,3},{6,4},{4,5},{7,6},{5,7},{10,8},{8,9},{11,1... | collective-permute-start | bytes 1572872 | tf_op jit(solution)/shard_map/ppermute | solution.py:770
  116.2 12.3 %adjoint.3 = (f32[2,4,128,128]{3,2,1,0:T(8,128)S(1)}, f32[2,4,128,128]{3,2,1,0:T(8,128)S(1)}) custom-call(s32[4]{0:T(128)S(1)} %copy-done.2, f32[3,6,144,128]{3,2,1,0:T(8,128)S(1)} %get-tuple-element.56.refs_0_, f32[3,6,144,128]{3,2,1,0:T(8,128)S(1)} %get-tuple-element.57.refs_1_, f32[3,6,144,128]{3,2,1,0:T(8,128)S(1)} %collective-permute-done.2.refs_2_, ...), custom_call_target="tpu_custom_call" | custom-call | flops 13271040000 | bytes 9895952 | tf_op jit(solution)/shard_map/adjoint/pallas_call | solution.py:376
  129.3 2.7 %collective-permute-start.19 = (f32[2,4,128,128]{3,2,1,0:T(8,128)S(1)}, f32[2,4,128,128]{3,2,1,0:T(8,128)S(1)}, u32[]{:S(2)}, u32[]{:S(2)}) collective-permute-start(f32[2,4,128,128]{3,2,1,0:T(8,128)S(1)} %get-tuple-element.77), channel_id=1, source_target_pairs={{2,0},{0,1},{3,2},{1,3},{6,4},{4,5},{7,6},{5,7},{10,8},{8,9},{11,1... | collective-permute-start | bytes 1572872 | tf_op jit(solution)/shard_map/ppermute | solution.py:770
  132.0 2.6 %projections.2 = (f32[8,128]{1,0:T(8,128)S(1)}, f32[2,1024,128]{2,1,0:T(8,128)S(1)}, f32[16,1024,128]{2,1,0:T(8,128)S(1)}) custom-call(f32[16,1024,128]{2,1,0:T(8,128)S(1)} %bitcast.14, f32[4,1024,128]{2,1,0:T(8,128)S(1)} %bitcast.9, f32[2,4,128,128]{3,2,1,0:T(8,128)S(1)} %collective-permute-done.10.own_hbm, ...), custom_call_target="tpu_custom_call" | custom-call | flops 1258291200 | bytes 20979712 | tf_op jit(solution)/shard_map/projections/pallas_call | solution.py:376
  134.7 10.9 %collective-permute-done.19.other_hbm = f32[2,4,128,128]{3,2,1,0:T(8,128)S(1)} collective-permute-done((f32[2,4,128,128]{3,2,1,0:T(8,128)S(1)}, f32[2,4,128,128]{3,2,1,0:T(8,128)S(1)}, u32[]{:S(2)}, u32[]{:S(2)}) %collective-permute-start.19) | collective-permute-done | bytes 524320 | tf_op jit(solution)/shard_map/ppermute | solution.py:770
  147.5 21.5 %all_gather.3.parts_ref = f32[128,128]{1,0:T(8,128)S(1)} all-gather(f32[8,128]{1,0:T(8,128)S(1)} %get-tuple-element.79), channel_id=1, replica_groups=mesh['grp'=2,'slab'=16] {'slab'}, dimensions={0}, use_global_device_ids=true | all-gather | bytes 69632 | tf_op jit(solution)/shard_map/all_gather | solution.py:117
  169.0 6.0 %remainder.1 = (f32[4,1024,128]{2,1,0:T(8,128)}, f32[4,16]{1,0:T(4,128)}, f32[8,128]{1,0:T(8,128)S(1)}, s32[1]{0:T(128)}) custom-call(f32[128,128]{1,0:T(8,128)S(1)} %all_gather.3.parts_ref, f32[16,1024,128]{2,1,0:T(8,128)S(1)} %get-tuple-element.68.basis_in.basis_ref, f32[2,1024,128]{2,1,0:T(8,128)S(1)} %get-tuple-element.80.refs_0_, ...), custom_call_target="tpu_custom_call" | custom-call | flops 2516582400 | bytes 12652804 | tf_op jit(solution)/shard_map/remainder/pallas_call | solution.py:376
  (46 shorter events, 21.5 us)
Async XLA Ops:
  3.3 23.9 %collective-permute-start = (f32[12,144,128]{2,1,0:T(8,128)}, f32[12,144,128]{2,1,0:T(8,128)S(1)}, u32[]{:S(2)}, u32[]{:S(2)}) collective-permute-start(f32[12,144,128]{2,1,0:T(8,128)} %get-tuple-element.54), channel_id=1, source_target_pairs={{0,0},{1,2},{2,1},{3,3},{4,4},{5,6},{6,5},{7,7},{8,8},{9,10},{10,9... | collective-permute-start | bytes 2654216 | tf_op jit(solution)/shard_map/ppermute | solution.py:725
  5.1 23.4 %collective-permute-start.1 = (f32[12,144,128]{2,1,0:T(8,128)}, f32[12,144,128]{2,1,0:T(8,128)S(1)}, u32[]{:S(2)}, u32[]{:S(2)}) collective-permute-start(f32[12,144,128]{2,1,0:T(8,128)} %get-tuple-element.55), channel_id=1, source_target_pairs={{0,2},{1,0},{2,3},{3,1},{4,6},{5,4},{6,7},{7,5},{8,10},{9,8},{10,1... | collective-permute-start | bytes 2654216 | tf_op jit(solution)/shard_map/ppermute | solution.py:725
  20.4 15.4 %collective-permute-start.4 = (f32[1216,128]{1,0:T(8,128)}, f32[1216,128]{1,0:T(8,128)S(1)}, u32[]{:S(2)}, u32[]{:S(2)}) collective-permute-start(f32[1216,128]{1,0:T(8,128)} %get-tuple-element.58), channel_id=1, source_target_pairs={{0,0},{1,2},{2,1},{3,3},{4,4},{5,6},{6,5},{7,7},{8,8},{9,10},{10,9... | collective-permute-start | bytes 1867784 | tf_op jit(solution)/shard_map/ppermute | solution.py:725
  22.1 19.7 %collective-permute-start.5 = (f32[1216,128]{1,0:T(8,128)}, f32[1216,128]{1,0:T(8,128)S(1)}, u32[]{:S(2)}, u32[]{:S(2)}) collective-permute-start(f32[1216,128]{1,0:T(8,128)} %get-tuple-element.59), channel_id=1, source_target_pairs={{0,2},{1,0},{2,3},{3,1},{4,6},{5,4},{6,7},{7,5},{8,10},{9,8},{10,1... | collective-permute-start | bytes 1867784 | tf_op jit(solution)/shard_map/ppermute | solution.py:725
  27.2 20.1 %copy-start.3 = (f32[1152,128]{1,0:T(8,128)S(1)}, f32[1152,128]{1,0:T(8,128)}, u32[]{:S(2)}) copy-start(f32[1152,128]{1,0:T(8,128)} %get-tuple-element.71) | copy-start | bytes 1769476
  29.4 32.5 %copy-start.2 = (s32[4]{0:T(128)S(1)}, s32[4]{0:T(128)}, u32[]{:S(2)}) copy-start(s32[4]{0:T(128)} %code_ref.7) | copy-start | bytes 52
  29.4 32.5 %collective-permute-start.2 = (f32[3,6,144,128]{3,2,1,0:T(8,128)S(1)}, f32[3,6,144,128]{3,2,1,0:T(8,128)S(1)}, u32[]{:S(2)}, u32[]{:S(2)}) collective-permute-start(f32[3,6,144,128]{3,2,1,0:T(8,128)S(1)} %get-tuple-element.56.refs_0_), channel_id=1, source_target_pairs={{0,1},{1,4},{2,3},{3,6},{4,5},{5,8},{6,7},{7,10},{8,9},{9,12},{10,... | collective-permute-start | bytes 3981320 | tf_op jit(solution)/shard_map/ppermute | solution.py:728
  32.8 29.1 %collective-permute-start.3 = (f32[3,6,144,128]{3,2,1,0:T(8,128)S(1)}, f32[3,6,144,128]{3,2,1,0:T(8,128)S(1)}, u32[]{:S(2)}, u32[]{:S(2)}) collective-permute-start(f32[3,6,144,128]{3,2,1,0:T(8,128)S(1)} %get-tuple-element.57.refs_1_), channel_id=1, source_target_pairs={{1,0},{4,1},{3,2},{6,3},{5,4},{8,5},{7,6},{10,7},{9,8},{12,9},{11,... | collective-permute-start | bytes 3981320 | tf_op jit(solution)/shard_map/ppermute | solution.py:728
  34.1 13.2 %collective-permute-start.12 = (f32[1152,128]{1,0:T(8,128)}, f32[1152,128]{1,0:T(8,128)S(1)}, u32[]{:S(2)}, u32[]{:S(2)}) collective-permute-start(f32[1152,128]{1,0:T(8,128)} %get-tuple-element.70), channel_id=1, source_target_pairs={{0,0},{1,2},{2,1},{3,3},{4,4},{5,6},{6,5},{7,7},{8,8},{9,10},{10,9... | collective-permute-start | bytes 1769480 | tf_op jit(solution)/shard_map/ppermute | solution.py:725
  42.6 17.7 %collective-permute-start.6 = (f32[2,6,144,128]{3,2,1,0:T(8,128)S(1)}, f32[2,6,144,128]{3,2,1,0:T(8,128)S(1)}, u32[]{:S(2)}, u32[]{:S(2)}) collective-permute-start(f32[2,6,144,128]{3,2,1,0:T(8,128)S(1)} %get-tuple-element.60.refs_4_), channel_id=1, source_target_pairs={{0,1},{1,4},{2,3},{3,6},{4,5},{5,8},{6,7},{7,10},{8,9},{9,12},{10,... | collective-permute-start | bytes 2654216 | tf_op jit(solution)/shard_map/ppermute | solution.py:728
  46.0 15.8 %collective-permute-start.7 = (f32[2,6,144,128]{3,2,1,0:T(8,128)S(1)}, f32[2,6,144,128]{3,2,1,0:T(8,128)S(1)}, u32[]{:S(2)}, u32[]{:S(2)}) collective-permute-start(f32[2,6,144,128]{3,2,1,0:T(8,128)S(1)} %get-tuple-element.61.refs_5_), channel_id=1, source_target_pairs={{1,0},{4,1},{3,2},{6,3},{5,4},{8,5},{7,6},{10,7},{9,8},{12,9},{11,... | collective-permute-start | bytes 2654216 | tf_op jit(solution)/shard_map/ppermute | solution.py:728
  47.3 10.1 %collective-permute-start.13 = (f32[1152,128]{1,0:T(8,128)S(1)}, f32[1152,128]{1,0:T(8,128)S(1)}, u32[]{:S(2)}, u32[]{:S(2)}) collective-permute-start(f32[1152,128]{1,0:T(8,128)S(1)} %copy-done.3), channel_id=1, source_target_pairs={{0,2},{1,0},{2,3},{3,1},{4,6},{5,4},{6,7},{7,5},{8,10},{9,8},{10,1... | collective-permute-start | bytes 1769480 | tf_op jit(solution)/shard_map/ppermute | solution.py:725
  58.2 22.5 %collective-permute-start.14 = (f32[2,6,144,128]{3,2,1,0:T(8,128)S(1)}, f32[2,6,144,128]{3,2,1,0:T(8,128)S(1)}, u32[]{:S(2)}, u32[]{:S(2)}) collective-permute-start(f32[2,6,144,128]{3,2,1,0:T(8,128)S(1)} %get-tuple-element.72.refs_4_), channel_id=1, source_target_pairs={{0,1},{1,4},{2,3},{3,6},{4,5},{5,8},{6,7},{7,10},{8,9},{9,12},{10,... | collective-permute-start | bytes 2654216 | tf_op jit(solution)/shard_map/ppermute | solution.py:728
  60.4 20.4 %collective-permute-start.15 = (f32[2,6,144,128]{3,2,1,0:T(8,128)S(1)}, f32[2,6,144,128]{3,2,1,0:T(8,128)S(1)}, u32[]{:S(2)}, u32[]{:S(2)}) collective-permute-start(f32[2,6,144,128]{3,2,1,0:T(8,128)S(1)} %get-tuple-element.73.refs_5_), channel_id=1, source_target_pairs={{1,0},{4,1},{3,2},{6,3},{5,4},{8,5},{7,6},{10,7},{9,8},{12,9},{11,... | collective-permute-start | bytes 2654216 | tf_op jit(solution)/shard_map/ppermute | solution.py:728
  74.7 24.4 %collective-permute-start.8 = (f32[2,6,144,128]{3,2,1,0:T(8,128)S(1)}, f32[2,6,144,128]{3,2,1,0:T(8,128)S(1)}, u32[]{:S(2)}, u32[]{:S(2)}) collective-permute-start(f32[2,6,144,128]{3,2,1,0:T(8,128)S(1)} %get-tuple-element.63.refs_4_), channel_id=1, source_target_pairs={{0,1},{1,4},{2,3},{3,6},{4,5},{5,8},{6,7},{7,10},{8,9},{9,12},{10,... | collective-permute-start | bytes 2654216 | tf_op jit(solution)/shard_map/ppermute | solution.py:728
  79.4 19.7 %collective-permute-start.9 = (f32[2,6,144,128]{3,2,1,0:T(8,128)S(1)}, f32[2,6,144,128]{3,2,1,0:T(8,128)S(1)}, u32[]{:S(2)}, u32[]{:S(2)}) collective-permute-start(f32[2,6,144,128]{3,2,1,0:T(8,128)S(1)} %get-tuple-element.64.refs_5_), channel_id=1, source_target_pairs={{1,0},{4,1},{3,2},{6,3},{5,4},{8,5},{7,6},{10,7},{9,8},{12,9},{11,... | collective-permute-start | bytes 2654216 | tf_op jit(solution)/shard_map/ppermute | solution.py:728
  93.5 22.7 %collective-permute-start.16 = (f32[2,6,144,128]{3,2,1,0:T(8,128)S(1)}, f32[2,6,144,128]{3,2,1,0:T(8,128)S(1)}, u32[]{:S(2)}, u32[]{:S(2)}) collective-permute-start(f32[2,6,144,128]{3,2,1,0:T(8,128)S(1)} %get-tuple-element.74.refs_4_), channel_id=1, source_target_pairs={{0,1},{1,4},{2,3},{3,6},{4,5},{5,8},{6,7},{7,10},{8,9},{9,12},{10,... | collective-permute-start | bytes 2654216 | tf_op jit(solution)/shard_map/ppermute | solution.py:728
  97.8 18.4 %collective-permute-start.17 = (f32[2,6,144,128]{3,2,1,0:T(8,128)S(1)}, f32[2,6,144,128]{3,2,1,0:T(8,128)S(1)}, u32[]{:S(2)}, u32[]{:S(2)}) collective-permute-start(f32[2,6,144,128]{3,2,1,0:T(8,128)S(1)} %get-tuple-element.75.refs_5_), channel_id=1, source_target_pairs={{1,0},{4,1},{3,2},{6,3},{5,4},{8,5},{7,6},{10,7},{9,8},{12,9},{11,... | collective-permute-start | bytes 2654216 | tf_op jit(solution)/shard_map/ppermute | solution.py:728
  111.5 20.5 %collective-permute-start.10 = (f32[2,4,128,128]{3,2,1,0:T(8,128)S(1)}, f32[2,4,128,128]{3,2,1,0:T(8,128)S(1)}, u32[]{:S(2)}, u32[]{:S(2)}) collective-permute-start(f32[2,4,128,128]{3,2,1,0:T(8,128)S(1)} %get-tuple-element.65), channel_id=1, source_target_pairs={{0,0},{2,1},{1,2},{3,3},{4,4},{6,5},{5,6},{7,7},{8,8},{10,9},{9,10... | collective-permute-start | bytes 1572872 | tf_op jit(solution)/shard_map/ppermute | solution.py:770
  112.2 19.8 %slice-start = ((s8[8388608]{0:T(1024)(128)(4,1)}), s8[4194304]{0:T(1024)(128)(4,1)S(1)}, s32[]{:S(2)}) async-start(s8[8388608]{0:T(1024)(128)(4,1)} %bitcast.12), calls=%async_computation.1 | async-start | bytes 8388608
  112.2 19.8 %copy-start = (f32[4,4,256,128]{3,2,1,0:T(8,128)S(1)}, f32[4,4,256,128]{3,2,1,0:T(8,128)}, u32[]{:S(2)}) copy-start(f32[4,4,256,128]{3,2,1,0:T(8,128)} %refs_2_.3) | copy-start | bytes 6291460
  112.2 19.8 %collective-permute-start.11 = (f32[2,4,128,128]{3,2,1,0:T(8,128)S(1)}, f32[2,4,128,128]{3,2,1,0:T(8,128)S(1)}, u32[]{:S(2)}, u32[]{:S(2)}) collective-permute-start(f32[2,4,128,128]{3,2,1,0:T(8,128)S(1)} %get-tuple-element.66), channel_id=1, source_target_pairs={{2,0},{0,1},{3,2},{1,3},{6,4},{4,5},{7,6},{5,7},{10,8},{8,9},{11,1... | collective-permute-start | bytes 1572872 | tf_op jit(solution)/shard_map/ppermute | solution.py:770
  128.6 6.1 %collective-permute-start.18 = (f32[2,4,128,128]{3,2,1,0:T(8,128)S(1)}, f32[2,4,128,128]{3,2,1,0:T(8,128)S(1)}, u32[]{:S(2)}, u32[]{:S(2)}) collective-permute-start(f32[2,4,128,128]{3,2,1,0:T(8,128)S(1)} %get-tuple-element.76), channel_id=1, source_target_pairs={{0,0},{2,1},{1,2},{3,3},{4,4},{6,5},{5,6},{7,7},{8,8},{10,9},{9,10... | collective-permute-start | bytes 1572872 | tf_op jit(solution)/shard_map/ppermute | solution.py:770
  129.3 16.3 %collective-permute-start.19 = (f32[2,4,128,128]{3,2,1,0:T(8,128)S(1)}, f32[2,4,128,128]{3,2,1,0:T(8,128)S(1)}, u32[]{:S(2)}, u32[]{:S(2)}) collective-permute-start(f32[2,4,128,128]{3,2,1,0:T(8,128)S(1)} %get-tuple-element.77), channel_id=1, source_target_pairs={{2,0},{0,1},{3,2},{1,3},{6,4},{4,5},{7,6},{5,7},{10,8},{8,9},{11,1... | collective-permute-start | bytes 1572872 | tf_op jit(solution)/shard_map/ppermute | solution.py:770
  (2 other events, 39.7 us)
